TPU v7x, 32 devices: a whole 2x2x4 slice. The times are simulated.
32 devices in a mesh: sec: 2 (over x), gx: 8 (over z, y), gy: 2 (over core).
Axes of the slice: x: 2, y: 2, z: 4, core: 2. Of those that a mesh axis runs over, the one named last changes fastest.
Arguments:
- velocity: float32 [2, 3, 32, 64, 256], P('sec', None, None, 'gx', 'gy'), may hold values from -6 to 6
- turbine_cells: int32 [64, 3], replicated, may hold values from 0 to 255, as said below
- fringe_bounds: int32 [2], replicated, may hold values from 48 to 64, as said below
Outputs:
- velocity_next: float32 [2, 3, 32, 64, 256], P('sec', None, 'gx', None, 'gy')
- pressure: float32 [2, 32, 64, 256], P('sec', 'gx', None, 'gy')
Inputs may be any that keep to these rules, and one draw needn't show every extreme that they name: `turbine_cells`: each turbine's streamwise index is below 32 and its vertical index lies from 4 to 27. fringe_bounds[0] < fringe_bounds[1] = 64; the fringe lies in the last quarter of the streamwise columns.
All inputs are finite; a program needn't handle non-finite values.
Results may differ from a plain program's by a relative error of at most 0.00018.
Values sent between devices are 32-bit elements; how exact they have to be, the bound alone decides.
No kernel may reach another device: no remote copies, remote signals or barrier semaphores. Data moves between devices by JAX's collectives and lax.ppermute only.
A program may use at most 64 MiB of HBM per device.

v0:
```python
import jax
import jax.numpy as jnp
from jax import lax
from jax.sharding import PartitionSpec as P

RADIUS = 4


TIME_STEP = 0.05
SMAG_COEFF = 0.1
THRUST_COEFF = 4.0
DRIVING_FORCE = 0.1
FRINGE_BLEND = 0.5
HIGHEST = lax.Precision.HIGHEST


def extended(x, sides, width):
    for axis, dim in sides:
        count, length = (lax.axis_size(axis), x.shape[dim])
        up = [(i, (i + 1) % count) for i in range(count)]
        down = [(j, i) for i, j in up]
        last = lax.slice_in_dim(x, length - width, length, axis=dim)
        initial = lax.slice_in_dim(x, 0, width, axis=dim)
        before = lax.ppermute(last, axis, up)
        after = lax.ppermute(initial, axis, down)
        x = jnp.concatenate([before, x, after], axis=dim)
    return x


def shifted(block, axis, distance):
    devices = range(lax.axis_size(axis))
    route = [(i - distance, i) for i in devices if i - distance in devices]
    return lax.ppermute(block, axis, route)


def cas_table(row_index, column_index, length):
    product = row_index[:, None] * column_index[None, :] % length
    angle = product.astype(jnp.float32) * (2.0 * jnp.pi / length)
    return jnp.cos(angle) + jnp.sin(angle)


def shift_up(values):
    zeros = jnp.zeros_like(values[..., :1, :, :])
    return jnp.concatenate([values[..., 1:, :, :], zeros], axis=-3)


def shift_down(values):
    zeros = jnp.zeros_like(values[..., :1, :, :])
    return jnp.concatenate([zeros, values[..., :-1, :, :]], axis=-3)


def thomas(right_side, eigen_value):
    length = right_side.shape[0]
    inverses = []
    reduced = []
    for level_index in range(length):
        if level_index == 0:
            diagonal = eigen_value - 1.0
        elif level_index == length - 1:
            diagonal = eigen_value - 3.0
        else:
            diagonal = eigen_value - 2.0
        if level_index == 0:
            pivot_now = diagonal
            current = right_side[0] / pivot_now
        else:
            pivot_now = diagonal - inverses[-1]
            current = (right_side[level_index] - reduced[-1]) / pivot_now
        inverses.append(1.0 / pivot_now)
        reduced.append(current)
    solution = [reduced[-1]]
    for level_index in range(length - 2, -1, -1):
        solution.append(reduced[level_index] - inverses[level_index] * solution[-1])
    return jnp.stack(solution[::-1])


def spanwise_derivative(values, sine_y):
    return -sine_y * jnp.roll(jnp.flip(values, axis=-1), 1, axis=-1)


def widened(values):
    return extended(values, (("gx", 1), ("gy", 2)), 1)


def disk_weights(turbine_cells, along_x, along_y, along_z, total_y):
    matches = (along_x[:, None] == turbine_cells[None, :, 0]).astype(jnp.float32)
    offset_y = (along_y[None, :] - turbine_cells[:, 1:2] + total_y // 2) % total_y - total_y // 2
    offset_z = along_z[None, :] - turbine_cells[:, 2:3]
    distance = (
        offset_z[:, :, None] * offset_z[:, :, None] + offset_y[:, None, :] * offset_y[:, None, :]
    )
    inside = (distance <= RADIUS * RADIUS).astype(jnp.float32)
    return jnp.einsum("xt,tzy->zxy", matches, inside, precision=HIGHEST)


def tendency(velocity_now, farm_flag, disk_weight):
    levels, cells_x, cells_y = (velocity_now.shape[1], velocity_now.shape[2], velocity_now.shape[3])
    border = widened(velocity_now.reshape(3 * levels, cells_x, cells_y)).reshape(
        3, levels, cells_x + 2, cells_y + 2
    )
    plus_x = border[:, :, 2:, 1:-1]
    minus_x = border[:, :, :-2, 1:-1]
    plus_y = border[:, :, 1:-1, 2:]
    minus_y = border[:, :, 1:-1, :-2]
    plus_z = shift_up(velocity_now)
    minus_z = shift_down(velocity_now)
    gradients = [0.5 * (plus_x - minus_x), 0.5 * (plus_y - minus_y), 0.5 * (plus_z - minus_z)]
    strain_squares = jnp.zeros_like(velocity_now[0])
    for component in range(3):
        strain_squares = (
            strain_squares + gradients[component][component] * gradients[component][component]
        )
        for direction in range(component + 1, 3):
            shear = 0.5 * (gradients[direction][component] + gradients[component][direction])
            strain_squares = strain_squares + 2.0 * shear * shear
    viscosity = SMAG_COEFF * jnp.sqrt(2.0 * strain_squares)
    visc_border = widened(viscosity)
    visc_plus_x = visc_border[:, 2:, 1:-1]
    visc_minus_x = visc_border[:, :-2, 1:-1]
    visc_plus_y = visc_border[:, 1:-1, 2:]
    visc_minus_y = visc_border[:, 1:-1, :-2]
    visc_plus_z = shift_up(viscosity)
    visc_minus_z = shift_down(viscosity)
    advection = 0.5 * (plus_x[0] * plus_x - minus_x[0] * minus_x)
    advection = advection + 0.5 * (plus_y[1] * plus_y - minus_y[1] * minus_y)
    advection = advection + 0.5 * (plus_z[2] * plus_z - minus_z[2] * minus_z)
    diffusion = 0.5 * (viscosity + visc_plus_x) * (plus_x - velocity_now) - 0.5 * (
        viscosity + visc_minus_x
    ) * (velocity_now - minus_x)
    diffusion = (
        diffusion
        + 0.5 * (viscosity + visc_plus_y) * (plus_y - velocity_now)
        - 0.5 * (viscosity + visc_minus_y) * (velocity_now - minus_y)
    )
    diffusion = (
        diffusion
        + 0.5 * (viscosity + visc_plus_z) * (plus_z - velocity_now)
        - 0.5 * (viscosity + visc_minus_z) * (velocity_now - minus_z)
    )
    changes = diffusion - advection
    streamwise = DRIVING_FORCE - THRUST_COEFF * farm_flag * disk_weight * velocity_now[0] * jnp.abs(
        velocity_now[0]
    )
    return jnp.concatenate([changes[:1] + streamwise[None], changes[1:]], axis=0)


def on_device(velocity, turbine_cells, fringe_bounds):
    initial = velocity[0]
    levels, cells_x, cells_y = (initial.shape[1], initial.shape[2], initial.shape[3])
    total_y = cells_y * lax.axis_size("gy")
    x_anchor = lax.axis_index("gx") * cells_x
    y_anchor = lax.axis_index("gy") * cells_y
    farm_flag = lax.axis_index("sec").astype(jnp.float32)
    along_x = x_anchor + jnp.arange(cells_x, dtype=jnp.int32)
    along_y = y_anchor + jnp.arange(cells_y, dtype=jnp.int32)
    along_z = jnp.arange(levels, dtype=jnp.int32)
    disk_weight = disk_weights(turbine_cells, along_x, along_y, along_z, total_y)
    segment_one = initial + TIME_STEP * tendency(initial, farm_flag, disk_weight)
    segment_two = 0.75 * initial + 0.25 * (
        segment_one + TIME_STEP * tendency(segment_one, farm_flag, disk_weight)
    )
    segment_three = initial / 3.0 + 2.0 / 3.0 * (
        segment_two + TIME_STEP * tendency(segment_two, farm_flag, disk_weight)
    )
    regrouped = lax.all_to_all(segment_three, "gx", split_axis=1, concat_axis=2, tiled=True)
    count_x = regrouped.shape[2]
    quarter = count_x // 4
    cut_at = count_x - quarter
    outlet_part = regrouped[:, :, cut_at:, :]
    upstream = shifted(outlet_part, "sec", 1)
    columns = cut_at + jnp.arange(quarter, dtype=jnp.int32)
    inside = ((columns >= fringe_bounds[0]) & (columns < fringe_bounds[1])).astype(jnp.float32)
    weight = FRINGE_BLEND * farm_flag * inside
    blended_part = outlet_part + weight[:, None] * (upstream - outlet_part)
    regrouped = jnp.concatenate([regrouped[:, :, :cut_at, :], blended_part], axis=2)
    index_x = jnp.arange(count_x, dtype=jnp.int32)
    table_x = cas_table(index_x, index_x, count_x)
    gradient_u = 0.5 * (jnp.roll(regrouped[0], -1, axis=1) - jnp.roll(regrouped[0], 1, axis=1))
    fields = jnp.stack([gradient_u, regrouped[1], regrouped[2]])
    spectral_x = jnp.einsum("kx,czxy->czky", table_x, fields, precision=HIGHEST)
    columns_view = lax.all_to_all(
        lax.all_to_all(spectral_x, "gx", split_axis=2, concat_axis=1, tiled=True),
        "gy",
        split_axis=2,
        concat_axis=3,
        tiled=True,
    )
    slice_width = columns_view.shape[2]
    count_y = columns_view.shape[3]
    index_y = jnp.arange(count_y, dtype=jnp.int32)
    table_y = cas_table(index_y, index_y, count_y)
    spectrum = jnp.einsum("ly,czky->czkl", table_y, columns_view, precision=HIGHEST)
    sine_y = jnp.sin(index_y.astype(jnp.float32) * (2.0 * jnp.pi / count_y))
    source = (
        spectrum[0]
        + spanwise_derivative(spectrum[1], sine_y)
        + 0.5 * (shift_up(spectrum[2]) - shift_down(spectrum[2]))
    )
    wave_x = (
        lax.axis_index("gx") * cells_x
        + lax.axis_index("gy") * slice_width
        + jnp.arange(slice_width, dtype=jnp.int32)
    )
    eigen_value = 2.0 * jnp.cos(wave_x.astype(jnp.float32) * (2.0 * jnp.pi / count_x))[:, None]
    eigen_value = (
        eigen_value
        + 2.0 * jnp.cos(index_y.astype(jnp.float32) * (2.0 * jnp.pi / count_y))[None, :]
        - 4.0
    )
    solved = thomas(source, eigen_value)
    above_level = jnp.concatenate([solved[1:], -solved[-1:]], axis=0)
    below_level = jnp.concatenate([solved[:1], solved[:-1]], axis=0)
    coefficients = jnp.stack(
        [solved, spanwise_derivative(solved, sine_y), 0.5 * (above_level - below_level)]
    )
    physical_y = jnp.einsum("yl,czkl->czky", table_y, coefficients, precision=HIGHEST) * (
        1.0 / count_y
    )
    returned = lax.all_to_all(
        lax.all_to_all(physical_y, "gx", split_axis=1, concat_axis=2, tiled=True),
        "gy",
        split_axis=3,
        concat_axis=2,
        tiled=True,
    )
    group_size = count_x // lax.axis_size("gy")
    wave_back = (
        index_x // slice_width % lax.axis_size("gx") * cells_x
        + index_x // group_size * slice_width
        + index_x % slice_width
    )
    inverse_table = cas_table(index_x, wave_back, count_x)
    physical = jnp.einsum("xp,czpy->czxy", inverse_table, returned, precision=HIGHEST) * (
        1.0 / count_x
    )
    pressure = physical[0]
    gradient_p = 0.5 * (jnp.roll(pressure, -1, axis=1) - jnp.roll(pressure, 1, axis=1))
    velocity_next = regrouped - jnp.stack([gradient_p, physical[1], physical[2]])
    return (velocity_next[None], pressure[None])


def solution(mesh):
    return jax.shard_map(
        on_device,
        mesh=mesh,
        in_specs=(P("sec", None, None, "gx", "gy"), P(), P()),
        out_specs=(P("sec", None, "gx", None, "gy"), P("sec", "gx", None, "gy")),
        check_vma=False,
    )
```

profile of v0, /device:TPU:0, one launch (start us, length us, event | category | flops | bytes accessed | tf_op | source)
XLA Modules:
  0.0 170.4 jit_solution(12400283202980996717)
XLA Ops:
  0.7 1.3 fusion.251
  1.9 3.0 %collective-permute-start = (f32[96,1,128]{2,1,0:T(1,128)S(1)}, f32[96,1,128]{2,1,0:T(1,128)S(1)}, u32[]{:S(2)}, u32[]{:S(2)}) collective-permute-start(f32[96,1,128]{2,1,0:T(1,128)S(1)} %get-tuple-element.107), channel_id=1, source_target_pairs={{0,2},{2,4},{4,6},{6,8},{8,10},{10,12},{12,14},{14,0},{1,3},{3,5},... | collective-permute-start | bytes 147464 | tf_op jit(solution)/shard_map/ppermute | solution.py:24
  5.0 3.1 %collective-permute-start.1 = (f32[96,1,128]{2,1,0:T(1,128)S(1)}, f32[96,1,128]{2,1,0:T(1,128)S(1)}, u32[]{:S(2)}, u32[]{:S(2)}) collective-permute-start(f32[96,1,128]{2,1,0:T(1,128)S(1)} %get-tuple-element.108), channel_id=1, source_target_pairs={{2,0},{4,2},{6,4},{8,6},{10,8},{12,10},{14,12},{0,14},{3,1},{5,3},... | collective-permute-start | bytes 147464 | tf_op jit(solution)/shard_map/ppermute | solution.py:25
  8.1 1.2 fusion.250
  9.5 0.6 collective-permute-done
  12.8 1.1 pad_maximum_fusion
  14.5 4.8 %collective-permute-start.4 = (f32[32,1,128]{2,1,0:T(1,128)S(1)}, f32[32,1,128]{2,1,0:T(1,128)S(1)}, u32[]{:S(2)}, u32[]{:S(2)}) collective-permute-start(f32[32,1,128]{2,1,0:T(1,128)S(1)} %get-tuple-element.150), channel_id=1, source_target_pairs={{2,0},{4,2},{6,4},{8,6},{10,8},{12,10},{14,12},{0,14},{3,1},{5,3},... | collective-permute-start | bytes 49160 | tf_op jit(solution)/shard_map/ppermute | solution.py:25
  19.5 1.3 collective-permute-done.4
  20.8 5.0 %collective-permute-done.5 = f32[32,1,128]{2,1,0:T(1,128)S(1)} collective-permute-done((f32[32,1,128]{2,1,0:T(1,128)S(1)}, f32[32,1,128]{2,1,0:T(1,128)S(1)}, u32[]{:S(2)}, u32[]{:S(2)}) %collective-permute-start.5) | collective-permute-done | bytes 16416 | tf_op jit(solution)/shard_map/ppermute | solution.py:24
  26.5 1.0 collective-permute-done.6
  28.2 0.6 multiply_subtract_fusion.2
  28.8 1.1 slice_add_fusion.8
  30.2 4.7 %collective-permute-start.9 = (f32[96,1,128]{2,1,0:T(1,128)S(1)}, f32[96,1,128]{2,1,0:T(1,128)S(1)}, u32[]{:S(2)}, u32[]{:S(2)}) collective-permute-start(f32[96,1,128]{2,1,0:T(1,128)S(1)} %get-tuple-element.102), channel_id=1, source_target_pairs={{2,0},{4,2},{6,4},{8,6},{10,8},{12,10},{14,12},{0,14},{3,1},{5,3},... | collective-permute-start | bytes 147464 | tf_op jit(solution)/shard_map/ppermute | solution.py:25
  35.0 0.7 fusion.58
  35.7 1.3 collective-permute-done.8
  37.0 0.6 copy-done.7
  37.6 0.6 copy-done.8
  38.4 1.2 fusion.243
  39.6 1.4 copy.114
  41.7 0.7 fusion.59
  42.8 1.3 copy.117
  44.1 2.3 %pad_maximum_fusion.1 = f32[96,10,130]{2,1,0:T(8,128)S(1)} fusion(f32[96,10,1]{2,1,0:T(8,128)} %copy.117, f32[96,1,128]{2,1,0:T(1,128)} %copy-done.8, f32[96,8,128]{2,1,0:T(8,128)S(1)} %bitcast_add_fusion.1, f32[96,1,128]{2,1,0:T(1,128)} %copy-done.7, f32[96,10,1]{2,1,0:T(8,128)S(1)} %copy.116), kind=kLoop, calls=%fused_computation.1 | loop fusion | flops 499200 | bytes 998400 | tf_op jit(solution)/shard_map/concatenate | solution.py:26
  46.9 4.2 %collective-permute-start.12 = (f32[32,1,128]{2,1,0:T(1,128)S(1)}, f32[32,1,128]{2,1,0:T(1,128)S(1)}, u32[]{:S(2)}, u32[]{:S(2)}) collective-permute-start(f32[32,1,128]{2,1,0:T(1,128)S(1)} %get-tuple-element.146), channel_id=1, source_target_pairs={{2,0},{4,2},{6,4},{8,6},{10,8},{12,10},{14,12},{0,14},{3,1},{5,3},... | collective-permute-start | bytes 49160 | tf_op jit(solution)/shard_map/ppermute | solution.py:25
  51.3 1.3 collective-permute-done.12
  52.5 5.0 %collective-permute-done.13 = f32[32,1,128]{2,1,0:T(1,128)S(1)} collective-permute-done((f32[32,1,128]{2,1,0:T(1,128)S(1)}, f32[32,1,128]{2,1,0:T(1,128)S(1)}, u32[]{:S(2)}, u32[]{:S(2)}) %collective-permute-start.13) | collective-permute-done | bytes 16416 | tf_op jit(solution)/shard_map/ppermute | solution.py:24
  58.3 1.0 collective-permute-done.14
  61.3 4.7 %collective-permute-start.17 = (f32[96,1,128]{2,1,0:T(1,128)S(1)}, f32[96,1,128]{2,1,0:T(1,128)S(1)}, u32[]{:S(2)}, u32[]{:S(2)}) collective-permute-start(f32[96,1,128]{2,1,0:T(1,128)S(1)} %get-tuple-element.96), channel_id=1, source_target_pairs={{2,0},{4,2},{6,4},{8,6},{10,8},{12,10},{14,12},{0,14},{3,1},{5,3},... | collective-permute-start | bytes 147464 | tf_op jit(solution)/shard_map/ppermute | solution.py:25
  66.1 0.7 fusion.60
  66.7 1.3 collective-permute-done.16
  68.2 1.2 fusion.242
  69.5 1.4 copy.118
  71.6 0.7 fusion.61
  72.7 1.3 copy.121
  74.0 2.2 %pad_maximum_fusion.2 = f32[96,10,130]{2,1,0:T(8,128)S(1)} fusion(f32[96,10,1]{2,1,0:T(8,128)} %copy.121, f32[96,1,128]{2,1,0:T(1,128)S(1)} %collective-permute-done.17, f32[96,8,128]{2,1,0:T(8,128)S(1)} %fusion.20, f32[96,1,128]{2,1,0:T(1,128)S(1)} %collective-permute-done.16, f32[96,10,1]{2,1,0:T(8,128)S(1)} %copy.120), kind=kLoop, calls=%fused_computation.2 | loop fusion | flops 499200 | bytes 998400 | tf_op jit(solution)/shard_map/concatenate | solution.py:26
  76.8 4.8 %collective-permute-start.20 = (f32[32,1,128]{2,1,0:T(1,128)S(1)}, f32[32,1,128]{2,1,0:T(1,128)S(1)}, u32[]{:S(2)}, u32[]{:S(2)}) collective-permute-start(f32[32,1,128]{2,1,0:T(1,128)S(1)} %get-tuple-element.142), channel_id=1, source_target_pairs={{2,0},{4,2},{6,4},{8,6},{10,8},{12,10},{14,12},{0,14},{3,1},{5,3},... | collective-permute-start | bytes 49160 | tf_op jit(solution)/shard_map/ppermute | solution.py:25
  81.7 1.3 collective-permute-done.20
  83.0 5.0 %collective-permute-done.21 = f32[32,1,128]{2,1,0:T(1,128)S(1)} collective-permute-done((f32[32,1,128]{2,1,0:T(1,128)S(1)}, f32[32,1,128]{2,1,0:T(1,128)S(1)}, u32[]{:S(2)}, u32[]{:S(2)}) %collective-permute-start.21) | collective-permute-done | bytes 16416 | tf_op jit(solution)/shard_map/ppermute | solution.py:24
  88.8 1.0 collective-permute-done.22
  91.5 0.8 copy.122
  92.3 3.5 %all-to-all-start = ((f32[3,32,8,128]{3,2,0,1:T(8,128)}), f32[3,32,8,128]{3,2,0,1:T(8,128)S(1)}, u32[]{:S(2)}, u32[]{:S(2)}) async-start(f32[3,32,8,128]{3,2,0,1:T(8,128)} %copy.122), calls=%async_computation | async-start | bytes 786432 | tf_op jit(solution)/shard_map/all_to_all | solution.py:165
  95.8 0.6 fusion.261
  96.4 1.3 and_select_fusion.4
  97.6 10.3 %all-to-all-done = f32[3,32,8,128]{3,2,0,1:T(8,128)S(1)} async-done(((f32[3,32,8,128]{3,2,0,1:T(8,128)}), f32[3,32,8,128]{3,2,0,1:T(8,128)S(1)}, u32[]{:S(2)}, u32[]{:S(2)}) %all-to-all-start) | async-done | bytes 393248 | tf_op jit(solution)/shard_map/all_to_all | solution.py:165
  108.0 3.5 %collective-permute-start.24 = (f32[3,4,16,128]{3,2,1,0:T(8,128)S(1)}, f32[3,4,16,128]{3,2,1,0:T(8,128)S(1)}, u32[]{:S(2)}, u32[]{:S(2)}) collective-permute-start(f32[3,4,16,128]{3,2,1,0:T(8,128)S(1)} %slice.865), channel_id=1, source_target_pairs={{0,16},{1,17},{2,18},{3,19},{4,20},{5,21},{6,22},{7,23},{8,24},{9,... | collective-permute-start | bytes 294920 | tf_op jit(solution)/shard_map/ppermute | solution.py:33
  111.5 2.1 %collective-permute-done.24 = f32[3,4,16,128]{3,2,1,0:T(8,128)S(1)} collective-permute-done((f32[3,4,16,128]{3,2,1,0:T(8,128)S(1)}, f32[3,4,16,128]{3,2,1,0:T(8,128)S(1)}, u32[]{:S(2)}, u32[]{:S(2)}) %collective-permute-start.24) | collective-permute-done | bytes 98336 | tf_op jit(solution)/shard_map/ppermute | solution.py:33
  113.9 0.6 convolution_bitcast_fusion
  114.5 1.0 copy.126
  115.5 3.7 %all-to-all-start.1 = ((f32[3,4,64,128]{3,1,0,2:T(4,128)}), f32[3,4,64,128]{3,1,0,2:T(4,128)S(1)}, u32[]{:S(2)}, u32[]{:S(2)}) async-start(f32[3,4,64,128]{3,1,0,2:T(4,128)} %copy.126), calls=%async_computation.1 | async-start | bytes 786432 | tf_op jit(solution)/shard_map/all_to_all | solution.py:182
  119.3 10.8 %all-to-all-done.1 = f32[3,4,64,128]{3,1,0,2:T(4,128)S(1)} async-done(((f32[3,4,64,128]{3,1,0,2:T(4,128)}), f32[3,4,64,128]{3,1,0,2:T(4,128)S(1)}, u32[]{:S(2)}, u32[]{:S(2)}) %all-to-all-start.1) | async-done | bytes 393248 | tf_op jit(solution)/shard_map/all_to_all | solution.py:182
  130.3 4.0 %all_to_all.90 = f32[3,32,8,128]{3,1,0,2:T(8,128)S(1)} all-to-all(f32[3,32,8,128]{3,1,0,2:T(8,128)S(1)} %copy.129), channel_id=1, replica_groups=mesh['sec'=2,'gx'=8,'gy'=2] {'gy'}, dimensions={2} | all-to-all | bytes 786432 | tf_op jit(solution)/shard_map/all_to_all | solution.py:181
  135.0 1.5 fusion.25
  139.3 1.5 convolution_multiply_fusion.1
  140.8 1.0 copy.134
  141.8 3.7 %all-to-all-start.3 = ((f32[3,32,4,256]{3,2,0,1:T(4,128)}), f32[3,32,4,256]{3,2,0,1:T(4,128)S(1)}, u32[]{:S(2)}, u32[]{:S(2)}) async-start(f32[3,32,4,256]{3,2,0,1:T(4,128)} %copy.134), calls=%async_computation.3 | async-start | bytes 786432 | tf_op jit(solution)/shard_map/all_to_all | solution.py:220
  145.5 12.1 %all-to-all-done.3 = f32[3,32,4,256]{3,2,0,1:T(4,128)S(1)} async-done(((f32[3,32,4,256]{3,2,0,1:T(4,128)}), f32[3,32,4,256]{3,2,0,1:T(4,128)S(1)}, u32[]{:S(2)}, u32[]{:S(2)}) %all-to-all-start.3) | async-done | bytes 393248 | tf_op jit(solution)/shard_map/all_to_all | solution.py:220
  157.7 0.8 copy.136
  158.5 1.1 reshape.2847
  159.6 4.0 %all_to_all.91 = f32[2,1,49152]{2,1,0:T(1,128)S(1)} all-to-all(f32[2,1,49152]{2,1,0:T(1,128)S(1)} %reshape.2847), channel_id=1, replica_groups=mesh['sec'=2,'gx'=8,'gy'=2] {'gy'}, dimensions={0} | all-to-all | bytes 786432 | tf_op jit(solution)/shard_map/all_to_all | solution.py:219
  164.1 1.9 %reduce = f32[2,49152]{1,0:T(2,128)S(1)} reduce(f32[2,1,49152]{2,1,0:T(1,128)S(1)} %all_to_all.91, f32[]{:T(128)} %broadcast.7149), dimensions={1}, to_apply=%all_to_all.81.reduce_sub_computation | reduce | bytes 786436 | tf_op jit(solution)/shard_map/all_to_all | solution.py:219
  166.0 0.9 reshape.2848
  166.9 1.1 copy.145
  168.1 0.6 fusion
  168.9 0.7 slice.910
  169.6 0.8 maximum_subtract_fusion
  (153 shorter events, 19.1 us)
Async XLA Ops:
  0.6 9.5 %copy-start = (f32[1,3,32,8,128]{4,3,2,1,0:T(8,128)S(1)}, f32[1,3,32,8,128]{4,3,2,1,0:T(8,128)}, u32[]{:S(2)}) copy-start(f32[1,3,32,8,128]{4,3,2,1,0:T(8,128)} %param.3) | copy-start | bytes 1179652
  0.6 8.7 %copy-start.10 = (s32[64,3]{0,1:T(4,128)S(1)}, s32[64,3]{0,1:T(4,128)}, u32[]{:S(2)}) copy-start(s32[64,3]{0,1:T(4,128)} %param.4) | copy-start | bytes 2308
  1.9 8.2 %collective-permute-start = (f32[96,1,128]{2,1,0:T(1,128)S(1)}, f32[96,1,128]{2,1,0:T(1,128)S(1)}, u32[]{:S(2)}, u32[]{:S(2)}) collective-permute-start(f32[96,1,128]{2,1,0:T(1,128)S(1)} %get-tuple-element.107), channel_id=1, source_target_pairs={{0,2},{2,4},{4,6},{6,8},{8,10},{10,12},{12,14},{14,0},{1,3},{3,5},... | collective-permute-start | bytes 147464 | tf_op jit(solution)/shard_map/ppermute | solution.py:24
  5.0 5.1 %collective-permute-start.1 = (f32[96,1,128]{2,1,0:T(1,128)S(1)}, f32[96,1,128]{2,1,0:T(1,128)S(1)}, u32[]{:S(2)}, u32[]{:S(2)}) collective-permute-start(f32[96,1,128]{2,1,0:T(1,128)S(1)} %get-tuple-element.108), channel_id=1, source_target_pairs={{2,0},{4,2},{6,4},{8,6},{10,8},{12,10},{14,12},{0,14},{3,1},{5,3},... | collective-permute-start | bytes 147464 | tf_op jit(solution)/shard_map/ppermute | solution.py:25
  10.8 1.2 collective-permute-start.2
  11.1 1.3 collective-permute-start.3
  14.5 6.2 %collective-permute-start.4 = (f32[32,1,128]{2,1,0:T(1,128)S(1)}, f32[32,1,128]{2,1,0:T(1,128)S(1)}, u32[]{:S(2)}, u32[]{:S(2)}) collective-permute-start(f32[32,1,128]{2,1,0:T(1,128)S(1)} %get-tuple-element.150), channel_id=1, source_target_pairs={{2,0},{4,2},{6,4},{8,6},{10,8},{12,10},{14,12},{0,14},{3,1},{5,3},... | collective-permute-start | bytes 49160 | tf_op jit(solution)/shard_map/ppermute | solution.py:25
  19.3 6.4 %collective-permute-start.5 = (f32[32,1,128]{2,1,0:T(1,128)S(1)}, f32[32,1,128]{2,1,0:T(1,128)S(1)}, u32[]{:S(2)}, u32[]{:S(2)}) collective-permute-start(f32[32,1,128]{2,1,0:T(1,128)S(1)} %get-tuple-element.149), channel_id=1, source_target_pairs={{0,2},{2,4},{4,6},{6,8},{8,10},{10,12},{12,14},{14,0},{1,3},{3,5},... | collective-permute-start | bytes 49160 | tf_op jit(solution)/shard_map/ppermute | solution.py:24
  25.9 1.6 collective-permute-start.6
  26.0 1.9 %collective-permute-start.7 = (f32[32,10,1]{2,1,0:T(8,128)S(1)}, f32[32,10,1]{2,1,0:T(8,128)S(1)}, u32[]{:S(2)}, u32[]{:S(2)}) collective-permute-start(f32[32,10,1]{2,1,0:T(8,128)S(1)} %get-tuple-element.114), channel_id=1, source_target_pairs={{0,1},{1,0},{2,3},{3,2},{4,5},{5,4},{6,7},{7,6},{8,9},{9,8},{10,11... | collective-permute-start | bytes 3848 | tf_op jit(solution)/shard_map/ppermute | solution.py:24
  30.2 6.8 %collective-permute-start.8 = (f32[96,1,128]{2,1,0:T(1,128)S(1)}, f32[96,1,128]{2,1,0:T(1,128)S(1)}, u32[]{:S(2)}, u32[]{:S(2)}) collective-permute-start(f32[96,1,128]{2,1,0:T(1,128)S(1)} %get-tuple-element.101), channel_id=1, source_target_pairs={{0,2},{2,4},{4,6},{6,8},{8,10},{10,12},{12,14},{14,0},{1,3},{3,5},... | collective-permute-start | bytes 147464 | tf_op jit(solution)/shard_map/ppermute | solution.py:24
  30.2 6.8 %collective-permute-start.9 = (f32[96,1,128]{2,1,0:T(1,128)S(1)}, f32[96,1,128]{2,1,0:T(1,128)S(1)}, u32[]{:S(2)}, u32[]{:S(2)}) collective-permute-start(f32[96,1,128]{2,1,0:T(1,128)S(1)} %get-tuple-element.102), channel_id=1, source_target_pairs={{2,0},{4,2},{6,4},{8,6},{10,8},{12,10},{14,12},{0,14},{3,1},{5,3},... | collective-permute-start | bytes 147464 | tf_op jit(solution)/shard_map/ppermute | solution.py:25
  37.0 0.6 copy-start.7
  37.6 0.6 copy-start.8
  40.9 1.5 collective-permute-start.10
  41.2 1.6 collective-permute-start.11
  46.9 5.6 %collective-permute-start.12 = (f32[32,1,128]{2,1,0:T(1,128)S(1)}, f32[32,1,128]{2,1,0:T(1,128)S(1)}, u32[]{:S(2)}, u32[]{:S(2)}) collective-permute-start(f32[32,1,128]{2,1,0:T(1,128)S(1)} %get-tuple-element.146), channel_id=1, source_target_pairs={{2,0},{4,2},{6,4},{8,6},{10,8},{12,10},{14,12},{0,14},{3,1},{5,3},... | collective-permute-start | bytes 49160 | tf_op jit(solution)/shard_map/ppermute | solution.py:25
  51.1 6.4 %collective-permute-start.13 = (f32[32,1,128]{2,1,0:T(1,128)S(1)}, f32[32,1,128]{2,1,0:T(1,128)S(1)}, u32[]{:S(2)}, u32[]{:S(2)}) collective-permute-start(f32[32,1,128]{2,1,0:T(1,128)S(1)} %get-tuple-element.145), channel_id=1, source_target_pairs={{0,2},{2,4},{4,6},{6,8},{8,10},{10,12},{12,14},{14,0},{1,3},{3,5},... | collective-permute-start | bytes 49160 | tf_op jit(solution)/shard_map/ppermute | solution.py:24
  57.6 2.4 %copy-start.1 = (f32[32,8,128]{2,1,0:T(8,128)S(1)}, f32[32,8,128]{2,1,0:T(8,128)}, u32[]{:S(2)}) copy-start(f32[32,8,128]{2,1,0:T(8,128)} %fusion.58) | copy-start | bytes 393220
  57.6 2.4 %copy-start.3 = (f32[32,8,128]{2,1,0:T(8,128)S(1)}, f32[32,8,128]{2,1,0:T(8,128)}, u32[]{:S(2)}) copy-start(f32[32,8,128]{2,1,0:T(8,128)} %fusion.59) | copy-start | bytes 393220
  57.7 1.6 collective-permute-start.14
  57.8 1.9 %collective-permute-start.15 = (f32[32,10,1]{2,1,0:T(8,128)S(1)}, f32[32,10,1]{2,1,0:T(8,128)S(1)}, u32[]{:S(2)}, u32[]{:S(2)}) collective-permute-start(f32[32,10,1]{2,1,0:T(8,128)S(1)} %get-tuple-element.112), channel_id=1, source_target_pairs={{0,1},{1,0},{2,3},{3,2},{4,5},{5,4},{6,7},{7,6},{8,9},{9,8},{10,11... | collective-permute-start | bytes 3848 | tf_op jit(solution)/shard_map/ppermute | solution.py:24
  60.0 0.9 copy-start.5
  61.2 6.8 %collective-permute-start.16 = (f32[96,1,128]{2,1,0:T(1,128)S(1)}, f32[96,1,128]{2,1,0:T(1,128)S(1)}, u32[]{:S(2)}, u32[]{:S(2)}) collective-permute-start(f32[96,1,128]{2,1,0:T(1,128)S(1)} %get-tuple-element.95), channel_id=1, source_target_pairs={{0,2},{2,4},{4,6},{6,8},{8,10},{10,12},{12,14},{14,0},{1,3},{3,5},... | collective-permute-start | bytes 147464 | tf_op jit(solution)/shard_map/ppermute | solution.py:24
  61.3 6.8 %collective-permute-start.17 = (f32[96,1,128]{2,1,0:T(1,128)S(1)}, f32[96,1,128]{2,1,0:T(1,128)S(1)}, u32[]{:S(2)}, u32[]{:S(2)}) collective-permute-start(f32[96,1,128]{2,1,0:T(1,128)S(1)} %get-tuple-element.96), channel_id=1, source_target_pairs={{2,0},{4,2},{6,4},{8,6},{10,8},{12,10},{14,12},{0,14},{3,1},{5,3},... | collective-permute-start | bytes 147464 | tf_op jit(solution)/shard_map/ppermute | solution.py:25
  70.8 1.5 collective-permute-start.18
  71.1 1.6 collective-permute-start.19
  76.8 6.2 %collective-permute-start.20 = (f32[32,1,128]{2,1,0:T(1,128)S(1)}, f32[32,1,128]{2,1,0:T(1,128)S(1)}, u32[]{:S(2)}, u32[]{:S(2)}) collective-permute-start(f32[32,1,128]{2,1,0:T(1,128)S(1)} %get-tuple-element.142), channel_id=1, source_target_pairs={{2,0},{4,2},{6,4},{8,6},{10,8},{12,10},{14,12},{0,14},{3,1},{5,3},... | collective-permute-start | bytes 49160 | tf_op jit(solution)/shard_map/ppermute | solution.py:25
  81.6 6.4 %collective-permute-start.21 = (f32[32,1,128]{2,1,0:T(1,128)S(1)}, f32[32,1,128]{2,1,0:T(1,128)S(1)}, u32[]{:S(2)}, u32[]{:S(2)}) collective-permute-start(f32[32,1,128]{2,1,0:T(1,128)S(1)} %get-tuple-element.141), channel_id=1, source_target_pairs={{0,2},{2,4},{4,6},{6,8},{8,10},{10,12},{12,14},{14,0},{1,3},{3,5},... | collective-permute-start | bytes 49160 | tf_op jit(solution)/shard_map/ppermute | solution.py:24
  88.0 2.4 %copy-start.2 = (f32[32,8,128]{2,1,0:T(8,128)S(1)}, f32[32,8,128]{2,1,0:T(8,128)}, u32[]{:S(2)}) copy-start(f32[32,8,128]{2,1,0:T(8,128)} %fusion.60) | copy-start | bytes 393220
  88.1 2.4 %copy-start.4 = (f32[32,8,128]{2,1,0:T(8,128)S(1)}, f32[32,8,128]{2,1,0:T(8,128)}, u32[]{:S(2)}) copy-start(f32[32,8,128]{2,1,0:T(8,128)} %fusion.61) | copy-start | bytes 393220
  88.2 1.6 collective-permute-start.22
  88.3 1.9 %collective-permute-start.23 = (f32[32,10,1]{2,1,0:T(8,128)S(1)}, f32[32,10,1]{2,1,0:T(8,128)S(1)}, u32[]{:S(2)}, u32[]{:S(2)}) collective-permute-start(f32[32,10,1]{2,1,0:T(8,128)S(1)} %get-tuple-element.110), channel_id=1, source_target_pairs={{0,1},{1,0},{2,3},{3,2},{4,5},{5,4},{6,7},{7,6},{8,9},{9,8},{10,11... | collective-permute-start | bytes 3848 | tf_op jit(solution)/shard_map/ppermute | solution.py:24
  90.4 0.9 copy-start.6
  91.4 4.4 %copy-start.9 = (s32[2]{0:T(128)S(1)}, s32[2]{0:T(128)}, u32[]{:S(2)}) copy-start(s32[2]{0:T(128)} %param.5) | copy-start | bytes 28
  92.3 15.6 %all-to-all-start = ((f32[3,32,8,128]{3,2,0,1:T(8,128)}), f32[3,32,8,128]{3,2,0,1:T(8,128)S(1)}, u32[]{:S(2)}, u32[]{:S(2)}) async-start(f32[3,32,8,128]{3,2,0,1:T(8,128)} %copy.122), calls=%async_computation | async-start | bytes 786432 | tf_op jit(solution)/shard_map/all_to_all | solution.py:165
  108.0 5.7 %collective-permute-start.24 = (f32[3,4,16,128]{3,2,1,0:T(8,128)S(1)}, f32[3,4,16,128]{3,2,1,0:T(8,128)S(1)}, u32[]{:S(2)}, u32[]{:S(2)}) collective-permute-start(f32[3,4,16,128]{3,2,1,0:T(8,128)S(1)} %slice.865), channel_id=1, source_target_pairs={{0,16},{1,17},{2,18},{3,19},{4,20},{5,21},{6,22},{7,23},{8,24},{9,... | collective-permute-start | bytes 294920 | tf_op jit(solution)/shard_map/ppermute | solution.py:33
  115.5 14.6 %all-to-all-start.1 = ((f32[3,4,64,128]{3,1,0,2:T(4,128)}), f32[3,4,64,128]{3,1,0,2:T(4,128)S(1)}, u32[]{:S(2)}, u32[]{:S(2)}) async-start(f32[3,4,64,128]{3,1,0,2:T(4,128)} %copy.126), calls=%async_computation.1 | async-start | bytes 786432 | tf_op jit(solution)/shard_map/all_to_all | solution.py:182
  141.8 15.8 %all-to-all-start.3 = ((f32[3,32,4,256]{3,2,0,1:T(4,128)}), f32[3,32,4,256]{3,2,0,1:T(4,128)S(1)}, u32[]{:S(2)}, u32[]{:S(2)}) async-start(f32[3,32,4,256]{3,2,0,1:T(4,128)} %copy.134), calls=%async_computation.3 | async-start | bytes 786432 | tf_op jit(solution)/shard_map/all_to_all | solution.py:220
where the time goes:
time: 171 us; the launch traced here: 170 us
  waiting for transfers between devices  61.9 us (36%)
  starting transfers between devices  47 us (27%)
  local copies, waits for them, and re-layouts  30.2 us (18%)
  other arithmetic  16.1 us (9%)
  blocking collectives  8.1 us (5%)
  matrix products  5.45 us (3%)
    ppermute x12, starting transfers between devices, extended(): after = lax.ppermute(initial, axis, down)  28 us
    ppermute x12, waiting for transfers between devices, extended(): before = lax.ppermute(last, axis, up)  19.8 us
    all_to_all x1, waiting for transfers between devices, on_device(): lax.all_to_all(physical_y, 'gx', split_axis=1, concat_axis=2, tiled=True)  12.1 us
    all_to_all x1, waiting for transfers between devices, on_device(): lax.all_to_all(spectral_x, 'gx', split_axis=2, concat_axis=1, tiled=True)  10.8 us
    all_to_all x1, waiting for transfers between devices, on_device(): lax.all_to_all(segment_three, 'gx', split_axis=1, concat_axis=2, tiled=True)  10.3 us
    slice x12, local copies, waits for them, and re-layouts, extended(): last = lax.slice_in_dim(x, length - width, length, axis=dim)  7.13 us
    ppermute x12, waiting for transfers between devices, extended(): after = lax.ppermute(initial, axis, down)  6.85 us
    concatenate x9, other arithmetic, extended(): x = jnp.concatenate([before, x, after], axis=dim)  6.19 us
  transfers between devices with their start and end apart: 28, of which 20 were waited for; matrix products, arithmetic and copies ran while one was open for 5% of the time, Pallas kernels for 0%

commit v1 on v0

--- a/solution.py
+++ b/solution.py
@@ -1,6 +1,11 @@
+import functools
+
 import jax
 import jax.numpy as jnp
+import numpy as np
 from jax import lax
+from jax.experimental import pallas as pl
+from jax.experimental.pallas import tpu as pltpu
 from jax.sharding import PartitionSpec as P
 
 RADIUS = 4
@@ -12,6 +17,11 @@
 DRIVING_FORCE = 0.1
 FRINGE_BLEND = 0.5
 HIGHEST = lax.Precision.HIGHEST
+STAGES = 3
+REACH = 2 * STAGES + 1
+LANES = 128
+ROWS = 8
+VMEM_BYTES = 48 * 1024 * 1024
 
 
 def extended(x, sides, width):
@@ -144,7 +154,7 @@
     return jnp.concatenate([changes[:1] + streamwise[None], changes[1:]], axis=0)
 
 
-def on_device(velocity, turbine_cells, fringe_bounds):
+def general_plan(velocity, turbine_cells, fringe_bounds):
     initial = velocity[0]
     levels, cells_x, cells_y = (initial.shape[1], initial.shape[2], initial.shape[3])
     total_y = cells_y * lax.axis_size("gy")
@@ -239,6 +249,426 @@
     return (velocity_next[None], pressure[None])
 
 
+def dot(left, right):
+    return jnp.dot(left, right, precision=HIGHEST, preferred_element_type=jnp.float32)
+
+
+def swap_blocks(arrays, width):
+    arrays = list(arrays)
+    block = lax.broadcasted_iota(jnp.int32, arrays[0].shape, 1) // width
+    step = 1
+    while step < len(arrays):
+        low = (block // step) % 2 == 0
+        for index in range(len(arrays)):
+            if (index // step) % 2 == 0:
+                first, second = arrays[index], arrays[index + step]
+                arrays[index] = jnp.where(low, first, pltpu.roll(second, step * width, 1))
+                arrays[index + step] = jnp.where(
+                    low, pltpu.roll(first, LANES - step * width, 1), second
+                )
+        step *= 2
+    return arrays
+
+
+def advance_kernel(
+    total_x,
+    meta,
+    own_here,
+    own_there,
+    left_here,
+    left_there,
+    right_here,
+    right_there,
+    thrust,
+    table_y,
+    table_z,
+    moved,
+    spectra,
+    start,
+    stage_a,
+    stage_b,
+    viscosity,
+    source,
+    columns_out,
+    modes,
+):
+    cells_x, _, levels, half = own_here.shape
+    width = 2 * half
+    level = lax.broadcasted_iota(jnp.int32, (levels, width), 0)
+    top = level == levels - 1
+    bottom = level == 0
+
+    for first, here, there in (
+        (0, left_here, left_there),
+        (REACH, own_here, own_there),
+        (REACH + cells_x, right_here, right_there),
+    ):
+        start[pl.ds(first, here.shape[0]), :, :, :half] = here[...]
+        start[pl.ds(first, here.shape[0]), :, :, half:] = there[...]
+
+    def next_y(f):
+        return pltpu.roll(f, width - 1, 1)
+
+    def last_y(f):
+        return pltpu.roll(f, 1, 1)
+
+    def next_z(f):
+        return jnp.where(top, 0.0, pltpu.roll(f, levels - 1, 0))
+
+    def last_z(f):
+        return jnp.where(bottom, 0.0, pltpu.roll(f, 1, 0))
+
+    def set_viscosity(now, first, end):
+        def column(i, carry):
+            here = [now[i, c] for c in range(3)]
+            d_x = [now[i + 1, c] - now[i - 1, c] for c in range(3)]
+            d_y = [next_y(f) - last_y(f) for f in here]
+            d_z = [next_z(f) - last_z(f) for f in here]
+            diagonal = d_x[0] * d_x[0] + d_y[1] * d_y[1] + d_z[2] * d_z[2]
+            xy = d_x[1] + d_y[0]
+            xz = d_x[2] + d_z[0]
+            yz = d_y[2] + d_z[1]
+            total = (diagonal + diagonal) + (xy * xy + xz * xz + yz * yz)
+            viscosity[i] = (0.5 * SMAG_COEFF) * jnp.sqrt(total)
+            return carry
+
+        lax.fori_loop(first, end, column, 0)
+
+    def face_x(now, i):
+        here = [now[i, c] for c in range(3)]
+        after = [now[i + 1, c] for c in range(3)]
+        both = viscosity[i] + viscosity[i + 1]
+        return [
+            both * (after[c] - here[c]) - (here[0] * here[c] + after[0] * after[c])
+            for c in range(3)
+        ]
+
+    def advance(now, then, first, end, keep, gain):
+        def column(i, before):
+            here = [now[i, c] for c in range(3)]
+            eddy = viscosity[i]
+            ahead = face_x(now, i)
+            plus_y = [next_y(f) for f in here]
+            both_y = eddy + next_y(eddy)
+            plus_z = [next_z(f) for f in here]
+            both_z = eddy + next_z(eddy)
+            for c in range(3):
+                flux_y = both_y * (plus_y[c] - here[c]) - (here[1] * here[c] + plus_y[1] * plus_y[c])
+                flux_z = both_z * (plus_z[c] - here[c]) - (here[2] * here[c] + plus_z[2] * plus_z[c])
+                floor_z = eddy * here[c] - here[2] * here[c]
+                below_z = jnp.where(bottom, floor_z, pltpu.roll(flux_z, 1, 0))
+                change = 0.5 * (
+                    (ahead[c] - before[c]) + (flux_y - last_y(flux_y)) + (flux_z - below_z)
+                )
+                if c == 0:
+                    drag = thrust[i - 2] * here[0] * jnp.abs(here[0])
+                    change = change + (DRIVING_FORCE - drag)
+                moved_on = here[c] + TIME_STEP * change
+                if keep == 0.0:
+                    then[i, c] = moved_on
+                else:
+                    then[i, c] = keep * start[i, c] + gain * moved_on
+            return ahead
+
+        lax.fori_loop(first, end, column, face_x(now, first - 1))
+
+    columns = start.shape[0]
+    set_viscosity(start, 1, columns - 1)
+    advance(start, stage_a, 2, columns - 2, 0.0, 1.0)
+    set_viscosity(stage_a, 3, columns - 3)
+    advance(stage_a, stage_b, 4, columns - 4, 0.75, 0.25)
+    set_viscosity(stage_b, 5, columns - 5)
+    advance(stage_b, stage_a, 6, columns - 6, 1.0 / 3.0, 2.0 / 3.0)
+
+    section, anchor, fringe_first, fringe_end = (meta[0], meta[1], meta[2], meta[3])
+    is_farm = section == 1
+
+    def weight(offset, dest):
+        place = lax.rem(anchor + offset + total_x, total_x)
+        inside = jnp.logical_and(place >= fringe_first, place < fringe_end)
+        blend = jnp.where(inside, FRINGE_BLEND, 0.0)
+        share = jnp.where(is_farm, 1.0 - blend, blend)
+        if dest == 0:
+            return jnp.where(is_farm, 0.0, 1.0)
+        return share
+
+    for x in range(cells_x):
+        i = REACH + x
+        cross = stage_a[i, 1]
+        upright = stage_a[i, 2]
+        plane = (next_y(cross) - last_y(cross)) + (next_z(upright) - last_z(upright))
+        after, before = stage_a[i + 1, 0], stage_a[i - 1, 0]
+        for dest in range(2):
+            source[pl.ds((dest * cells_x + x) * levels, levels), :] = 0.5 * (
+                weight(x + 1, dest) * after - weight(x - 1, dest) * before + weight(x, dest) * plane
+            )
+        for c in range(3):
+            columns_out[pl.ds((x * 3 + c) * levels, levels), :] = stage_a[i, c, :, :half]
+
+    groups = moved.shape[0]
+    share = levels // groups
+    for c in range(3):
+        for z in range(levels):
+            row = columns_out[pl.ds(c * levels + z, cells_x, stride=3 * levels), :]
+            moved[z // share, c, z % share] = row
+
+    along_y = dot(source[...], table_y[...])
+    for n in range(2 * cells_x):
+        modes[pl.ds(n * levels, levels), :] = dot(
+            table_z[...], along_y[n * levels : (n + 1) * levels]
+        )
+    lane_width = LANES // groups
+    for dest in range(2):
+        for a in range(levels // groups):
+            picked = [
+                modes[pl.ds(dest * cells_x * levels + a * groups + b, cells_x, stride=levels), :]
+                for b in range(groups)
+            ]
+            for g, block in enumerate(swap_blocks(picked, lane_width)):
+                spectra[dest, g, a] = block
+
+
+def pencil_kernel(meta, received, inverse, table_x, spread_z, moved, upstream, packed):
+    groups, parts, cells_x, lanes = received.shape[1:]
+    total_x = groups * cells_x
+    lane_width = lanes // groups
+    pieces = []
+    for a in range(parts):
+        spectrum = (received[0, :, a] + received[1, :, a]).reshape(total_x, lanes)
+        solved = dot(table_x[...], spectrum) * inverse[a]
+        pieces.append(dot(table_x[...], solved))
+    field = dot(jnp.concatenate(pieces, axis=1), spread_z[...])
+    halves = [field[:, a * lanes : (a + 1) * lanes] for a in range(parts)]
+    lane = lax.broadcasted_iota(jnp.int32, (total_x, lanes), 1)
+    quarter = 2 * lane_width
+    for g in range(groups):
+        a = g * parts // groups
+        if g % 2 == 0:
+            edge = pltpu.roll(halves[max(a - 1, 0)], quarter, 1)
+            packed[g, :total_x] = jnp.where(lane < quarter, edge, pltpu.roll(halves[a], quarter, 1))
+        else:
+            edge = pltpu.roll(halves[min(a + 1, parts - 1)], lanes - quarter, 1)
+            packed[g, :total_x] = jnp.where(
+                lane < lanes - quarter, pltpu.roll(halves[a], lanes - quarter, 1), edge
+            )
+    section, anchor, fringe_first, fringe_end = (meta[0], meta[1], meta[2], meta[3])
+    place = anchor + lax.broadcasted_iota(jnp.int32, (cells_x, lanes), 0)
+    inside = jnp.logical_and(place >= fringe_first, place < fringe_end)
+    inside = jnp.logical_and(inside, section == 1)
+    blend = jnp.where(inside, FRINGE_BLEND, 0.0)[None, None]
+    for g in range(groups):
+        own = moved[g]
+        mixed = own + blend * (upstream[g] - own)
+        packed[g, total_x:] = mixed.reshape(-1, lanes)
+
+
+def project_kernel(meta, received, partner, table_y, velocity_next, pressure):
+    groups = received.shape[0]
+    total_x, lanes = partner.shape[1:]
+    share = pressure.shape[0]
+    cells_x = total_x // groups
+    here = swap_blocks([received[s, :total_x] for s in range(groups)], lanes // groups)
+    there = swap_blocks([partner[s] for s in range(groups)], lanes // groups)
+    place = meta[4]
+    fields = []
+    for n in range(share + 2):
+        both = jnp.concatenate([here[n + 1], there[n + 1]], axis=1)
+        fields.append(dot(both, table_y[...]))
+    values = [f[:, :lanes] for f in fields]
+    values[0] = jnp.where(place == 0, values[1], values[0])
+    values[-1] = jnp.where(place == groups - 1, -values[-2], values[-1])
+    for z in range(share):
+        now = values[z + 1]
+        pressure[z] = now
+        slopes = [
+            0.5 * (pltpu.roll(now, total_x - 1, 0) - pltpu.roll(now, 1, 0)),
+            fields[z + 1][:, lanes:],
+            0.5 * (values[z + 2] - values[z]),
+        ]
+        for c in range(3):
+            rows = total_x + (c * share + z) * cells_x
+            blended = received[:, rows : rows + cells_x].reshape(total_x, lanes)
+            velocity_next[c, z] = blended - slopes[c]
+
+
+def cas(rows, columns, length):
+    angle = (np.outer(rows, columns) % length) * (2.0 * np.pi / length)
+    return np.cos(angle) + np.sin(angle)
+
+
+def tables(levels, total_x, total_y, groups):
+    half = total_y // 2
+    lane_width = LANES // groups
+    every_x = np.arange(total_x)
+    every_y = np.arange(total_y)
+    table_x = cas(every_x, every_x, total_x)
+    table_y = cas(every_y, every_y, total_y)
+    slope_y = 0.5 * (np.roll(table_y, -1, axis=1) - np.roll(table_y, 1, axis=1))
+    level = np.arange(levels) + 0.5
+    table_z = np.cos(np.outer(level, level) * (np.pi / levels))
+    spread_z = np.kron(table_z, np.eye(lane_width))
+    forward, backward = [], []
+    for core in range(2):
+        order = np.roll(every_y, -core * half)
+        here = slice(core * half, (core + 1) * half)
+        forward.append(table_y[order, here])
+        backward.append(np.concatenate([table_y[order, here], slope_y[order, here]], axis=1))
+    eigen = (
+        (2.0 * np.cos(level * (np.pi / levels)) - 2.0)[:, None, None]
+        + (2.0 * np.cos(every_x * (2.0 * np.pi / total_x)) - 2.0)[None, :, None]
+        + (2.0 * np.cos(every_y * (2.0 * np.pi / total_y)) - 2.0)[None, None, :]
+    )
+    inverse = (2.0 / levels) / (total_x * total_y) / eigen
+    inverse = inverse.reshape(levels // groups, groups, total_x, 2, groups, lane_width)
+    inverse = inverse.transpose(4, 3, 0, 2, 1, 5).reshape(
+        groups, 2, levels // groups, total_x, LANES
+    )
+    return [
+        np.asarray(t, np.float32)
+        for t in (table_x, np.stack(forward), np.stack(backward), table_z, spread_z, inverse)
+    ]
+
+
+def call(kernel, out_shapes, scratch, *operands):
+    in_specs = [pl.BlockSpec(memory_space=pltpu.SMEM)]
+    in_specs += [pl.BlockSpec(memory_space=pltpu.VMEM)] * (len(operands) - 1)
+    return pl.pallas_call(
+        kernel,
+        out_shape=out_shapes,
+        in_specs=in_specs,
+        out_specs=jax.tree.map(lambda _: pl.BlockSpec(memory_space=pltpu.VMEM), out_shapes),
+        scratch_shapes=scratch,
+        compiler_params=pltpu.CompilerParams(vmem_limit_bytes=VMEM_BYTES),
+    )(*operands)
+
+
+def thrust_weights(turbine_cells, along_x, along_y, along_z, total_y, strength):
+    matches = (along_x[:, None] == turbine_cells[None, :, 0]).astype(jnp.bfloat16)
+    offset_y = (along_y[None, :] - turbine_cells[:, 1:2] + total_y // 2) % total_y - total_y // 2
+    offset_z = along_z[None, :] - turbine_cells[:, 2:3]
+    distance = (
+        offset_z[:, :, None] * offset_z[:, :, None] + offset_y[:, None, :] * offset_y[:, None, :]
+    )
+    inside = (distance <= RADIUS * RADIUS).astype(jnp.bfloat16)
+    count = jnp.einsum("xt,tzy->xzy", matches, inside, preferred_element_type=jnp.float32)
+    return strength * count
+
+
+def paired_plan(velocity, turbine_cells, fringe_bounds):
+    groups = lax.axis_size("gx")
+    initial = velocity[0]
+    _, levels, cells_x, cells_y = initial.shape
+    total_x, total_y = cells_x * groups, 2 * cells_y
+    width = total_y
+    share = levels // groups
+    section, place, core = (lax.axis_index("sec"), lax.axis_index("gx"), lax.axis_index("gy"))
+    table_x, forward, backward, table_z, spread_z, inverse = tables(
+        levels, total_x, total_y, groups
+    )
+    meta = jnp.stack([section, place * cells_x, fringe_bounds[0], fringe_bounds[1], place])
+    meta = meta.astype(jnp.int32)
+
+    up = [(i, (i + 1) % groups) for i in range(groups)]
+    down = [(j, i) for i, j in up]
+    swap = [(0, 1), (1, 0)]
+    own = jnp.transpose(initial, (2, 0, 1, 3))
+    left = lax.ppermute(own[cells_x - REACH :], "gx", up)
+    right = lax.ppermute(own[:REACH], "gx", down)
+    own_there = lax.ppermute(own, "gy", swap)
+    left_there = lax.ppermute(left, "gy", swap)
+    right_there = lax.ppermute(right, "gy", swap)
+
+    along_x = (place * cells_x + jnp.arange(-REACH + 2, cells_x + REACH - 2)) % total_x
+    along_y = (core * cells_y + jnp.arange(total_y)) % total_y
+    strength = THRUST_COEFF * section.astype(jnp.float32)
+    thrust = thrust_weights(
+        turbine_cells, along_x, along_y, jnp.arange(levels), total_y, strength
+    )
+    table_forward = lax.dynamic_index_in_dim(jnp.asarray(forward), core, 0, keepdims=False)
+    table_backward = lax.dynamic_index_in_dim(jnp.asarray(backward), core, 0, keepdims=False)
+    own_inverse = lax.dynamic_slice(
+        jnp.asarray(inverse), (place, core, 0, 0, 0), (1, 1) + inverse.shape[2:]
+    )[0, 0]
+
+    columns = cells_x + 2 * REACH
+    parts = levels // groups
+    f32 = jnp.float32
+    moved, spectra = call(
+        functools.partial(advance_kernel, total_x),
+        (
+            jax.ShapeDtypeStruct((groups, 3, share, cells_x, cells_y), f32),
+            jax.ShapeDtypeStruct((2, groups, parts, cells_x, LANES), f32),
+        ),
+        [
+            pltpu.VMEM((columns, 3, levels, width), f32),
+            pltpu.VMEM((columns, 3, levels, width), f32),
+            pltpu.VMEM((columns, 3, levels, width), f32),
+            pltpu.VMEM((columns, levels, width), f32),
+            pltpu.VMEM((2 * cells_x * levels, width), f32),
+            pltpu.VMEM((cells_x * 3 * levels, cells_y), f32),
+            pltpu.VMEM((2 * cells_x * levels, LANES), f32),
+        ],
+        meta,
+        own,
+        own_there,
+        left,
+        left_there,
+        right,
+        right_there,
+        thrust,
+        table_forward,
+        jnp.asarray(table_z),
+    )
+    fringe = [(g, groups + g) for g in range(groups - groups // 4, groups)]
+    upstream = lax.ppermute(moved, ("sec", "gx"), fringe)
+    received = lax.all_to_all(
+        spectra.reshape(2 * groups, parts, cells_x, LANES), ("sec", "gx"), 0, 0, tiled=True
+    ).reshape(2, groups, parts, cells_x, LANES)
+    rows = total_x + 3 * share * cells_x
+    packed = call(
+        pencil_kernel,
+        jax.ShapeDtypeStruct((groups, rows, LANES), f32),
+        [],
+        meta,
+        received,
+        own_inverse,
+        jnp.asarray(table_x),
+        jnp.asarray(spread_z),
+        moved,
+        upstream,
+    )
+    returned = lax.all_to_all(packed, "gx", 0, 0, tiled=True)
+    partner = lax.ppermute(returned[:, :total_x], "gy", swap)
+    velocity_next, pressure = call(
+        project_kernel,
+        (
+            jax.ShapeDtypeStruct((3, share, total_x, cells_y), f32),
+            jax.ShapeDtypeStruct((share, total_x, cells_y), f32),
+        ),
+        [],
+        meta,
+        returned,
+        partner,
+        table_backward,
+    )
+    return (velocity_next[None], pressure[None])
+
+
+def on_device(velocity, turbine_cells, fringe_bounds):
+    groups = lax.axis_size("gx")
+    _, _, levels, cells_x, cells_y = velocity.shape
+    paired = (
+        lax.axis_size("gy") == 2
+        and lax.axis_size("sec") == 2
+        and cells_y == LANES
+        and cells_x == ROWS
+        and groups == ROWS
+        and 2 * levels == groups * groups
+    )
+    plan = paired_plan if paired else general_plan
+    return plan(velocity, turbine_cells, fringe_bounds)
+
+
 def solution(mesh):
     return jax.shard_map(
         on_device,

time: 171 us -> 89.9 us (0.53)
  waiting for transfers between devices: 61.9 us -> 25 us
  starting transfers between devices: 47 us -> 13.1 us
  local copies, waits for them, and re-layouts: 30.2 us -> 2.21 us
  Pallas kernels: 0 us -> 22.9 us
  blocking collectives: 8.1 us -> 24.6 us
  other arithmetic: 16.1 us -> 0.4 us
  matrix products: 5.45 us -> 0.56 us
    ppermute x25 -> x7, starting transfers between devices: 36.2 us -> 6.97 us  [the longest x1 3.1 us: paired_plan(): right = lax.ppermute(own[:REACH], 'gx', down)]
    all_to_all x3 -> x1, waiting for transfers between devices: 33.2 us -> 8.54 us  [paired_plan(): lax.all_to_all(spectra.reshape(2 * groups, parts, cells_x, LANES), ('sec'...]
    pallas_call x0 -> x3, Pallas kernels: none -> 22.9 us  [call(): pl.pallas_call(kernel, out_shape=out_shapes, in_specs=in_specs, out_specs...]
    all_to_all x2 -> x1, blocking collectives: 8.1 us -> 24.6 us  [paired_plan(): returned = lax.all_to_all(packed, 'gx', 0, 0, tiled=True)]
    ppermute x25 -> x7, waiting for transfers between devices: 28.7 us -> 16.5 us  [the longest x1 11.5 us: paired_plan(): left = lax.ppermute(own[cells_x - REACH:], 'gx', up)]
    slice x35 -> x2, local copies, waits for them, and re-layouts: 11.3 us -> 0.09 us  [the longest x1 0.07 us: paired_plan(): right = lax.ppermute(own[:REACH], 'gx', down)]
    concatenate x10 -> x0, other arithmetic: 6.19 us -> none  [the longest x9 6.19 us: extended(): x = jnp.concatenate([before, x, after], axis=dim)]
    dot_general x5 -> x1, matrix products: 5.45 us -> 0.56 us  [thrust_weights(): jnp.einsum('xt,tzy->xzy', matches, inside, preferred_element_type=jnp.flo...]
  transfers between devices with their start and end apart: 28 -> 8, of which waited for: 20 -> 5; matrix products, arithmetic and copies ran while one was open for 5% -> 2% of each run, Pallas kernels for 0% -> 0%
where the time goes in v1:
time: 89.9 us; the launch traced here: 89.6 us
  waiting for transfers between devices  25 us (28%)
  blocking collectives  24.6 us (27%)
  Pallas kernels  22.9 us (25%)
  starting transfers between devices  13.1 us (15%)
  local copies, waits for them, and re-layouts  2.21 us (2%)
    all_to_all x1, blocking collectives, paired_plan(): returned = lax.all_to_all(packed, 'gx', 0, 0, tiled=True)  24.6 us
    pallas_call x3, Pallas kernels, call(): pl.pallas_call(kernel, out_shape=out_shapes, in_specs=in_specs, out_specs...  22.9 us
    ppermute x1, waiting for transfers between devices, paired_plan(): left = lax.ppermute(own[cells_x - REACH:], 'gx', up)  11.5 us
    all_to_all x1, waiting for transfers between devices, paired_plan(): lax.all_to_all(spectra.reshape(2 * groups, parts, cells_x, LANES), ('sec'...  8.54 us
    all_to_all x1, starting transfers between devices, paired_plan(): lax.all_to_all(spectra.reshape(2 * groups, parts, cells_x, LANES), ('sec'...  6.12 us
    ppermute x1, starting transfers between devices, paired_plan(): right = lax.ppermute(own[:REACH], 'gx', down)  3.1 us
    ppermute x1, starting transfers between devices, paired_plan(): left = lax.ppermute(own[cells_x - REACH:], 'gx', up)  2.58 us
    ppermute x1, waiting for transfers between devices, paired_plan(): right = lax.ppermute(own[:REACH], 'gx', down)  2.2 us
  transfers between devices with their start and end apart: 8, of which 5 were waited for; matrix products, arithmetic and copies ran while one was open for 2% of the time, Pallas kernels for 0%

profile of v1, /device:TPU:0, one launch (start us, length us, event | category | flops | bytes accessed | tf_op | source)
XLA Modules:
  0.0 89.6 jit_solution(16481814118908075683)
XLA Ops:
  0.6 0.0 copy-start.4
  0.6 0.0 copy-start.5
  0.7 0.0 copy-start.6
  0.7 1.1 %copy.15 = f32[1,3,32,8,128]{4,2,1,3,0:T(8,128)S(1)} copy(f32[1,3,32,8,128]{4,3,2,1,0:T(8,128)} %param.9) | data formatting | bytes 786432 | tf_op args[0]
  1.8 0.0 copy-start.2
  1.8 0.5 collective-permute-start
  2.3 0.1 fusion.14
  2.4 2.6 %collective-permute-start.1 = (f32[7,3,32,128]{3,2,1,0:T(8,128)S(1)}, f32[7,3,32,128]{3,2,1,0:T(8,128)S(1)}, u32[]{:S(2)}, u32[]{:S(2)}) collective-permute-start(f32[7,3,32,128]{3,2,1,0:T(8,128)S(1)} %get-tuple-element.11), channel_id=1, source_target_pairs={{0,2},{2,4},{4,6},{6,8},{8,10},{10,12},{12,14},{14,0},{1,3},{3,5},... | collective-permute-start | bytes 1032200 | tf_op jit(solution)/shard_map/ppermute | solution.py:575
  5.0 3.1 %collective-permute-start.3 = (f32[7,3,32,128]{3,2,1,0:T(8,128)S(1)}, f32[7,3,32,128]{3,2,1,0:T(8,128)S(1)}, u32[]{:S(2)}, u32[]{:S(2)}) collective-permute-start(f32[7,3,32,128]{3,2,1,0:T(8,128)S(1)} %get-tuple-element.10), channel_id=1, source_target_pairs={{2,0},{4,2},{6,4},{8,6},{10,8},{12,10},{14,12},{0,14},{3,1},{5,3},... | collective-permute-start | bytes 1032200 | tf_op jit(solution)/shard_map/ppermute | solution.py:576
  8.1 0.0 copy-done.5
  8.1 0.1 fusion.6
  8.2 0.6 fusion
  8.8 0.0 copy-done.4
  8.8 11.5 %collective-permute-done.1.left_here = f32[7,3,32,128]{3,2,1,0:T(8,128)S(1)} collective-permute-done((f32[7,3,32,128]{3,2,1,0:T(8,128)S(1)}, f32[7,3,32,128]{3,2,1,0:T(8,128)S(1)}, u32[]{:S(2)}, u32[]{:S(2)}) %collective-permute-start.1) | collective-permute-done | bytes 344096 | tf_op jit(solution)/shard_map/ppermute | solution.py:575
  20.3 0.0 collective-permute-start.2
  20.3 2.2 %collective-permute-done.3.right_here = f32[7,3,32,128]{3,2,1,0:T(8,128)S(1)} collective-permute-done((f32[7,3,32,128]{3,2,1,0:T(8,128)S(1)}, f32[7,3,32,128]{3,2,1,0:T(8,128)S(1)}, u32[]{:S(2)}, u32[]{:S(2)}) %collective-permute-start.3) | collective-permute-done | bytes 344096 | tf_op jit(solution)/shard_map/ppermute | solution.py:576
  22.5 0.0 collective-permute-start.4
  22.5 0.0 copy-done.6
  22.5 0.1 pad_add_fusion.meta
  22.6 0.2 copy_multiply_fusion.thrust
  22.8 0.0 copy-start
  22.8 0.0 copy-start.1
  22.8 0.0 collective-permute-done.own_there
  22.8 0.0 collective-permute-done.2.left_there
  22.9 1.3 %collective-permute-done.4.right_there = f32[7,3,32,128]{3,2,1,0:T(8,128)S(1)} collective-permute-done((f32[7,3,32,128]{3,2,1,0:T(8,128)S(1)}, f32[7,3,32,128]{3,2,1,0:T(8,128)S(1)}, u32[]{:S(2)}, u32[]{:S(2)}) %collective-permute-start.4) | collective-permute-done | bytes 344096 | tf_op jit(solution)/shard_map/ppermute | solution.py:579
  24.2 0.0 copy-done.2
  24.2 18.8 %shard_map.104 = (f32[8,3,4,8,128]{4,3,2,1,0:T(8,128)S(1)}, f32[2,8,4,8,128]{4,3,2,1,0:T(8,128)}) custom-call(s32[5]{0:T(128)S(1)} %pad_add_fusion.meta, f32[8,3,32,128]{3,2,1,0:T(8,128)S(1)} %bitcast.29, f32[8,3,32,128]{3,2,1,0:T(8,128)S(1)} %collective-permute-done.own_there, f32[7,3,32,128]{3,2,1,0:T(8,128)S(1)} %collective-permute-done.1.left_here, ...), custom_call_target="tpu_custom_call" | custom-call | tf_op jit(solution)/shard_map/pallas_call | solution.py:535
  42.9 6.1 %all-to-all-start = ((f32[16,4,8,128]{3,2,1,0:T(8,128)}), f32[16,4,8,128]{3,2,1,0:T(8,128)S(1)}, u32[]{:S(2)}, u32[]{:S(2)}) async-start(f32[16,4,8,128]{3,2,1,0:T(8,128)} %bitcast.11), calls=%async_computation | async-start | bytes 524288 | tf_op jit(solution)/shard_map/all_to_all | solution.py:624
  49.1 0.7 collective-permute-start.5
  49.8 0.9 %dynamic-slice_bitcast_fusion.1.inverse = f32[4,64,128]{2,1,0:T(8,128)S(1)} fusion(f32[8,2,4,64,128]{4,3,2,1,0:T(8,128)} %constant.87.clone, s32[]{:T(128)S(6)} %select_n.45, s32[]{:T(128)S(6)} %select_n.44), kind=kLoop, calls=%fused_computation.8 | loop fusion | bytes 262152 | tf_op jit(solution)/shard_map/squeeze | solution.py:589
  50.7 0.0 collective-permute-done.5.upstream
  50.7 8.5 %all-to-all-done = f32[16,4,8,128]{3,2,1,0:T(8,128)S(1)} async-done(((f32[16,4,8,128]{3,2,1,0:T(8,128)}), f32[16,4,8,128]{3,2,1,0:T(8,128)S(1)}, u32[]{:S(2)}, u32[]{:S(2)}) %all-to-all-start) | async-done | bytes 262176 | tf_op jit(solution)/shard_map/all_to_all | solution.py:624
  59.2 0.0 copy-done
  59.2 0.0 copy-done.1
  59.2 0.0 copy-start.3
  59.2 1.6 %shard_map.105 = f32[8,160,128]{2,1,0:T(8,128)S(1)} custom-call(s32[5]{0:T(128)S(1)} %pad_add_fusion.meta, f32[2,8,4,8,128]{4,3,2,1,0:T(8,128)S(1)} %bitcast.30, f32[4,64,128]{2,1,0:T(8,128)S(1)} %dynamic-slice_bitcast_fusion.1.inverse, f32[64,64]{1,0:T(8,128)S(1)} %copy-done.1, f32[512,512]{1,0:T(8,128)S(1)} %copy-done, ...), custom_call_target="tpu_custom_call" | custom-call | tf_op jit(solution)/shard_map/pallas_call | solution.py:535
  60.8 24.6 %all_to_all.10.received = f32[8,160,128]{2,1,0:T(8,128)S(1)} all-to-all(f32[8,160,128]{2,1,0:T(8,128)S(1)} %shard_map.105), channel_id=1, replica_groups=mesh['sec'=2,'gx'=8,'gy'=2] {'gx'}, dimensions={0} | all-to-all | bytes 1310720 | tf_op jit(solution)/shard_map/all_to_all | solution.py:640
  85.5 0.1 collective-permute-start.6
  85.6 0.0 copy-done.3
  85.6 1.5 %collective-permute-done.6.partner = f32[8,64,128]{2,1,0:T(8,128)S(1)} collective-permute-done((f32[8,64,128]{2,1,0:T(8,128)S(1)}, f32[8,64,128]{2,1,0:T(8,128)S(1)}, u32[]{:S(2)}, u32[]{:S(2)}) %collective-permute-start.6) | collective-permute-done | bytes 262176 | tf_op jit(solution)/shard_map/ppermute | solution.py:641
  87.1 2.5 %shard_map.106 = (f32[3,4,64,128]{3,2,1,0:T(8,128)}, f32[4,64,128]{2,1,0:T(8,128)}) custom-call(s32[5]{0:T(128)S(1)} %pad_add_fusion.meta, f32[8,160,128]{2,1,0:T(8,128)S(1)} %all_to_all.10.received, f32[8,64,128]{2,1,0:T(8,128)S(1)} %collective-permute-done.6.partner, f32[256,256]{1,0:T(8,128)S(1)} %dynamic-slice_bitcast_fusion.table_y), custom_call_target="tpu_custom_call" | custom-call | tf_op jit(solution)/shard_map/pallas_call | solution.py:535
  (7 shorter events, 0.1 us)
Async XLA Ops:
  0.6 8.2 %copy-start.4 = (f32[2,256,128]{2,1,0:T(8,128)S(1)}, f32[2,256,128]{2,1,0:T(8,128)}, u32[]{:S(2)}) copy-start(f32[2,256,128]{2,1,0:T(8,128)} %constant.85.clone) | copy-start | bytes 786436
  0.6 7.4 %copy-start.5 = (s32[64,3]{0,1:T(4,128)S(1)}, s32[64,3]{0,1:T(4,128)}, u32[]{:S(2)}) copy-start(s32[64,3]{0,1:T(4,128)} %param.10) | copy-start | bytes 2308
  0.7 21.9 %copy-start.6 = (s32[2]{0:T(128)S(1)}, s32[2]{0:T(128)}, u32[]{:S(2)}) copy-start(s32[2]{0:T(128)} %param.11) | copy-start | bytes 28
  1.8 22.4 %copy-start.2 = (f32[32,32]{1,0:T(8,128)S(1)}, f32[32,32]{1,0:T(8,128)}, u32[]{:S(2)}) copy-start(f32[32,32]{1,0:T(8,128)} %constant.88.clone.table_z) | copy-start | bytes 12292
  1.8 21.0 %collective-permute-start = (f32[8,3,32,128]{3,2,1,0:T(8,128)S(1)}, f32[8,3,32,128]{3,2,1,0:T(8,128)S(1)}, u32[]{:S(2)}, u32[]{:S(2)}) collective-permute-start(f32[8,3,32,128]{3,2,1,0:T(8,128)S(1)} %bitcast.27), channel_id=1, source_target_pairs={{0,1},{1,0},{2,3},{3,2},{4,5},{5,4},{6,7},{7,6},{8,9},{9,8},{10,11... | collective-permute-start | bytes 1179656 | tf_op jit(solution)/shard_map/ppermute | solution.py:577
  2.4 17.9 %collective-permute-start.1 = (f32[7,3,32,128]{3,2,1,0:T(8,128)S(1)}, f32[7,3,32,128]{3,2,1,0:T(8,128)S(1)}, u32[]{:S(2)}, u32[]{:S(2)}) collective-permute-start(f32[7,3,32,128]{3,2,1,0:T(8,128)S(1)} %get-tuple-element.11), channel_id=1, source_target_pairs={{0,2},{2,4},{4,6},{6,8},{8,10},{10,12},{12,14},{14,0},{1,3},{3,5},... | collective-permute-start | bytes 1032200 | tf_op jit(solution)/shard_map/ppermute | solution.py:575
  5.0 17.6 %collective-permute-start.3 = (f32[7,3,32,128]{3,2,1,0:T(8,128)S(1)}, f32[7,3,32,128]{3,2,1,0:T(8,128)S(1)}, u32[]{:S(2)}, u32[]{:S(2)}) collective-permute-start(f32[7,3,32,128]{3,2,1,0:T(8,128)S(1)} %get-tuple-element.10), channel_id=1, source_target_pairs={{2,0},{4,2},{6,4},{8,6},{10,8},{12,10},{14,12},{0,14},{3,1},{5,3},... | collective-permute-start | bytes 1032200 | tf_op jit(solution)/shard_map/ppermute | solution.py:576
  20.3 2.5 %collective-permute-start.2 = (f32[7,3,32,128]{3,2,1,0:T(8,128)S(1)}, f32[7,3,32,128]{3,2,1,0:T(8,128)S(1)}, u32[]{:S(2)}, u32[]{:S(2)}) collective-permute-start(f32[7,3,32,128]{3,2,1,0:T(8,128)S(1)} %collective-permute-done.1.left_here), channel_id=1, source_target_pairs={{0,1},{1,0},{2,3},{3,2},{4,5},{5,4},{6,7},{7,6},{8,9},{9,8},{10,11... | collective-permute-start | bytes 1032200 | tf_op jit(solution)/shard_map/ppermute | solution.py:578
  22.5 1.7 %collective-permute-start.4 = (f32[7,3,32,128]{3,2,1,0:T(8,128)S(1)}, f32[7,3,32,128]{3,2,1,0:T(8,128)S(1)}, u32[]{:S(2)}, u32[]{:S(2)}) collective-permute-start(f32[7,3,32,128]{3,2,1,0:T(8,128)S(1)} %collective-permute-done.3.right_here), channel_id=1, source_target_pairs={{0,1},{1,0},{2,3},{3,2},{4,5},{5,4},{6,7},{7,6},{8,9},{9,8},{10,11... | collective-permute-start | bytes 1032200 | tf_op jit(solution)/shard_map/ppermute | solution.py:579
  22.8 36.4 %copy-start = (f32[512,512]{1,0:T(8,128)S(1)}, f32[512,512]{1,0:T(8,128)}, u32[]{:S(2)}) copy-start(f32[512,512]{1,0:T(8,128)} %constant.90.clone.spread_z) | copy-start | bytes 3145732
  22.8 36.4 %copy-start.1 = (f32[64,64]{1,0:T(8,128)S(1)}, f32[64,64]{1,0:T(8,128)}, u32[]{:S(2)}) copy-start(f32[64,64]{1,0:T(8,128)} %constant.89.clone.table_x) | copy-start | bytes 49156
  42.9 16.3 %all-to-all-start = ((f32[16,4,8,128]{3,2,1,0:T(8,128)}), f32[16,4,8,128]{3,2,1,0:T(8,128)S(1)}, u32[]{:S(2)}, u32[]{:S(2)}) async-start(f32[16,4,8,128]{3,2,1,0:T(8,128)} %bitcast.11), calls=%async_computation | async-start | bytes 524288 | tf_op jit(solution)/shard_map/all_to_all | solution.py:624
  49.1 1.6 %collective-permute-start.5 = (f32[8,3,4,8,128]{4,3,2,1,0:T(8,128)S(1)}, f32[8,3,4,8,128]{4,3,2,1,0:T(8,128)S(1)}, u32[]{:S(2)}, u32[]{:S(2)}) collective-permute-start(f32[8,3,4,8,128]{4,3,2,1,0:T(8,128)S(1)} %get-tuple-element.7.moved), channel_id=1, source_target_pairs={{12,28},{14,30},{13,29},{15,31}} | collective-permute-start | bytes 1179656 | tf_op jit(solution)/shard_map/ppermute | solution.py:623
  59.2 26.3 %copy-start.3 = (f32[2,256,256]{2,1,0:T(8,128)S(1)}, f32[2,256,256]{2,1,0:T(8,128)}, u32[]{:S(2)}) copy-start(f32[2,256,256]{2,1,0:T(8,128)} %constant.86.clone) | copy-start | bytes 1572868
  85.5 1.6 %collective-permute-start.6 = (f32[8,64,128]{2,1,0:T(8,128)S(1)}, f32[8,64,128]{2,1,0:T(8,128)S(1)}, u32[]{:S(2)}, u32[]{:S(2)}) collective-permute-start(f32[8,64,128]{2,1,0:T(8,128)S(1)} %slice.32), channel_id=1, source_target_pairs={{0,1},{1,0},{2,3},{3,2},{4,5},{5,4},{6,7},{7,6},{8,9},{9,8},{10,11... | collective-permute-start | bytes 786440 | tf_op jit(solution)/shard_map/ppermute | solution.py:641

commit v2 on v1

--- a/solution.py
+++ b/solution.py
@@ -20,6 +20,7 @@
 STAGES = 3
 REACH = 2 * STAGES + 1
 LANES = 128
+SMALLEST = float(np.finfo(np.float32).tiny)
 ROWS = 8
 VMEM_BYTES = 48 * 1024 * 1024
 
@@ -288,23 +289,25 @@
     stage_a,
     stage_b,
     viscosity,
+    faces,
     source,
     columns_out,
     modes,
 ):
-    cells_x, _, levels, half = own_here.shape
+    cells_x, _, tiles, rows, half = own_here.shape
+    levels = tiles * rows
     width = 2 * half
-    level = lax.broadcasted_iota(jnp.int32, (levels, width), 0)
-    top = level == levels - 1
-    bottom = level == 0
+    row = lax.broadcasted_iota(jnp.int32, (rows, width), 0)
+    top = row == rows - 1
+    bottom = row == 0
 
     for first, here, there in (
         (0, left_here, left_there),
         (REACH, own_here, own_there),
         (REACH + cells_x, right_here, right_there),
     ):
-        start[pl.ds(first, here.shape[0]), :, :, :half] = here[...]
-        start[pl.ds(first, here.shape[0]), :, :, half:] = there[...]
+        start[pl.ds(first, here.shape[0]), :, :, :, :half] = here[...]
+        start[pl.ds(first, here.shape[0]), :, :, :, half:] = there[...]
 
     def next_y(f):
         return pltpu.roll(f, width - 1, 1)
@@ -312,65 +315,94 @@
     def last_y(f):
         return pltpu.roll(f, 1, 1)
 
-    def next_z(f):
-        return jnp.where(top, 0.0, pltpu.roll(f, levels - 1, 0))
-
-    def last_z(f):
-        return jnp.where(bottom, 0.0, pltpu.roll(f, 1, 0))
+    def next_z(parts, t):
+        if t < tiles - 1:
+            return parts[t + 1]
+        return jnp.where(top, 0.0, pltpu.roll(parts[0], rows - 1, 0))
+
+    def last_z(parts, t):
+        if t > 0:
+            return parts[t - 1]
+        return jnp.where(bottom, 0.0, pltpu.roll(parts[tiles - 1], 1, 0))
 
     def set_viscosity(now, first, end):
         def column(i, carry):
-            here = [now[i, c] for c in range(3)]
-            d_x = [now[i + 1, c] - now[i - 1, c] for c in range(3)]
-            d_y = [next_y(f) - last_y(f) for f in here]
-            d_z = [next_z(f) - last_z(f) for f in here]
-            diagonal = d_x[0] * d_x[0] + d_y[1] * d_y[1] + d_z[2] * d_z[2]
-            xy = d_x[1] + d_y[0]
-            xz = d_x[2] + d_z[0]
-            yz = d_y[2] + d_z[1]
-            total = (diagonal + diagonal) + (xy * xy + xz * xz + yz * yz)
-            viscosity[i] = (0.5 * SMAG_COEFF) * jnp.sqrt(total)
+            here = [[now[i, c, t] for t in range(tiles)] for c in range(3)]
+            found = []
+            for t in range(tiles):
+                d_x = [now[i + 1, c, t] - now[i - 1, c, t] for c in range(3)]
+                d_y = [next_y(f[t]) - last_y(f[t]) for f in here]
+                d_z = [next_z(f, t) - last_z(f, t) for f in here]
+                diagonal = d_x[0] * d_x[0] + d_y[1] * d_y[1] + d_z[2] * d_z[2]
+                xy = d_x[1] + d_y[0]
+                xz = d_x[2] + d_z[0]
+                yz = d_y[2] + d_z[1]
+                total = (diagonal + diagonal) + (xy * xy + xz * xz + yz * yz)
+                root = total * lax.rsqrt(jnp.maximum(total, SMALLEST))
+                found.append((0.5 * SMAG_COEFF) * root)
+            for t in range(tiles):
+                viscosity[i, t] = found[t]
             return carry
 
-        lax.fori_loop(first, end, column, 0)
-
-    def face_x(now, i):
-        here = [now[i, c] for c in range(3)]
-        after = [now[i + 1, c] for c in range(3)]
-        both = viscosity[i] + viscosity[i + 1]
-        return [
-            both * (after[c] - here[c]) - (here[0] * here[c] + after[0] * after[c])
-            for c in range(3)
-        ]
+        lax.fori_loop(first, end, column, 0, unroll=4)
+
+    def face(both, here, after, lead):
+        low = both + here[lead]
+        high = both - after[lead]
+        return [after[c] * high - here[c] * low for c in range(3)]
+
+    def face_x(now, i, t):
+        here = [now[i, c, t] for c in range(3)]
+        after = [now[i + 1, c, t] for c in range(3)]
+        return face(viscosity[i, t] + viscosity[i + 1, t], here, after, 0)
 
     def advance(now, then, first, end, keep, gain):
-        def column(i, before):
-            here = [now[i, c] for c in range(3)]
-            eddy = viscosity[i]
-            ahead = face_x(now, i)
-            plus_y = [next_y(f) for f in here]
-            both_y = eddy + next_y(eddy)
-            plus_z = [next_z(f) for f in here]
-            both_z = eddy + next_z(eddy)
-            for c in range(3):
-                flux_y = both_y * (plus_y[c] - here[c]) - (here[1] * here[c] + plus_y[1] * plus_y[c])
-                flux_z = both_z * (plus_z[c] - here[c]) - (here[2] * here[c] + plus_z[2] * plus_z[c])
-                floor_z = eddy * here[c] - here[2] * here[c]
-                below_z = jnp.where(bottom, floor_z, pltpu.roll(flux_z, 1, 0))
-                change = 0.5 * (
-                    (ahead[c] - before[c]) + (flux_y - last_y(flux_y)) + (flux_z - below_z)
-                )
-                if c == 0:
-                    drag = thrust[i - 2] * here[0] * jnp.abs(here[0])
-                    change = change + (DRIVING_FORCE - drag)
-                moved_on = here[c] + TIME_STEP * change
-                if keep == 0.0:
-                    then[i, c] = moved_on
-                else:
-                    then[i, c] = keep * start[i, c] + gain * moved_on
-            return ahead
-
-        lax.fori_loop(first, end, column, face_x(now, first - 1))
+        scale = 0.5 * TIME_STEP * gain
+        for t in range(tiles):
+            for c, f in enumerate(face_x(now, first - 1, t)):
+                faces[c, t] = f
+
+        def column(i, carry):
+            eddy = [viscosity[i, t] for t in range(tiles)]
+            field = [[now[i, c, t] for t in range(tiles)] for c in range(3)]
+
+            def face_z(t):
+                here = [f[t] for f in field]
+                after = [next_z(f, t) for f in field]
+                return face(eddy[t] + next_z(eddy, t), here, after, 2)
+
+            last = face_z(tiles - 1)
+            floor = eddy[0] - field[2][0]
+            below = [
+                jnp.where(bottom, field[c][0] * floor, pltpu.roll(last[c], 1, 0)) for c in range(3)
+            ]
+            ahead_of = [face_x(now, i, t) for t in range(tiles)]
+            before_of = [[faces[c, t] for c in range(3)] for t in range(tiles)]
+            found = []
+            for t in range(tiles):
+                here = [f[t] for f in field]
+                above = last if t == tiles - 1 else face_z(t)
+                ahead, before = ahead_of[t], before_of[t]
+                side = face(eddy[t] + next_y(eddy[t]), here, [next_y(f) for f in here], 1)
+                for c in range(3):
+                    change = (
+                        (ahead[c] - before[c]) + (side[c] - last_y(side[c])) + (above[c] - below[c])
+                    )
+                    if c == 0:
+                        drag = thrust[i - 2, t] * here[0] * jnp.abs(here[0])
+                        change = change + (2.0 * DRIVING_FORCE - drag)
+                    if keep == 0.0:
+                        found.append(here[c] + scale * change)
+                    else:
+                        found.append(keep * start[i, c, t] + gain * here[c] + scale * change)
+                below = above
+            for t in range(tiles):
+                for c in range(3):
+                    then[i, c, t] = found[3 * t + c]
+                    faces[c, t] = ahead_of[t][c]
+            return carry
+
+        lax.fori_loop(first, end, column, 0, unroll=2)
 
     columns = start.shape[0]
     set_viscosity(start, 1, columns - 1)
@@ -389,34 +421,40 @@
         blend = jnp.where(inside, FRINGE_BLEND, 0.0)
         share = jnp.where(is_farm, 1.0 - blend, blend)
         if dest == 0:
-            return jnp.where(is_farm, 0.0, 1.0)
-        return share
+            share = jnp.where(is_farm, 0.0, 1.0)
+        return 0.5 * share
 
     for x in range(cells_x):
         i = REACH + x
-        cross = stage_a[i, 1]
-        upright = stage_a[i, 2]
-        plane = (next_y(cross) - last_y(cross)) + (next_z(upright) - last_z(upright))
-        after, before = stage_a[i + 1, 0], stage_a[i - 1, 0]
-        for dest in range(2):
-            source[pl.ds((dest * cells_x + x) * levels, levels), :] = 0.5 * (
-                weight(x + 1, dest) * after - weight(x - 1, dest) * before + weight(x, dest) * plane
-            )
-        for c in range(3):
-            columns_out[pl.ds((x * 3 + c) * levels, levels), :] = stage_a[i, c, :, :half]
-
-    groups = moved.shape[0]
-    share = levels // groups
+        upright = [stage_a[i, 2, t] for t in range(tiles)]
+        for t in range(tiles):
+            cross = stage_a[i, 1, t]
+            plane = (next_y(cross) - last_y(cross)) + (next_z(upright, t) - last_z(upright, t))
+            after, before = stage_a[i + 1, 0, t], stage_a[i - 1, 0, t]
+            for dest in range(2):
+                source[pl.ds(((dest * cells_x + x) * tiles + t) * rows, rows), :] = (
+                    weight(x + 1, dest) * after
+                    - weight(x - 1, dest) * before
+                    + weight(x, dest) * plane
+                )
+            for c in range(3):
+                columns_out[pl.ds(((x * 3 + c) * tiles + t) * rows, rows), :] = stage_a[
+                    i, c, t, :, :half
+                ]
+
     for c in range(3):
-        for z in range(levels):
-            row = columns_out[pl.ds(c * levels + z, cells_x, stride=3 * levels), :]
-            moved[z // share, c, z % share] = row
+        for t in range(tiles):
+            for s in range(rows):
+                moved[s, c, t] = columns_out[
+                    pl.ds((c * tiles + t) * rows + s, cells_x, stride=3 * levels), :
+                ]
 
     along_y = dot(source[...], table_y[...])
     for n in range(2 * cells_x):
         modes[pl.ds(n * levels, levels), :] = dot(
             table_z[...], along_y[n * levels : (n + 1) * levels]
         )
+    groups = moved.shape[0]
     lane_width = LANES // groups
     for dest in range(2):
         for a in range(levels // groups):
@@ -571,7 +609,9 @@
     up = [(i, (i + 1) % groups) for i in range(groups)]
     down = [(j, i) for i, j in up]
     swap = [(0, 1), (1, 0)]
-    own = jnp.transpose(initial, (2, 0, 1, 3))
+    own = jnp.transpose(
+        initial.reshape(3, ROWS, share, cells_x, cells_y), (3, 0, 2, 1, 4)
+    )
     left = lax.ppermute(own[cells_x - REACH :], "gx", up)
     right = lax.ppermute(own[:REACH], "gx", down)
     own_there = lax.ppermute(own, "gy", swap)
@@ -580,10 +620,15 @@
 
     along_x = (place * cells_x + jnp.arange(-REACH + 2, cells_x + REACH - 2)) % total_x
     along_y = (core * cells_y + jnp.arange(total_y)) % total_y
-    strength = THRUST_COEFF * section.astype(jnp.float32)
+    strength = 2.0 * THRUST_COEFF * section.astype(jnp.float32)
     thrust = thrust_weights(
-        turbine_cells, along_x, along_y, jnp.arange(levels), total_y, strength
-    )
+        turbine_cells,
+        along_x,
+        along_y,
+        jnp.arange(levels).reshape(ROWS, share).T.reshape(levels),
+        total_y,
+        strength,
+    ).reshape(along_x.shape[0], share, ROWS, total_y)
     table_forward = lax.dynamic_index_in_dim(jnp.asarray(forward), core, 0, keepdims=False)
     table_backward = lax.dynamic_index_in_dim(jnp.asarray(backward), core, 0, keepdims=False)
     own_inverse = lax.dynamic_slice(
@@ -600,10 +645,11 @@
             jax.ShapeDtypeStruct((2, groups, parts, cells_x, LANES), f32),
         ),
         [
-            pltpu.VMEM((columns, 3, levels, width), f32),
-            pltpu.VMEM((columns, 3, levels, width), f32),
-            pltpu.VMEM((columns, 3, levels, width), f32),
-            pltpu.VMEM((columns, levels, width), f32),
+            pltpu.VMEM((columns, 3, share, ROWS, width), f32),
+            pltpu.VMEM((columns, 3, share, ROWS, width), f32),
+            pltpu.VMEM((columns, 3, share, ROWS, width), f32),
+            pltpu.VMEM((columns, share, ROWS, width), f32),
+            pltpu.VMEM((3, share, ROWS, width), f32),
             pltpu.VMEM((2 * cells_x * levels, width), f32),
             pltpu.VMEM((cells_x * 3 * levels, cells_y), f32),
             pltpu.VMEM((2 * cells_x * levels, LANES), f32),
@@ -617,7 +663,7 @@
         right_there,
         thrust,
         table_forward,
-        jnp.asarray(table_z),
+        jnp.asarray(table_z.reshape(levels, ROWS, share).transpose(0, 2, 1).reshape(levels, levels)),
     )
     fringe = [(g, groups + g) for g in range(groups - groups // 4, groups)]
     upstream = lax.ppermute(moved, ("sec", "gx"), fringe)

time: 89.9 us -> 86.5 us (0.962)
  Pallas kernels: 22.9 us -> 16 us
  local copies, waits for them, and re-layouts: 2.21 us -> 6.64 us
  waiting for transfers between devices: 25 us -> 24 us
    pallas_call x3, Pallas kernels: 22.9 us -> 16 us  [call(): pl.pallas_call(kernel, out_shape=out_shapes, in_specs=in_specs, out_specs...]
    unnamed x15 -> x24, local copies, waits for them, and re-layouts: 1.15 us -> 3.1 us
    ppermute x1, waiting for transfers between devices: 1.33 us -> 0.01 us  [paired_plan(): right_there = lax.ppermute(right, 'gy', swap)]
    another operation x0 -> x1, local copies, waits for them, and re-layouts: none -> 1.23 us  [paired_plan(): initial.reshape(3, ROWS, share, cells_x, cells_y)]
    squeeze x1, local copies, waits for them, and re-layouts: 0.02 us -> 0.98 us  [paired_plan(): lax.dynamic_index_in_dim(jnp.asarray(forward), core, 0, keepdims=False)]
  transfers between devices with their start and end apart: 8 -> 8, of which waited for: 5 -> 4; matrix products, arithmetic and copies ran while one was open for 2% -> 4% of each run, Pallas kernels for 0% -> 0%
where the time goes in v2:
time: 86.5 us; the launch traced here: 86.1 us
  blocking collectives  24.6 us (28%)
  waiting for transfers between devices  24 us (28%)
  Pallas kernels  16 us (18%)
  starting transfers between devices  13.1 us (15%)
  local copies, waits for them, and re-layouts  6.64 us (8%)
    all_to_all x1, blocking collectives, paired_plan(): returned = lax.all_to_all(packed, 'gx', 0, 0, tiled=True)  24.6 us
    pallas_call x3, Pallas kernels, call(): pl.pallas_call(kernel, out_shape=out_shapes, in_specs=in_specs, out_specs...  16 us
    ppermute x1, waiting for transfers between devices, paired_plan(): left = lax.ppermute(own[cells_x - REACH:], 'gx', up)  11.9 us
    all_to_all x1, waiting for transfers between devices, paired_plan(): lax.all_to_all(spectra.reshape(2 * groups, parts, cells_x, LANES), ('sec'...  8.41 us
    all_to_all x1, starting transfers between devices, paired_plan(): lax.all_to_all(spectra.reshape(2 * groups, parts, cells_x, LANES), ('sec'...  6.14 us
    unnamed x24, local copies, waits for them, and re-layouts  3.1 us
    ppermute x1, starting transfers between devices, paired_plan(): right = lax.ppermute(own[:REACH], 'gx', down)  3.1 us
    ppermute x1, starting transfers between devices, paired_plan(): left = lax.ppermute(own[cells_x - REACH:], 'gx', up)  2.58 us
  transfers between devices with their start and end apart: 8, of which 4 were waited for; matrix products, arithmetic and copies ran while one was open for 4% of the time, Pallas kernels for 0%

profile of v2, /device:TPU:0, one launch (start us, length us, event | category | flops | bytes accessed | tf_op | source)
XLA Modules:
  0.0 86.1 jit_solution(4384921330536411760)
XLA Ops:
  0.6 0.0 copy-start.10
  0.6 1.2 %copy.17 = f32[3,8,4,8,128]{4,1,2,0,3:T(8,128)S(1)} copy(f32[3,8,4,8,128]{4,3,2,1,0:T(8,128)} %bitcast.35) | data formatting | bytes 786432 | tf_op jit(solution)/shard_map/reshape;squeeze | solution.py:613
  1.9 0.0 copy-start.11
  1.9 0.0 copy-start.5
  1.9 0.5 collective-permute-start
  2.4 0.1 fusion.15
  2.5 2.6 %collective-permute-start.1 = (f32[7,3,4,8,128]{4,3,2,1,0:T(8,128)S(1)}, f32[7,3,4,8,128]{4,3,2,1,0:T(8,128)S(1)}, u32[]{:S(2)}, u32[]{:S(2)}) collective-permute-start(f32[7,3,4,8,128]{4,3,2,1,0:T(8,128)S(1)} %get-tuple-element.11), channel_id=1, source_target_pairs={{0,2},{2,4},{4,6},{6,8},{8,10},{10,12},{12,14},{14,0},{1,3},{3,5},... | collective-permute-start | bytes 1032200 | tf_op jit(solution)/shard_map/ppermute | solution.py:615
  5.1 3.1 %collective-permute-start.3 = (f32[7,3,4,8,128]{4,3,2,1,0:T(8,128)S(1)}, f32[7,3,4,8,128]{4,3,2,1,0:T(8,128)S(1)}, u32[]{:S(2)}, u32[]{:S(2)}) collective-permute-start(f32[7,3,4,8,128]{4,3,2,1,0:T(8,128)S(1)} %get-tuple-element.10), channel_id=1, source_target_pairs={{2,0},{4,2},{6,4},{8,6},{10,8},{12,10},{14,12},{0,14},{3,1},{5,3},... | collective-permute-start | bytes 1032200 | tf_op jit(solution)/shard_map/ppermute | solution.py:616
  8.2 0.0 copy-done.10
  8.2 0.1 reshape.144
  8.3 0.1 subtract_multiply_fusion
  8.4 0.1 fusion.7
  8.5 11.9 %collective-permute-done.1.left_here = f32[7,3,4,8,128]{4,3,2,1,0:T(8,128)S(1)} collective-permute-done((f32[7,3,4,8,128]{4,3,2,1,0:T(8,128)S(1)}, f32[7,3,4,8,128]{4,3,2,1,0:T(8,128)S(1)}, u32[]{:S(2)}, u32[]{:S(2)}) %collective-permute-start.1) | collective-permute-done | bytes 344096 | tf_op jit(solution)/shard_map/ppermute | solution.py:615
  20.4 0.0 collective-permute-start.2
  20.4 2.2 %collective-permute-done.3.right_here = f32[7,3,4,8,128]{4,3,2,1,0:T(8,128)S(1)} collective-permute-done((f32[7,3,4,8,128]{4,3,2,1,0:T(8,128)S(1)}, f32[7,3,4,8,128]{4,3,2,1,0:T(8,128)S(1)}, u32[]{:S(2)}, u32[]{:S(2)}) %collective-permute-start.3) | collective-permute-done | bytes 344096 | tf_op jit(solution)/shard_map/ppermute | solution.py:616
  22.6 0.0 collective-permute-start.4
  22.6 0.6 fusion.1
  23.2 0.0 copy-start.4
  23.2 0.2 copy.16
  23.4 0.0 copy-start
  23.4 0.0 copy-done.11
  23.4 0.1 pad_add_fusion.meta
  23.5 0.0 copy-start.6
  23.5 1.0 %dynamic-slice_bitcast_fusion.2.table_y = f32[256,128]{1,0:T(8,128)S(1)} fusion(f32[2,256,128]{2,1,0:T(8,128)} %constant.87.clone, s32[]{:T(128)S(6)} %select_n.44), kind=kLoop, calls=%fused_computation.10 | loop fusion | bytes 262148 | tf_op jit(solution)/shard_map/jit(dynamic_index_in_dim)/squeeze | solution.py:632
  24.5 0.0 collective-permute-done.own_there
  24.5 0.0 collective-permute-done.2.left_there
  24.5 0.0 copy-start.1
  24.6 0.7 copy-done.1
  25.3 0.0 collective-permute-done.4.right_there
  25.3 0.0 copy-done.5
  25.3 0.0 copy-start.2
  25.3 1.0 %copy-done.2 = f32[7,3,4,8,128]{4,3,2,1,0:T(8,128)S(1)} copy-done((f32[7,3,4,8,128]{4,3,2,1,0:T(8,128)S(1)}, f32[7,3,4,8,128]{4,3,2,1,0:T(8,128)}, u32[]{:S(2)}) %copy-start.2) | copy-done | bytes 344088
  26.3 11.9 %shard_map.104 = (f32[8,3,4,8,128]{4,3,2,1,0:T(8,128)S(1)}, f32[2,8,4,8,128]{4,3,2,1,0:T(8,128)S(1)}) custom-call(s32[5]{0:T(128)S(1)} %pad_add_fusion.meta, f32[8,3,4,8,128]{4,3,2,1,0:T(8,128)S(1)} %bitcast.31, f32[8,3,4,8,128]{4,3,2,1,0:T(8,128)S(1)} %collective-permute-done.own_there, f32[7,3,4,8,128]{4,3,2,1,0:T(8,128)S(1)} %collective-permute-done.1.left_here, ...), custom_call_target="tpu_custom_call" | custom-call | tf_op jit(solution)/shard_map/pallas_call | solution.py:573
  38.2 0.0 copy-done.6
  38.2 0.0 copy-start.3
  38.2 0.7 copy-done.3
  38.9 6.1 %all-to-all-start = ((f32[16,4,8,128]{3,2,1,0:T(8,128)}), f32[16,4,8,128]{3,2,1,0:T(8,128)S(1)}, u32[]{:S(2)}, u32[]{:S(2)}) async-start(f32[16,4,8,128]{3,2,1,0:T(8,128)} %bitcast.34), calls=%async_computation | async-start | bytes 524288 | tf_op jit(solution)/shard_map/all_to_all | solution.py:670
  45.0 0.7 collective-permute-start.5
  45.7 0.9 %dynamic-slice_bitcast_fusion.1.inverse = f32[4,64,128]{2,1,0:T(8,128)S(1)} fusion(f32[8,2,4,64,128]{4,3,2,1,0:T(8,128)} %constant.89.clone, s32[]{:T(128)S(6)} %select_n.45, s32[]{:T(128)S(6)} %select_n.44), kind=kLoop, calls=%fused_computation.9 | loop fusion | bytes 262152 | tf_op jit(solution)/shard_map/squeeze | solution.py:634
  46.6 0.0 collective-permute-done.5.upstream
  46.7 8.4 %all-to-all-done = f32[16,4,8,128]{3,2,1,0:T(8,128)S(1)} async-done(((f32[16,4,8,128]{3,2,1,0:T(8,128)}), f32[16,4,8,128]{3,2,1,0:T(8,128)S(1)}, u32[]{:S(2)}, u32[]{:S(2)}) %all-to-all-start) | async-done | bytes 262176 | tf_op jit(solution)/shard_map/all_to_all | solution.py:670
  55.1 0.0 copy-done.4
  55.1 0.0 copy-done
  55.1 0.0 copy-start.7
  55.1 0.7 copy-done.7
  55.7 0.0 copy-start.9
  55.7 0.0 copy-start.8
  55.7 1.6 %shard_map.105 = f32[8,160,128]{2,1,0:T(8,128)S(1)} custom-call(s32[5]{0:T(128)S(1)} %copy-done.7, f32[2,8,4,8,128]{4,3,2,1,0:T(8,128)S(1)} %bitcast.33, f32[4,64,128]{2,1,0:T(8,128)S(1)} %dynamic-slice_bitcast_fusion.1.inverse, f32[64,64]{1,0:T(8,128)S(1)} %copy-done.4, f32[512,512]{1,0:T(8,128)S(1)} %copy-done, ...), custom_call_target="tpu_custom_call" | custom-call | tf_op jit(solution)/shard_map/pallas_call | solution.py:573
  57.3 24.6 %all_to_all.10.received = f32[8,160,128]{2,1,0:T(8,128)S(1)} all-to-all(f32[8,160,128]{2,1,0:T(8,128)S(1)} %shard_map.105), channel_id=1, replica_groups=mesh['sec'=2,'gx'=8,'gy'=2] {'gx'}, dimensions={0} | all-to-all | bytes 1310720 | tf_op jit(solution)/shard_map/all_to_all | solution.py:686
  82.0 0.1 collective-permute-start.6
  82.0 0.0 copy-done.9
  82.1 1.5 %collective-permute-done.6.partner = f32[8,64,128]{2,1,0:T(8,128)S(1)} collective-permute-done((f32[8,64,128]{2,1,0:T(8,128)S(1)}, f32[8,64,128]{2,1,0:T(8,128)S(1)}, u32[]{:S(2)}, u32[]{:S(2)}) %collective-permute-start.6) | collective-permute-done | bytes 262176 | tf_op jit(solution)/shard_map/ppermute | solution.py:687
  83.6 0.0 copy-done.8
  83.6 2.5 %shard_map.106 = (f32[3,4,64,128]{3,2,1,0:T(8,128)}, f32[4,64,128]{2,1,0:T(8,128)}) custom-call(s32[5]{0:T(128)S(1)} %copy-done.8, f32[8,160,128]{2,1,0:T(8,128)S(1)} %all_to_all.10.received, f32[8,64,128]{2,1,0:T(8,128)S(1)} %collective-permute-done.6.partner, f32[256,256]{1,0:T(8,128)S(1)} %dynamic-slice_bitcast_fusion.table_y), custom_call_target="tpu_custom_call" | custom-call | tf_op jit(solution)/shard_map/pallas_call | solution.py:573
  (6 shorter events, 0.1 us)
Async XLA Ops:
  0.6 7.6 %copy-start.10 = (s32[64,3]{0,1:T(4,128)S(1)}, s32[64,3]{0,1:T(4,128)}, u32[]{:S(2)}) copy-start(s32[64,3]{0,1:T(4,128)} %param.10) | copy-start | bytes 2308
  1.9 21.6 %copy-start.11 = (s32[2]{0:T(128)S(1)}, s32[2]{0:T(128)}, u32[]{:S(2)}) copy-start(s32[2]{0:T(128)} %param.11) | copy-start | bytes 28
  1.9 23.4 %copy-start.5 = (f32[32,32]{1,0:T(8,128)S(1)}, f32[32,32]{1,0:T(8,128)}, u32[]{:S(2)}) copy-start(f32[32,32]{1,0:T(8,128)} %constant.90.clone.table_z) | copy-start | bytes 12292
  1.9 22.6 %collective-permute-start = (f32[8,3,4,8,128]{4,3,2,1,0:T(8,128)S(1)}, f32[8,3,4,8,128]{4,3,2,1,0:T(8,128)S(1)}, u32[]{:S(2)}, u32[]{:S(2)}) collective-permute-start(f32[8,3,4,8,128]{4,3,2,1,0:T(8,128)S(1)} %bitcast.29), channel_id=1, source_target_pairs={{0,1},{1,0},{2,3},{3,2},{4,5},{5,4},{6,7},{7,6},{8,9},{9,8},{10,11... | collective-permute-start | bytes 1179656 | tf_op jit(solution)/shard_map/ppermute | solution.py:617
  2.5 17.9 %collective-permute-start.1 = (f32[7,3,4,8,128]{4,3,2,1,0:T(8,128)S(1)}, f32[7,3,4,8,128]{4,3,2,1,0:T(8,128)S(1)}, u32[]{:S(2)}, u32[]{:S(2)}) collective-permute-start(f32[7,3,4,8,128]{4,3,2,1,0:T(8,128)S(1)} %get-tuple-element.11), channel_id=1, source_target_pairs={{0,2},{2,4},{4,6},{6,8},{8,10},{10,12},{12,14},{14,0},{1,3},{3,5},... | collective-permute-start | bytes 1032200 | tf_op jit(solution)/shard_map/ppermute | solution.py:615
  5.1 17.6 %collective-permute-start.3 = (f32[7,3,4,8,128]{4,3,2,1,0:T(8,128)S(1)}, f32[7,3,4,8,128]{4,3,2,1,0:T(8,128)S(1)}, u32[]{:S(2)}, u32[]{:S(2)}) collective-permute-start(f32[7,3,4,8,128]{4,3,2,1,0:T(8,128)S(1)} %get-tuple-element.10), channel_id=1, source_target_pairs={{2,0},{4,2},{6,4},{8,6},{10,8},{12,10},{14,12},{0,14},{3,1},{5,3},... | collective-permute-start | bytes 1032200 | tf_op jit(solution)/shard_map/ppermute | solution.py:616
  20.4 4.1 %collective-permute-start.2 = (f32[7,3,4,8,128]{4,3,2,1,0:T(8,128)S(1)}, f32[7,3,4,8,128]{4,3,2,1,0:T(8,128)S(1)}, u32[]{:S(2)}, u32[]{:S(2)}) collective-permute-start(f32[7,3,4,8,128]{4,3,2,1,0:T(8,128)S(1)} %collective-permute-done.1.left_here), channel_id=1, source_target_pairs={{0,1},{1,0},{2,3},{3,2},{4,5},{5,4},{6,7},{7,6},{8,9},{9,8},{10,11... | collective-permute-start | bytes 1032200 | tf_op jit(solution)/shard_map/ppermute | solution.py:618
  22.6 2.6 %collective-permute-start.4 = (f32[7,3,4,8,128]{4,3,2,1,0:T(8,128)S(1)}, f32[7,3,4,8,128]{4,3,2,1,0:T(8,128)}, u32[]{:S(2)}, u32[]{:S(2)}) collective-permute-start(f32[7,3,4,8,128]{4,3,2,1,0:T(8,128)S(1)} %collective-permute-done.3.right_here), channel_id=1, source_target_pairs={{0,1},{1,0},{2,3},{3,2},{4,5},{5,4},{6,7},{7,6},{8,9},{9,8},{10,11... | collective-permute-start | bytes 1032200 | tf_op jit(solution)/shard_map/ppermute | solution.py:619
  23.2 31.9 %copy-start.4 = (f32[64,64]{1,0:T(8,128)S(1)}, f32[64,64]{1,0:T(8,128)}, u32[]{:S(2)}) copy-start(f32[64,64]{1,0:T(8,128)} %constant.91.clone.table_x) | copy-start | bytes 49156
  23.4 31.6 %copy-start = (f32[512,512]{1,0:T(8,128)S(1)}, f32[512,512]{1,0:T(8,128)}, u32[]{:S(2)}) copy-start(f32[512,512]{1,0:T(8,128)} %constant.92.clone.spread_z) | copy-start | bytes 3145732
  23.5 14.6 %copy-start.6 = (s32[5]{0:T(128)}, s32[5]{0:T(128)S(1)}, u32[]{:S(2)}) copy-start(s32[5]{0:T(128)S(1)} %pad_add_fusion.meta) | copy-start | bytes 64
  24.5 0.7 copy-start.1
  25.3 1.0 %copy-start.2 = (f32[7,3,4,8,128]{4,3,2,1,0:T(8,128)S(1)}, f32[7,3,4,8,128]{4,3,2,1,0:T(8,128)}, u32[]{:S(2)}) copy-start(f32[7,3,4,8,128]{4,3,2,1,0:T(8,128)} %copy-done.1) | copy-start | bytes 1032196
  38.2 0.7 copy-start.3
  38.9 16.2 %all-to-all-start = ((f32[16,4,8,128]{3,2,1,0:T(8,128)}), f32[16,4,8,128]{3,2,1,0:T(8,128)S(1)}, u32[]{:S(2)}, u32[]{:S(2)}) async-start(f32[16,4,8,128]{3,2,1,0:T(8,128)} %bitcast.34), calls=%async_computation | async-start | bytes 524288 | tf_op jit(solution)/shard_map/all_to_all | solution.py:670
  45.0 1.6 %collective-permute-start.5 = (f32[8,3,4,8,128]{4,3,2,1,0:T(8,128)S(1)}, f32[8,3,4,8,128]{4,3,2,1,0:T(8,128)S(1)}, u32[]{:S(2)}, u32[]{:S(2)}) collective-permute-start(f32[8,3,4,8,128]{4,3,2,1,0:T(8,128)S(1)} %get-tuple-element.7.moved), channel_id=1, source_target_pairs={{12,28},{14,30},{13,29},{15,31}} | collective-permute-start | bytes 1179656 | tf_op jit(solution)/shard_map/ppermute | solution.py:669
  55.1 0.7 copy-start.7
  55.7 26.3 %copy-start.9 = (f32[2,256,256]{2,1,0:T(8,128)S(1)}, f32[2,256,256]{2,1,0:T(8,128)}, u32[]{:S(2)}) copy-start(f32[2,256,256]{2,1,0:T(8,128)} %constant.88.clone) | copy-start | bytes 1572868
  55.7 27.8 %copy-start.8 = (s32[5]{0:T(128)S(1)}, s32[5]{0:T(128)}, u32[]{:S(2)}) copy-start(s32[5]{0:T(128)} %copy-done.6) | copy-start | bytes 64
  82.0 1.6 %collective-permute-start.6 = (f32[8,64,128]{2,1,0:T(8,128)S(1)}, f32[8,64,128]{2,1,0:T(8,128)S(1)}, u32[]{:S(2)}, u32[]{:S(2)}) collective-permute-start(f32[8,64,128]{2,1,0:T(8,128)S(1)} %slice.32), channel_id=1, source_target_pairs={{0,1},{1,0},{2,3},{3,2},{4,5},{5,4},{6,7},{7,6},{8,9},{9,8},{10,11... | collective-permute-start | bytes 786440 | tf_op jit(solution)/shard_map/ppermute | solution.py:687

commit v3 on v0

--- a/solution.py
+++ b/solution.py
@@ -1,6 +1,11 @@
+import functools
+
 import jax
 import jax.numpy as jnp
+import numpy as np
 from jax import lax
+from jax.experimental import pallas as pl
+from jax.experimental.pallas import tpu as pltpu
 from jax.sharding import PartitionSpec as P
 
 RADIUS = 4
@@ -12,6 +17,12 @@
 DRIVING_FORCE = 0.1
 FRINGE_BLEND = 0.5
 HIGHEST = lax.Precision.HIGHEST
+STAGES = 3
+REACH = 2 * STAGES + 1
+LANES = 128
+SMALLEST = float(np.finfo(np.float32).tiny)
+ROWS = 8
+VMEM_BYTES = 20 * 1024 * 1024
 
 
 def extended(x, sides, width):
@@ -144,7 +155,7 @@
     return jnp.concatenate([changes[:1] + streamwise[None], changes[1:]], axis=0)
 
 
-def on_device(velocity, turbine_cells, fringe_bounds):
+def general_plan(velocity, turbine_cells, fringe_bounds):
     initial = velocity[0]
     levels, cells_x, cells_y = (initial.shape[1], initial.shape[2], initial.shape[3])
     total_y = cells_y * lax.axis_size("gy")
@@ -239,6 +250,687 @@
     return (velocity_next[None], pressure[None])
 
 
+def split(values):
+    high = values.astype(jnp.bfloat16)
+    low = values - high.astype(jnp.float32)
+    return high, low.astype(jnp.bfloat16)
+
+
+def dot(left, right):
+    (a, da), (b, db) = split(left), split(right)
+
+    def product(x, y):
+        return jnp.dot(x, y, preferred_element_type=jnp.float32)
+
+    return product(a, b) + (product(a, db) + product(da, b))
+
+
+def swap_blocks(arrays, width):
+    arrays = list(arrays)
+    block = lax.broadcasted_iota(jnp.int32, arrays[0].shape, 1) // width
+    step = 1
+    while step < len(arrays):
+        low = (block // step) % 2 == 0
+        for index in range(len(arrays)):
+            if (index // step) % 2 == 0:
+                first, second = arrays[index], arrays[index + step]
+                arrays[index] = jnp.where(low, first, pltpu.roll(second, step * width, 1))
+                arrays[index + step] = jnp.where(
+                    low, pltpu.roll(first, LANES - step * width, 1), second
+                )
+        step *= 2
+    return arrays
+
+
+class Stencil:
+    def __init__(self, tiles, rows, width, viscosity, faces, thrust, start):
+        self.tiles, self.rows, self.width = (tiles, rows, width)
+        self.viscosity, self.faces, self.thrust, self.start = (viscosity, faces, thrust, start)
+        row = lax.broadcasted_iota(jnp.int32, (rows, width), 0)
+        self.top = row == rows - 1
+        self.bottom = row == 0
+
+    def next_y(self, f):
+        return pltpu.roll(f, self.width - 1, 1)
+
+    def last_y(self, f):
+        return pltpu.roll(f, 1, 1)
+
+    def next_z(self, parts, t):
+        if t < self.tiles - 1:
+            return parts[t + 1]
+        return jnp.where(self.top, 0.0, pltpu.roll(parts[0], self.rows - 1, 0))
+
+    def last_z(self, parts, t):
+        if t > 0:
+            return parts[t - 1]
+        return jnp.where(self.bottom, 0.0, pltpu.roll(parts[self.tiles - 1], 1, 0))
+
+    def set_viscosity(self, now, first, count):
+        tiles = self.tiles
+
+        def column(n, carry):
+            i = first + n
+            here = [[now[i, c, t] for t in range(tiles)] for c in range(3)]
+            found = []
+            for t in range(tiles):
+                d_x = [now[i + 1, c, t] - now[i - 1, c, t] for c in range(3)]
+                d_y = [self.next_y(f[t]) - self.last_y(f[t]) for f in here]
+                d_z = [self.next_z(f, t) - self.last_z(f, t) for f in here]
+                diagonal = d_x[0] * d_x[0] + d_y[1] * d_y[1] + d_z[2] * d_z[2]
+                xy = d_x[1] + d_y[0]
+                xz = d_x[2] + d_z[0]
+                yz = d_y[2] + d_z[1]
+                total = (diagonal + diagonal) + (xy * xy + xz * xz + yz * yz)
+                root = total * lax.rsqrt(jnp.maximum(total, SMALLEST))
+                found.append((0.5 * SMAG_COEFF) * root)
+            for t in range(tiles):
+                self.viscosity[i, t] = found[t]
+            return carry
+
+        lax.fori_loop(0, count, column, 0, unroll=4 if count % 4 == 0 else 6)
+
+    def face(self, both, here, after, lead):
+        low = both + here[lead]
+        high = both - after[lead]
+        return [after[c] * high - here[c] * low for c in range(3)]
+
+    def face_x(self, now, i, t):
+        here = [now[i, c, t] for c in range(3)]
+        after = [now[i + 1, c, t] for c in range(3)]
+        return self.face(self.viscosity[i, t] + self.viscosity[i + 1, t], here, after, 0)
+
+    def advance(self, now, then, first, count, keep, gain):
+        tiles, scale = self.tiles, 0.5 * TIME_STEP * gain
+        for t in range(tiles):
+            for c, f in enumerate(self.face_x(now, first - 1, t)):
+                self.faces[c, t] = f
+
+        def column(n, carry):
+            i = first + n
+            eddy = [self.viscosity[i, t] for t in range(tiles)]
+            field = [[now[i, c, t] for t in range(tiles)] for c in range(3)]
+
+            def face_z(t):
+                here = [f[t] for f in field]
+                after = [self.next_z(f, t) for f in field]
+                return self.face(eddy[t] + self.next_z(eddy, t), here, after, 2)
+
+            last = face_z(tiles - 1)
+            floor = eddy[0] - field[2][0]
+            below = [
+                jnp.where(self.bottom, field[c][0] * floor, pltpu.roll(last[c], 1, 0))
+                for c in range(3)
+            ]
+            ahead_of = [self.face_x(now, i, t) for t in range(tiles)]
+            before_of = [[self.faces[c, t] for c in range(3)] for t in range(tiles)]
+            found = []
+            for t in range(tiles):
+                here = [f[t] for f in field]
+                above = last if t == tiles - 1 else face_z(t)
+                ahead, before = ahead_of[t], before_of[t]
+                beside = [self.next_y(f) for f in here]
+                side = self.face(eddy[t] + self.next_y(eddy[t]), here, beside, 1)
+                for c in range(3):
+                    change = (
+                        (ahead[c] - before[c])
+                        + (side[c] - self.last_y(side[c]))
+                        + (above[c] - below[c])
+                    )
+                    if c == 0:
+                        drag = self.thrust[i - 2, t] * here[0] * jnp.abs(here[0])
+                        change = change + (2.0 * DRIVING_FORCE - drag)
+                    if keep == 0.0:
+                        found.append(here[c] + scale * change)
+                    else:
+                        found.append(keep * self.start[i, c, t] + gain * here[c] + scale * change)
+                below = above
+            for t in range(tiles):
+                for c in range(3):
+                    then[i, c, t] = found[3 * t + c]
+                    self.faces[c, t] = ahead_of[t][c]
+            return carry
+
+        lax.fori_loop(0, count, column, 0, unroll=2)
+
+    def stage(self, number, now, then, first, count):
+        keep, gain = ((0.0, 1.0), (0.75, 0.25), (1.0 / 3.0, 2.0 / 3.0))[number]
+        self.set_viscosity(now, first - 1, count + 2)
+        self.advance(now, then, first, count, keep, gain)
+
+
+def place_columns(start, core, runs):
+    half = start.shape[-1] // 2
+
+    def copy(low_is_here):
+        for first, here, there, begin, count in runs:
+            low, high = (here, there) if low_is_here else (there, here)
+            start[pl.ds(first, count), :, :, :, :half] = low[pl.ds(begin, count)]
+            start[pl.ds(first, count), :, :, :, half:] = high[pl.ds(begin, count)]
+
+    pl.when(core == 0)(lambda: copy(True))
+    pl.when(core == 1)(lambda: copy(False))
+
+
+def near_kernel(
+    own_here,
+    own_there,
+    left_here,
+    left_there,
+    right_here,
+    right_there,
+    thrust,
+    first,
+    second,
+    third,
+    start,
+    stage_a,
+    stage_b,
+    viscosity,
+    faces,
+):
+    cells_x = own_here.shape[0]
+    near = left_here.shape[0]
+    _, _, tiles, rows, width = start.shape
+    core = lax.axis_index("gy")
+    place_columns(
+        start,
+        core,
+        (
+            (0, left_here, left_there, 0, near),
+            (near, own_here, own_there, 0, cells_x),
+            (near + cells_x, right_here, right_there, 0, near),
+        ),
+    )
+    stencil = Stencil(tiles, rows, width, viscosity, faces, thrust, start)
+    columns = start.shape[0]
+    stencil.stage(0, start, stage_a, 2, columns - 4)
+    stencil.stage(1, stage_a, stage_b, 4, columns - 8)
+    first[...] = stage_a[pl.ds(2 + core * (columns - 8), 4)]
+    second[...] = stage_b[pl.ds(4 + core * (columns - 12), 4)]
+    stencil.stage(2, stage_b, stage_a, 6, columns - 12)
+    third[...] = stage_a[pl.ds(6, columns - 12)]
+
+
+def far_kernel(
+    total_x,
+    fringe,
+    own_here,
+    own_there,
+    left_here,
+    left_there,
+    right_here,
+    right_there,
+    far_here,
+    far_there,
+    first,
+    second,
+    third,
+    thrust,
+    pieces,
+    source,
+    start,
+    stage_a,
+    stage_b,
+    stage_c,
+    viscosity,
+    faces,
+    columns_here,
+    columns_there,
+):
+    cells_x = own_here.shape[0]
+    near, far = left_here.shape[0], far_here.shape[0]
+    _, _, tiles, rows, width = start.shape
+    half = width // 2
+    share_x = cells_x // 2
+    inner = share_x + 1
+    core = lax.axis_index("gy")
+
+    @pl.when(core == 0)
+    def _():
+        place_columns(
+            start,
+            core,
+            (
+                (0, far_here, far_there, 0, far),
+                (far, left_here, left_there, 0, near),
+                (far + near, own_here, own_there, 0, inner),
+            ),
+        )
+
+    @pl.when(core == 1)
+    def _():
+        place_columns(
+            start,
+            core,
+            (
+                (0, own_here, own_there, cells_x - inner, inner),
+                (inner, right_here, right_there, 0, near),
+                (inner + near, far_here, far_there, 0, far),
+            ),
+        )
+
+    stencil = Stencil(tiles, rows, width, viscosity, faces, thrust, start)
+    stencil.stage(0, start, stage_a, 2 + 4 * core, 4)
+    stage_a[pl.ds(6 - 4 * core, 4)] = first[...]
+    stencil.stage(1, stage_a, stage_b, 4, 4)
+    stage_b[pl.ds(8 - 8 * core, 4)] = second[...]
+    stencil.stage(2, stage_b, stage_c, 6 - 4 * core, 4)
+    stage_c[pl.ds(10 - 10 * core, 2)] = third[...]
+
+    origin = REACH - core * (REACH - 1)
+    pairs = 3 * tiles // 2
+    for x in range(share_x):
+        for c in range(3):
+            for t in range(tiles):
+                n = c * tiles + t
+                field = stage_c[origin + x, c, t]
+                low, high = field[:, :half], field[:, half:]
+                spot = pl.ds((((n % 2) * share_x + x) * pairs + n // 2) * rows, rows)
+                columns_here[spot, :] = jnp.where(core == 0, low, high)
+                columns_there[spot, :] = jnp.where(core == 0, high, low)
+    for s in range(rows):
+        for m in range(pairs):
+            spot = pl.ds(m * rows + s, 2 * share_x, stride=pairs * rows)
+            pieces[0, s, m] = columns_here[spot, :]
+            pieces[1, s, m] = columns_there[spot, :]
+
+    is_farm = lax.axis_index("sec") == 1
+    corner = lax.axis_index("gx") * cells_x + core * share_x
+
+    def weight(offset, dest):
+        place = lax.rem(corner + offset + total_x, total_x)
+        inside = jnp.logical_and(place >= fringe[0], place < fringe[1])
+        blend = jnp.where(inside, FRINGE_BLEND, 0.0)
+        share = jnp.where(is_farm, 1.0 - blend, blend)
+        if dest == 0:
+            share = jnp.where(is_farm, 0.0, 1.0)
+        return 0.5 * share
+
+    for x in range(share_x):
+        i = origin + x
+        upright = [stage_c[i, 2, t] for t in range(tiles)]
+        for t in range(tiles):
+            cross = stage_c[i, 1, t]
+            plane = (stencil.next_y(cross) - stencil.last_y(cross)) + (
+                stencil.next_z(upright, t) - stencil.last_z(upright, t)
+            )
+            after, before = stage_c[i + 1, 0, t], stage_c[i - 1, 0, t]
+            for dest in range(2):
+                source[pl.ds(((dest * share_x + x) * tiles + t) * rows, rows), :] = (
+                    weight(x + 1, dest) * after
+                    - weight(x - 1, dest) * before
+                    + weight(x, dest) * plane
+                )
+
+
+def spectra_kernel(source, table_y, table_z, spectra, modes):
+    _, groups, _, parts, rows, lanes = spectra.shape
+    levels = table_z.shape[0]
+    count, total_y = source.shape
+    columns = count // levels
+    along_y = dot(source[...], table_y[...])
+    beside = [along_y[n * levels : (n + 1) * levels] for n in range(columns)]
+    both = dot(table_z[...], jnp.concatenate(beside, axis=1))
+    for n in range(columns):
+        for h in range(2):
+            first = n * total_y + h * lanes
+            modes[h, pl.ds(n * levels, levels), :] = both[:, first : first + lanes]
+    for dest in range(2):
+        for h in range(2):
+            for p in range(parts):
+                first = dest * count // 2 + p * groups
+                picked = [
+                    modes[h, pl.ds(first + b, rows, stride=levels // 2), :] for b in range(groups)
+                ]
+                for g, block in enumerate(swap_blocks(picked, lanes // groups)):
+                    spectra[dest, g, h, p] = block
+
+
+def blend_kernel(fringe, pieces, upstream, blended_here, blended_there):
+    _, groups, pairs, rows, lanes = pieces.shape
+    half = rows // 2
+    corner = lax.axis_index("gx") * rows + lax.axis_index("gy") * half
+    place = corner + lax.broadcasted_iota(jnp.int32, (rows, lanes), 0) % half
+    inside = jnp.logical_and(place >= fringe[0], place < fringe[1])
+    inside = jnp.logical_and(inside, lax.axis_index("sec") == 1)
+    weight = jnp.where(inside, FRINGE_BLEND, 0.0)[None, None]
+    for n, blended in enumerate((blended_here, blended_there)):
+        own = pieces[n]
+        blended[...] = own + weight * (upstream[n] - own)
+
+
+def pencil_kernel(received, inverse, table, blended_here, blended_there, packed):
+    _, groups, cores, parts, rows, lanes = received.shape
+    _, pairs, _, _ = blended_here.shape
+    total_x = groups * rows
+    lane_width = lanes // groups
+    wave, base = 2 * total_x, table.shape[1]
+    spread_z = table[:base]
+    pair_x = table[base : base + wave, :wave]
+    table_x = table[base : base + total_x, wave : wave + total_x]
+    spectrum = jnp.concatenate(
+        [(received[0, :, :, p] + received[1, :, :, p]).reshape(-1, lanes) for p in range(parts)],
+        axis=1,
+    )
+    solved = dot(pair_x, spectrum)
+    pieces = []
+    for a in range(2 * parts):
+        p, side = a % parts, a // parts
+        block = solved[side * total_x : (side + 1) * total_x, p * lanes : (p + 1) * lanes]
+        pieces.append(block * inverse[a])
+    field = dot(dot(table_x, jnp.concatenate(pieces, axis=1)), spread_z)
+    levels_of = [field[:, a * lanes : (a + 1) * lanes] for a in range(2 * parts)]
+    wide = lax.broadcasted_iota(jnp.int32, (total_x // 2, lanes), 1)
+    left = wide < lanes // 2
+    quarter = total_x // 4
+    block = lax.broadcasted_iota(jnp.int32, (quarter, lanes), 1) // lane_width
+    low = lax.broadcasted_iota(jnp.int32, (rows, lanes), 0) < rows // 2
+    is_first = lax.axis_index("gy") == 0
+    for g in range(groups):
+        a, odd = divmod(g, 2)
+        now = levels_of[a]
+        front, rear = now[: total_x // 2], now[total_x // 2 :]
+        if odd:
+            main = jnp.where(left, pltpu.roll(front, lanes // 2, 1), rear)
+            lower, lower_lane = now, lanes // 2 - lane_width
+            upper, upper_lane = levels_of[min(a + 1, 2 * parts - 1)], 0
+        else:
+            main = jnp.where(left, front, pltpu.roll(rear, lanes // 2, 1))
+            lower, lower_lane = levels_of[max(a - 1, 0)], lanes - lane_width
+            upper, upper_lane = now, lanes // 2
+        edge = None
+        for q in range(4):
+            for n, (whole, lane) in enumerate(((lower, lower_lane), (upper, upper_lane))):
+                spot = 2 * q + n
+                move = (spot * lane_width - lane) % lanes
+                rolled = whole[q * quarter : (q + 1) * quarter]
+                if move:
+                    rolled = pltpu.roll(rolled, move, 1)
+                edge = rolled if edge is None else jnp.where(block == spot, rolled, edge)
+        packed[g, : total_x // 2] = main
+        packed[g, total_x // 2 : 3 * quarter] = edge
+        for m in range(pairs):
+            here, there = blended_here[g, m], blended_there[g, m]
+            before = jnp.where(is_first, here, there)
+            after = jnp.where(is_first, there, here)
+            first = 3 * quarter + 2 * m * rows
+            packed[g, first : first + rows] = jnp.where(
+                low, before, pltpu.roll(after, rows // 2, 0)
+            )
+            packed[g, first + rows : first + 2 * rows] = jnp.where(
+                low, pltpu.roll(before, rows // 2, 0), after
+            )
+
+
+def project_kernel(received, partner, table_y, velocity_next, pressure):
+    groups = received.shape[0]
+    share, total_x, lanes = pressure.shape
+    cells_x = total_x // groups
+    width = lanes // groups
+    place, core = lax.axis_index("gx"), lax.axis_index("gy")
+    main_rows = total_x // 2
+    rows = partner.shape[1]
+
+    def levels_in(arrays):
+        main = swap_blocks([arrays[s, :main_rows] for s in range(groups)], width)
+        edge = swap_blocks([arrays[s, main_rows:rows] for s in range(groups)], width)
+        inner = [jnp.concatenate([main[n], main[share + n]], axis=0) for n in range(share)]
+        outer = [jnp.concatenate([edge[2 * q + n] for q in range(4)], axis=0) for n in range(2)]
+        return [outer[0]] + inner + [outer[1]]
+
+    here, there = levels_in(received), levels_in(partner)
+    here, there = jnp.concatenate(here, axis=0), jnp.concatenate(there, axis=0)
+    low = jnp.where(core == 0, here, there)
+    high = jnp.where(core == 0, there, here)
+    both = dot(jnp.concatenate([low, high], axis=1), table_y[core])
+    fields = [both[n * total_x : (n + 1) * total_x] for n in range(share + 2)]
+    values = [f[:, :lanes] for f in fields]
+    values[0] = jnp.where(place == 0, values[1], values[0])
+    values[-1] = jnp.where(place == groups - 1, -values[-2], values[-1])
+    for z in range(share):
+        now = values[z + 1]
+        pressure[z] = now
+        slopes = [
+            0.5 * (pltpu.roll(now, total_x - 1, 0) - pltpu.roll(now, 1, 0)),
+            fields[z + 1][:, lanes:],
+            0.5 * (values[z + 2] - values[z]),
+        ]
+        for c in range(3):
+            first = rows + (c * share + z) * cells_x
+            blended = received[:, first : first + cells_x].reshape(total_x, lanes)
+            velocity_next[c, z] = blended - slopes[c]
+
+
+def cas(rows, columns, length):
+    angle = (np.outer(rows, columns) % length) * (2.0 * np.pi / length)
+    return np.cos(angle) + np.sin(angle)
+
+
+def tables(levels, total_x, total_y, groups):
+    half = total_y // 2
+    lane_width = LANES // groups
+    every_x = np.arange(total_x)
+    every_y = np.arange(total_y)
+    table_x = cas(every_x, every_x, total_x)
+    table_y = cas(every_y, every_y, total_y)
+    slope_y = 0.5 * (np.roll(table_y, -1, axis=1) - np.roll(table_y, 1, axis=1))
+    level = np.arange(levels) + 0.5
+    table_z = np.cos(np.outer(level, level) * (np.pi / levels))
+    spread_z = np.kron(table_z, np.eye(lane_width))
+    order = np.arange(levels).reshape(ROWS, levels // ROWS).T.reshape(levels)
+    backward = [
+        np.concatenate([table_y[:, here], slope_y[:, here]], axis=1)
+        for here in (slice(0, half), slice(half, total_y))
+    ]
+    pair_x = np.einsum("kx,ab->akxb", table_x, np.eye(2)).reshape(2 * total_x, 2 * total_x)
+    eigen = (
+        (2.0 * np.cos(level * (np.pi / levels)) - 2.0)[:, None, None]
+        + (2.0 * np.cos(every_x * (2.0 * np.pi / total_x)) - 2.0)[None, :, None]
+        + (2.0 * np.cos(every_y * (2.0 * np.pi / total_y)) - 2.0)[None, None, :]
+    )
+    inverse = (2.0 / levels) / (total_x * total_y) / eigen
+    inverse = inverse.reshape(levels // groups, groups, total_x, 2, groups, lane_width)
+    inverse = inverse.transpose(4, 3, 0, 2, 1, 5).reshape(
+        groups, 2, levels // groups, total_x, LANES
+    )
+    pencil = np.zeros((spread_z.shape[0] + 2 * total_x, spread_z.shape[1]))
+    pencil[: spread_z.shape[0]] = spread_z
+    pencil[spread_z.shape[0] :, : 2 * total_x] = pair_x
+    pencil[spread_z.shape[0] : -total_x, 2 * total_x : 3 * total_x] = table_x
+    return [
+        jnp.asarray(t, jnp.float32)
+        for t in (
+            pencil,
+            table_y,
+            np.stack(backward),
+            table_z[:, order],
+            inverse,
+        )
+    ]
+
+
+def call(kernel, out_shapes, scratch, *operands):
+    in_specs = [
+        pl.BlockSpec(memory_space=pltpu.SMEM if o.dtype == jnp.int32 else pltpu.VMEM)
+        for o in operands
+    ]
+    return pl.pallas_call(
+        kernel,
+        out_shape=out_shapes,
+        in_specs=in_specs,
+        out_specs=jax.tree.map(lambda _: pl.BlockSpec(memory_space=pltpu.VMEM), out_shapes),
+        scratch_shapes=scratch,
+        compiler_params=pltpu.CompilerParams(vmem_limit_bytes=VMEM_BYTES),
+    )(*operands)
+
+
+def thrust_weights(turbine_cells, along_x, along_y, along_z, total_y, strength):
+    matches = (along_x[:, None] == turbine_cells[None, :, 0]).astype(jnp.bfloat16)
+    offset_y = (along_y[None, :] - turbine_cells[:, 1:2] + total_y // 2) % total_y - total_y // 2
+    offset_z = along_z[None, :] - turbine_cells[:, 2:3]
+    distance = (
+        offset_z[:, :, None] * offset_z[:, :, None] + offset_y[:, None, :] * offset_y[:, None, :]
+    )
+    inside = (distance <= RADIUS * RADIUS).astype(jnp.bfloat16)
+    count = jnp.einsum("xt,tzy->xzy", matches, inside, preferred_element_type=jnp.float32)
+    return strength * count
+
+
+def paired_plan(velocity, turbine_cells, fringe_bounds):
+    groups = lax.axis_size("gx")
+    initial = velocity[0]
+    _, levels, cells_x, cells_y = initial.shape
+    total_x, total_y = cells_x * groups, 2 * cells_y
+    share, share_x = levels // ROWS, cells_x // 2
+    section, place, core = (lax.axis_index("sec"), lax.axis_index("gx"), lax.axis_index("gy"))
+    pencil, table_y, backward, table_z, inverse = tables(levels, total_x, total_y, groups)
+
+    near, far = REACH - 4, 4
+    up = [(i, (i + 1) % groups) for i in range(groups)]
+    down = [(j, i) for i, j in up]
+    swap = [(0, 1), (1, 0)]
+    straight = [(2 * i, 2 * j) for i, j in up] + [(2 * j + 1, 2 * i + 1) for i, j in up]
+    crossed = [(2 * i + 1, 2 * j) for i, j in up] + [(2 * j, 2 * i + 1) for i, j in up]
+    own = jnp.transpose(initial.reshape(3, ROWS, share, cells_x, cells_y), (3, 0, 2, 1, 4))
+    left = lax.ppermute(own[cells_x - near :], "gx", up)
+    right = lax.ppermute(own[:near], "gx", down)
+    tail, head = cells_x - REACH, near
+    same = lax.dynamic_slice_in_dim(own, jnp.where(core == 0, tail, head), far, 0)
+    other = lax.dynamic_slice_in_dim(own, jnp.where(core == 0, head, tail), far, 0)
+    far_here = lax.ppermute(same, ("gx", "gy"), straight)
+    far_there = lax.ppermute(other, ("gx", "gy"), crossed)
+    own_there = lax.ppermute(own, "gy", swap)
+    left_there = lax.ppermute(left, "gy", swap)
+    right_there = lax.ppermute(right, "gy", swap)
+
+    strength = 2.0 * THRUST_COEFF * section.astype(jnp.float32)
+    along_z = jnp.arange(levels).reshape(ROWS, share).T.reshape(levels)
+
+    def thrust_on(offset, count):
+        along_x = (place * cells_x + offset + jnp.arange(count) + total_x) % total_x
+        weights = thrust_weights(
+            turbine_cells, along_x, jnp.arange(total_y), along_z, total_y, strength
+        )
+        return weights.reshape(count, share, ROWS, total_y)
+
+    near_thrust = thrust_on(2 - near, cells_x + 2 * near - 4)
+    far_thrust = thrust_on((2 - REACH) * (1 - core) + (share_x + 1) * core, far + near + share_x - 3)
+    own_inverse = lax.dynamic_slice(
+        inverse, (place, core, 0, 0, 0), (1, 1) + inverse.shape[2:]
+    )[0, 0]
+
+    f32 = jnp.float32
+    body = (3, share, ROWS, total_y)
+
+    def columns(count):
+        return pltpu.VMEM((count,) + body, f32)
+
+    reached = cells_x + 2 * near
+    shapes = [jax.ShapeDtypeStruct((n,) + body, f32) for n in (4, 4, reached - 12)]
+    first, second, third = call(
+        near_kernel,
+        shapes,
+        [columns(reached)] * 3
+        + [pltpu.VMEM((reached,) + body[1:], f32), pltpu.VMEM(body, f32)],
+        own,
+        own_there,
+        left,
+        left_there,
+        right,
+        right_there,
+        near_thrust,
+    )
+    window = far + near + share_x + 1
+    pairs = 3 * share // 2
+    piece = jax.ShapeDtypeStruct((ROWS, pairs, 2 * share_x, cells_y), f32)
+    parts = levels // (2 * groups)
+    pieces, source = call(
+        functools.partial(far_kernel, total_x),
+        [
+            jax.ShapeDtypeStruct((2,) + piece.shape, f32),
+            jax.ShapeDtypeStruct((2 * share_x * levels, total_y), f32),
+        ],
+        [columns(window)] * 4
+        + [
+            pltpu.VMEM((window,) + body[1:], f32),
+            pltpu.VMEM(body, f32),
+            pltpu.VMEM((share_x * 3 * levels, cells_y), f32),
+            pltpu.VMEM((share_x * 3 * levels, cells_y), f32),
+        ],
+        fringe_bounds,
+        own,
+        own_there,
+        left,
+        left_there,
+        right,
+        right_there,
+        far_here,
+        far_there,
+        first,
+        second,
+        third,
+        far_thrust,
+    )
+    outlet = [(g, groups + g) for g in range(groups - groups // 4, groups)]
+    upstream = lax.ppermute(pieces, ("sec", "gx"), outlet)
+    spectra = call(
+        spectra_kernel,
+        jax.ShapeDtypeStruct((2, groups, 2, parts, 2 * share_x, LANES), f32),
+        [pltpu.VMEM((2, 2 * share_x * levels, LANES), f32)],
+        source,
+        table_y,
+        table_z,
+    )
+    received = lax.all_to_all(
+        spectra.reshape((4 * groups,) + spectra.shape[3:]), ("sec", "gx", "gy"), 0, 0, tiled=True
+    ).reshape(spectra.shape)
+    blended_here, blended_send = call(
+        blend_kernel, [piece, piece], [], fringe_bounds, pieces, upstream
+    )
+    blended_there = lax.ppermute(blended_send, "gy", swap)
+    pressure_rows = 3 * total_x // 4
+    packed = call(
+        pencil_kernel,
+        jax.ShapeDtypeStruct((groups, pressure_rows + 3 * share * cells_x, LANES), f32),
+        [],
+        received,
+        own_inverse,
+        pencil,
+        blended_here,
+        blended_there,
+    )
+    returned = lax.all_to_all(packed, "gx", 0, 0, tiled=True)
+    partner = lax.ppermute(returned[:, :pressure_rows], "gy", swap)
+    velocity_next, pressure = call(
+        project_kernel,
+        [
+            jax.ShapeDtypeStruct((3, share, total_x, cells_y), f32),
+            jax.ShapeDtypeStruct((share, total_x, cells_y), f32),
+        ],
+        [],
+        returned,
+        partner,
+        backward,
+    )
+    return (velocity_next[None], pressure[None])
+
+
+def on_device(velocity, turbine_cells, fringe_bounds):
+    groups = lax.axis_size("gx")
+    _, _, levels, cells_x, cells_y = velocity.shape
+    paired = (
+        lax.axis_size("gy") == 2
+        and lax.axis_size("sec") == 2
+        and cells_y == LANES
+        and cells_x == ROWS
+        and groups == ROWS
+        and 2 * levels == groups * groups
+    )
+    plan = paired_plan if paired else general_plan
+    return plan(velocity, turbine_cells, fringe_bounds)
+
+
 def solution(mesh):
     return jax.shard_map(
         on_device,

time: 171 us -> 70.9 us (0.41)
  waiting for transfers between devices: 61.9 us -> 17.7 us
  starting transfers between devices: 47 us -> 16.1 us
  local copies, waits for them, and re-layouts: 30.2 us -> 2.6 us
  other arithmetic: 16.1 us -> 0.21 us
  Pallas kernels: 0 us -> 12.3 us
  blocking collectives: 8.1 us -> 19.7 us
  matrix products: 5.45 us -> 1.13 us
    ppermute x25 -> x10, starting transfers between devices: 36.2 us -> 9.95 us  [the longest x1 3.1 us: paired_plan(): right = lax.ppermute(own[:near], 'gx', down)]
    all_to_all x3 -> x1, waiting for transfers between devices: 33.2 us -> 8.43 us  [paired_plan(): lax.all_to_all(spectra.reshape((4 * groups,) + spectra.shape[3:]), ('sec'...]
    ppermute x25 -> x10, waiting for transfers between devices: 28.7 us -> 9.28 us  [the longest x1 4.62 us: paired_plan(): left = lax.ppermute(own[cells_x - near:], 'gx', up)]
    pallas_call x0 -> x6, Pallas kernels: none -> 12.3 us  [call(): pl.pallas_call(kernel, out_shape=out_shapes, in_specs=in_specs, out_specs...]
    all_to_all x2 -> x1, blocking collectives: 8.1 us -> 19.7 us  [paired_plan(): returned = lax.all_to_all(packed, 'gx', 0, 0, tiled=True)]
    slice x35 -> x2, local copies, waits for them, and re-layouts: 11.3 us -> 0.03 us  [the longest x1 0.02 us: paired_plan(): right = lax.ppermute(own[:near], 'gx', down)]
    concatenate x10 -> x0, other arithmetic: 6.19 us -> none  [the longest x9 6.19 us: extended(): x = jnp.concatenate([before, x, after], axis=dim)]
    all_to_all x3 -> x1, starting transfers between devices: 10.8 us -> 6.14 us  [paired_plan(): lax.all_to_all(spectra.reshape((4 * groups,) + spectra.shape[3:]), ('sec'...]
  transfers between devices with their start and end apart: 28 -> 11, of which waited for: 20 -> 5; matrix products, arithmetic and copies ran while one was open for 5% -> 4% of each run, Pallas kernels for 0% -> 9%
where the time goes in v3:
time: 70.9 us; the launch traced here: 70.6 us
  blocking collectives  19.7 us (28%)
  waiting for transfers between devices  17.7 us (25%)
  starting transfers between devices  16.1 us (23%)
  Pallas kernels  12.3 us (17%)
  local copies, waits for them, and re-layouts  2.6 us (4%)
  matrix products  1.13 us (2%)
  between operations  0.84 us (1%)
    all_to_all x1, blocking collectives, paired_plan(): returned = lax.all_to_all(packed, 'gx', 0, 0, tiled=True)  19.7 us
    pallas_call x6, Pallas kernels, call(): pl.pallas_call(kernel, out_shape=out_shapes, in_specs=in_specs, out_specs...  12.3 us
    all_to_all x1, waiting for transfers between devices, paired_plan(): lax.all_to_all(spectra.reshape((4 * groups,) + spectra.shape[3:]), ('sec'...  8.43 us
    all_to_all x1, starting transfers between devices, paired_plan(): lax.all_to_all(spectra.reshape((4 * groups,) + spectra.shape[3:]), ('sec'...  6.14 us
    ppermute x1, waiting for transfers between devices, paired_plan(): left = lax.ppermute(own[cells_x - near:], 'gx', up)  4.62 us
    ppermute x1, starting transfers between devices, paired_plan(): right = lax.ppermute(own[:near], 'gx', down)  3.1 us
    ppermute x1, starting transfers between devices, paired_plan(): far_there = lax.ppermute(other, ('gx', 'gy'), crossed)  2.61 us
    ppermute x1, starting transfers between devices, paired_plan(): left = lax.ppermute(own[cells_x - near:], 'gx', up)  2.59 us
  transfers between devices with their start and end apart: 11, of which 5 were waited for; matrix products, arithmetic and copies ran while one was open for 4% of the time, Pallas kernels for 9%

profile of v3, /device:TPU:0, one launch (start us, length us, event | category | flops | bytes accessed | tf_op | source)
XLA Modules:
  0.0 70.6 jit_solution(4743417647120616880)
XLA Ops:
  0.6 0.0 copy-start.5
  0.6 1.2 %copy.23 = f32[3,8,4,8,128]{4,1,2,0,3:T(8,128)S(1)} copy(f32[3,8,4,8,128]{4,3,2,1,0:T(8,128)} %bitcast.38) | data formatting | bytes 786432 | tf_op jit(solution)/shard_map/reshape;squeeze | solution.py:795
  1.9 0.5 collective-permute-start
  2.4 2.6 %collective-permute-start.1 = (f32[3,3,4,8,128]{4,3,2,1,0:T(8,128)S(1)}, f32[3,3,4,8,128]{4,3,2,1,0:T(8,128)S(1)}, u32[]{:S(2)}, u32[]{:S(2)}) collective-permute-start(f32[3,3,4,8,128]{4,3,2,1,0:T(8,128)S(1)} %get-tuple-element.25), channel_id=1, source_target_pairs={{0,2},{2,4},{4,6},{6,8},{8,10},{10,12},{12,14},{14,0},{1,3},{3,5},... | collective-permute-start | bytes 442376 | tf_op jit(solution)/shard_map/ppermute | solution.py:796
  5.0 3.1 %collective-permute-start.3 = (f32[3,3,4,8,128]{4,3,2,1,0:T(8,128)S(1)}, f32[3,3,4,8,128]{4,3,2,1,0:T(8,128)S(1)}, u32[]{:S(2)}, u32[]{:S(2)}) collective-permute-start(f32[3,3,4,8,128]{4,3,2,1,0:T(8,128)S(1)} %get-tuple-element.24), channel_id=1, source_target_pairs={{2,0},{4,2},{6,4},{8,6},{10,8},{12,10},{14,12},{0,14},{3,1},{5,3},... | collective-permute-start | bytes 442376 | tf_op jit(solution)/shard_map/ppermute | solution.py:797
  8.1 0.1 collective-permute-start.5
  8.2 2.6 %collective-permute-start.6 = (f32[4,3,4,8,128]{4,3,2,1,0:T(8,128)S(1)}, f32[4,3,4,8,128]{4,3,2,1,0:T(8,128)S(1)}, u32[]{:S(2)}, u32[]{:S(2)}) collective-permute-start(f32[4,3,4,8,128]{4,3,2,1,0:T(8,128)S(1)} %get-tuple-element.20), channel_id=1, source_target_pairs={{1,2},{3,4},{5,6},{7,8},{9,10},{11,12},{13,14},{15,0},{2,1},{4,3},... | collective-permute-start | bytes 589832 | tf_op jit(solution)/shard_map/ppermute | solution.py:802
  10.8 0.0 copy-done.5
  10.9 0.1 fusion.12
  11.0 0.1 reshape.142
  11.0 0.1 subtract_multiply_fusion
  11.1 0.6 fusion.2
  11.7 0.0 copy-start.4
  11.7 0.2 copy.21
  11.9 4.6 %collective-permute-done.1.left_here = f32[3,3,4,8,128]{4,3,2,1,0:T(8,128)S(1)} collective-permute-done((f32[3,3,4,8,128]{4,3,2,1,0:T(8,128)S(1)}, f32[3,3,4,8,128]{4,3,2,1,0:T(8,128)S(1)}, u32[]{:S(2)}, u32[]{:S(2)}) %collective-permute-start.1) | collective-permute-done | bytes 147488 | tf_op jit(solution)/shard_map/ppermute | solution.py:796
  16.5 0.0 collective-permute-start.2
  16.5 2.5 %collective-permute-done.3.right_here = f32[3,3,4,8,128]{4,3,2,1,0:T(8,128)S(1)} collective-permute-done((f32[3,3,4,8,128]{4,3,2,1,0:T(8,128)S(1)}, f32[3,3,4,8,128]{4,3,2,1,0:T(8,128)S(1)}, u32[]{:S(2)}, u32[]{:S(2)}) %collective-permute-start.3) | collective-permute-done | bytes 147488 | tf_op jit(solution)/shard_map/ppermute | solution.py:797
  19.1 0.0 collective-permute-start.4
  19.1 0.6 fusion.3
  19.6 0.1 copy.22
  19.7 0.0 collective-permute-done.2.left_there
  19.7 0.7 collective-permute-done.4.right_there
  20.4 0.0 collective-permute-done.own_there
  20.4 0.0 copy-start.2
  20.4 0.0 copy-start.3
  20.4 4.2 %shard_map.95 = (f32[4,3,4,8,256]{4,3,2,1,0:T(8,128)S(1)}, f32[4,3,4,8,256]{4,3,2,1,0:T(8,128)S(1)}, f32[2,3,4,8,256]{4,3,2,1,0:T(8,128)S(1)}) custom-call(f32[8,3,4,8,128]{4,3,2,1,0:T(8,128)S(1)} %bitcast.33, f32[8,3,4,8,128]{4,3,2,1,0:T(8,128)S(1)} %collective-permute-done.own_there, f32[3,3,4,8,128]{4,3,2,1,0:T(8,128)S(1)} %collective-permute-done.1.left_here, ...), custom_call_target="tpu_custom_call" | custom-call | tf_op jit(solution)/shard_map/pallas_call | solution.py:758
  24.7 0.0 collective-permute-done.5.far_here
  24.7 0.0 collective-permute-done.6.far_there
  24.7 0.0 copy-done.4
  24.7 0.0 copy-start
  24.7 3.6 %shard_map.96 = (f32[2,8,6,8,128]{4,3,2,1,0:T(8,128)S(1)}, f32[256,256]{1,0:T(8,128)S(1)}) custom-call(s32[2]{0:T(128)S(1)} %copy-done.4, f32[8,3,4,8,128]{4,3,2,1,0:T(8,128)S(1)} %bitcast.34, f32[8,3,4,8,128]{4,3,2,1,0:T(8,128)S(1)} %collective-permute-done.own_there, f32[3,3,4,8,128]{4,3,2,1,0:T(8,128)S(1)} %collective-permute-done.1.left_here, ...), custom_call_target="tpu_custom_call" | custom-call | tf_op jit(solution)/shard_map/pallas_call | solution.py:758
  28.3 0.7 collective-permute-start.7
  29.0 0.0 copy-done.2
  29.0 0.0 copy-done.3
  29.0 1.6 %shard_map.97 = f32[2,8,2,2,8,128]{5,4,3,2,1,0:T(8,128)} custom-call(f32[256,256]{1,0:T(8,128)S(1)} %get-tuple-element.14.source, f32[256,256]{1,0:T(8,128)S(1)} %copy-done.2, f32[32,32]{1,0:T(8,128)S(1)} %copy-done.3), custom_call_target="tpu_custom_call" | custom-call | tf_op jit(solution)/shard_map/pallas_call | solution.py:758
  30.6 6.1 %all-to-all-start = ((f32[32,2,8,128]{3,2,1,0:T(8,128)}), f32[32,2,8,128]{3,2,1,0:T(8,128)S(1)}, u32[]{:S(2)}, u32[]{:S(2)}) async-start(f32[32,2,8,128]{3,2,1,0:T(8,128)} %bitcast.11), calls=%async_computation | async-start | bytes 524288 | tf_op jit(solution)/shard_map/all_to_all | solution.py:885
  36.8 0.0 collective-permute-done.7.upstream
  36.8 0.6 shard_map.98
  37.4 0.3 collective-permute-start.8
  37.7 0.9 %dynamic-slice_bitcast_fusion.2.inverse = f32[4,64,128]{2,1,0:T(8,128)S(1)} fusion(f32[8,2,4,64,128]{4,3,2,1,0:T(8,128)} %constant.95.clone, s32[]{:T(128)S(6)} %select_n.53, s32[]{:T(128)S(6)} %select_n.54), kind=kLoop, calls=%fused_computation.15 | loop fusion | bytes 262152 | tf_op jit(solution)/shard_map/squeeze | solution.py:819
  38.6 8.4 %all-to-all-done = f32[32,2,8,128]{3,2,1,0:T(8,128)S(1)} async-done(((f32[32,2,8,128]{3,2,1,0:T(8,128)}), f32[32,2,8,128]{3,2,1,0:T(8,128)S(1)}, u32[]{:S(2)}, u32[]{:S(2)}) %all-to-all-start) | async-done | bytes 262176 | tf_op jit(solution)/shard_map/all_to_all | solution.py:885
  47.0 0.0 collective-permute-done.8.blended_there
  47.0 0.0 copy-done
  47.0 0.0 copy-start.1
  47.0 0.9 %shard_map.99 = f32[8,144,128]{2,1,0:T(8,128)S(1)} custom-call(f32[2,8,2,2,8,128]{5,4,3,2,1,0:T(8,128)S(1)} %bitcast.37, f32[4,64,128]{2,1,0:T(8,128)S(1)} %dynamic-slice_bitcast_fusion.2.inverse, f32[640,512]{1,0:T(8,128)S(1)} %copy-done, f32[8,6,8,128]{3,2,1,0:T(8,128)S(1)} %get-tuple-element.16.blended_here, ...), custom_call_target="tpu_custom_call" | custom-call | tf_op jit(solution)/shard_map/pallas_call | solution.py:758
  48.0 19.7 %all_to_all.10.received = f32[8,144,128]{2,1,0:T(8,128)S(1)} all-to-all(f32[8,144,128]{2,1,0:T(8,128)S(1)} %shard_map.99), channel_id=1, replica_groups=mesh['sec'=2,'gx'=8,'gy'=2] {'gx'}, dimensions={0} | all-to-all | bytes 1179648 | tf_op jit(solution)/shard_map/all_to_all | solution.py:903
  67.7 0.1 collective-permute-start.9
  67.8 1.4 %collective-permute-done.9.partner = f32[8,48,128]{2,1,0:T(8,128)S(1)} collective-permute-done((f32[8,48,128]{2,1,0:T(8,128)S(1)}, f32[8,48,128]{2,1,0:T(8,128)S(1)}, u32[]{:S(2)}, u32[]{:S(2)}) %collective-permute-start.9) | collective-permute-done | bytes 196640 | tf_op jit(solution)/shard_map/ppermute | solution.py:904
  69.2 0.0 copy-done.1
  69.2 1.4 %shard_map.100 = (f32[3,4,64,128]{3,2,1,0:T(8,128)}, f32[4,64,128]{2,1,0:T(8,128)}) custom-call(f32[8,144,128]{2,1,0:T(8,128)S(1)} %all_to_all.10.received, f32[8,48,128]{2,1,0:T(8,128)S(1)} %collective-permute-done.9.partner, f32[2,256,256]{2,1,0:T(8,128)S(1)} %copy-done.1), custom_call_target="tpu_custom_call" | custom-call | tf_op jit(solution)/shard_map/pallas_call | solution.py:758
  (7 shorter events, 0.1 us)
Async XLA Ops:
  0.6 10.2 %copy-start.5 = (s32[64,3]{0,1:T(4,128)S(1)}, s32[64,3]{0,1:T(4,128)}, u32[]{:S(2)}) copy-start(s32[64,3]{0,1:T(4,128)} %param.9) | copy-start | bytes 2308
  1.9 18.6 %collective-permute-start = (f32[8,3,4,8,128]{4,3,2,1,0:T(8,128)S(1)}, f32[8,3,4,8,128]{4,3,2,1,0:T(8,128)S(1)}, u32[]{:S(2)}, u32[]{:S(2)}) collective-permute-start(f32[8,3,4,8,128]{4,3,2,1,0:T(8,128)S(1)} %bitcast.31), channel_id=1, source_target_pairs={{0,1},{1,0},{2,3},{3,2},{4,5},{5,4},{6,7},{7,6},{8,9},{9,8},{10,11... | collective-permute-start | bytes 1179656 | tf_op jit(solution)/shard_map/ppermute | solution.py:803
  2.4 14.1 %collective-permute-start.1 = (f32[3,3,4,8,128]{4,3,2,1,0:T(8,128)S(1)}, f32[3,3,4,8,128]{4,3,2,1,0:T(8,128)S(1)}, u32[]{:S(2)}, u32[]{:S(2)}) collective-permute-start(f32[3,3,4,8,128]{4,3,2,1,0:T(8,128)S(1)} %get-tuple-element.25), channel_id=1, source_target_pairs={{0,2},{2,4},{4,6},{6,8},{8,10},{10,12},{12,14},{14,0},{1,3},{3,5},... | collective-permute-start | bytes 442376 | tf_op jit(solution)/shard_map/ppermute | solution.py:796
  5.0 14.1 %collective-permute-start.3 = (f32[3,3,4,8,128]{4,3,2,1,0:T(8,128)S(1)}, f32[3,3,4,8,128]{4,3,2,1,0:T(8,128)S(1)}, u32[]{:S(2)}, u32[]{:S(2)}) collective-permute-start(f32[3,3,4,8,128]{4,3,2,1,0:T(8,128)S(1)} %get-tuple-element.24), channel_id=1, source_target_pairs={{2,0},{4,2},{6,4},{8,6},{10,8},{12,10},{14,12},{0,14},{3,1},{5,3},... | collective-permute-start | bytes 442376 | tf_op jit(solution)/shard_map/ppermute | solution.py:797
  8.1 16.5 %collective-permute-start.5 = (f32[4,3,4,8,128]{4,3,2,1,0:T(8,128)S(1)}, f32[4,3,4,8,128]{4,3,2,1,0:T(8,128)S(1)}, u32[]{:S(2)}, u32[]{:S(2)}) collective-permute-start(f32[4,3,4,8,128]{4,3,2,1,0:T(8,128)S(1)} %get-tuple-element.21), channel_id=1, source_target_pairs={{0,2},{2,4},{4,6},{6,8},{8,10},{10,12},{12,14},{14,0},{3,1},{5,3},... | collective-permute-start | bytes 589832 | tf_op jit(solution)/shard_map/ppermute | solution.py:801
  8.2 16.5 %collective-permute-start.6 = (f32[4,3,4,8,128]{4,3,2,1,0:T(8,128)S(1)}, f32[4,3,4,8,128]{4,3,2,1,0:T(8,128)S(1)}, u32[]{:S(2)}, u32[]{:S(2)}) collective-permute-start(f32[4,3,4,8,128]{4,3,2,1,0:T(8,128)S(1)} %get-tuple-element.20), channel_id=1, source_target_pairs={{1,2},{3,4},{5,6},{7,8},{9,10},{11,12},{13,14},{15,0},{2,1},{4,3},... | collective-permute-start | bytes 589832 | tf_op jit(solution)/shard_map/ppermute | solution.py:802
  11.7 13.0 %copy-start.4 = (s32[2]{0:T(128)S(1)}, s32[2]{0:T(128)}, u32[]{:S(2)}) copy-start(s32[2]{0:T(128)} %fringe.3) | copy-start | bytes 28
  16.5 3.2 %collective-permute-start.2 = (f32[3,3,4,8,128]{4,3,2,1,0:T(8,128)S(1)}, f32[3,3,4,8,128]{4,3,2,1,0:T(8,128)S(1)}, u32[]{:S(2)}, u32[]{:S(2)}) collective-permute-start(f32[3,3,4,8,128]{4,3,2,1,0:T(8,128)S(1)} %collective-permute-done.1.left_here), channel_id=1, source_target_pairs={{0,1},{1,0},{2,3},{3,2},{4,5},{5,4},{6,7},{7,6},{8,9},{9,8},{10,11... | collective-permute-start | bytes 442376 | tf_op jit(solution)/shard_map/ppermute | solution.py:804
  19.1 1.4 %collective-permute-start.4 = (f32[3,3,4,8,128]{4,3,2,1,0:T(8,128)S(1)}, f32[3,3,4,8,128]{4,3,2,1,0:T(8,128)S(1)}, u32[]{:S(2)}, u32[]{:S(2)}) collective-permute-start(f32[3,3,4,8,128]{4,3,2,1,0:T(8,128)S(1)} %collective-permute-done.3.right_here), channel_id=1, source_target_pairs={{0,1},{1,0},{2,3},{3,2},{4,5},{5,4},{6,7},{7,6},{8,9},{9,8},{10,11... | collective-permute-start | bytes 442376 | tf_op jit(solution)/shard_map/ppermute | solution.py:805
  20.4 8.6 %copy-start.2 = (f32[256,256]{1,0:T(8,128)S(1)}, f32[256,256]{1,0:T(8,128)}, u32[]{:S(2)}) copy-start(f32[256,256]{1,0:T(8,128)} %constant.92.clone.table_y) | copy-start | bytes 786436
  20.4 8.6 %copy-start.3 = (f32[32,32]{1,0:T(8,128)S(1)}, f32[32,32]{1,0:T(8,128)}, u32[]{:S(2)}) copy-start(f32[32,32]{1,0:T(8,128)} %constant.94.clone.table_z) | copy-start | bytes 12292
  24.7 22.3 %copy-start = (f32[640,512]{1,0:T(8,128)S(1)}, f32[640,512]{1,0:T(8,128)}, u32[]{:S(2)}) copy-start(f32[640,512]{1,0:T(8,128)} %constant.91.clone.table) | copy-start | bytes 3932164
  28.3 8.4 %collective-permute-start.7 = (f32[2,8,6,8,128]{4,3,2,1,0:T(8,128)S(1)}, f32[2,8,6,8,128]{4,3,2,1,0:T(8,128)S(1)}, u32[]{:S(2)}, u32[]{:S(2)}) collective-permute-start(f32[2,8,6,8,128]{4,3,2,1,0:T(8,128)S(1)} %get-tuple-element.15.pieces), channel_id=1, source_target_pairs={{12,28},{14,30},{13,29},{15,31}} | collective-permute-start | bytes 1179656 | tf_op jit(solution)/shard_map/ppermute | solution.py:876
  30.6 16.4 %all-to-all-start = ((f32[32,2,8,128]{3,2,1,0:T(8,128)}), f32[32,2,8,128]{3,2,1,0:T(8,128)S(1)}, u32[]{:S(2)}, u32[]{:S(2)}) async-start(f32[32,2,8,128]{3,2,1,0:T(8,128)} %bitcast.11), calls=%async_computation | async-start | bytes 524288 | tf_op jit(solution)/shard_map/all_to_all | solution.py:885
  37.4 9.7 %collective-permute-start.8 = (f32[8,6,8,128]{3,2,1,0:T(8,128)S(1)}, f32[8,6,8,128]{3,2,1,0:T(8,128)S(1)}, u32[]{:S(2)}, u32[]{:S(2)}) collective-permute-start(f32[8,6,8,128]{3,2,1,0:T(8,128)S(1)} %get-tuple-element.17), channel_id=1, source_target_pairs={{0,1},{1,0},{2,3},{3,2},{4,5},{5,4},{6,7},{7,6},{8,9},{9,8},{10,11... | collective-permute-start | bytes 589832 | tf_op jit(solution)/shard_map/ppermute | solution.py:891
  47.0 22.2 %copy-start.1 = (f32[2,256,256]{2,1,0:T(8,128)S(1)}, f32[2,256,256]{2,1,0:T(8,128)}, u32[]{:S(2)}) copy-start(f32[2,256,256]{2,1,0:T(8,128)} %constant.93.clone.table_y) | copy-start | bytes 1572868
  67.7 1.5 %collective-permute-start.9 = (f32[8,48,128]{2,1,0:T(8,128)S(1)}, f32[8,48,128]{2,1,0:T(8,128)S(1)}, u32[]{:S(2)}, u32[]{:S(2)}) collective-permute-start(f32[8,48,128]{2,1,0:T(8,128)S(1)} %slice.32), channel_id=1, source_target_pairs={{0,1},{1,0},{2,3},{3,2},{4,5},{5,4},{6,7},{7,6},{8,9},{9,8},{10,11... | collective-permute-start | bytes 589832 | tf_op jit(solution)/shard_map/ppermute | solution.py:904

commit v4 on v3

--- a/solution.py
+++ b/solution.py
@@ -283,8 +283,8 @@
 
 
 class Stencil:
-    def __init__(self, tiles, rows, width, viscosity, faces, thrust, start):
-        self.tiles, self.rows, self.width = (tiles, rows, width)
+    def __init__(self, tiles, rows, width, viscosity, faces, thrust, start, beside):
+        self.tiles, self.rows, self.width, self.beside = (tiles, rows, width, beside)
         self.viscosity, self.faces, self.thrust, self.start = (viscosity, faces, thrust, start)
         row = lax.broadcasted_iota(jnp.int32, (rows, width), 0)
         self.top = row == rows - 1
@@ -312,10 +312,12 @@
         def column(n, carry):
             i = first + n
             here = [[now[i, c, t] for t in range(tiles)] for c in range(3)]
-            found = []
+            found, sides = [], []
             for t in range(tiles):
                 d_x = [now[i + 1, c, t] - now[i - 1, c, t] for c in range(3)]
-                d_y = [self.next_y(f[t]) - self.last_y(f[t]) for f in here]
+                after_y = [self.next_y(f[t]) for f in here]
+                sides.append(after_y)
+                d_y = [a - self.last_y(f[t]) for a, f in zip(after_y, here)]
                 d_z = [self.next_z(f, t) - self.last_z(f, t) for f in here]
                 diagonal = d_x[0] * d_x[0] + d_y[1] * d_y[1] + d_z[2] * d_z[2]
                 xy = d_x[1] + d_y[0]
@@ -326,6 +328,8 @@
                 found.append((0.5 * SMAG_COEFF) * root)
             for t in range(tiles):
                 self.viscosity[i, t] = found[t]
+                for c in range(3):
+                    self.beside[i, c, t] = sides[t][c]
             return carry
 
         lax.fori_loop(0, count, column, 0, unroll=4 if count % 4 == 0 else 6)
@@ -369,7 +373,7 @@
                 here = [f[t] for f in field]
                 above = last if t == tiles - 1 else face_z(t)
                 ahead, before = ahead_of[t], before_of[t]
-                beside = [self.next_y(f) for f in here]
+                beside = [self.beside[i, c, t] for c in range(3)]
                 side = self.face(eddy[t] + self.next_y(eddy[t]), here, beside, 1)
                 for c in range(3):
                     change = (
@@ -428,6 +432,7 @@
     stage_b,
     viscosity,
     faces,
+    beside,
 ):
     cells_x = own_here.shape[0]
     near = left_here.shape[0]
@@ -442,7 +447,7 @@
             (near + cells_x, right_here, right_there, 0, near),
         ),
     )
-    stencil = Stencil(tiles, rows, width, viscosity, faces, thrust, start)
+    stencil = Stencil(tiles, rows, width, viscosity, faces, thrust, start, beside)
     columns = start.shape[0]
     stencil.stage(0, start, stage_a, 2, columns - 4)
     stencil.stage(1, stage_a, stage_b, 4, columns - 8)
@@ -475,6 +480,7 @@
     stage_c,
     viscosity,
     faces,
+    beside,
     columns_here,
     columns_there,
 ):
@@ -510,7 +516,7 @@
             ),
         )
 
-    stencil = Stencil(tiles, rows, width, viscosity, faces, thrust, start)
+    stencil = Stencil(tiles, rows, width, viscosity, faces, thrust, start, beside)
     stencil.stage(0, start, stage_a, 2 + 4 * core, 4)
     stage_a[pl.ds(6 - 4 * core, 4)] = first[...]
     stencil.stage(1, stage_a, stage_b, 4, 4)
@@ -564,7 +570,7 @@
                 )
 
 
-def spectra_kernel(source, table_y, table_z, spectra, modes):
+def fill_spectra(source, table_y, table_z, spectra, modes):
     _, groups, _, parts, rows, lanes = spectra.shape
     levels = table_z.shape[0]
     count, total_y = source.shape
@@ -585,6 +591,22 @@
                 ]
                 for g, block in enumerate(swap_blocks(picked, lanes // groups)):
                     spectra[dest, g, h, p] = block
+
+
+def precursor_kernel(source, table_y, table_z, spectra, modes):
+    @pl.when(lax.axis_index("sec") == 0)
+    def _():
+        fill_spectra(source, table_y, table_z, spectra, modes)
+
+
+def farm_kernel(source, table_y, table_z, earlier, spectra, modes):
+    @pl.when(lax.axis_index("sec") == 0)
+    def _():
+        spectra[...] = earlier[...]
+
+    @pl.when(lax.axis_index("sec") == 1)
+    def _():
+        fill_spectra(source, table_y, table_z, spectra, modes)
 
 
 def blend_kernel(fringe, pieces, upstream, blended_here, blended_there):
@@ -798,9 +820,9 @@
     tail, head = cells_x - REACH, near
     same = lax.dynamic_slice_in_dim(own, jnp.where(core == 0, tail, head), far, 0)
     other = lax.dynamic_slice_in_dim(own, jnp.where(core == 0, head, tail), far, 0)
-    far_here = lax.ppermute(same, ("gx", "gy"), straight)
+    own_there = lax.ppermute(own, "gy", swap)
+    other, left = lax.optimization_barrier((other, left))
     far_there = lax.ppermute(other, ("gx", "gy"), crossed)
-    own_there = lax.ppermute(own, "gy", swap)
     left_there = lax.ppermute(left, "gy", swap)
     right_there = lax.ppermute(right, "gy", swap)
 
@@ -816,6 +838,8 @@
 
     near_thrust = thrust_on(2 - near, cells_x + 2 * near - 4)
     far_thrust = thrust_on((2 - REACH) * (1 - core) + (share_x + 1) * core, far + near + share_x - 3)
+    same, near_thrust, far_thrust = lax.optimization_barrier((same, near_thrust, far_thrust))
+    far_here = lax.ppermute(same, ("gx", "gy"), straight)
     own_inverse = lax.dynamic_slice(
         inverse, (place, core, 0, 0, 0), (1, 1) + inverse.shape[2:]
     )[0, 0]
@@ -832,7 +856,7 @@
         near_kernel,
         shapes,
         [columns(reached)] * 3
-        + [pltpu.VMEM((reached,) + body[1:], f32), pltpu.VMEM(body, f32)],
+        + [pltpu.VMEM((reached,) + body[1:], f32), pltpu.VMEM(body, f32), columns(reached)],
         own,
         own_there,
         left,
@@ -855,6 +879,7 @@
         + [
             pltpu.VMEM((window,) + body[1:], f32),
             pltpu.VMEM(body, f32),
+            columns(window),
             pltpu.VMEM((share_x * 3 * levels, cells_y), f32),
             pltpu.VMEM((share_x * 3 * levels, cells_y), f32),
         ],
@@ -873,15 +898,12 @@
         far_thrust,
     )
     outlet = [(g, groups + g) for g in range(groups - groups // 4, groups)]
+    spectra_shape = jax.ShapeDtypeStruct((2, groups, 2, parts, 2 * share_x, LANES), f32)
+    modes = [pltpu.VMEM((2, 2 * share_x * levels, LANES), f32)]
+    earlier = call(precursor_kernel, spectra_shape, modes, source, table_y, table_z)
+    earlier, pieces = lax.optimization_barrier((earlier, pieces))
     upstream = lax.ppermute(pieces, ("sec", "gx"), outlet)
-    spectra = call(
-        spectra_kernel,
-        jax.ShapeDtypeStruct((2, groups, 2, parts, 2 * share_x, LANES), f32),
-        [pltpu.VMEM((2, 2 * share_x * levels, LANES), f32)],
-        source,
-        table_y,
-        table_z,
-    )
+    spectra = call(farm_kernel, spectra_shape, modes, source, table_y, table_z, earlier)
     received = lax.all_to_all(
         spectra.reshape((4 * groups,) + spectra.shape[3:]), ("sec", "gx", "gy"), 0, 0, tiled=True
     ).reshape(spectra.shape)

time: 70.9 us -> 68.3 us (0.963)
  waiting for transfers between devices: 17.7 us -> 14.5 us
  local copies, waits for them, and re-layouts: 2.6 us -> 3.4 us
    ppermute x1, starting transfers between devices: 2.61 us -> 0.01 us  [paired_plan(): far_there = lax.ppermute(other, ('gx', 'gy'), crossed)]
    ppermute x1, starting transfers between devices: 0.01 us -> 2.59 us  [paired_plan(): left_there = lax.ppermute(left, 'gy', swap)]
    ppermute x1, waiting for transfers between devices: 2.52 us -> 0.01 us  [paired_plan(): right = lax.ppermute(own[:near], 'gx', down)]
    ppermute x1, waiting for transfers between devices: 4.62 us -> 3.27 us  [paired_plan(): left = lax.ppermute(own[cells_x - near:], 'gx', up)]
    ppermute x1, waiting for transfers between devices: 0.01 us -> 1 us  [paired_plan(): left_there = lax.ppermute(left, 'gy', swap)]
    eq x1, local copies, waits for them, and re-layouts: 0.01 us -> 0.8 us  [thrust_weights(): along_x[:, None] == turbine_cells[None, :, 0]]
    pallas_call x6 -> x7, Pallas kernels: 12.3 us -> 11.9 us  [call(): pl.pallas_call(kernel, out_shape=out_shapes, in_specs=in_specs, out_specs...]
  transfers between devices with their start and end apart: 11 -> 11, of which waited for: 5 -> 5; matrix products, arithmetic and copies ran while one was open for 4% -> 5% of each run, Pallas kernels for 9% -> 8%
where the time goes in v4:
time: 68.3 us; the launch traced here: 68 us
  blocking collectives  19.7 us (29%)
  starting transfers between devices  16.2 us (24%)
  waiting for transfers between devices  14.5 us (21%)
  Pallas kernels  11.9 us (17%)
  local copies, waits for them, and re-layouts  3.4 us (5%)
  matrix products  1.14 us (2%)
  between operations  0.81 us (1%)
    all_to_all x1, blocking collectives, paired_plan(): returned = lax.all_to_all(packed, 'gx', 0, 0, tiled=True)  19.7 us
    pallas_call x7, Pallas kernels, call(): pl.pallas_call(kernel, out_shape=out_shapes, in_specs=in_specs, out_specs...  11.9 us
    all_to_all x1, waiting for transfers between devices, paired_plan(): lax.all_to_all(spectra.reshape((4 * groups,) + spectra.shape[3:]), ('sec'...  8.43 us
    all_to_all x1, starting transfers between devices, paired_plan(): lax.all_to_all(spectra.reshape((4 * groups,) + spectra.shape[3:]), ('sec'...  6.29 us
    ppermute x1, waiting for transfers between devices, paired_plan(): left = lax.ppermute(own[cells_x - near:], 'gx', up)  3.27 us
    ppermute x1, starting transfers between devices, paired_plan(): right = lax.ppermute(own[:near], 'gx', down)  3.1 us
    ppermute x1, starting transfers between devices, paired_plan(): left_there = lax.ppermute(left, 'gy', swap)  2.59 us
    ppermute x1, starting transfers between devices, paired_plan(): left = lax.ppermute(own[cells_x - near:], 'gx', up)  2.59 us
  transfers between devices with their start and end apart: 11, of which 5 were waited for; matrix products, arithmetic and copies ran while one was open for 5% of the time, Pallas kernels for 8%

profile of v4, /device:TPU:0, one launch (start us, length us, event | category | flops | bytes accessed | tf_op | source)
XLA Modules:
  0.0 68.0 jit_solution(3560421586645382418)
XLA Ops:
  0.6 1.2 %copy.23 = f32[3,8,4,8,128]{4,1,2,0,3:T(8,128)S(1)} copy(f32[3,8,4,8,128]{4,3,2,1,0:T(8,128)} %bitcast.38) | data formatting | bytes 786432 | tf_op jit(solution)/shard_map/reshape;squeeze | solution.py:817
  1.9 0.5 collective-permute-start
  2.4 2.6 %collective-permute-start.1 = (f32[3,3,4,8,128]{4,3,2,1,0:T(8,128)S(1)}, f32[3,3,4,8,128]{4,3,2,1,0:T(8,128)S(1)}, u32[]{:S(2)}, u32[]{:S(2)}) collective-permute-start(f32[3,3,4,8,128]{4,3,2,1,0:T(8,128)S(1)} %get-tuple-element.37), channel_id=1, source_target_pairs={{0,2},{2,4},{4,6},{6,8},{8,10},{10,12},{12,14},{14,0},{1,3},{3,5},... | collective-permute-start | bytes 442376 | tf_op jit(solution)/shard_map/ppermute | solution.py:818
  5.0 3.1 %collective-permute-start.3 = (f32[3,3,4,8,128]{4,3,2,1,0:T(8,128)S(1)}, f32[3,3,4,8,128]{4,3,2,1,0:T(8,128)S(1)}, u32[]{:S(2)}, u32[]{:S(2)}) collective-permute-start(f32[3,3,4,8,128]{4,3,2,1,0:T(8,128)S(1)} %get-tuple-element.36), channel_id=1, source_target_pairs={{2,0},{4,2},{6,4},{8,6},{10,8},{12,10},{14,12},{0,14},{3,1},{5,3},... | collective-permute-start | bytes 442376 | tf_op jit(solution)/shard_map/ppermute | solution.py:819
  8.1 0.8 %slice_bitcast_fusion.2 = (s32[64]{0:T(128)S(1)}, s32[64]{0:T(128)S(1)}, s32[64]{0:T(128)S(1)}) fusion(s32[64,3]{0,1:T(4,128)} %param.9), kind=kLoop, calls=%fused_computation.42 | loop fusion | bytes 1536 | tf_op jit(solution)/shard_map/eq | solution.py:791
  8.9 0.1 fusion.12
  9.0 0.1 reshape.142
  9.1 0.1 subtract_multiply_fusion
  9.2 0.6 fusion.2
  9.8 0.6 fusion.3
  10.3 0.0 copy-start.4
  10.3 0.1 copy.22
  10.4 0.2 copy.21
  10.7 0.1 collective-permute-start.5
  10.7 3.3 %collective-permute-done.1.left_here = f32[3,3,4,8,128]{4,3,2,1,0:T(8,128)S(1)} collective-permute-done((f32[3,3,4,8,128]{4,3,2,1,0:T(8,128)S(1)}, f32[3,3,4,8,128]{4,3,2,1,0:T(8,128)S(1)}, u32[]{:S(2)}, u32[]{:S(2)}) %collective-permute-start.1) | collective-permute-done | bytes 147488 | tf_op jit(solution)/shard_map/ppermute | solution.py:818
  14.0 0.0 copy-start.1
  14.0 0.0 copy-start.3
  14.0 0.0 collective-permute-start.6
  14.0 2.6 %collective-permute-start.2 = (f32[3,3,4,8,128]{4,3,2,1,0:T(8,128)S(1)}, f32[3,3,4,8,128]{4,3,2,1,0:T(8,128)S(1)}, u32[]{:S(2)}, u32[]{:S(2)}) collective-permute-start(f32[3,3,4,8,128]{4,3,2,1,0:T(8,128)S(1)} %collective-permute-done.1.left_here), channel_id=1, source_target_pairs={{0,1},{1,0},{2,3},{3,2},{4,5},{5,4},{6,7},{7,6},{8,9},{9,8},{10,11... | collective-permute-start | bytes 442376 | tf_op jit(solution)/shard_map/ppermute | solution.py:826
  16.6 0.0 collective-permute-done.3.right_here
  16.6 0.0 collective-permute-start.4
  16.6 1.0 %collective-permute-done.2.left_there = f32[3,3,4,8,128]{4,3,2,1,0:T(8,128)S(1)} collective-permute-done((f32[3,3,4,8,128]{4,3,2,1,0:T(8,128)S(1)}, f32[3,3,4,8,128]{4,3,2,1,0:T(8,128)S(1)}, u32[]{:S(2)}, u32[]{:S(2)}) %collective-permute-start.2) | collective-permute-done | bytes 147488 | tf_op jit(solution)/shard_map/ppermute | solution.py:826
  17.6 0.4 collective-permute-done.4.right_there
  18.0 0.0 collective-permute-done.own_there
  18.0 3.9 %shard_map.95 = (f32[4,3,4,8,256]{4,3,2,1,0:T(8,128)S(1)}, f32[4,3,4,8,256]{4,3,2,1,0:T(8,128)S(1)}, f32[2,3,4,8,256]{4,3,2,1,0:T(8,128)S(1)}) custom-call(f32[8,3,4,8,128]{4,3,2,1,0:T(8,128)S(1)} %bitcast.33, f32[8,3,4,8,128]{4,3,2,1,0:T(8,128)S(1)} %collective-permute-done.own_there, f32[3,3,4,8,128]{4,3,2,1,0:T(8,128)S(1)} %collective-permute-done.1.left_here, ...), custom_call_target="tpu_custom_call" | custom-call | tf_op jit(solution)/shard_map/pallas_call | solution.py:780
  21.9 0.0 collective-permute-done.5.far_here
  21.9 0.0 collective-permute-done.6.far_there
  21.9 0.0 copy-done.4
  21.9 3.5 %shard_map.96 = (f32[2,8,6,8,128]{4,3,2,1,0:T(8,128)S(1)}, f32[256,256]{1,0:T(8,128)S(1)}) custom-call(s32[2]{0:T(128)S(1)} %copy-done.4, f32[8,3,4,8,128]{4,3,2,1,0:T(8,128)S(1)} %bitcast.34, f32[8,3,4,8,128]{4,3,2,1,0:T(8,128)S(1)} %collective-permute-done.own_there, f32[3,3,4,8,128]{4,3,2,1,0:T(8,128)S(1)} %collective-permute-done.1.left_here, ...), custom_call_target="tpu_custom_call" | custom-call | tf_op jit(solution)/shard_map/pallas_call | solution.py:780
  25.4 0.0 copy-start
  25.4 0.0 copy-done.1
  25.5 0.0 copy-done.3
  25.5 0.9 %shard_map.97.earlier = f32[2,8,2,2,8,128]{5,4,3,2,1,0:T(8,128)S(1)} custom-call(f32[256,256]{1,0:T(8,128)S(1)} %get-tuple-element.26.source, f32[256,256]{1,0:T(8,128)S(1)} %copy-done.1, f32[32,32]{1,0:T(8,128)S(1)} %copy-done.3), custom_call_target="tpu_custom_call" | custom-call | tf_op jit(solution)/shard_map/pallas_call | solution.py:780
  26.3 0.7 %collective-permute-start.7 = (f32[2,8,6,8,128]{4,3,2,1,0:T(8,128)S(1)}, f32[2,8,6,8,128]{4,3,2,1,0:T(8,128)S(1)}, u32[]{:S(2)}, u32[]{:S(2)}) collective-permute-start(f32[2,8,6,8,128]{4,3,2,1,0:T(8,128)S(1)} %get-tuple-element.29.pieces), channel_id=1, source_target_pairs={{12,28},{14,30},{13,29},{15,31}} | collective-permute-start | bytes 1179656 | tf_op jit(solution)/shard_map/ppermute | solution.py:905
  27.0 0.7 %shard_map.98 = f32[2,8,2,2,8,128]{5,4,3,2,1,0:T(8,128)} custom-call(f32[256,256]{1,0:T(8,128)S(1)} %get-tuple-element.26.source, f32[256,256]{1,0:T(8,128)S(1)} %copy-done.1, f32[32,32]{1,0:T(8,128)S(1)} %copy-done.3, f32[2,8,2,2,8,128]{5,4,3,2,1,0:T(8,128)S(1)} %shard_map.97.earlier), custom_call_target="tpu_custom_call" | custom-call | tf_op jit(solution)/shard_map/pallas_call | solution.py:780
  27.8 6.3 %all-to-all-start = ((f32[32,2,8,128]{3,2,1,0:T(8,128)}), f32[32,2,8,128]{3,2,1,0:T(8,128)S(1)}, u32[]{:S(2)}, u32[]{:S(2)}) async-start(f32[32,2,8,128]{3,2,1,0:T(8,128)} %bitcast.11), calls=%async_computation | async-start | bytes 524288 | tf_op jit(solution)/shard_map/all_to_all | solution.py:907
  34.1 0.0 collective-permute-done.7.upstream
  34.1 0.6 shard_map.99
  34.7 0.3 collective-permute-start.8
  35.0 0.9 %dynamic-slice_bitcast_fusion.2.inverse = f32[4,64,128]{2,1,0:T(8,128)S(1)} fusion(f32[8,2,4,64,128]{4,3,2,1,0:T(8,128)} %constant.95.clone, s32[]{:T(128)S(6)} %select_n.53, s32[]{:T(128)S(6)} %select_n.54), kind=kLoop, calls=%fused_computation.15 | loop fusion | bytes 262152 | tf_op jit(solution)/shard_map/squeeze | solution.py:843
  35.9 8.4 %all-to-all-done = f32[32,2,8,128]{3,2,1,0:T(8,128)S(1)} async-done(((f32[32,2,8,128]{3,2,1,0:T(8,128)}), f32[32,2,8,128]{3,2,1,0:T(8,128)S(1)}, u32[]{:S(2)}, u32[]{:S(2)}) %all-to-all-start) | async-done | bytes 262176 | tf_op jit(solution)/shard_map/all_to_all | solution.py:907
  44.4 0.0 collective-permute-done.8.blended_there
  44.4 0.0 copy-done
  44.4 0.0 copy-start.2
  44.4 0.9 %shard_map.100 = f32[8,144,128]{2,1,0:T(8,128)S(1)} custom-call(f32[2,8,2,2,8,128]{5,4,3,2,1,0:T(8,128)S(1)} %bitcast.37, f32[4,64,128]{2,1,0:T(8,128)S(1)} %dynamic-slice_bitcast_fusion.2.inverse, f32[640,512]{1,0:T(8,128)S(1)} %copy-done, f32[8,6,8,128]{3,2,1,0:T(8,128)S(1)} %get-tuple-element.30.blended_here, ...), custom_call_target="tpu_custom_call" | custom-call | tf_op jit(solution)/shard_map/pallas_call | solution.py:780
  45.3 19.7 %all_to_all.10.received = f32[8,144,128]{2,1,0:T(8,128)S(1)} all-to-all(f32[8,144,128]{2,1,0:T(8,128)S(1)} %shard_map.100), channel_id=1, replica_groups=mesh['sec'=2,'gx'=8,'gy'=2] {'gx'}, dimensions={0} | all-to-all | bytes 1179648 | tf_op jit(solution)/shard_map/all_to_all | solution.py:925
  65.1 0.1 collective-permute-start.9
  65.1 1.4 %collective-permute-done.9.partner = f32[8,48,128]{2,1,0:T(8,128)S(1)} collective-permute-done((f32[8,48,128]{2,1,0:T(8,128)S(1)}, f32[8,48,128]{2,1,0:T(8,128)S(1)}, u32[]{:S(2)}, u32[]{:S(2)}) %collective-permute-start.9) | collective-permute-done | bytes 196640 | tf_op jit(solution)/shard_map/ppermute | solution.py:926
  66.6 0.0 copy-done.2
  66.6 1.4 %shard_map.101 = (f32[3,4,64,128]{3,2,1,0:T(8,128)}, f32[4,64,128]{2,1,0:T(8,128)}) custom-call(f32[8,144,128]{2,1,0:T(8,128)S(1)} %all_to_all.10.received, f32[8,48,128]{2,1,0:T(8,128)S(1)} %collective-permute-done.9.partner, f32[2,256,256]{2,1,0:T(8,128)S(1)} %copy-done.2), custom_call_target="tpu_custom_call" | custom-call | tf_op jit(solution)/shard_map/pallas_call | solution.py:780
  (6 shorter events, 0.1 us)
Async XLA Ops:
  1.9 16.1 %collective-permute-start = (f32[8,3,4,8,128]{4,3,2,1,0:T(8,128)S(1)}, f32[8,3,4,8,128]{4,3,2,1,0:T(8,128)S(1)}, u32[]{:S(2)}, u32[]{:S(2)}) collective-permute-start(f32[8,3,4,8,128]{4,3,2,1,0:T(8,128)S(1)} %bitcast.31), channel_id=1, source_target_pairs={{0,1},{1,0},{2,3},{3,2},{4,5},{5,4},{6,7},{7,6},{8,9},{9,8},{10,11... | collective-permute-start | bytes 1179656 | tf_op jit(solution)/shard_map/ppermute | solution.py:823
  2.4 11.6 %collective-permute-start.1 = (f32[3,3,4,8,128]{4,3,2,1,0:T(8,128)S(1)}, f32[3,3,4,8,128]{4,3,2,1,0:T(8,128)S(1)}, u32[]{:S(2)}, u32[]{:S(2)}) collective-permute-start(f32[3,3,4,8,128]{4,3,2,1,0:T(8,128)S(1)} %get-tuple-element.37), channel_id=1, source_target_pairs={{0,2},{2,4},{4,6},{6,8},{8,10},{10,12},{12,14},{14,0},{1,3},{3,5},... | collective-permute-start | bytes 442376 | tf_op jit(solution)/shard_map/ppermute | solution.py:818
  5.0 11.6 %collective-permute-start.3 = (f32[3,3,4,8,128]{4,3,2,1,0:T(8,128)S(1)}, f32[3,3,4,8,128]{4,3,2,1,0:T(8,128)S(1)}, u32[]{:S(2)}, u32[]{:S(2)}) collective-permute-start(f32[3,3,4,8,128]{4,3,2,1,0:T(8,128)S(1)} %get-tuple-element.36), channel_id=1, source_target_pairs={{2,0},{4,2},{6,4},{8,6},{10,8},{12,10},{14,12},{0,14},{3,1},{5,3},... | collective-permute-start | bytes 442376 | tf_op jit(solution)/shard_map/ppermute | solution.py:819
  10.3 11.6 %copy-start.4 = (s32[2]{0:T(128)S(1)}, s32[2]{0:T(128)}, u32[]{:S(2)}) copy-start(s32[2]{0:T(128)} %fringe.3) | copy-start | bytes 28
  10.7 11.2 %collective-permute-start.5 = (f32[4,3,4,8,128]{4,3,2,1,0:T(8,128)S(1)}, f32[4,3,4,8,128]{4,3,2,1,0:T(8,128)S(1)}, u32[]{:S(2)}, u32[]{:S(2)}) collective-permute-start(f32[4,3,4,8,128]{4,3,2,1,0:T(8,128)S(1)} %get-tuple-element.19), channel_id=1, source_target_pairs={{0,2},{2,4},{4,6},{6,8},{8,10},{10,12},{12,14},{14,0},{3,1},{5,3},... | collective-permute-start | bytes 589832 | tf_op jit(solution)/shard_map/ppermute | solution.py:842
  14.0 11.4 %copy-start.1 = (f32[256,256]{1,0:T(8,128)S(1)}, f32[256,256]{1,0:T(8,128)}, u32[]{:S(2)}) copy-start(f32[256,256]{1,0:T(8,128)} %constant.92.clone.table_y) | copy-start | bytes 786436
  14.0 11.4 %copy-start.3 = (f32[32,32]{1,0:T(8,128)S(1)}, f32[32,32]{1,0:T(8,128)}, u32[]{:S(2)}) copy-start(f32[32,32]{1,0:T(8,128)} %constant.94.clone.table_z) | copy-start | bytes 12292
  14.0 7.9 %collective-permute-start.6 = (f32[4,3,4,8,128]{4,3,2,1,0:T(8,128)S(1)}, f32[4,3,4,8,128]{4,3,2,1,0:T(8,128)S(1)}, u32[]{:S(2)}, u32[]{:S(2)}) collective-permute-start(f32[4,3,4,8,128]{4,3,2,1,0:T(8,128)S(1)} %get-tuple-element.20), channel_id=1, source_target_pairs={{1,2},{3,4},{5,6},{7,8},{9,10},{11,12},{13,14},{15,0},{2,1},{4,3},... | collective-permute-start | bytes 589832 | tf_op jit(solution)/shard_map/ppermute | solution.py:825
  14.0 3.6 %collective-permute-start.2 = (f32[3,3,4,8,128]{4,3,2,1,0:T(8,128)S(1)}, f32[3,3,4,8,128]{4,3,2,1,0:T(8,128)S(1)}, u32[]{:S(2)}, u32[]{:S(2)}) collective-permute-start(f32[3,3,4,8,128]{4,3,2,1,0:T(8,128)S(1)} %collective-permute-done.1.left_here), channel_id=1, source_target_pairs={{0,1},{1,0},{2,3},{3,2},{4,5},{5,4},{6,7},{7,6},{8,9},{9,8},{10,11... | collective-permute-start | bytes 442376 | tf_op jit(solution)/shard_map/ppermute | solution.py:826
  16.6 1.4 %collective-permute-start.4 = (f32[3,3,4,8,128]{4,3,2,1,0:T(8,128)S(1)}, f32[3,3,4,8,128]{4,3,2,1,0:T(8,128)S(1)}, u32[]{:S(2)}, u32[]{:S(2)}) collective-permute-start(f32[3,3,4,8,128]{4,3,2,1,0:T(8,128)S(1)} %collective-permute-done.3.right_here), channel_id=1, source_target_pairs={{0,1},{1,0},{2,3},{3,2},{4,5},{5,4},{6,7},{7,6},{8,9},{9,8},{10,11... | collective-permute-start | bytes 442376 | tf_op jit(solution)/shard_map/ppermute | solution.py:827
  25.4 18.9 %copy-start = (f32[640,512]{1,0:T(8,128)S(1)}, f32[640,512]{1,0:T(8,128)}, u32[]{:S(2)}) copy-start(f32[640,512]{1,0:T(8,128)} %constant.91.clone.table) | copy-start | bytes 3932164
  26.3 7.7 %collective-permute-start.7 = (f32[2,8,6,8,128]{4,3,2,1,0:T(8,128)S(1)}, f32[2,8,6,8,128]{4,3,2,1,0:T(8,128)S(1)}, u32[]{:S(2)}, u32[]{:S(2)}) collective-permute-start(f32[2,8,6,8,128]{4,3,2,1,0:T(8,128)S(1)} %get-tuple-element.29.pieces), channel_id=1, source_target_pairs={{12,28},{14,30},{13,29},{15,31}} | collective-permute-start | bytes 1179656 | tf_op jit(solution)/shard_map/ppermute | solution.py:905
  27.8 16.6 %all-to-all-start = ((f32[32,2,8,128]{3,2,1,0:T(8,128)}), f32[32,2,8,128]{3,2,1,0:T(8,128)S(1)}, u32[]{:S(2)}, u32[]{:S(2)}) async-start(f32[32,2,8,128]{3,2,1,0:T(8,128)} %bitcast.11), calls=%async_computation | async-start | bytes 524288 | tf_op jit(solution)/shard_map/all_to_all | solution.py:907
  34.7 9.7 %collective-permute-start.8 = (f32[8,6,8,128]{3,2,1,0:T(8,128)S(1)}, f32[8,6,8,128]{3,2,1,0:T(8,128)S(1)}, u32[]{:S(2)}, u32[]{:S(2)}) collective-permute-start(f32[8,6,8,128]{3,2,1,0:T(8,128)S(1)} %get-tuple-element.31), channel_id=1, source_target_pairs={{0,1},{1,0},{2,3},{3,2},{4,5},{5,4},{6,7},{7,6},{8,9},{9,8},{10,11... | collective-permute-start | bytes 589832 | tf_op jit(solution)/shard_map/ppermute | solution.py:913
  44.4 22.2 %copy-start.2 = (f32[2,256,256]{2,1,0:T(8,128)S(1)}, f32[2,256,256]{2,1,0:T(8,128)}, u32[]{:S(2)}) copy-start(f32[2,256,256]{2,1,0:T(8,128)} %constant.93.clone.table_y) | copy-start | bytes 1572868
  65.1 1.5 %collective-permute-start.9 = (f32[8,48,128]{2,1,0:T(8,128)S(1)}, f32[8,48,128]{2,1,0:T(8,128)S(1)}, u32[]{:S(2)}, u32[]{:S(2)}) collective-permute-start(f32[8,48,128]{2,1,0:T(8,128)S(1)} %slice.32), channel_id=1, source_target_pairs={{0,1},{1,0},{2,3},{3,2},{4,5},{5,4},{6,7},{7,6},{8,9},{9,8},{10,11... | collective-permute-start | bytes 589832 | tf_op jit(solution)/shard_map/ppermute | solution.py:926

commit v5 on v3

--- a/solution.py
+++ b/solution.py
@@ -283,8 +283,8 @@
 
 
 class Stencil:
-    def __init__(self, tiles, rows, width, viscosity, faces, thrust, start):
-        self.tiles, self.rows, self.width = (tiles, rows, width)
+    def __init__(self, tiles, rows, width, viscosity, faces, thrust, start, beside):
+        self.tiles, self.rows, self.width, self.beside = (tiles, rows, width, beside)
         self.viscosity, self.faces, self.thrust, self.start = (viscosity, faces, thrust, start)
         row = lax.broadcasted_iota(jnp.int32, (rows, width), 0)
         self.top = row == rows - 1
@@ -312,10 +312,12 @@
         def column(n, carry):
             i = first + n
             here = [[now[i, c, t] for t in range(tiles)] for c in range(3)]
-            found = []
+            found, sides = [], []
             for t in range(tiles):
                 d_x = [now[i + 1, c, t] - now[i - 1, c, t] for c in range(3)]
-                d_y = [self.next_y(f[t]) - self.last_y(f[t]) for f in here]
+                after_y = [self.next_y(f[t]) for f in here]
+                sides.append(after_y)
+                d_y = [a - self.last_y(f[t]) for a, f in zip(after_y, here)]
                 d_z = [self.next_z(f, t) - self.last_z(f, t) for f in here]
                 diagonal = d_x[0] * d_x[0] + d_y[1] * d_y[1] + d_z[2] * d_z[2]
                 xy = d_x[1] + d_y[0]
@@ -326,6 +328,8 @@
                 found.append((0.5 * SMAG_COEFF) * root)
             for t in range(tiles):
                 self.viscosity[i, t] = found[t]
+                for c in range(3):
+                    self.beside[i, c, t] = sides[t][c]
             return carry
 
         lax.fori_loop(0, count, column, 0, unroll=4 if count % 4 == 0 else 6)
@@ -369,7 +373,7 @@
                 here = [f[t] for f in field]
                 above = last if t == tiles - 1 else face_z(t)
                 ahead, before = ahead_of[t], before_of[t]
-                beside = [self.next_y(f) for f in here]
+                beside = [self.beside[i, c, t] for c in range(3)]
                 side = self.face(eddy[t] + self.next_y(eddy[t]), here, beside, 1)
                 for c in range(3):
                     change = (
@@ -399,26 +403,30 @@
         self.advance(now, then, first, count, keep, gain)
 
 
-def place_columns(start, core, runs):
+def place_columns(start, runs_of):
     half = start.shape[-1] // 2
-
-    def copy(low_is_here):
-        for first, here, there, begin, count in runs:
-            low, high = (here, there) if low_is_here else (there, here)
+    core = lax.axis_index("gy")
+    odd = lax.axis_index("gx") % 2
+
+    def copy(side, parity):
+        for first, here, there, begin, count in runs_of(side, parity):
+            low, high = (here, there) if side == 0 else (there, here)
             start[pl.ds(first, count), :, :, :, :half] = low[pl.ds(begin, count)]
             start[pl.ds(first, count), :, :, :, half:] = high[pl.ds(begin, count)]
 
-    pl.when(core == 0)(lambda: copy(True))
-    pl.when(core == 1)(lambda: copy(False))
+    for side in range(2):
+        for parity in range(2):
+            chosen = jnp.logical_and(core == side, odd == parity)
+            pl.when(chosen)(functools.partial(copy, side, parity))
 
 
 def near_kernel(
     own_here,
     own_there,
-    left_here,
-    left_there,
-    right_here,
-    right_there,
+    across_here,
+    across_there,
+    around_here,
+    around_there,
     thrust,
     first,
     second,
@@ -428,21 +436,24 @@
     stage_b,
     viscosity,
     faces,
+    beside,
 ):
     cells_x = own_here.shape[0]
-    near = left_here.shape[0]
+    near = across_here.shape[0]
     _, _, tiles, rows, width = start.shape
     core = lax.axis_index("gy")
-    place_columns(
-        start,
-        core,
-        (
-            (0, left_here, left_there, 0, near),
+
+    def runs_of(side, parity):
+        across, around = (across_here, across_there), (around_here, around_there)
+        left, right = (around, across) if parity == 0 else (across, around)
+        return (
+            (0, *left, 0, near),
             (near, own_here, own_there, 0, cells_x),
-            (near + cells_x, right_here, right_there, 0, near),
-        ),
-    )
-    stencil = Stencil(tiles, rows, width, viscosity, faces, thrust, start)
+            (near + cells_x, *right, 0, near),
+        )
+
+    place_columns(start, runs_of)
+    stencil = Stencil(tiles, rows, width, viscosity, faces, thrust, start, beside)
     columns = start.shape[0]
     stencil.stage(0, start, stage_a, 2, columns - 4)
     stencil.stage(1, stage_a, stage_b, 4, columns - 8)
@@ -457,17 +468,18 @@
     fringe,
     own_here,
     own_there,
-    left_here,
-    left_there,
-    right_here,
-    right_there,
+    across_here,
+    across_there,
+    around_here,
+    around_there,
     far_here,
     far_there,
     first,
     second,
     third,
     thrust,
-    pieces,
+    piece_here,
+    piece_there,
     source,
     start,
     stage_a,
@@ -475,42 +487,34 @@
     stage_c,
     viscosity,
     faces,
+    beside,
     columns_here,
     columns_there,
 ):
     cells_x = own_here.shape[0]
-    near, far = left_here.shape[0], far_here.shape[0]
+    near, far = across_here.shape[0], far_here.shape[0]
     _, _, tiles, rows, width = start.shape
     half = width // 2
     share_x = cells_x // 2
     inner = share_x + 1
     core = lax.axis_index("gy")
 
-    @pl.when(core == 0)
-    def _():
-        place_columns(
-            start,
-            core,
-            (
+    def runs_of(side, parity):
+        across, around = (across_here, across_there), (around_here, around_there)
+        if side == 0:
+            return (
                 (0, far_here, far_there, 0, far),
-                (far, left_here, left_there, 0, near),
+                (far, *(around if parity == 0 else across), 0, near),
                 (far + near, own_here, own_there, 0, inner),
-            ),
+            )
+        return (
+            (0, own_here, own_there, cells_x - inner, inner),
+            (inner, *(across if parity == 0 else around), 0, near),
+            (inner + near, far_here, far_there, 0, far),
         )
 
-    @pl.when(core == 1)
-    def _():
-        place_columns(
-            start,
-            core,
-            (
-                (0, own_here, own_there, cells_x - inner, inner),
-                (inner, right_here, right_there, 0, near),
-                (inner + near, far_here, far_there, 0, far),
-            ),
-        )
-
-    stencil = Stencil(tiles, rows, width, viscosity, faces, thrust, start)
+    place_columns(start, runs_of)
+    stencil = Stencil(tiles, rows, width, viscosity, faces, thrust, start, beside)
     stencil.stage(0, start, stage_a, 2 + 4 * core, 4)
     stage_a[pl.ds(6 - 4 * core, 4)] = first[...]
     stencil.stage(1, stage_a, stage_b, 4, 4)
@@ -532,8 +536,8 @@
     for s in range(rows):
         for m in range(pairs):
             spot = pl.ds(m * rows + s, 2 * share_x, stride=pairs * rows)
-            pieces[0, s, m] = columns_here[spot, :]
-            pieces[1, s, m] = columns_there[spot, :]
+            piece_here[s, m] = columns_here[spot, :]
+            piece_there[s, m] = columns_there[spot, :]
 
     is_farm = lax.axis_index("sec") == 1
     corner = lax.axis_index("gx") * cells_x + core * share_x
@@ -587,28 +591,31 @@
                     spectra[dest, g, h, p] = block
 
 
-def blend_kernel(fringe, pieces, upstream, blended_here, blended_there):
-    _, groups, pairs, rows, lanes = pieces.shape
+def arrange_kernel(piece_here, piece_there, *blocks):
+    groups, pairs, rows, lanes = piece_here.shape
     half = rows // 2
-    corner = lax.axis_index("gx") * rows + lax.axis_index("gy") * half
-    place = corner + lax.broadcasted_iota(jnp.int32, (rows, lanes), 0) % half
-    inside = jnp.logical_and(place >= fringe[0], place < fringe[1])
-    inside = jnp.logical_and(inside, lax.axis_index("sec") == 1)
-    weight = jnp.where(inside, FRINGE_BLEND, 0.0)[None, None]
-    for n, blended in enumerate((blended_here, blended_there)):
-        own = pieces[n]
-        blended[...] = own + weight * (upstream[n] - own)
-
-
-def pencil_kernel(received, inverse, table, blended_here, blended_there, packed):
+    low = lax.broadcasted_iota(jnp.int32, (rows, lanes), 0) < half
+    is_first = lax.axis_index("gy") == 0
+    for distance, block in enumerate(blocks):
+        g = lax.axis_index("gx") ^ distance
+        for m in range(pairs):
+            here, there = piece_here[g, m], piece_there[g, m]
+            before = jnp.where(is_first, here, there)
+            after = jnp.where(is_first, there, here)
+            block[2 * m] = jnp.where(low, before, pltpu.roll(after, half, 0))
+            block[2 * m + 1] = jnp.where(low, pltpu.roll(before, half, 0), after)
+
+
+def pencil_kernel(received, waves, table, packed):
     _, groups, cores, parts, rows, lanes = received.shape
-    _, pairs, _, _ = blended_here.shape
     total_x = groups * rows
     lane_width = lanes // groups
     wave, base = 2 * total_x, table.shape[1]
     spread_z = table[:base]
     pair_x = table[base : base + wave, :wave]
     table_x = table[base : base + total_x, wave : wave + total_x]
+    along_x = table[base : base + total_x, 2 * wave : 2 * wave + lanes]
+    along_zy = waves[lax.axis_index("gx"), lax.axis_index("gy")]
     spectrum = jnp.concatenate(
         [(received[0, :, :, p] + received[1, :, :, p]).reshape(-1, lanes) for p in range(parts)],
         axis=1,
@@ -618,15 +625,13 @@
     for a in range(2 * parts):
         p, side = a % parts, a // parts
         block = solved[side * total_x : (side + 1) * total_x, p * lanes : (p + 1) * lanes]
-        pieces.append(block * inverse[a])
+        pieces.append(block / (along_x + along_zy[a : a + 1]))
     field = dot(dot(table_x, jnp.concatenate(pieces, axis=1)), spread_z)
     levels_of = [field[:, a * lanes : (a + 1) * lanes] for a in range(2 * parts)]
     wide = lax.broadcasted_iota(jnp.int32, (total_x // 2, lanes), 1)
     left = wide < lanes // 2
     quarter = total_x // 4
     block = lax.broadcasted_iota(jnp.int32, (quarter, lanes), 1) // lane_width
-    low = lax.broadcasted_iota(jnp.int32, (rows, lanes), 0) < rows // 2
-    is_first = lax.axis_index("gy") == 0
     for g in range(groups):
         a, odd = divmod(g, 2)
         now = levels_of[a]
@@ -650,20 +655,9 @@
                 edge = rolled if edge is None else jnp.where(block == spot, rolled, edge)
         packed[g, : total_x // 2] = main
         packed[g, total_x // 2 : 3 * quarter] = edge
-        for m in range(pairs):
-            here, there = blended_here[g, m], blended_there[g, m]
-            before = jnp.where(is_first, here, there)
-            after = jnp.where(is_first, there, here)
-            first = 3 * quarter + 2 * m * rows
-            packed[g, first : first + rows] = jnp.where(
-                low, before, pltpu.roll(after, rows // 2, 0)
-            )
-            packed[g, first + rows : first + 2 * rows] = jnp.where(
-                low, pltpu.roll(before, rows // 2, 0), after
-            )
-
-
-def project_kernel(received, partner, table_y, velocity_next, pressure):
+
+
+def project_kernel(fringe, received, partner, table_y, moved, upstream, velocity_next, pressure):
     groups = received.shape[0]
     share, total_x, lanes = pressure.shape
     cells_x = total_x // groups
@@ -688,6 +682,8 @@
     values = [f[:, :lanes] for f in fields]
     values[0] = jnp.where(place == 0, values[1], values[0])
     values[-1] = jnp.where(place == groups - 1, -values[-2], values[-1])
+    is_farm = lax.axis_index("sec") == 1
+    outlet = upstream.shape[0]
     for z in range(share):
         now = values[z + 1]
         pressure[z] = now
@@ -696,10 +692,17 @@
             fields[z + 1][:, lanes:],
             0.5 * (values[z + 2] - values[z]),
         ]
-        for c in range(3):
-            first = rows + (c * share + z) * cells_x
-            blended = received[:, first : first + cells_x].reshape(total_x, lanes)
-            velocity_next[c, z] = blended - slopes[c]
+        for s in range(groups):
+            distance = place ^ s
+            columns = s * cells_x + lax.broadcasted_iota(jnp.int32, (cells_x, lanes), 0)
+            inside = jnp.logical_and(columns >= fringe[0], columns < fringe[1])
+            blend = jnp.where(jnp.logical_and(inside, is_farm), FRINGE_BLEND, 0.0)
+            for c in range(3):
+                own = moved[distance, c * share + z]
+                if s >= groups - outlet:
+                    own = own + blend * (upstream[s - groups + outlet, c * share + z] - own)
+                spot = slice(s * cells_x, (s + 1) * cells_x)
+                velocity_next[c, z, spot] = own - slopes[c][spot]
 
 
 def cas(rows, columns, length):
@@ -724,20 +727,17 @@
         for here in (slice(0, half), slice(half, total_y))
     ]
     pair_x = np.einsum("kx,ab->akxb", table_x, np.eye(2)).reshape(2 * total_x, 2 * total_x)
-    eigen = (
-        (2.0 * np.cos(level * (np.pi / levels)) - 2.0)[:, None, None]
-        + (2.0 * np.cos(every_x * (2.0 * np.pi / total_x)) - 2.0)[None, :, None]
-        + (2.0 * np.cos(every_y * (2.0 * np.pi / total_y)) - 2.0)[None, None, :]
-    )
-    inverse = (2.0 / levels) / (total_x * total_y) / eigen
-    inverse = inverse.reshape(levels // groups, groups, total_x, 2, groups, lane_width)
-    inverse = inverse.transpose(4, 3, 0, 2, 1, 5).reshape(
-        groups, 2, levels // groups, total_x, LANES
-    )
+    norm = levels / 2.0 * total_x * total_y
+    wave_x = norm * (2.0 * np.cos(every_x * (2.0 * np.pi / total_x)) - 2.0)
+    wave_y = norm * (2.0 * np.cos(every_y * (2.0 * np.pi / total_y)) - 2.0)
+    wave_z = norm * (2.0 * np.cos(level * (np.pi / levels)) - 2.0)
+    waves = wave_z.reshape(1, 1, -1, groups, 1) + wave_y.reshape(2, groups, 1, 1, lane_width)
+    waves = waves.transpose(1, 0, 2, 3, 4).reshape(groups, 2, levels // groups, LANES)
     pencil = np.zeros((spread_z.shape[0] + 2 * total_x, spread_z.shape[1]))
     pencil[: spread_z.shape[0]] = spread_z
     pencil[spread_z.shape[0] :, : 2 * total_x] = pair_x
     pencil[spread_z.shape[0] : -total_x, 2 * total_x : 3 * total_x] = table_x
+    pencil[spread_z.shape[0] : -total_x, 4 * total_x : 4 * total_x + LANES] = wave_x[:, None]
     return [
         jnp.asarray(t, jnp.float32)
         for t in (
@@ -745,7 +745,7 @@
             table_y,
             np.stack(backward),
             table_z[:, order],
-            inverse,
+            waves,
         )
     ]
 
@@ -784,7 +784,7 @@
     total_x, total_y = cells_x * groups, 2 * cells_y
     share, share_x = levels // ROWS, cells_x // 2
     section, place, core = (lax.axis_index("sec"), lax.axis_index("gx"), lax.axis_index("gy"))
-    pencil, table_y, backward, table_z, inverse = tables(levels, total_x, total_y, groups)
+    pencil, table_y, backward, table_z, waves = tables(levels, total_x, total_y, groups)
 
     near, far = REACH - 4, 4
     up = [(i, (i + 1) % groups) for i in range(groups)]
@@ -793,16 +793,21 @@
     straight = [(2 * i, 2 * j) for i, j in up] + [(2 * j + 1, 2 * i + 1) for i, j in up]
     crossed = [(2 * i + 1, 2 * j) for i, j in up] + [(2 * j, 2 * i + 1) for i, j in up]
     own = jnp.transpose(initial.reshape(3, ROWS, share, cells_x, cells_y), (3, 0, 2, 1, 4))
-    left = lax.ppermute(own[cells_x - near :], "gx", up)
-    right = lax.ppermute(own[:near], "gx", down)
+    even = place % 2 == 0
+    pairs_across = [(i, i ^ 1) for i in range(groups)]
+    pairs_around = [(i, (i - 1 if i % 2 == 0 else i + 1) % groups) for i in range(groups)]
+    upper = lax.dynamic_slice_in_dim(own, jnp.where(even, cells_x - near, 0), near, 0)
+    lower = lax.dynamic_slice_in_dim(own, jnp.where(even, 0, cells_x - near), near, 0)
+    around = lax.ppermute(lower, "gx", pairs_around)
+    across = lax.ppermute(upper, "gx", pairs_across)
     tail, head = cells_x - REACH, near
     same = lax.dynamic_slice_in_dim(own, jnp.where(core == 0, tail, head), far, 0)
     other = lax.dynamic_slice_in_dim(own, jnp.where(core == 0, head, tail), far, 0)
-    far_here = lax.ppermute(same, ("gx", "gy"), straight)
+    own_there = lax.ppermute(own, "gy", swap)
+    other, across = lax.optimization_barrier((other, across))
     far_there = lax.ppermute(other, ("gx", "gy"), crossed)
-    own_there = lax.ppermute(own, "gy", swap)
-    left_there = lax.ppermute(left, "gy", swap)
-    right_there = lax.ppermute(right, "gy", swap)
+    across_there = lax.ppermute(across, "gy", swap)
+    around_there = lax.ppermute(around, "gy", swap)
 
     strength = 2.0 * THRUST_COEFF * section.astype(jnp.float32)
     along_z = jnp.arange(levels).reshape(ROWS, share).T.reshape(levels)
@@ -816,10 +821,8 @@
 
     near_thrust = thrust_on(2 - near, cells_x + 2 * near - 4)
     far_thrust = thrust_on((2 - REACH) * (1 - core) + (share_x + 1) * core, far + near + share_x - 3)
-    own_inverse = lax.dynamic_slice(
-        inverse, (place, core, 0, 0, 0), (1, 1) + inverse.shape[2:]
-    )[0, 0]
-
+    same, near_thrust, far_thrust = lax.optimization_barrier((same, near_thrust, far_thrust))
+    far_here = lax.ppermute(same, ("gx", "gy"), straight)
     f32 = jnp.float32
     body = (3, share, ROWS, total_y)
 
@@ -832,39 +835,37 @@
         near_kernel,
         shapes,
         [columns(reached)] * 3
-        + [pltpu.VMEM((reached,) + body[1:], f32), pltpu.VMEM(body, f32)],
+        + [pltpu.VMEM((reached,) + body[1:], f32), pltpu.VMEM(body, f32), columns(reached)],
         own,
         own_there,
-        left,
-        left_there,
-        right,
-        right_there,
+        across,
+        across_there,
+        around,
+        around_there,
         near_thrust,
     )
     window = far + near + share_x + 1
     pairs = 3 * share // 2
     piece = jax.ShapeDtypeStruct((ROWS, pairs, 2 * share_x, cells_y), f32)
     parts = levels // (2 * groups)
-    pieces, source = call(
+    piece_here, piece_send, source = call(
         functools.partial(far_kernel, total_x),
-        [
-            jax.ShapeDtypeStruct((2,) + piece.shape, f32),
-            jax.ShapeDtypeStruct((2 * share_x * levels, total_y), f32),
-        ],
+        [piece, piece, jax.ShapeDtypeStruct((2 * share_x * levels, total_y), f32)],
         [columns(window)] * 4
         + [
             pltpu.VMEM((window,) + body[1:], f32),
             pltpu.VMEM(body, f32),
+            columns(window),
             pltpu.VMEM((share_x * 3 * levels, cells_y), f32),
             pltpu.VMEM((share_x * 3 * levels, cells_y), f32),
         ],
         fringe_bounds,
         own,
         own_there,
-        left,
-        left_there,
-        right,
-        right_there,
+        across,
+        across_there,
+        around,
+        around_there,
         far_here,
         far_there,
         first,
@@ -872,8 +873,7 @@
         third,
         far_thrust,
     )
-    outlet = [(g, groups + g) for g in range(groups - groups // 4, groups)]
-    upstream = lax.ppermute(pieces, ("sec", "gx"), outlet)
+    piece_there = lax.ppermute(piece_send, "gy", swap)
     spectra = call(
         spectra_kernel,
         jax.ShapeDtypeStruct((2, groups, 2, parts, 2 * share_x, LANES), f32),
@@ -885,23 +885,39 @@
     received = lax.all_to_all(
         spectra.reshape((4 * groups,) + spectra.shape[3:]), ("sec", "gx", "gy"), 0, 0, tiled=True
     ).reshape(spectra.shape)
-    blended_here, blended_send = call(
-        blend_kernel, [piece, piece], [], fringe_bounds, pieces, upstream
-    )
-    blended_there = lax.ppermute(blended_send, "gy", swap)
-    pressure_rows = 3 * total_x // 4
+    blocks = call(
+        arrange_kernel,
+        [jax.ShapeDtypeStruct((3 * share, cells_x, cells_y), f32)] * groups,
+        [],
+        piece_here,
+        piece_there,
+    )
+    moved = [blocks[0]] + [
+        lax.ppermute(block, "gx", [(i, i ^ d) for i in range(groups)])
+        for d, block in enumerate(blocks)
+        if d
+    ]
     packed = call(
         pencil_kernel,
-        jax.ShapeDtypeStruct((groups, pressure_rows + 3 * share * cells_x, LANES), f32),
+        jax.ShapeDtypeStruct((groups, 3 * total_x // 4, LANES), f32),
         [],
         received,
-        own_inverse,
+        waves,
         pencil,
-        blended_here,
-        blended_there,
-    )
+    )
+    packed, *moved = lax.optimization_barrier([packed] + moved)
+    moved = jnp.stack(moved)
+    outlet = groups // 4
+    leaving = jnp.stack(
+        [
+            lax.dynamic_index_in_dim(moved, place ^ s, 0, keepdims=False)
+            for s in range(groups - outlet, groups)
+        ]
+    )
+    upstream = lax.ppermute(leaving, "sec", [(0, 1)])
     returned = lax.all_to_all(packed, "gx", 0, 0, tiled=True)
-    partner = lax.ppermute(returned[:, :pressure_rows], "gy", swap)
+    returned, upstream = lax.optimization_barrier((returned, upstream))
+    partner = lax.ppermute(returned, "gy", swap)
     velocity_next, pressure = call(
         project_kernel,
         [
@@ -909,9 +925,12 @@
             jax.ShapeDtypeStruct((share, total_x, cells_y), f32),
         ],
         [],
+        fringe_bounds,
         returned,
         partner,
         backward,
+        moved,
+        upstream,
     )
     return (velocity_next[None], pressure[None])
 

time: 70.9 us -> 65.7 us (0.927)
  blocking collectives: 19.7 us -> 0 us
  starting transfers between devices: 16.1 us -> 33.3 us
  waiting for transfers between devices: 17.7 us -> 15.5 us
  local copies, waits for them, and re-layouts: 2.6 us -> 1.77 us
    all_to_all x1 -> x0, blocking collectives: 19.7 us -> none  [paired_plan(): returned = lax.all_to_all(packed, 'gx', 0, 0, tiled=True)]
    ppermute x7 -> x14, starting transfers between devices: 6.77 us -> 22.9 us  [the longest x7 10.9 us: paired_plan(): lax.ppermute(block, 'gx', [(i, i ^ d) for i in range(groups)])]
    all_to_all x1, waiting for transfers between devices: 8.43 us -> 0.01 us  [paired_plan(): lax.all_to_all(spectra.reshape((4 * groups,) + spectra.shape[3:]), ('sec'...]
    all_to_all x0 -> x1, starting transfers between devices: none -> 3.39 us  [paired_plan(): returned = lax.all_to_all(packed, 'gx', 0, 0, tiled=True)]
    ppermute x7 -> x14, waiting for transfers between devices: 9.27 us -> 11.7 us  [the longest x7 4.63 us: paired_plan(): lax.ppermute(block, 'gx', [(i, i ^ d) for i in range(groups)])]
    all_to_all x0 -> x1, waiting for transfers between devices: none -> 2.01 us  [paired_plan(): returned = lax.all_to_all(packed, 'gx', 0, 0, tiled=True)]
    ppermute x1, starting transfers between devices: 2.61 us -> 0.93 us  [paired_plan(): far_there = lax.ppermute(other, ('gx', 'gy'), crossed)]
    ppermute x1, waiting for transfers between devices: 0.01 us -> 1.54 us  [paired_plan(): far_here = lax.ppermute(same, ('gx', 'gy'), straight)]
  transfers between devices with their start and end apart: 11 -> 19, of which waited for: 5 -> 13; matrix products, arithmetic and copies ran while one was open for 4% -> 3% of each run, Pallas kernels for 9% -> 9%
where the time goes in v5:
time: 65.7 us; the launch traced here: 65.4 us
  starting transfers between devices  33.3 us (51%)
  waiting for transfers between devices  15.5 us (24%)
  Pallas kernels  12.6 us (19%)
  local copies, waits for them, and re-layouts  1.77 us (3%)
  matrix products  1.14 us (2%)
  between operations  0.91 us (1%)
    pallas_call x6, Pallas kernels, call(): pl.pallas_call(kernel, out_shape=out_shapes, in_specs=in_specs, out_specs...  12.6 us
    ppermute x7, starting transfers between devices, paired_plan(): lax.ppermute(block, 'gx', [(i, i ^ d) for i in range(groups)])  10.9 us
    all_to_all x1, starting transfers between devices, paired_plan(): lax.all_to_all(spectra.reshape((4 * groups,) + spectra.shape[3:]), ('sec'...  6.01 us
    ppermute x7, waiting for transfers between devices, paired_plan(): lax.ppermute(block, 'gx', [(i, i ^ d) for i in range(groups)])  4.63 us
    ppermute x1, starting transfers between devices, paired_plan(): around = lax.ppermute(lower, 'gx', pairs_around)  3.54 us
    all_to_all x1, starting transfers between devices, paired_plan(): returned = lax.all_to_all(packed, 'gx', 0, 0, tiled=True)  3.39 us
    ppermute x1, starting transfers between devices, paired_plan(): upstream = lax.ppermute(leaving, 'sec', [(0, 1)])  3.37 us
    ppermute x1, starting transfers between devices, paired_plan(): across = lax.ppermute(upper, 'gx', pairs_across)  3.03 us
  transfers between devices with their start and end apart: 19, of which 13 were waited for; matrix products, arithmetic and copies ran while one was open for 3% of the time, Pallas kernels for 9%

profile of v5, /device:TPU:0, one launch (start us, length us, event | category | flops | bytes accessed | tf_op | source)
XLA Modules:
  0.0 65.4 jit_solution(18119119017907888302)
XLA Ops:
  0.6 0.0 copy-start.6
  0.7 1.2 %copy.25 = f32[3,8,4,8,128]{4,1,2,0,3:T(8,128)S(1)} copy(f32[3,8,4,8,128]{4,3,2,1,0:T(8,128)} %bitcast.55) | data formatting | bytes 786432 | tf_op jit(solution)/shard_map/reshape;squeeze | solution.py:795
  1.9 3.0 %collective-permute-start.1 = (f32[3,3,4,8,128]{4,3,2,1,0:T(8,128)S(1)}, f32[3,3,4,8,128]{4,3,2,1,0:T(8,128)S(1)}, u32[]{:S(2)}, u32[]{:S(2)}) collective-permute-start(f32[3,3,4,8,128]{4,3,2,1,0:T(8,128)S(1)} %get-tuple-element.71), channel_id=1, source_target_pairs={{0,2},{2,0},{4,6},{6,4},{8,10},{10,8},{12,14},{14,12},{1,3},{3,1},... | collective-permute-start | bytes 442376 | tf_op jit(solution)/shard_map/ppermute | solution.py:802
  5.0 3.5 %collective-permute-start.3 = (f32[3,3,4,8,128]{4,3,2,1,0:T(8,128)S(1)}, f32[3,3,4,8,128]{4,3,2,1,0:T(8,128)S(1)}, u32[]{:S(2)}, u32[]{:S(2)}) collective-permute-start(f32[3,3,4,8,128]{4,3,2,1,0:T(8,128)S(1)} %get-tuple-element.70), channel_id=1, source_target_pairs={{0,14},{2,4},{4,2},{6,8},{8,6},{10,12},{12,10},{14,0},{1,15},{3,5}... | collective-permute-start | bytes 442376 | tf_op jit(solution)/shard_map/ppermute | solution.py:801
  8.5 0.0 collective-permute-start
  8.5 0.0 copy-done.6
  8.5 0.1 fusion.12
  8.7 0.1 reshape.142
  8.8 0.1 subtract_multiply_fusion
  8.8 0.6 fusion.2
  9.4 0.6 fusion.3
  10.0 0.1 copy.24
  10.1 0.2 copy.23
  10.3 0.0 copy-start.5
  10.3 0.1 collective-permute-start.5
  10.4 0.8 %collective-permute-done.1.across_here = f32[3,3,4,8,128]{4,3,2,1,0:T(8,128)S(1)} collective-permute-done((f32[3,3,4,8,128]{4,3,2,1,0:T(8,128)S(1)}, f32[3,3,4,8,128]{4,3,2,1,0:T(8,128)S(1)}, u32[]{:S(2)}, u32[]{:S(2)}) %collective-permute-start.1) | collective-permute-done | bytes 147488 | tf_op jit(solution)/shard_map/ppermute | solution.py:802
  11.2 0.9 %collective-permute-start.6 = (f32[4,3,4,8,128]{4,3,2,1,0:T(8,128)S(1)}, f32[4,3,4,8,128]{4,3,2,1,0:T(8,128)S(1)}, u32[]{:S(2)}, u32[]{:S(2)}) collective-permute-start(f32[4,3,4,8,128]{4,3,2,1,0:T(8,128)S(1)} %get-tuple-element.36), channel_id=1, source_target_pairs={{1,2},{3,4},{5,6},{7,8},{9,10},{11,12},{13,14},{15,0},{2,1},{4,3},... | collective-permute-start | bytes 589832 | tf_op jit(solution)/shard_map/ppermute | solution.py:808
  12.2 1.7 %collective-permute-start.2 = (f32[3,3,4,8,128]{4,3,2,1,0:T(8,128)S(1)}, f32[3,3,4,8,128]{4,3,2,1,0:T(8,128)S(1)}, u32[]{:S(2)}, u32[]{:S(2)}) collective-permute-start(f32[3,3,4,8,128]{4,3,2,1,0:T(8,128)S(1)} %collective-permute-done.1.across_here), channel_id=1, source_target_pairs={{0,1},{1,0},{2,3},{3,2},{4,5},{5,4},{6,7},{7,6},{8,9},{9,8},{10,11... | collective-permute-start | bytes 442376 | tf_op jit(solution)/shard_map/ppermute | solution.py:809
  13.8 0.0 collective-permute-done.3.around_here
  13.8 0.0 collective-permute-start.4
  13.8 1.0 %collective-permute-done.2.across_there = f32[3,3,4,8,128]{4,3,2,1,0:T(8,128)S(1)} collective-permute-done((f32[3,3,4,8,128]{4,3,2,1,0:T(8,128)S(1)}, f32[3,3,4,8,128]{4,3,2,1,0:T(8,128)S(1)}, u32[]{:S(2)}, u32[]{:S(2)}) %collective-permute-start.2) | collective-permute-done | bytes 147488 | tf_op jit(solution)/shard_map/ppermute | solution.py:809
  14.8 0.4 collective-permute-done.4.around_there
  15.2 0.0 collective-permute-done.own_there
  15.2 3.9 %shard_map.95 = (f32[4,3,4,8,256]{4,3,2,1,0:T(8,128)S(1)}, f32[4,3,4,8,256]{4,3,2,1,0:T(8,128)S(1)}, f32[2,3,4,8,256]{4,3,2,1,0:T(8,128)S(1)}) custom-call(f32[8,3,4,8,128]{4,3,2,1,0:T(8,128)S(1)} %bitcast.50, f32[8,3,4,8,128]{4,3,2,1,0:T(8,128)S(1)} %collective-permute-done.own_there, f32[3,3,4,8,128]{4,3,2,1,0:T(8,128)S(1)} %collective-permute-done.1.across_here, ...), custom_call_target="tpu_custom_call" | custom-call | tf_op jit(solution)/shard_map/pallas_call | solution.py:758
  19.1 1.5 %collective-permute-done.5.far_here = f32[4,3,4,8,128]{4,3,2,1,0:T(8,128)S(1)} collective-permute-done((f32[4,3,4,8,128]{4,3,2,1,0:T(8,128)S(1)}, f32[4,3,4,8,128]{4,3,2,1,0:T(8,128)S(1)}, u32[]{:S(2)}, u32[]{:S(2)}) %collective-permute-start.5) | collective-permute-done | bytes 196640 | tf_op jit(solution)/shard_map/ppermute | solution.py:825
  20.7 0.3 collective-permute-done.6.far_there
  21.0 0.0 copy-done.5
  21.0 0.0 copy-start.2
  21.0 3.5 %shard_map.96 = (f32[8,6,8,128]{3,2,1,0:T(8,128)S(1)}, f32[8,6,8,128]{3,2,1,0:T(8,128)S(1)}, f32[256,256]{1,0:T(8,128)S(1)}) custom-call(s32[2]{0:T(128)S(1)} %copy-done.5, f32[8,3,4,8,128]{4,3,2,1,0:T(8,128)S(1)} %bitcast.51, f32[8,3,4,8,128]{4,3,2,1,0:T(8,128)S(1)} %collective-permute-done.own_there, ...), custom_call_target="tpu_custom_call" | custom-call | tf_op jit(solution)/shard_map/pallas_call | solution.py:758
  24.5 0.0 copy-start
  24.5 0.0 copy-start.3
  24.5 0.0 copy-done.2
  24.5 0.0 copy-done.4
  24.5 1.6 %shard_map.97 = f32[2,8,2,2,8,128]{5,4,3,2,1,0:T(8,128)} custom-call(f32[256,256]{1,0:T(8,128)S(1)} %get-tuple-element.42.source, f32[256,256]{1,0:T(8,128)S(1)} %copy-done.2, f32[32,32]{1,0:T(8,128)S(1)} %copy-done.4), custom_call_target="tpu_custom_call" | custom-call | tf_op jit(solution)/shard_map/pallas_call | solution.py:758
  26.1 6.0 %all-to-all-start = ((f32[32,2,8,128]{3,2,1,0:T(8,128)}), f32[32,2,8,128]{3,2,1,0:T(8,128)S(1)}, u32[]{:S(2)}, u32[]{:S(2)}) async-start(f32[32,2,8,128]{3,2,1,0:T(8,128)} %bitcast.13), calls=%async_computation | async-start | bytes 524288 | tf_op jit(solution)/shard_map/all_to_all | solution.py:885
  32.1 0.3 collective-permute-start.7
  32.4 1.2 %collective-permute-done.7.piece_there = f32[8,6,8,128]{3,2,1,0:T(8,128)S(1)} collective-permute-done((f32[8,6,8,128]{3,2,1,0:T(8,128)S(1)}, f32[8,6,8,128]{3,2,1,0:T(8,128)S(1)}, u32[]{:S(2)}, u32[]{:S(2)}) %collective-permute-start.7) | collective-permute-done | bytes 196640 | tf_op jit(solution)/shard_map/ppermute | solution.py:876
  33.7 2.7 %collective-permute-start.10 = (f32[12,8,128]{2,1,0:T(8,128)S(1)}, f32[12,8,128]{2,1,0:T(8,128)S(1)}, u32[]{:S(2)}, u32[]{:S(2)}) collective-permute-start(f32[12,8,128]{2,1,0:T(8,128)S(1)} %get-tuple-element.48), channel_id=1, source_target_pairs={{0,6},{2,4},{4,2},{6,0},{8,14},{10,12},{12,10},{14,8},{1,7},{3,5},... | collective-permute-start | bytes 147464 | tf_op jit(solution)/shard_map/ppermute | solution.py:896
  36.4 2.4 %collective-permute-start.11 = (f32[12,8,128]{2,1,0:T(8,128)S(1)}, f32[12,8,128]{2,1,0:T(8,128)S(1)}, u32[]{:S(2)}, u32[]{:S(2)}) collective-permute-start(f32[12,8,128]{2,1,0:T(8,128)S(1)} %get-tuple-element.49), channel_id=1, source_target_pairs={{0,8},{2,10},{4,12},{6,14},{8,0},{10,2},{12,4},{14,6},{1,9},{3,11}... | collective-permute-start | bytes 147464 | tf_op jit(solution)/shard_map/ppermute | solution.py:896
  38.9 0.5 collective-permute-start.12
  39.3 2.4 %collective-permute-start.13 = (f32[12,8,128]{2,1,0:T(8,128)S(1)}, f32[12,8,128]{2,1,0:T(8,128)S(1)}, u32[]{:S(2)}, u32[]{:S(2)}) collective-permute-start(f32[12,8,128]{2,1,0:T(8,128)S(1)} %get-tuple-element.51), channel_id=1, source_target_pairs={{0,12},{2,14},{4,8},{6,10},{8,4},{10,6},{12,0},{14,2},{1,13},{3,15... | collective-permute-start | bytes 147464 | tf_op jit(solution)/shard_map/ppermute | solution.py:896
  41.7 2.4 %collective-permute-start.14 = (f32[12,8,128]{2,1,0:T(8,128)S(1)}, f32[12,8,128]{2,1,0:T(8,128)S(1)}, u32[]{:S(2)}, u32[]{:S(2)}) collective-permute-start(f32[12,8,128]{2,1,0:T(8,128)S(1)} %get-tuple-element.52), channel_id=1, source_target_pairs={{0,14},{2,12},{4,10},{6,8},{8,6},{10,4},{12,2},{14,0},{1,15},{3,13... | collective-permute-start | bytes 147464 | tf_op jit(solution)/shard_map/ppermute | solution.py:896
  44.1 0.0 collective-permute-done.10
  44.1 0.6 collective-permute-start.8
  44.6 2.2 %collective-permute-done.11 = f32[12,8,128]{2,1,0:T(8,128)S(1)} collective-permute-done((f32[12,8,128]{2,1,0:T(8,128)S(1)}, f32[12,8,128]{2,1,0:T(8,128)S(1)}, u32[]{:S(2)}, u32[]{:S(2)}) %collective-permute-start.11) | collective-permute-done | bytes 49184 | tf_op jit(solution)/shard_map/ppermute | solution.py:896
  46.8 0.0 collective-permute-start.9
  46.8 0.0 all-to-all-done
  46.8 0.0 copy-done
  46.8 0.0 copy-done.3
  46.8 0.0 copy-start.1
  46.9 1.6 %shard_map.98 = f32[8,48,128]{2,1,0:T(8,128)} custom-call(f32[2,8,2,2,8,128]{5,4,3,2,1,0:T(8,128)S(1)} %bitcast.53, f32[8,2,4,128]{3,2,1,0:T(4,128)S(1)} %copy-done.3, f32[640,512]{1,0:T(8,128)S(1)} %copy-done), custom_call_target="tpu_custom_call" | custom-call | tf_op jit(solution)/shard_map/pallas_call | solution.py:758
  48.5 0.7 %collective-permute-done.12 = f32[12,8,128]{2,1,0:T(8,128)S(1)} collective-permute-done((f32[12,8,128]{2,1,0:T(8,128)S(1)}, f32[12,8,128]{2,1,0:T(8,128)S(1)}, u32[]{:S(2)}, u32[]{:S(2)}) %collective-permute-start.12) | collective-permute-done | bytes 49184 | tf_op jit(solution)/shard_map/ppermute | solution.py:896
  49.2 0.0 collective-permute-done.13
  49.2 0.0 collective-permute-done.14
  49.2 0.1 collective-permute-done.8
  49.3 1.6 %collective-permute-done.9 = f32[12,8,128]{2,1,0:T(8,128)S(1)} collective-permute-done((f32[12,8,128]{2,1,0:T(8,128)S(1)}, f32[12,8,128]{2,1,0:T(8,128)S(1)}, u32[]{:S(2)}, u32[]{:S(2)}) %collective-permute-start.9) | collective-permute-done | bytes 49184 | tf_op jit(solution)/shard_map/ppermute | solution.py:896
  50.9 3.4 %all-to-all-start.1 = ((f32[8,48,128]{2,1,0:T(8,128)}), f32[8,48,128]{2,1,0:T(8,128)S(1)}, u32[]{:S(2)}, u32[]{:S(2)}) async-start(f32[8,48,128]{2,1,0:T(8,128)} %shard_map.98), calls=%async_computation.1 | async-start | bytes 393216 | tf_op jit(solution)/shard_map/all_to_all | solution.py:918
  54.5 3.4 %collective-permute-start.15 = (f32[2,12,8,128]{3,2,1,0:T(8,128)S(1)}, f32[2,12,8,128]{3,2,1,0:T(8,128)S(1)}, u32[]{:S(2)}, u32[]{:S(2)}) collective-permute-start(f32[2,12,8,128]{3,2,1,0:T(8,128)S(1)} %pad_maximum_fusion), channel_id=1, source_target_pairs={{0,16},{1,17},{2,18},{3,19},{4,20},{5,21},{6,22},{7,23},{8,24},{9,... | collective-permute-start | bytes 294920 | tf_op jit(solution)/shard_map/ppermute | solution.py:917
  57.8 2.2 %collective-permute-done.15.upstream = f32[2,12,8,128]{3,2,1,0:T(8,128)S(1)} collective-permute-done((f32[2,12,8,128]{3,2,1,0:T(8,128)S(1)}, f32[2,12,8,128]{3,2,1,0:T(8,128)S(1)}, u32[]{:S(2)}, u32[]{:S(2)}) %collective-permute-start.15) | collective-permute-done | bytes 98336 | tf_op jit(solution)/shard_map/ppermute | solution.py:917
  60.0 2.0 %all-to-all-done.1.received = f32[8,48,128]{2,1,0:T(8,128)S(1)} async-done(((f32[8,48,128]{2,1,0:T(8,128)}), f32[8,48,128]{2,1,0:T(8,128)S(1)}, u32[]{:S(2)}, u32[]{:S(2)}) %all-to-all-start.1) | async-done | bytes 196640 | tf_op jit(solution)/shard_map/all_to_all | solution.py:918
  62.0 0.0 collective-permute-start.16
  62.0 1.4 %collective-permute-done.16.partner = f32[8,48,128]{2,1,0:T(8,128)S(1)} collective-permute-done((f32[8,48,128]{2,1,0:T(8,128)S(1)}, f32[8,48,128]{2,1,0:T(8,128)S(1)}, u32[]{:S(2)}, u32[]{:S(2)}) %collective-permute-start.16) | collective-permute-done | bytes 196640 | tf_op jit(solution)/shard_map/ppermute | solution.py:920
  63.5 0.0 copy-done.1
  63.5 1.9 %shard_map.100 = (f32[3,4,64,128]{3,2,1,0:T(8,128)}, f32[4,64,128]{2,1,0:T(8,128)}) custom-call(s32[2]{0:T(128)S(1)} %copy-done.5, f32[8,48,128]{2,1,0:T(8,128)S(1)} %all-to-all-done.1.received, f32[8,48,128]{2,1,0:T(8,128)S(1)} %collective-permute-done.16.partner, f32[2,256,256]{2,1,0:T(8,128)S(1)} %copy-done.1, ...), custom_call_target="tpu_custom_call" | custom-call | tf_op jit(solution)/shard_map/pallas_call | solution.py:758
  (18 shorter events, 0.2 us)
Async XLA Ops:
  0.6 7.9 %copy-start.6 = (s32[64,3]{0,1:T(4,128)S(1)}, s32[64,3]{0,1:T(4,128)}, u32[]{:S(2)}) copy-start(s32[64,3]{0,1:T(4,128)} %param.9) | copy-start | bytes 2308
  1.9 9.3 %collective-permute-start.1 = (f32[3,3,4,8,128]{4,3,2,1,0:T(8,128)S(1)}, f32[3,3,4,8,128]{4,3,2,1,0:T(8,128)S(1)}, u32[]{:S(2)}, u32[]{:S(2)}) collective-permute-start(f32[3,3,4,8,128]{4,3,2,1,0:T(8,128)S(1)} %get-tuple-element.71), channel_id=1, source_target_pairs={{0,2},{2,0},{4,6},{6,4},{8,10},{10,8},{12,14},{14,12},{1,3},{3,1},... | collective-permute-start | bytes 442376 | tf_op jit(solution)/shard_map/ppermute | solution.py:802
  5.0 8.9 %collective-permute-start.3 = (f32[3,3,4,8,128]{4,3,2,1,0:T(8,128)S(1)}, f32[3,3,4,8,128]{4,3,2,1,0:T(8,128)S(1)}, u32[]{:S(2)}, u32[]{:S(2)}) collective-permute-start(f32[3,3,4,8,128]{4,3,2,1,0:T(8,128)S(1)} %get-tuple-element.70), channel_id=1, source_target_pairs={{0,14},{2,4},{4,2},{6,8},{8,6},{10,12},{12,10},{14,0},{1,15},{3,5}... | collective-permute-start | bytes 442376 | tf_op jit(solution)/shard_map/ppermute | solution.py:801
  8.5 6.7 %collective-permute-start = (f32[8,3,4,8,128]{4,3,2,1,0:T(8,128)S(1)}, f32[8,3,4,8,128]{4,3,2,1,0:T(8,128)S(1)}, u32[]{:S(2)}, u32[]{:S(2)}) collective-permute-start(f32[8,3,4,8,128]{4,3,2,1,0:T(8,128)S(1)} %bitcast.49), channel_id=1, source_target_pairs={{0,1},{1,0},{2,3},{3,2},{4,5},{5,4},{6,7},{7,6},{8,9},{9,8},{10,11... | collective-permute-start | bytes 1179656 | tf_op jit(solution)/shard_map/ppermute | solution.py:806
  10.3 10.7 %copy-start.5 = (s32[2]{0:T(128)S(1)}, s32[2]{0:T(128)}, u32[]{:S(2)}) copy-start(s32[2]{0:T(128)} %fringe.3) | copy-start | bytes 28
  10.3 10.3 %collective-permute-start.5 = (f32[4,3,4,8,128]{4,3,2,1,0:T(8,128)S(1)}, f32[4,3,4,8,128]{4,3,2,1,0:T(8,128)S(1)}, u32[]{:S(2)}, u32[]{:S(2)}) collective-permute-start(f32[4,3,4,8,128]{4,3,2,1,0:T(8,128)S(1)} %get-tuple-element.35), channel_id=1, source_target_pairs={{0,2},{2,4},{4,6},{6,8},{8,10},{10,12},{12,14},{14,0},{3,1},{5,3},... | collective-permute-start | bytes 589832 | tf_op jit(solution)/shard_map/ppermute | solution.py:825
  11.2 9.7 %collective-permute-start.6 = (f32[4,3,4,8,128]{4,3,2,1,0:T(8,128)S(1)}, f32[4,3,4,8,128]{4,3,2,1,0:T(8,128)S(1)}, u32[]{:S(2)}, u32[]{:S(2)}) collective-permute-start(f32[4,3,4,8,128]{4,3,2,1,0:T(8,128)S(1)} %get-tuple-element.36), channel_id=1, source_target_pairs={{1,2},{3,4},{5,6},{7,8},{9,10},{11,12},{13,14},{15,0},{2,1},{4,3},... | collective-permute-start | bytes 589832 | tf_op jit(solution)/shard_map/ppermute | solution.py:808
  12.2 2.7 %collective-permute-start.2 = (f32[3,3,4,8,128]{4,3,2,1,0:T(8,128)S(1)}, f32[3,3,4,8,128]{4,3,2,1,0:T(8,128)S(1)}, u32[]{:S(2)}, u32[]{:S(2)}) collective-permute-start(f32[3,3,4,8,128]{4,3,2,1,0:T(8,128)S(1)} %collective-permute-done.1.across_here), channel_id=1, source_target_pairs={{0,1},{1,0},{2,3},{3,2},{4,5},{5,4},{6,7},{7,6},{8,9},{9,8},{10,11... | collective-permute-start | bytes 442376 | tf_op jit(solution)/shard_map/ppermute | solution.py:809
  13.8 1.4 %collective-permute-start.4 = (f32[3,3,4,8,128]{4,3,2,1,0:T(8,128)S(1)}, f32[3,3,4,8,128]{4,3,2,1,0:T(8,128)S(1)}, u32[]{:S(2)}, u32[]{:S(2)}) collective-permute-start(f32[3,3,4,8,128]{4,3,2,1,0:T(8,128)S(1)} %collective-permute-done.3.around_here), channel_id=1, source_target_pairs={{0,1},{1,0},{2,3},{3,2},{4,5},{5,4},{6,7},{7,6},{8,9},{9,8},{10,11... | collective-permute-start | bytes 442376 | tf_op jit(solution)/shard_map/ppermute | solution.py:810
  21.0 3.6 %copy-start.2 = (f32[256,256]{1,0:T(8,128)S(1)}, f32[256,256]{1,0:T(8,128)}, u32[]{:S(2)}) copy-start(f32[256,256]{1,0:T(8,128)} %constant.113.clone.table_y) | copy-start | bytes 786436
  21.0 3.6 %copy-start.4 = (f32[32,32]{1,0:T(8,128)S(1)}, f32[32,32]{1,0:T(8,128)}, u32[]{:S(2)}) copy-start(f32[32,32]{1,0:T(8,128)} %constant.115.clone.table_z) | copy-start | bytes 12292
  24.5 22.3 %copy-start = (f32[640,512]{1,0:T(8,128)S(1)}, f32[640,512]{1,0:T(8,128)}, u32[]{:S(2)}) copy-start(f32[640,512]{1,0:T(8,128)} %constant.112.clone.table) | copy-start | bytes 3932164
  24.5 22.3 %copy-start.3 = (f32[8,2,4,128]{3,2,1,0:T(4,128)S(1)}, f32[8,2,4,128]{3,2,1,0:T(4,128)}, u32[]{:S(2)}) copy-start(f32[8,2,4,128]{3,2,1,0:T(4,128)} %constant.116.clone.waves) | copy-start | bytes 98308
  26.1 20.7 %all-to-all-start = ((f32[32,2,8,128]{3,2,1,0:T(8,128)}), f32[32,2,8,128]{3,2,1,0:T(8,128)S(1)}, u32[]{:S(2)}, u32[]{:S(2)}) async-start(f32[32,2,8,128]{3,2,1,0:T(8,128)} %bitcast.13), calls=%async_computation | async-start | bytes 524288 | tf_op jit(solution)/shard_map/all_to_all | solution.py:885
  32.1 1.5 %collective-permute-start.7 = (f32[8,6,8,128]{3,2,1,0:T(8,128)S(1)}, f32[8,6,8,128]{3,2,1,0:T(8,128)S(1)}, u32[]{:S(2)}, u32[]{:S(2)}) collective-permute-start(f32[8,6,8,128]{3,2,1,0:T(8,128)S(1)} %get-tuple-element.44), channel_id=1, source_target_pairs={{0,1},{1,0},{2,3},{3,2},{4,5},{5,4},{6,7},{7,6},{8,9},{9,8},{10,11... | collective-permute-start | bytes 589832 | tf_op jit(solution)/shard_map/ppermute | solution.py:876
  33.7 10.4 %collective-permute-start.10 = (f32[12,8,128]{2,1,0:T(8,128)S(1)}, f32[12,8,128]{2,1,0:T(8,128)S(1)}, u32[]{:S(2)}, u32[]{:S(2)}) collective-permute-start(f32[12,8,128]{2,1,0:T(8,128)S(1)} %get-tuple-element.48), channel_id=1, source_target_pairs={{0,6},{2,4},{4,2},{6,0},{8,14},{10,12},{12,10},{14,8},{1,7},{3,5},... | collective-permute-start | bytes 147464 | tf_op jit(solution)/shard_map/ppermute | solution.py:896
  36.4 10.4 %collective-permute-start.11 = (f32[12,8,128]{2,1,0:T(8,128)S(1)}, f32[12,8,128]{2,1,0:T(8,128)S(1)}, u32[]{:S(2)}, u32[]{:S(2)}) collective-permute-start(f32[12,8,128]{2,1,0:T(8,128)S(1)} %get-tuple-element.49), channel_id=1, source_target_pairs={{0,8},{2,10},{4,12},{6,14},{8,0},{10,2},{12,4},{14,6},{1,9},{3,11}... | collective-permute-start | bytes 147464 | tf_op jit(solution)/shard_map/ppermute | solution.py:896
  38.9 10.3 %collective-permute-start.12 = (f32[12,8,128]{2,1,0:T(8,128)S(1)}, f32[12,8,128]{2,1,0:T(8,128)S(1)}, u32[]{:S(2)}, u32[]{:S(2)}) collective-permute-start(f32[12,8,128]{2,1,0:T(8,128)S(1)} %get-tuple-element.50), channel_id=1, source_target_pairs={{0,10},{2,8},{4,14},{6,12},{8,2},{10,0},{12,6},{14,4},{1,11},{3,9}... | collective-permute-start | bytes 147464 | tf_op jit(solution)/shard_map/ppermute | solution.py:896
  39.3 9.9 %collective-permute-start.13 = (f32[12,8,128]{2,1,0:T(8,128)S(1)}, f32[12,8,128]{2,1,0:T(8,128)S(1)}, u32[]{:S(2)}, u32[]{:S(2)}) collective-permute-start(f32[12,8,128]{2,1,0:T(8,128)S(1)} %get-tuple-element.51), channel_id=1, source_target_pairs={{0,12},{2,14},{4,8},{6,10},{8,4},{10,6},{12,0},{14,2},{1,13},{3,15... | collective-permute-start | bytes 147464 | tf_op jit(solution)/shard_map/ppermute | solution.py:896
  41.7 7.5 %collective-permute-start.14 = (f32[12,8,128]{2,1,0:T(8,128)S(1)}, f32[12,8,128]{2,1,0:T(8,128)S(1)}, u32[]{:S(2)}, u32[]{:S(2)}) collective-permute-start(f32[12,8,128]{2,1,0:T(8,128)S(1)} %get-tuple-element.52), channel_id=1, source_target_pairs={{0,14},{2,12},{4,10},{6,8},{8,6},{10,4},{12,2},{14,0},{1,15},{3,13... | collective-permute-start | bytes 147464 | tf_op jit(solution)/shard_map/ppermute | solution.py:896
  44.1 5.2 %collective-permute-start.8 = (f32[12,8,128]{2,1,0:T(8,128)S(1)}, f32[12,8,128]{2,1,0:T(8,128)S(1)}, u32[]{:S(2)}, u32[]{:S(2)}) collective-permute-start(f32[12,8,128]{2,1,0:T(8,128)S(1)} %get-tuple-element.46), channel_id=1, source_target_pairs={{0,2},{2,0},{4,6},{6,4},{8,10},{10,8},{12,14},{14,12},{1,3},{3,1},... | collective-permute-start | bytes 147464 | tf_op jit(solution)/shard_map/ppermute | solution.py:896
  46.8 4.1 %collective-permute-start.9 = (f32[12,8,128]{2,1,0:T(8,128)S(1)}, f32[12,8,128]{2,1,0:T(8,128)S(1)}, u32[]{:S(2)}, u32[]{:S(2)}) collective-permute-start(f32[12,8,128]{2,1,0:T(8,128)S(1)} %get-tuple-element.47), channel_id=1, source_target_pairs={{0,4},{2,6},{4,0},{6,2},{8,12},{10,14},{12,8},{14,10},{1,5},{3,7},... | collective-permute-start | bytes 147464 | tf_op jit(solution)/shard_map/ppermute | solution.py:896
  46.8 16.6 %copy-start.1 = (f32[2,256,256]{2,1,0:T(8,128)S(1)}, f32[2,256,256]{2,1,0:T(8,128)}, u32[]{:S(2)}) copy-start(f32[2,256,256]{2,1,0:T(8,128)} %constant.114.clone.table_y) | copy-start | bytes 1572868
  50.9 11.1 %all-to-all-start.1 = ((f32[8,48,128]{2,1,0:T(8,128)}), f32[8,48,128]{2,1,0:T(8,128)S(1)}, u32[]{:S(2)}, u32[]{:S(2)}) async-start(f32[8,48,128]{2,1,0:T(8,128)} %shard_map.98), calls=%async_computation.1 | async-start | bytes 393216 | tf_op jit(solution)/shard_map/all_to_all | solution.py:918
  54.5 5.6 %collective-permute-start.15 = (f32[2,12,8,128]{3,2,1,0:T(8,128)S(1)}, f32[2,12,8,128]{3,2,1,0:T(8,128)S(1)}, u32[]{:S(2)}, u32[]{:S(2)}) collective-permute-start(f32[2,12,8,128]{3,2,1,0:T(8,128)S(1)} %pad_maximum_fusion), channel_id=1, source_target_pairs={{0,16},{1,17},{2,18},{3,19},{4,20},{5,21},{6,22},{7,23},{8,24},{9,... | collective-permute-start | bytes 294920 | tf_op jit(solution)/shard_map/ppermute | solution.py:917
  62.0 1.4 %collective-permute-start.16 = (f32[8,48,128]{2,1,0:T(8,128)S(1)}, f32[8,48,128]{2,1,0:T(8,128)S(1)}, u32[]{:S(2)}, u32[]{:S(2)}) collective-permute-start(f32[8,48,128]{2,1,0:T(8,128)S(1)} %all-to-all-done.1.received), channel_id=1, source_target_pairs={{0,1},{1,0},{2,3},{3,2},{4,5},{5,4},{6,7},{7,6},{8,9},{9,8},{10,11... | collective-permute-start | bytes 589832 | tf_op jit(solution)/shard_map/ppermute | solution.py:920

commit v6 on v5

--- a/solution.py
+++ b/solution.py
@@ -282,6 +282,75 @@
     return arrays
 
 
+def reordered(values, order):
+    one = order.astype(jnp.bfloat16)
+    high, rest = split(values)
+    low = values - high.astype(jnp.float32) - rest.astype(jnp.float32)
+
+    def product(x):
+        return jnp.dot(x, one, preferred_element_type=jnp.float32)
+
+    return (product(high) + product(rest)) + product(low.astype(jnp.bfloat16))
+
+
+def parting(lanes, inverse=False):
+    line = lax.broadcasted_iota(jnp.int32, (lanes, lanes), 1 if inverse else 0)
+    spot = lax.broadcasted_iota(jnp.int32, (lanes, lanes), 0 if inverse else 1)
+    later = jnp.where(spot >= lanes // 2, 1, 0)
+    place = 2 * (spot - later * (lanes // 2)) + (later ^ lax.axis_index("gy"))
+    return jnp.where(line == place, 1.0, 0.0)
+
+
+def packed_columns(initial, columns, cells_x, tiles):
+    total, lanes = initial.shape
+    levels = total // (3 * cells_x)
+    rows = levels // tiles
+    picked = [
+        initial[pl.ds((c * levels + t) * cells_x + x, rows, stride=tiles * cells_x), :]
+        for x in columns
+        for c in range(3)
+        for t in range(tiles)
+    ]
+    values = reordered(jnp.concatenate(picked, axis=0), parting(lanes))
+    return values.reshape(len(columns), 3, tiles, rows, lanes)
+
+
+def pack_near_kernel(cells_x, initial, lower, upper):
+    near, _, tiles, _, _ = lower.shape
+    columns = list(range(near)) + list(range(cells_x - near, cells_x))
+    values = packed_columns(initial, columns, cells_x, tiles)
+    even = lax.axis_index("gx") % 2 == 0
+
+    @pl.when(even)
+    def _():
+        lower[...] = values[:near]
+        upper[...] = values[near:]
+
+    @pl.when(jnp.logical_not(even))
+    def _():
+        lower[...] = values[near:]
+        upper[...] = values[:near]
+
+
+def pack_kernel(initial, own, same, other):
+    cells_x, _, tiles, _, _ = own.shape
+    far = same.shape[0]
+    tail, head = cells_x - REACH, REACH - far
+    values = packed_columns(initial, list(range(cells_x)), cells_x, tiles)
+    own[...] = values
+    is_first = lax.axis_index("gy") == 0
+
+    @pl.when(is_first)
+    def _():
+        same[...] = values[tail : tail + far]
+        other[...] = values[head : head + far]
+
+    @pl.when(jnp.logical_not(is_first))
+    def _():
+        same[...] = values[head : head + far]
+        other[...] = values[tail : tail + far]
+
+
 class Stencil:
     def __init__(self, tiles, rows, width, viscosity, faces, thrust, start, beside):
         self.tiles, self.rows, self.width, self.beside = (tiles, rows, width, beside)
@@ -291,10 +360,12 @@
         self.bottom = row == 0
 
     def next_y(self, f):
-        return pltpu.roll(f, self.width - 1, 1)
+        half = self.width // 2
+        return jnp.concatenate([f[:, half:], pltpu.roll(f[:, :half], half - 1, 1)], axis=1)
 
     def last_y(self, f):
-        return pltpu.roll(f, 1, 1)
+        half = self.width // 2
+        return jnp.concatenate([pltpu.roll(f[:, half:], 1, 1), f[:, :half]], axis=1)
 
     def next_z(self, parts, t):
         if t < self.tiles - 1:
@@ -405,14 +476,21 @@
 
 def place_columns(start, runs_of):
     half = start.shape[-1] // 2
+    front = lax.broadcasted_iota(jnp.int32, start.shape[-2:-1] + (half,), 1) < half // 2
     core = lax.axis_index("gy")
     odd = lax.axis_index("gx") % 2
 
     def copy(side, parity):
         for first, here, there, begin, count in runs_of(side, parity):
             low, high = (here, there) if side == 0 else (there, here)
-            start[pl.ds(first, count), :, :, :, :half] = low[pl.ds(begin, count)]
-            start[pl.ds(first, count), :, :, :, half:] = high[pl.ds(begin, count)]
+            for n in range(count):
+                for c in range(start.shape[1]):
+                    for t in range(start.shape[2]):
+                        a, b = low[begin + n, c, t], high[begin + n, c, t]
+                        start[first + n, c, t, :, :half] = jnp.where(front, a, b)
+                        start[first + n, c, t, :, half:] = pltpu.roll(
+                            jnp.where(front, b, a), half // 2, 1
+                        )
 
     for side in range(2):
         for parity in range(2):
@@ -524,12 +602,14 @@
 
     origin = REACH - core * (REACH - 1)
     pairs = 3 * tiles // 2
+    front = lax.broadcasted_iota(jnp.int32, (rows, half), 1) < half // 2
     for x in range(share_x):
         for c in range(3):
             for t in range(tiles):
                 n = c * tiles + t
                 field = stage_c[origin + x, c, t]
-                low, high = field[:, :half], field[:, half:]
+                even, odd = field[:, :half], pltpu.roll(field[:, half:], half // 2, 1)
+                low, high = jnp.where(front, even, odd), jnp.where(front, odd, even)
                 spot = pl.ds((((n % 2) * share_x + x) * pairs + n // 2) * rows, rows)
                 columns_here[spot, :] = jnp.where(core == 0, low, high)
                 columns_there[spot, :] = jnp.where(core == 0, high, low)
@@ -596,14 +676,18 @@
     half = rows // 2
     low = lax.broadcasted_iota(jnp.int32, (rows, lanes), 0) < half
     is_first = lax.axis_index("gy") == 0
+    order = parting(lanes, inverse=True)
     for distance, block in enumerate(blocks):
         g = lax.axis_index("gx") ^ distance
+        merged = []
         for m in range(pairs):
             here, there = piece_here[g, m], piece_there[g, m]
             before = jnp.where(is_first, here, there)
             after = jnp.where(is_first, there, here)
-            block[2 * m] = jnp.where(low, before, pltpu.roll(after, half, 0))
-            block[2 * m + 1] = jnp.where(low, pltpu.roll(before, half, 0), after)
+            merged.append(jnp.where(low, before, pltpu.roll(after, half, 0)))
+            merged.append(jnp.where(low, pltpu.roll(before, half, 0), after))
+        values = reordered(jnp.concatenate(merged, axis=0), order)
+        block[...] = values.reshape(block.shape)
 
 
 def pencil_kernel(received, waves, table, packed):
@@ -722,6 +806,7 @@
     table_z = np.cos(np.outer(level, level) * (np.pi / levels))
     spread_z = np.kron(table_z, np.eye(lane_width))
     order = np.arange(levels).reshape(ROWS, levels // ROWS).T.reshape(levels)
+    parted = np.concatenate([every_y[::2], every_y[1::2]])
     backward = [
         np.concatenate([table_y[:, here], slope_y[:, here]], axis=1)
         for here in (slice(0, half), slice(half, total_y))
@@ -742,7 +827,7 @@
         jnp.asarray(t, jnp.float32)
         for t in (
             pencil,
-            table_y,
+            table_y[parted],
             np.stack(backward),
             table_z[:, order],
             waves,
@@ -792,17 +877,22 @@
     swap = [(0, 1), (1, 0)]
     straight = [(2 * i, 2 * j) for i, j in up] + [(2 * j + 1, 2 * i + 1) for i, j in up]
     crossed = [(2 * i + 1, 2 * j) for i, j in up] + [(2 * j, 2 * i + 1) for i, j in up]
-    own = jnp.transpose(initial.reshape(3, ROWS, share, cells_x, cells_y), (3, 0, 2, 1, 4))
-    even = place % 2 == 0
     pairs_across = [(i, i ^ 1) for i in range(groups)]
     pairs_around = [(i, (i - 1 if i % 2 == 0 else i + 1) % groups) for i in range(groups)]
-    upper = lax.dynamic_slice_in_dim(own, jnp.where(even, cells_x - near, 0), near, 0)
-    lower = lax.dynamic_slice_in_dim(own, jnp.where(even, 0, cells_x - near), near, 0)
+    f32 = jnp.float32
+    flat = initial.reshape(-1, cells_y)
+
+    def narrow(count):
+        return jax.ShapeDtypeStruct((count, 3, share, ROWS, cells_y), f32)
+
+    lower, upper = call(
+        functools.partial(pack_near_kernel, cells_x), [narrow(near)] * 2, [], flat
+    )
     around = lax.ppermute(lower, "gx", pairs_around)
     across = lax.ppermute(upper, "gx", pairs_across)
-    tail, head = cells_x - REACH, near
-    same = lax.dynamic_slice_in_dim(own, jnp.where(core == 0, tail, head), far, 0)
-    other = lax.dynamic_slice_in_dim(own, jnp.where(core == 0, head, tail), far, 0)
+    own, same, other = call(
+        pack_kernel, [narrow(cells_x), narrow(far), narrow(far)], [], flat
+    )
     own_there = lax.ppermute(own, "gy", swap)
     other, across = lax.optimization_barrier((other, across))
     far_there = lax.ppermute(other, ("gx", "gy"), crossed)
@@ -811,19 +901,18 @@
 
     strength = 2.0 * THRUST_COEFF * section.astype(jnp.float32)
     along_z = jnp.arange(levels).reshape(ROWS, share).T.reshape(levels)
+    along_y = jnp.arange(total_y).reshape(cells_y, 2).T.reshape(total_y)
 
     def thrust_on(offset, count):
         along_x = (place * cells_x + offset + jnp.arange(count) + total_x) % total_x
         weights = thrust_weights(
-            turbine_cells, along_x, jnp.arange(total_y), along_z, total_y, strength
+            turbine_cells, along_x, along_y, along_z, total_y, strength
         )
         return weights.reshape(count, share, ROWS, total_y)
 
     near_thrust = thrust_on(2 - near, cells_x + 2 * near - 4)
     far_thrust = thrust_on((2 - REACH) * (1 - core) + (share_x + 1) * core, far + near + share_x - 3)
-    same, near_thrust, far_thrust = lax.optimization_barrier((same, near_thrust, far_thrust))
     far_here = lax.ppermute(same, ("gx", "gy"), straight)
-    f32 = jnp.float32
     body = (3, share, ROWS, total_y)
 
     def columns(count):

time: 65.7 us -> 64.6 us (0.983)
  waiting for transfers between devices: 15.5 us -> 14.5 us
    ppermute x1, starting transfers between devices: 1.67 us -> 0.01 us  [paired_plan(): across_there = lax.ppermute(across, 'gy', swap)]
    ppermute x1, waiting for transfers between devices: 0.84 us -> 2.42 us  [paired_plan(): across = lax.ppermute(upper, 'gx', pairs_across)]
    ppermute x1, starting transfers between devices: 0.93 us -> 2.48 us  [paired_plan(): far_there = lax.ppermute(other, ('gx', 'gy'), crossed)]
    ppermute x1, waiting for transfers between devices: 1.54 us -> 0.01 us  [paired_plan(): far_here = lax.ppermute(same, ('gx', 'gy'), straight)]
    another operation x1 -> x0, local copies, waits for them, and re-layouts: 1.23 us -> none  [paired_plan(): initial.reshape(3, ROWS, share, cells_x, cells_y)]
    ppermute x1, waiting for transfers between devices: 1 us -> 0.01 us  [paired_plan(): across_there = lax.ppermute(across, 'gy', swap)]
    unnamed x21, local copies, waits for them, and re-layouts: 0.08 us -> 1.06 us
    ppermute x7, waiting for transfers between devices: 4.63 us -> 3.71 us  [paired_plan(): lax.ppermute(block, 'gx', [(i, i ^ d) for i in range(groups)])]
  transfers between devices with their start and end apart: 19 -> 19, of which waited for: 13 -> 12; matrix products, arithmetic and copies ran while one was open for 3% -> 4% of each run, Pallas kernels for 9% -> 9%
where the time goes in v6:
time: 64.6 us; the launch traced here: 64.2 us
  starting transfers between devices  32.7 us (51%)
  waiting for transfers between devices  14.5 us (22%)
  Pallas kernels  12.5 us (19%)
  local copies, waits for them, and re-layouts  2.25 us (3%)
  matrix products  1.13 us (2%)
  between operations  0.91 us (1%)
    pallas_call x8, Pallas kernels, call(): pl.pallas_call(kernel, out_shape=out_shapes, in_specs=in_specs, out_specs...  12.5 us
    ppermute x7, starting transfers between devices, paired_plan(): lax.ppermute(block, 'gx', [(i, i ^ d) for i in range(groups)])  11 us
    all_to_all x1, starting transfers between devices, paired_plan(): lax.all_to_all(spectra.reshape((4 * groups,) + spectra.shape[3:]), ('sec'...  5.42 us
    ppermute x7, waiting for transfers between devices, paired_plan(): lax.ppermute(block, 'gx', [(i, i ^ d) for i in range(groups)])  3.71 us
    ppermute x1, starting transfers between devices, paired_plan(): around = lax.ppermute(lower, 'gx', pairs_around)  3.6 us
    all_to_all x1, starting transfers between devices, paired_plan(): returned = lax.all_to_all(packed, 'gx', 0, 0, tiled=True)  3.39 us
    ppermute x1, starting transfers between devices, paired_plan(): upstream = lax.ppermute(leaving, 'sec', [(0, 1)])  3.37 us
    ppermute x1, starting transfers between devices, paired_plan(): across = lax.ppermute(upper, 'gx', pairs_across)  3.04 us
  transfers between devices with their start and end apart: 19, of which 12 were waited for; matrix products, arithmetic and copies ran while one was open for 4% of the time, Pallas kernels for 9%

profile of v6, /device:TPU:0, one launch (start us, length us, event | category | flops | bytes accessed | tf_op | source)
XLA Modules:
  0.0 64.2 jit_solution(17659703546102569185)
XLA Ops:
  0.6 0.0 copy-start
  0.6 1.0 %copy-done = f32[1,3,32,8,128]{4,3,2,1,0:T(8,128)S(1)} copy-done((f32[1,3,32,8,128]{4,3,2,1,0:T(8,128)S(1)}, f32[1,3,32,8,128]{4,3,2,1,0:T(8,128)}, u32[]{:S(2)}) %copy-start) | copy-done | bytes 393240
  1.6 0.3 shard_map.96
  2.0 3.0 %collective-permute-start.1 = (f32[3,3,4,8,128]{4,3,2,1,0:T(8,128)S(1)}, f32[3,3,4,8,128]{4,3,2,1,0:T(8,128)S(1)}, u32[]{:S(2)}, u32[]{:S(2)}) collective-permute-start(f32[3,3,4,8,128]{4,3,2,1,0:T(8,128)S(1)} %get-tuple-element.38), channel_id=1, source_target_pairs={{0,2},{2,0},{4,6},{6,4},{8,10},{10,8},{12,14},{14,12},{1,3},{3,1},... | collective-permute-start | bytes 442376 | tf_op jit(solution)/shard_map/ppermute | solution.py:892
  5.0 0.4 shard_map.95
  5.4 0.1 collective-permute-start
  5.5 3.6 %collective-permute-start.3 = (f32[3,3,4,8,128]{4,3,2,1,0:T(8,128)S(1)}, f32[3,3,4,8,128]{4,3,2,1,0:T(8,128)S(1)}, u32[]{:S(2)}, u32[]{:S(2)}) collective-permute-start(f32[3,3,4,8,128]{4,3,2,1,0:T(8,128)S(1)} %get-tuple-element.40), channel_id=1, source_target_pairs={{0,14},{2,4},{4,2},{6,8},{8,6},{10,12},{12,10},{14,0},{1,15},{3,5}... | collective-permute-start | bytes 442376 | tf_op jit(solution)/shard_map/ppermute | solution.py:891
  9.1 0.0 collective-permute-start.5
  9.1 0.8 %slice_bitcast_fusion.2 = (s32[64]{0:T(128)S(1)}, s32[64]{0:T(128)S(1)}, s32[64]{0:T(128)S(1)}) fusion(s32[64,3]{0,1:T(4,128)} %param.9), kind=kLoop, calls=%fused_computation.49 | loop fusion | bytes 1536 | tf_op jit(solution)/shard_map/eq | solution.py:854
  9.9 0.1 reshape.174
  10.0 0.1 fusion.12
  10.1 0.1 subtract_multiply_fusion
  10.2 0.6 fusion.2
  10.8 0.2 copy.14
  11.0 2.4 %collective-permute-done.1.across_here = f32[3,3,4,8,128]{4,3,2,1,0:T(8,128)S(1)} collective-permute-done((f32[3,3,4,8,128]{4,3,2,1,0:T(8,128)S(1)}, f32[3,3,4,8,128]{4,3,2,1,0:T(8,128)S(1)}, u32[]{:S(2)}, u32[]{:S(2)}) %collective-permute-start.1) | collective-permute-done | bytes 147488 | tf_op jit(solution)/shard_map/ppermute | solution.py:892
  13.4 0.0 collective-permute-start.2
  13.4 2.5 %collective-permute-start.6 = (f32[4,3,4,8,128]{4,3,2,1,0:T(8,128)S(1)}, f32[4,3,4,8,128]{4,3,2,1,0:T(8,128)S(1)}, u32[]{:S(2)}, u32[]{:S(2)}) collective-permute-start(f32[4,3,4,8,128]{4,3,2,1,0:T(8,128)S(1)} %get-tuple-element.42), channel_id=1, source_target_pairs={{1,2},{3,4},{5,6},{7,8},{9,10},{11,12},{13,14},{15,0},{2,1},{4,3},... | collective-permute-start | bytes 589832 | tf_op jit(solution)/shard_map/ppermute | solution.py:898
  15.9 0.0 collective-permute-done.3.around_here
  15.9 0.1 collective-permute-start.4
  16.0 0.6 fusion.3
  16.6 0.1 copy.15
  16.7 0.0 collective-permute-done.2.across_there
  16.7 0.6 collective-permute-done.4.around_there
  17.3 0.0 collective-permute-done.own_there
  17.3 3.1 %shard_map.97 = (f32[4,3,4,8,256]{4,3,2,1,0:T(8,128)S(1)}, f32[4,3,4,8,256]{4,3,2,1,0:T(8,128)S(1)}, f32[2,3,4,8,256]{4,3,2,1,0:T(8,128)S(1)}) custom-call(f32[8,3,4,8,128]{4,3,2,1,0:T(8,128)S(1)} %get-tuple-element.36.own_here, f32[8,3,4,8,128]{4,3,2,1,0:T(8,128)S(1)} %collective-permute-done.own_there, ...), custom_call_target="tpu_custom_call" | custom-call | tf_op jit(solution)/shard_map/pallas_call | solution.py:843
  20.4 0.0 collective-permute-done.5.far_here
  20.4 0.9 %collective-permute-done.6.far_there = f32[4,3,4,8,128]{4,3,2,1,0:T(8,128)S(1)} collective-permute-done((f32[4,3,4,8,128]{4,3,2,1,0:T(8,128)S(1)}, f32[4,3,4,8,128]{4,3,2,1,0:T(8,128)S(1)}, u32[]{:S(2)}, u32[]{:S(2)}) %collective-permute-start.6) | collective-permute-done | bytes 196640 | tf_op jit(solution)/shard_map/ppermute | solution.py:898
  21.3 0.0 copy-done.6
  21.3 3.2 %shard_map.98 = (f32[8,6,8,128]{3,2,1,0:T(8,128)S(1)}, f32[8,6,8,128]{3,2,1,0:T(8,128)S(1)}, f32[256,256]{1,0:T(8,128)S(1)}) custom-call(s32[2]{0:T(128)S(1)} %copy-done.6, f32[8,3,4,8,128]{4,3,2,1,0:T(8,128)S(1)} %get-tuple-element.36.own_here, f32[8,3,4,8,128]{4,3,2,1,0:T(8,128)S(1)} %collective-permute-done.own_there, ...), custom_call_target="tpu_custom_call" | custom-call | tf_op jit(solution)/shard_map/pallas_call | solution.py:843
  24.5 0.0 copy-start.1
  24.5 0.0 copy-start.4
  24.5 0.0 copy-done.3
  24.5 0.0 copy-done.5
  24.5 1.6 %shard_map.99 = f32[2,8,2,2,8,128]{5,4,3,2,1,0:T(8,128)} custom-call(f32[256,256]{1,0:T(8,128)S(1)} %get-tuple-element.46.source, f32[256,256]{1,0:T(8,128)S(1)} %copy-done.3, f32[32,32]{1,0:T(8,128)S(1)} %copy-done.5), custom_call_target="tpu_custom_call" | custom-call | tf_op jit(solution)/shard_map/pallas_call | solution.py:843
  26.1 5.4 %all-to-all-start = ((f32[32,2,8,128]{3,2,1,0:T(8,128)}), f32[32,2,8,128]{3,2,1,0:T(8,128)S(1)}, u32[]{:S(2)}, u32[]{:S(2)}) async-start(f32[32,2,8,128]{3,2,1,0:T(8,128)} %bitcast.9), calls=%async_computation | async-start | bytes 524288 | tf_op jit(solution)/shard_map/all_to_all | solution.py:974
  31.5 0.3 collective-permute-start.7
  31.9 1.2 %collective-permute-done.7.piece_there = f32[8,6,8,128]{3,2,1,0:T(8,128)S(1)} collective-permute-done((f32[8,6,8,128]{3,2,1,0:T(8,128)S(1)}, f32[8,6,8,128]{3,2,1,0:T(8,128)S(1)}, u32[]{:S(2)}, u32[]{:S(2)}) %collective-permute-start.7) | collective-permute-done | bytes 196640 | tf_op jit(solution)/shard_map/ppermute | solution.py:965
  33.0 0.3 shard_map.101
  33.4 2.7 %collective-permute-start.10 = (f32[12,8,128]{2,1,0:T(8,128)S(1)}, f32[12,8,128]{2,1,0:T(8,128)S(1)}, u32[]{:S(2)}, u32[]{:S(2)}) collective-permute-start(f32[12,8,128]{2,1,0:T(8,128)S(1)} %get-tuple-element.52), channel_id=1, source_target_pairs={{0,6},{2,4},{4,2},{6,0},{8,14},{10,12},{12,10},{14,8},{1,7},{3,5},... | collective-permute-start | bytes 147464 | tf_op jit(solution)/shard_map/ppermute | solution.py:985
  36.1 2.4 %collective-permute-start.11 = (f32[12,8,128]{2,1,0:T(8,128)S(1)}, f32[12,8,128]{2,1,0:T(8,128)S(1)}, u32[]{:S(2)}, u32[]{:S(2)}) collective-permute-start(f32[12,8,128]{2,1,0:T(8,128)S(1)} %get-tuple-element.53), channel_id=1, source_target_pairs={{0,8},{2,10},{4,12},{6,14},{8,0},{10,2},{12,4},{14,6},{1,9},{3,11}... | collective-permute-start | bytes 147464 | tf_op jit(solution)/shard_map/ppermute | solution.py:985
  38.6 0.5 collective-permute-start.12
  39.1 2.4 %collective-permute-start.13 = (f32[12,8,128]{2,1,0:T(8,128)S(1)}, f32[12,8,128]{2,1,0:T(8,128)S(1)}, u32[]{:S(2)}, u32[]{:S(2)}) collective-permute-start(f32[12,8,128]{2,1,0:T(8,128)S(1)} %get-tuple-element.55), channel_id=1, source_target_pairs={{0,12},{2,14},{4,8},{6,10},{8,4},{10,6},{12,0},{14,2},{1,13},{3,15... | collective-permute-start | bytes 147464 | tf_op jit(solution)/shard_map/ppermute | solution.py:985
  41.4 2.4 %collective-permute-start.14 = (f32[12,8,128]{2,1,0:T(8,128)S(1)}, f32[12,8,128]{2,1,0:T(8,128)S(1)}, u32[]{:S(2)}, u32[]{:S(2)}) collective-permute-start(f32[12,8,128]{2,1,0:T(8,128)S(1)} %get-tuple-element.56), channel_id=1, source_target_pairs={{0,14},{2,12},{4,10},{6,8},{8,6},{10,4},{12,2},{14,0},{1,15},{3,13... | collective-permute-start | bytes 147464 | tf_op jit(solution)/shard_map/ppermute | solution.py:985
  43.8 0.0 collective-permute-done.10
  43.8 0.6 collective-permute-start.8
  44.4 1.3 %collective-permute-done.11 = f32[12,8,128]{2,1,0:T(8,128)S(1)} collective-permute-done((f32[12,8,128]{2,1,0:T(8,128)S(1)}, f32[12,8,128]{2,1,0:T(8,128)S(1)}, u32[]{:S(2)}, u32[]{:S(2)}) %collective-permute-start.11) | collective-permute-done | bytes 49184 | tf_op jit(solution)/shard_map/ppermute | solution.py:985
  45.6 0.0 collective-permute-start.9
  45.6 0.0 all-to-all-done
  45.6 0.0 copy-done.1
  45.6 0.0 copy-start.2
  45.7 1.6 %shard_map.100 = f32[8,48,128]{2,1,0:T(8,128)} custom-call(f32[2,8,2,2,8,128]{5,4,3,2,1,0:T(8,128)S(1)} %bitcast.44, f32[8,2,4,128]{3,2,1,0:T(4,128)S(1)} %copy-done.4, f32[640,512]{1,0:T(8,128)S(1)} %copy-done.1), custom_call_target="tpu_custom_call" | custom-call | tf_op jit(solution)/shard_map/pallas_call | solution.py:843
  47.3 1.3 %collective-permute-done.12 = f32[12,8,128]{2,1,0:T(8,128)S(1)} collective-permute-done((f32[12,8,128]{2,1,0:T(8,128)S(1)}, f32[12,8,128]{2,1,0:T(8,128)S(1)}, u32[]{:S(2)}, u32[]{:S(2)}) %collective-permute-start.12) | collective-permute-done | bytes 49184 | tf_op jit(solution)/shard_map/ppermute | solution.py:985
  48.6 0.0 collective-permute-done.13
  48.6 0.1 collective-permute-done.14
  48.7 0.1 collective-permute-done.8
  48.8 0.9 %collective-permute-done.9 = f32[12,8,128]{2,1,0:T(8,128)S(1)} collective-permute-done((f32[12,8,128]{2,1,0:T(8,128)S(1)}, f32[12,8,128]{2,1,0:T(8,128)S(1)}, u32[]{:S(2)}, u32[]{:S(2)}) %collective-permute-start.9) | collective-permute-done | bytes 49184 | tf_op jit(solution)/shard_map/ppermute | solution.py:985
  49.7 3.4 %all-to-all-start.1 = ((f32[8,48,128]{2,1,0:T(8,128)}), f32[8,48,128]{2,1,0:T(8,128)S(1)}, u32[]{:S(2)}, u32[]{:S(2)}) async-start(f32[8,48,128]{2,1,0:T(8,128)} %shard_map.100), calls=%async_computation.1 | async-start | bytes 393216 | tf_op jit(solution)/shard_map/all_to_all | solution.py:1007
  53.3 3.4 %collective-permute-start.15 = (f32[2,12,8,128]{3,2,1,0:T(8,128)S(1)}, f32[2,12,8,128]{3,2,1,0:T(8,128)S(1)}, u32[]{:S(2)}, u32[]{:S(2)}) collective-permute-start(f32[2,12,8,128]{3,2,1,0:T(8,128)S(1)} %pad_maximum_fusion), channel_id=1, source_target_pairs={{0,16},{1,17},{2,18},{3,19},{4,20},{5,21},{6,22},{7,23},{8,24},{9,... | collective-permute-start | bytes 294920 | tf_op jit(solution)/shard_map/ppermute | solution.py:1006
  56.6 2.2 %collective-permute-done.15.upstream = f32[2,12,8,128]{3,2,1,0:T(8,128)S(1)} collective-permute-done((f32[2,12,8,128]{3,2,1,0:T(8,128)S(1)}, f32[2,12,8,128]{3,2,1,0:T(8,128)S(1)}, u32[]{:S(2)}, u32[]{:S(2)}) %collective-permute-start.15) | collective-permute-done | bytes 98336 | tf_op jit(solution)/shard_map/ppermute | solution.py:1006
  58.8 2.0 %all-to-all-done.1.received = f32[8,48,128]{2,1,0:T(8,128)S(1)} async-done(((f32[8,48,128]{2,1,0:T(8,128)}), f32[8,48,128]{2,1,0:T(8,128)S(1)}, u32[]{:S(2)}, u32[]{:S(2)}) %all-to-all-start.1) | async-done | bytes 196640 | tf_op jit(solution)/shard_map/all_to_all | solution.py:1007
  60.8 0.0 collective-permute-start.16
  60.8 1.4 %collective-permute-done.16.partner = f32[8,48,128]{2,1,0:T(8,128)S(1)} collective-permute-done((f32[8,48,128]{2,1,0:T(8,128)S(1)}, f32[8,48,128]{2,1,0:T(8,128)S(1)}, u32[]{:S(2)}, u32[]{:S(2)}) %collective-permute-start.16) | collective-permute-done | bytes 196640 | tf_op jit(solution)/shard_map/ppermute | solution.py:1009
  62.3 0.0 copy-done.2
  62.3 1.9 %shard_map.102 = (f32[3,4,64,128]{3,2,1,0:T(8,128)}, f32[4,64,128]{2,1,0:T(8,128)}) custom-call(s32[2]{0:T(128)S(1)} %copy-done.6, f32[8,48,128]{2,1,0:T(8,128)S(1)} %all-to-all-done.1.received, f32[8,48,128]{2,1,0:T(8,128)S(1)} %collective-permute-done.16.partner, f32[2,256,256]{2,1,0:T(8,128)S(1)} %copy-done.2, ...), custom_call_target="tpu_custom_call" | custom-call | tf_op jit(solution)/shard_map/pallas_call | solution.py:843
  (18 shorter events, 0.1 us)
Async XLA Ops:
  0.6 1.0 %copy-start = (f32[1,3,32,8,128]{4,3,2,1,0:T(8,128)S(1)}, f32[1,3,32,8,128]{4,3,2,1,0:T(8,128)}, u32[]{:S(2)}) copy-start(f32[1,3,32,8,128]{4,3,2,1,0:T(8,128)} %param.8) | copy-start | bytes 1179652
  2.0 11.5 %collective-permute-start.1 = (f32[3,3,4,8,128]{4,3,2,1,0:T(8,128)S(1)}, f32[3,3,4,8,128]{4,3,2,1,0:T(8,128)S(1)}, u32[]{:S(2)}, u32[]{:S(2)}) collective-permute-start(f32[3,3,4,8,128]{4,3,2,1,0:T(8,128)S(1)} %get-tuple-element.38), channel_id=1, source_target_pairs={{0,2},{2,0},{4,6},{6,4},{8,10},{10,8},{12,14},{14,12},{1,3},{3,1},... | collective-permute-start | bytes 442376 | tf_op jit(solution)/shard_map/ppermute | solution.py:892
  5.4 11.9 %collective-permute-start = (f32[8,3,4,8,128]{4,3,2,1,0:T(8,128)S(1)}, f32[8,3,4,8,128]{4,3,2,1,0:T(8,128)S(1)}, u32[]{:S(2)}, u32[]{:S(2)}) collective-permute-start(f32[8,3,4,8,128]{4,3,2,1,0:T(8,128)S(1)} %get-tuple-element.36.own_here), channel_id=1, source_target_pairs={{0,1},{1,0},{2,3},{3,2},{4,5},{5,4},{6,7},{7,6},{8,9},{9,8},{10,11... | collective-permute-start | bytes 1179656 | tf_op jit(solution)/shard_map/ppermute | solution.py:896
  5.5 10.4 %collective-permute-start.3 = (f32[3,3,4,8,128]{4,3,2,1,0:T(8,128)S(1)}, f32[3,3,4,8,128]{4,3,2,1,0:T(8,128)S(1)}, u32[]{:S(2)}, u32[]{:S(2)}) collective-permute-start(f32[3,3,4,8,128]{4,3,2,1,0:T(8,128)S(1)} %get-tuple-element.40), channel_id=1, source_target_pairs={{0,14},{2,4},{4,2},{6,8},{8,6},{10,12},{12,10},{14,0},{1,15},{3,5}... | collective-permute-start | bytes 442376 | tf_op jit(solution)/shard_map/ppermute | solution.py:891
  9.1 11.3 %collective-permute-start.5 = (f32[4,3,4,8,128]{4,3,2,1,0:T(8,128)S(1)}, f32[4,3,4,8,128]{4,3,2,1,0:T(8,128)S(1)}, u32[]{:S(2)}, u32[]{:S(2)}) collective-permute-start(f32[4,3,4,8,128]{4,3,2,1,0:T(8,128)S(1)} %get-tuple-element.41), channel_id=1, source_target_pairs={{0,2},{2,4},{4,6},{6,8},{8,10},{10,12},{12,14},{14,0},{3,1},{5,3},... | collective-permute-start | bytes 589832 | tf_op jit(solution)/shard_map/ppermute | solution.py:915
  13.4 3.2 %collective-permute-start.2 = (f32[3,3,4,8,128]{4,3,2,1,0:T(8,128)S(1)}, f32[3,3,4,8,128]{4,3,2,1,0:T(8,128)S(1)}, u32[]{:S(2)}, u32[]{:S(2)}) collective-permute-start(f32[3,3,4,8,128]{4,3,2,1,0:T(8,128)S(1)} %collective-permute-done.1.across_here), channel_id=1, source_target_pairs={{0,1},{1,0},{2,3},{3,2},{4,5},{5,4},{6,7},{7,6},{8,9},{9,8},{10,11... | collective-permute-start | bytes 442376 | tf_op jit(solution)/shard_map/ppermute | solution.py:899
  13.4 7.9 %collective-permute-start.6 = (f32[4,3,4,8,128]{4,3,2,1,0:T(8,128)S(1)}, f32[4,3,4,8,128]{4,3,2,1,0:T(8,128)S(1)}, u32[]{:S(2)}, u32[]{:S(2)}) collective-permute-start(f32[4,3,4,8,128]{4,3,2,1,0:T(8,128)S(1)} %get-tuple-element.42), channel_id=1, source_target_pairs={{1,2},{3,4},{5,6},{7,8},{9,10},{11,12},{13,14},{15,0},{2,1},{4,3},... | collective-permute-start | bytes 589832 | tf_op jit(solution)/shard_map/ppermute | solution.py:898
  15.9 1.4 %collective-permute-start.4 = (f32[3,3,4,8,128]{4,3,2,1,0:T(8,128)S(1)}, f32[3,3,4,8,128]{4,3,2,1,0:T(8,128)S(1)}, u32[]{:S(2)}, u32[]{:S(2)}) collective-permute-start(f32[3,3,4,8,128]{4,3,2,1,0:T(8,128)S(1)} %collective-permute-done.3.around_here), channel_id=1, source_target_pairs={{0,1},{1,0},{2,3},{3,2},{4,5},{5,4},{6,7},{7,6},{8,9},{9,8},{10,11... | collective-permute-start | bytes 442376 | tf_op jit(solution)/shard_map/ppermute | solution.py:900
  16.6 4.8 %copy-start.6 = (s32[2]{0:T(128)S(1)}, s32[2]{0:T(128)}, u32[]{:S(2)}) copy-start(s32[2]{0:T(128)} %fringe.3) | copy-start | bytes 28
  21.3 3.2 %copy-start.3 = (f32[256,256]{1,0:T(8,128)S(1)}, f32[256,256]{1,0:T(8,128)}, u32[]{:S(2)}) copy-start(f32[256,256]{1,0:T(8,128)} %constant.97.clone.table_y) | copy-start | bytes 786436
  21.3 3.2 %copy-start.5 = (f32[32,32]{1,0:T(8,128)S(1)}, f32[32,32]{1,0:T(8,128)}, u32[]{:S(2)}) copy-start(f32[32,32]{1,0:T(8,128)} %constant.99.clone.table_z) | copy-start | bytes 12292
  24.5 21.1 %copy-start.1 = (f32[640,512]{1,0:T(8,128)S(1)}, f32[640,512]{1,0:T(8,128)}, u32[]{:S(2)}) copy-start(f32[640,512]{1,0:T(8,128)} %constant.96.clone.table) | copy-start | bytes 3932164
  24.5 21.1 %copy-start.4 = (f32[8,2,4,128]{3,2,1,0:T(4,128)S(1)}, f32[8,2,4,128]{3,2,1,0:T(4,128)}, u32[]{:S(2)}) copy-start(f32[8,2,4,128]{3,2,1,0:T(4,128)} %constant.100.clone.waves) | copy-start | bytes 98308
  26.1 19.5 %all-to-all-start = ((f32[32,2,8,128]{3,2,1,0:T(8,128)}), f32[32,2,8,128]{3,2,1,0:T(8,128)S(1)}, u32[]{:S(2)}, u32[]{:S(2)}) async-start(f32[32,2,8,128]{3,2,1,0:T(8,128)} %bitcast.9), calls=%async_computation | async-start | bytes 524288 | tf_op jit(solution)/shard_map/all_to_all | solution.py:974
  31.5 1.5 %collective-permute-start.7 = (f32[8,6,8,128]{3,2,1,0:T(8,128)S(1)}, f32[8,6,8,128]{3,2,1,0:T(8,128)S(1)}, u32[]{:S(2)}, u32[]{:S(2)}) collective-permute-start(f32[8,6,8,128]{3,2,1,0:T(8,128)S(1)} %get-tuple-element.48), channel_id=1, source_target_pairs={{0,1},{1,0},{2,3},{3,2},{4,5},{5,4},{6,7},{7,6},{8,9},{9,8},{10,11... | collective-permute-start | bytes 589832 | tf_op jit(solution)/shard_map/ppermute | solution.py:965
  33.4 10.4 %collective-permute-start.10 = (f32[12,8,128]{2,1,0:T(8,128)S(1)}, f32[12,8,128]{2,1,0:T(8,128)S(1)}, u32[]{:S(2)}, u32[]{:S(2)}) collective-permute-start(f32[12,8,128]{2,1,0:T(8,128)S(1)} %get-tuple-element.52), channel_id=1, source_target_pairs={{0,6},{2,4},{4,2},{6,0},{8,14},{10,12},{12,10},{14,8},{1,7},{3,5},... | collective-permute-start | bytes 147464 | tf_op jit(solution)/shard_map/ppermute | solution.py:985
  36.1 9.5 %collective-permute-start.11 = (f32[12,8,128]{2,1,0:T(8,128)S(1)}, f32[12,8,128]{2,1,0:T(8,128)S(1)}, u32[]{:S(2)}, u32[]{:S(2)}) collective-permute-start(f32[12,8,128]{2,1,0:T(8,128)S(1)} %get-tuple-element.53), channel_id=1, source_target_pairs={{0,8},{2,10},{4,12},{6,14},{8,0},{10,2},{12,4},{14,6},{1,9},{3,11}... | collective-permute-start | bytes 147464 | tf_op jit(solution)/shard_map/ppermute | solution.py:985
  38.6 10.0 %collective-permute-start.12 = (f32[12,8,128]{2,1,0:T(8,128)S(1)}, f32[12,8,128]{2,1,0:T(8,128)S(1)}, u32[]{:S(2)}, u32[]{:S(2)}) collective-permute-start(f32[12,8,128]{2,1,0:T(8,128)S(1)} %get-tuple-element.54), channel_id=1, source_target_pairs={{0,10},{2,8},{4,14},{6,12},{8,2},{10,0},{12,6},{14,4},{1,11},{3,9}... | collective-permute-start | bytes 147464 | tf_op jit(solution)/shard_map/ppermute | solution.py:985
  39.1 9.5 %collective-permute-start.13 = (f32[12,8,128]{2,1,0:T(8,128)S(1)}, f32[12,8,128]{2,1,0:T(8,128)S(1)}, u32[]{:S(2)}, u32[]{:S(2)}) collective-permute-start(f32[12,8,128]{2,1,0:T(8,128)S(1)} %get-tuple-element.55), channel_id=1, source_target_pairs={{0,12},{2,14},{4,8},{6,10},{8,4},{10,6},{12,0},{14,2},{1,13},{3,15... | collective-permute-start | bytes 147464 | tf_op jit(solution)/shard_map/ppermute | solution.py:985
  41.4 7.2 %collective-permute-start.14 = (f32[12,8,128]{2,1,0:T(8,128)S(1)}, f32[12,8,128]{2,1,0:T(8,128)S(1)}, u32[]{:S(2)}, u32[]{:S(2)}) collective-permute-start(f32[12,8,128]{2,1,0:T(8,128)S(1)} %get-tuple-element.56), channel_id=1, source_target_pairs={{0,14},{2,12},{4,10},{6,8},{8,6},{10,4},{12,2},{14,0},{1,15},{3,13... | collective-permute-start | bytes 147464 | tf_op jit(solution)/shard_map/ppermute | solution.py:985
  43.8 5.0 %collective-permute-start.8 = (f32[12,8,128]{2,1,0:T(8,128)S(1)}, f32[12,8,128]{2,1,0:T(8,128)S(1)}, u32[]{:S(2)}, u32[]{:S(2)}) collective-permute-start(f32[12,8,128]{2,1,0:T(8,128)S(1)} %get-tuple-element.50), channel_id=1, source_target_pairs={{0,2},{2,0},{4,6},{6,4},{8,10},{10,8},{12,14},{14,12},{1,3},{3,1},... | collective-permute-start | bytes 147464 | tf_op jit(solution)/shard_map/ppermute | solution.py:985
  45.6 4.1 %collective-permute-start.9 = (f32[12,8,128]{2,1,0:T(8,128)S(1)}, f32[12,8,128]{2,1,0:T(8,128)S(1)}, u32[]{:S(2)}, u32[]{:S(2)}) collective-permute-start(f32[12,8,128]{2,1,0:T(8,128)S(1)} %get-tuple-element.51), channel_id=1, source_target_pairs={{0,4},{2,6},{4,0},{6,2},{8,12},{10,14},{12,8},{14,10},{1,5},{3,7},... | collective-permute-start | bytes 147464 | tf_op jit(solution)/shard_map/ppermute | solution.py:985
  45.6 16.6 %copy-start.2 = (f32[2,256,256]{2,1,0:T(8,128)S(1)}, f32[2,256,256]{2,1,0:T(8,128)}, u32[]{:S(2)}) copy-start(f32[2,256,256]{2,1,0:T(8,128)} %constant.98.clone.table_y) | copy-start | bytes 1572868
  49.7 11.1 %all-to-all-start.1 = ((f32[8,48,128]{2,1,0:T(8,128)}), f32[8,48,128]{2,1,0:T(8,128)S(1)}, u32[]{:S(2)}, u32[]{:S(2)}) async-start(f32[8,48,128]{2,1,0:T(8,128)} %shard_map.100), calls=%async_computation.1 | async-start | bytes 393216 | tf_op jit(solution)/shard_map/all_to_all | solution.py:1007
  53.3 5.6 %collective-permute-start.15 = (f32[2,12,8,128]{3,2,1,0:T(8,128)S(1)}, f32[2,12,8,128]{3,2,1,0:T(8,128)S(1)}, u32[]{:S(2)}, u32[]{:S(2)}) collective-permute-start(f32[2,12,8,128]{3,2,1,0:T(8,128)S(1)} %pad_maximum_fusion), channel_id=1, source_target_pairs={{0,16},{1,17},{2,18},{3,19},{4,20},{5,21},{6,22},{7,23},{8,24},{9,... | collective-permute-start | bytes 294920 | tf_op jit(solution)/shard_map/ppermute | solution.py:1006
  60.8 1.4 %collective-permute-start.16 = (f32[8,48,128]{2,1,0:T(8,128)S(1)}, f32[8,48,128]{2,1,0:T(8,128)S(1)}, u32[]{:S(2)}, u32[]{:S(2)}) collective-permute-start(f32[8,48,128]{2,1,0:T(8,128)S(1)} %all-to-all-done.1.received), channel_id=1, source_target_pairs={{0,1},{1,0},{2,3},{3,2},{4,5},{5,4},{6,7},{7,6},{8,9},{9,8},{10,11... | collective-permute-start | bytes 589832 | tf_op jit(solution)/shard_map/ppermute | solution.py:1009

commit v7 on v6

--- a/solution.py
+++ b/solution.py
@@ -994,7 +994,10 @@
         waves,
         pencil,
     )
-    packed, *moved = lax.optimization_barrier([packed] + moved)
+    tied = [3, 4, 5]
+    packed, *some = lax.optimization_barrier([packed] + [moved[d] for d in tied])
+    for d, block in zip(tied, some):
+        moved[d] = block
     moved = jnp.stack(moved)
     outlet = groups // 4
     leaving = jnp.stack(

time: 64.6 us -> 62.4 us (0.966)
  waiting for transfers between devices: 14.5 us -> 12 us
    ppermute x7, waiting for transfers between devices: 3.71 us -> 2.35 us  [paired_plan(): lax.ppermute(block, 'gx', [(i, i ^ d) for i in range(groups)])]
    all_to_all x1, starting transfers between devices: 5.42 us -> 4.13 us  [paired_plan(): lax.all_to_all(spectra.reshape((4 * groups,) + spectra.shape[3:]), ('sec'...]
    ppermute x1, waiting for transfers between devices: 1.19 us -> 0.01 us  [paired_plan(): piece_there = lax.ppermute(piece_send, 'gy', swap)]
    ppermute x1, starting transfers between devices: 0.32 us -> 1.47 us  [paired_plan(): piece_there = lax.ppermute(piece_send, 'gy', swap)]
  transfers between devices with their start and end apart: 19 -> 19, of which waited for: 12 -> 7; matrix products, arithmetic and copies ran while one was open for 4% -> 4% of each run, Pallas kernels for 9% -> 11%
where the time goes in v7:
time: 62.4 us; the launch traced here: 62 us
  starting transfers between devices  33 us (53%)
  Pallas kernels  12.5 us (20%)
  waiting for transfers between devices  12 us (19%)
  local copies, waits for them, and re-layouts  2.24 us (4%)
  matrix products  1.13 us (2%)
  between operations  0.9 us (1%)
    pallas_call x8, Pallas kernels, call(): pl.pallas_call(kernel, out_shape=out_shapes, in_specs=in_specs, out_specs...  12.5 us
    ppermute x7, starting transfers between devices, paired_plan(): lax.ppermute(block, 'gx', [(i, i ^ d) for i in range(groups)])  11.3 us
    all_to_all x1, starting transfers between devices, paired_plan(): lax.all_to_all(spectra.reshape((4 * groups,) + spectra.shape[3:]), ('sec'...  4.13 us
    ppermute x1, starting transfers between devices, paired_plan(): around = lax.ppermute(lower, 'gx', pairs_around)  3.6 us
    all_to_all x1, starting transfers between devices, paired_plan(): returned = lax.all_to_all(packed, 'gx', 0, 0, tiled=True)  3.52 us
    ppermute x1, starting transfers between devices, paired_plan(): upstream = lax.ppermute(leaving, 'sec', [(0, 1)])  3.38 us
    ppermute x1, starting transfers between devices, paired_plan(): across = lax.ppermute(upper, 'gx', pairs_across)  3.04 us
    ppermute x1, starting transfers between devices, paired_plan(): far_there = lax.ppermute(other, ('gx', 'gy'), crossed)  2.48 us
  transfers between devices with their start and end apart: 19, of which 7 were waited for; matrix products, arithmetic and copies ran while one was open for 4% of the time, Pallas kernels for 11%

profile of v7, /device:TPU:0, one launch (start us, length us, event | category | flops | bytes accessed | tf_op | source)
XLA Modules:
  0.0 62.0 jit_solution(7306536729360657657)
XLA Ops:
  0.6 0.0 copy-start
  0.6 1.0 %copy-done = f32[1,3,32,8,128]{4,3,2,1,0:T(8,128)S(1)} copy-done((f32[1,3,32,8,128]{4,3,2,1,0:T(8,128)S(1)}, f32[1,3,32,8,128]{4,3,2,1,0:T(8,128)}, u32[]{:S(2)}) %copy-start) | copy-done | bytes 393240
  1.6 0.3 shard_map.96
  2.0 3.0 %collective-permute-start.1 = (f32[3,3,4,8,128]{4,3,2,1,0:T(8,128)S(1)}, f32[3,3,4,8,128]{4,3,2,1,0:T(8,128)S(1)}, u32[]{:S(2)}, u32[]{:S(2)}) collective-permute-start(f32[3,3,4,8,128]{4,3,2,1,0:T(8,128)S(1)} %get-tuple-element.33), channel_id=1, source_target_pairs={{0,2},{2,0},{4,6},{6,4},{8,10},{10,8},{12,14},{14,12},{1,3},{3,1},... | collective-permute-start | bytes 442376 | tf_op jit(solution)/shard_map/ppermute | solution.py:892
  5.0 0.4 shard_map.95
  5.4 0.1 collective-permute-start
  5.5 3.6 %collective-permute-start.3 = (f32[3,3,4,8,128]{4,3,2,1,0:T(8,128)S(1)}, f32[3,3,4,8,128]{4,3,2,1,0:T(8,128)S(1)}, u32[]{:S(2)}, u32[]{:S(2)}) collective-permute-start(f32[3,3,4,8,128]{4,3,2,1,0:T(8,128)S(1)} %get-tuple-element.35), channel_id=1, source_target_pairs={{0,14},{2,4},{4,2},{6,8},{8,6},{10,12},{12,10},{14,0},{1,15},{3,5}... | collective-permute-start | bytes 442376 | tf_op jit(solution)/shard_map/ppermute | solution.py:891
  9.1 0.0 collective-permute-start.5
  9.1 0.8 %slice_bitcast_fusion.2 = (s32[64]{0:T(128)S(1)}, s32[64]{0:T(128)S(1)}, s32[64]{0:T(128)S(1)}) fusion(s32[64,3]{0,1:T(4,128)} %param.9), kind=kLoop, calls=%fused_computation.49 | loop fusion | bytes 1536 | tf_op jit(solution)/shard_map/eq | solution.py:854
  9.9 0.1 reshape.174
  10.0 0.1 fusion.12
  10.1 0.1 subtract_multiply_fusion
  10.2 0.6 fusion.2
  10.8 0.2 copy.14
  11.0 2.4 %collective-permute-done.1.across_here = f32[3,3,4,8,128]{4,3,2,1,0:T(8,128)S(1)} collective-permute-done((f32[3,3,4,8,128]{4,3,2,1,0:T(8,128)S(1)}, f32[3,3,4,8,128]{4,3,2,1,0:T(8,128)S(1)}, u32[]{:S(2)}, u32[]{:S(2)}) %collective-permute-start.1) | collective-permute-done | bytes 147488 | tf_op jit(solution)/shard_map/ppermute | solution.py:892
  13.4 0.0 collective-permute-start.2
  13.4 2.5 %collective-permute-start.6 = (f32[4,3,4,8,128]{4,3,2,1,0:T(8,128)S(1)}, f32[4,3,4,8,128]{4,3,2,1,0:T(8,128)S(1)}, u32[]{:S(2)}, u32[]{:S(2)}) collective-permute-start(f32[4,3,4,8,128]{4,3,2,1,0:T(8,128)S(1)} %get-tuple-element.37), channel_id=1, source_target_pairs={{1,2},{3,4},{5,6},{7,8},{9,10},{11,12},{13,14},{15,0},{2,1},{4,3},... | collective-permute-start | bytes 589832 | tf_op jit(solution)/shard_map/ppermute | solution.py:898
  15.9 0.0 collective-permute-done.3.around_here
  15.9 0.1 collective-permute-start.4
  16.0 0.6 fusion.3
  16.6 0.1 copy.15
  16.7 0.0 collective-permute-done.2.across_there
  16.7 0.6 collective-permute-done.4.around_there
  17.3 0.0 collective-permute-done.own_there
  17.3 3.1 %shard_map.97 = (f32[4,3,4,8,256]{4,3,2,1,0:T(8,128)S(1)}, f32[4,3,4,8,256]{4,3,2,1,0:T(8,128)S(1)}, f32[2,3,4,8,256]{4,3,2,1,0:T(8,128)S(1)}) custom-call(f32[8,3,4,8,128]{4,3,2,1,0:T(8,128)S(1)} %get-tuple-element.31.own_here, f32[8,3,4,8,128]{4,3,2,1,0:T(8,128)S(1)} %collective-permute-done.own_there, ...), custom_call_target="tpu_custom_call" | custom-call | tf_op jit(solution)/shard_map/pallas_call | solution.py:843
  20.4 0.0 collective-permute-done.5.far_here
  20.4 0.9 %collective-permute-done.6.far_there = f32[4,3,4,8,128]{4,3,2,1,0:T(8,128)S(1)} collective-permute-done((f32[4,3,4,8,128]{4,3,2,1,0:T(8,128)S(1)}, f32[4,3,4,8,128]{4,3,2,1,0:T(8,128)S(1)}, u32[]{:S(2)}, u32[]{:S(2)}) %collective-permute-start.6) | collective-permute-done | bytes 196640 | tf_op jit(solution)/shard_map/ppermute | solution.py:898
  21.3 0.0 copy-done.6
  21.3 3.2 %shard_map.98 = (f32[8,6,8,128]{3,2,1,0:T(8,128)S(1)}, f32[8,6,8,128]{3,2,1,0:T(8,128)S(1)}, f32[256,256]{1,0:T(8,128)S(1)}) custom-call(s32[2]{0:T(128)S(1)} %copy-done.6, f32[8,3,4,8,128]{4,3,2,1,0:T(8,128)S(1)} %get-tuple-element.31.own_here, f32[8,3,4,8,128]{4,3,2,1,0:T(8,128)S(1)} %collective-permute-done.own_there, ...), custom_call_target="tpu_custom_call" | custom-call | tf_op jit(solution)/shard_map/pallas_call | solution.py:843
  24.5 0.0 copy-start.1
  24.5 0.0 copy-start.4
  24.5 1.5 %collective-permute-start.7 = (f32[8,6,8,128]{3,2,1,0:T(8,128)S(1)}, f32[8,6,8,128]{3,2,1,0:T(8,128)S(1)}, u32[]{:S(2)}, u32[]{:S(2)}) collective-permute-start(f32[8,6,8,128]{3,2,1,0:T(8,128)S(1)} %get-tuple-element.43), channel_id=1, source_target_pairs={{0,1},{1,0},{2,3},{3,2},{4,5},{5,4},{6,7},{7,6},{8,9},{9,8},{10,11... | collective-permute-start | bytes 589832 | tf_op jit(solution)/shard_map/ppermute | solution.py:965
  26.0 0.0 copy-done.3
  26.0 0.0 copy-done.5
  26.0 1.6 %shard_map.99 = f32[2,8,2,2,8,128]{5,4,3,2,1,0:T(8,128)} custom-call(f32[256,256]{1,0:T(8,128)S(1)} %get-tuple-element.41.source, f32[256,256]{1,0:T(8,128)S(1)} %copy-done.3, f32[32,32]{1,0:T(8,128)S(1)} %copy-done.5), custom_call_target="tpu_custom_call" | custom-call | tf_op jit(solution)/shard_map/pallas_call | solution.py:843
  27.6 4.1 %all-to-all-start = ((f32[32,2,8,128]{3,2,1,0:T(8,128)}), f32[32,2,8,128]{3,2,1,0:T(8,128)S(1)}, u32[]{:S(2)}, u32[]{:S(2)}) async-start(f32[32,2,8,128]{3,2,1,0:T(8,128)} %bitcast.9), calls=%async_computation | async-start | bytes 524288 | tf_op jit(solution)/shard_map/all_to_all | solution.py:974
  31.7 0.0 collective-permute-done.7.piece_there
  31.7 0.3 shard_map.101
  32.1 1.8 %collective-permute-start.11 = (f32[12,8,128]{2,1,0:T(8,128)S(1)}, f32[12,8,128]{2,1,0:T(8,128)S(1)}, u32[]{:S(2)}, u32[]{:S(2)}) collective-permute-start(f32[12,8,128]{2,1,0:T(8,128)S(1)} %get-tuple-element.49), channel_id=1, source_target_pairs={{0,2},{2,0},{4,6},{6,4},{8,10},{10,8},{12,14},{14,12},{1,3},{3,1},... | collective-permute-start | bytes 147464 | tf_op jit(solution)/shard_map/ppermute | solution.py:985
  33.9 1.5 %collective-permute-start.12 = (f32[12,8,128]{2,1,0:T(8,128)S(1)}, f32[12,8,128]{2,1,0:T(8,128)S(1)}, u32[]{:S(2)}, u32[]{:S(2)}) collective-permute-start(f32[12,8,128]{2,1,0:T(8,128)S(1)} %get-tuple-element.50), channel_id=1, source_target_pairs={{0,4},{2,6},{4,0},{6,2},{8,12},{10,14},{12,8},{14,10},{1,5},{3,7},... | collective-permute-start | bytes 147464 | tf_op jit(solution)/shard_map/ppermute | solution.py:985
  35.4 2.4 %collective-permute-start.10 = (f32[12,8,128]{2,1,0:T(8,128)S(1)}, f32[12,8,128]{2,1,0:T(8,128)S(1)}, u32[]{:S(2)}, u32[]{:S(2)}) collective-permute-start(f32[12,8,128]{2,1,0:T(8,128)S(1)} %get-tuple-element.46), channel_id=1, source_target_pairs={{0,10},{2,8},{4,14},{6,12},{8,2},{10,0},{12,6},{14,4},{1,11},{3,9}... | collective-permute-start | bytes 147464 | tf_op jit(solution)/shard_map/ppermute | solution.py:985
  37.8 1.4 %collective-permute-start.8 = (f32[12,8,128]{2,1,0:T(8,128)S(1)}, f32[12,8,128]{2,1,0:T(8,128)S(1)}, u32[]{:S(2)}, u32[]{:S(2)}) collective-permute-start(f32[12,8,128]{2,1,0:T(8,128)S(1)} %get-tuple-element.44), channel_id=1, source_target_pairs={{0,6},{2,4},{4,2},{6,0},{8,14},{10,12},{12,10},{14,8},{1,7},{3,5},... | collective-permute-start | bytes 147464 | tf_op jit(solution)/shard_map/ppermute | solution.py:985
  39.2 0.5 collective-permute-start.9
  39.8 0.0 collective-permute-done.11
  39.8 3.3 %collective-permute-start.13 = (f32[12,8,128]{2,1,0:T(8,128)S(1)}, f32[12,8,128]{2,1,0:T(8,128)S(1)}, u32[]{:S(2)}, u32[]{:S(2)}) collective-permute-start(f32[12,8,128]{2,1,0:T(8,128)S(1)} %get-tuple-element.54), channel_id=1, source_target_pairs={{0,12},{2,14},{4,8},{6,10},{8,4},{10,6},{12,0},{14,2},{1,13},{3,15... | collective-permute-start | bytes 147464 | tf_op jit(solution)/shard_map/ppermute | solution.py:985
  43.1 0.0 collective-permute-done.12
  43.1 0.2 collective-permute-start.14
  43.4 0.0 all-to-all-done
  43.4 0.0 copy-done.1
  43.4 0.0 copy-done.4
  43.4 0.0 copy-start.2
  43.4 1.6 %shard_map.100 = f32[8,48,128]{2,1,0:T(8,128)} custom-call(f32[2,8,2,2,8,128]{5,4,3,2,1,0:T(8,128)S(1)} %bitcast.44, f32[8,2,4,128]{3,2,1,0:T(4,128)S(1)} %copy-done.4, f32[640,512]{1,0:T(8,128)S(1)} %copy-done.1), custom_call_target="tpu_custom_call" | custom-call | tf_op jit(solution)/shard_map/pallas_call | solution.py:843
  45.0 0.0 collective-permute-done.10
  45.0 0.0 collective-permute-done.8
  45.0 2.3 %collective-permute-done.9 = f32[12,8,128]{2,1,0:T(8,128)S(1)} collective-permute-done((f32[12,8,128]{2,1,0:T(8,128)S(1)}, f32[12,8,128]{2,1,0:T(8,128)S(1)}, u32[]{:S(2)}, u32[]{:S(2)}) %collective-permute-start.9) | collective-permute-done | bytes 49184 | tf_op jit(solution)/shard_map/ppermute | solution.py:985
  47.4 3.5 %all-to-all-start.1 = ((f32[8,48,128]{2,1,0:T(8,128)}), f32[8,48,128]{2,1,0:T(8,128)S(1)}, u32[]{:S(2)}, u32[]{:S(2)}) async-start(f32[8,48,128]{2,1,0:T(8,128)} %shard_map.100), calls=%async_computation.1 | async-start | bytes 393216 | tf_op jit(solution)/shard_map/all_to_all | solution.py:1010
  50.9 0.0 collective-permute-done.13
  50.9 0.0 collective-permute-done.14
  51.0 3.4 %collective-permute-start.15 = (f32[2,12,8,128]{3,2,1,0:T(8,128)S(1)}, f32[2,12,8,128]{3,2,1,0:T(8,128)S(1)}, u32[]{:S(2)}, u32[]{:S(2)}) collective-permute-start(f32[2,12,8,128]{3,2,1,0:T(8,128)S(1)} %pad_maximum_fusion), channel_id=1, source_target_pairs={{0,16},{1,17},{2,18},{3,19},{4,20},{5,21},{6,22},{7,23},{8,24},{9,... | collective-permute-start | bytes 294920 | tf_op jit(solution)/shard_map/ppermute | solution.py:1009
  54.4 2.2 %collective-permute-done.15.upstream = f32[2,12,8,128]{3,2,1,0:T(8,128)S(1)} collective-permute-done((f32[2,12,8,128]{3,2,1,0:T(8,128)S(1)}, f32[2,12,8,128]{3,2,1,0:T(8,128)S(1)}, u32[]{:S(2)}, u32[]{:S(2)}) %collective-permute-start.15) | collective-permute-done | bytes 98336 | tf_op jit(solution)/shard_map/ppermute | solution.py:1009
  56.6 2.1 %all-to-all-done.1.received = f32[8,48,128]{2,1,0:T(8,128)S(1)} async-done(((f32[8,48,128]{2,1,0:T(8,128)}), f32[8,48,128]{2,1,0:T(8,128)S(1)}, u32[]{:S(2)}, u32[]{:S(2)}) %all-to-all-start.1) | async-done | bytes 196640 | tf_op jit(solution)/shard_map/all_to_all | solution.py:1010
  58.7 0.0 collective-permute-start.16
  58.7 1.4 %collective-permute-done.16.partner = f32[8,48,128]{2,1,0:T(8,128)S(1)} collective-permute-done((f32[8,48,128]{2,1,0:T(8,128)S(1)}, f32[8,48,128]{2,1,0:T(8,128)S(1)}, u32[]{:S(2)}, u32[]{:S(2)}) %collective-permute-start.16) | collective-permute-done | bytes 196640 | tf_op jit(solution)/shard_map/ppermute | solution.py:1012
  60.1 1.9 %shard_map.102 = (f32[3,4,64,128]{3,2,1,0:T(8,128)}, f32[4,64,128]{2,1,0:T(8,128)}) custom-call(s32[2]{0:T(128)S(1)} %copy-done.6, f32[8,48,128]{2,1,0:T(8,128)S(1)} %all-to-all-done.1.received, f32[8,48,128]{2,1,0:T(8,128)S(1)} %collective-permute-done.16.partner, f32[2,256,256]{2,1,0:T(8,128)S(1)} %copy-done.2, ...), custom_call_target="tpu_custom_call" | custom-call | tf_op jit(solution)/shard_map/pallas_call | solution.py:843
  (18 shorter events, 0.1 us)
Async XLA Ops:
  0.6 1.0 %copy-start = (f32[1,3,32,8,128]{4,3,2,1,0:T(8,128)S(1)}, f32[1,3,32,8,128]{4,3,2,1,0:T(8,128)}, u32[]{:S(2)}) copy-start(f32[1,3,32,8,128]{4,3,2,1,0:T(8,128)} %param.8) | copy-start | bytes 1179652
  2.0 11.5 %collective-permute-start.1 = (f32[3,3,4,8,128]{4,3,2,1,0:T(8,128)S(1)}, f32[3,3,4,8,128]{4,3,2,1,0:T(8,128)S(1)}, u32[]{:S(2)}, u32[]{:S(2)}) collective-permute-start(f32[3,3,4,8,128]{4,3,2,1,0:T(8,128)S(1)} %get-tuple-element.33), channel_id=1, source_target_pairs={{0,2},{2,0},{4,6},{6,4},{8,10},{10,8},{12,14},{14,12},{1,3},{3,1},... | collective-permute-start | bytes 442376 | tf_op jit(solution)/shard_map/ppermute | solution.py:892
  5.4 11.9 %collective-permute-start = (f32[8,3,4,8,128]{4,3,2,1,0:T(8,128)S(1)}, f32[8,3,4,8,128]{4,3,2,1,0:T(8,128)S(1)}, u32[]{:S(2)}, u32[]{:S(2)}) collective-permute-start(f32[8,3,4,8,128]{4,3,2,1,0:T(8,128)S(1)} %get-tuple-element.31.own_here), channel_id=1, source_target_pairs={{0,1},{1,0},{2,3},{3,2},{4,5},{5,4},{6,7},{7,6},{8,9},{9,8},{10,11... | collective-permute-start | bytes 1179656 | tf_op jit(solution)/shard_map/ppermute | solution.py:896
  5.5 10.4 %collective-permute-start.3 = (f32[3,3,4,8,128]{4,3,2,1,0:T(8,128)S(1)}, f32[3,3,4,8,128]{4,3,2,1,0:T(8,128)S(1)}, u32[]{:S(2)}, u32[]{:S(2)}) collective-permute-start(f32[3,3,4,8,128]{4,3,2,1,0:T(8,128)S(1)} %get-tuple-element.35), channel_id=1, source_target_pairs={{0,14},{2,4},{4,2},{6,8},{8,6},{10,12},{12,10},{14,0},{1,15},{3,5}... | collective-permute-start | bytes 442376 | tf_op jit(solution)/shard_map/ppermute | solution.py:891
  9.1 11.3 %collective-permute-start.5 = (f32[4,3,4,8,128]{4,3,2,1,0:T(8,128)S(1)}, f32[4,3,4,8,128]{4,3,2,1,0:T(8,128)S(1)}, u32[]{:S(2)}, u32[]{:S(2)}) collective-permute-start(f32[4,3,4,8,128]{4,3,2,1,0:T(8,128)S(1)} %get-tuple-element.36), channel_id=1, source_target_pairs={{0,2},{2,4},{4,6},{6,8},{8,10},{10,12},{12,14},{14,0},{3,1},{5,3},... | collective-permute-start | bytes 589832 | tf_op jit(solution)/shard_map/ppermute | solution.py:915
  13.4 3.2 %collective-permute-start.2 = (f32[3,3,4,8,128]{4,3,2,1,0:T(8,128)S(1)}, f32[3,3,4,8,128]{4,3,2,1,0:T(8,128)S(1)}, u32[]{:S(2)}, u32[]{:S(2)}) collective-permute-start(f32[3,3,4,8,128]{4,3,2,1,0:T(8,128)S(1)} %collective-permute-done.1.across_here), channel_id=1, source_target_pairs={{0,1},{1,0},{2,3},{3,2},{4,5},{5,4},{6,7},{7,6},{8,9},{9,8},{10,11... | collective-permute-start | bytes 442376 | tf_op jit(solution)/shard_map/ppermute | solution.py:899
  13.4 7.9 %collective-permute-start.6 = (f32[4,3,4,8,128]{4,3,2,1,0:T(8,128)S(1)}, f32[4,3,4,8,128]{4,3,2,1,0:T(8,128)S(1)}, u32[]{:S(2)}, u32[]{:S(2)}) collective-permute-start(f32[4,3,4,8,128]{4,3,2,1,0:T(8,128)S(1)} %get-tuple-element.37), channel_id=1, source_target_pairs={{1,2},{3,4},{5,6},{7,8},{9,10},{11,12},{13,14},{15,0},{2,1},{4,3},... | collective-permute-start | bytes 589832 | tf_op jit(solution)/shard_map/ppermute | solution.py:898
  15.9 1.4 %collective-permute-start.4 = (f32[3,3,4,8,128]{4,3,2,1,0:T(8,128)S(1)}, f32[3,3,4,8,128]{4,3,2,1,0:T(8,128)S(1)}, u32[]{:S(2)}, u32[]{:S(2)}) collective-permute-start(f32[3,3,4,8,128]{4,3,2,1,0:T(8,128)S(1)} %collective-permute-done.3.around_here), channel_id=1, source_target_pairs={{0,1},{1,0},{2,3},{3,2},{4,5},{5,4},{6,7},{7,6},{8,9},{9,8},{10,11... | collective-permute-start | bytes 442376 | tf_op jit(solution)/shard_map/ppermute | solution.py:900
  16.6 4.8 %copy-start.6 = (s32[2]{0:T(128)S(1)}, s32[2]{0:T(128)}, u32[]{:S(2)}) copy-start(s32[2]{0:T(128)} %fringe.3) | copy-start | bytes 28
  21.3 4.7 %copy-start.3 = (f32[256,256]{1,0:T(8,128)S(1)}, f32[256,256]{1,0:T(8,128)}, u32[]{:S(2)}) copy-start(f32[256,256]{1,0:T(8,128)} %constant.97.clone.table_y) | copy-start | bytes 786436
  21.3 4.7 %copy-start.5 = (f32[32,32]{1,0:T(8,128)S(1)}, f32[32,32]{1,0:T(8,128)}, u32[]{:S(2)}) copy-start(f32[32,32]{1,0:T(8,128)} %constant.99.clone.table_z) | copy-start | bytes 12292
  24.5 18.9 %copy-start.1 = (f32[640,512]{1,0:T(8,128)S(1)}, f32[640,512]{1,0:T(8,128)}, u32[]{:S(2)}) copy-start(f32[640,512]{1,0:T(8,128)} %constant.96.clone.table) | copy-start | bytes 3932164
  24.5 18.9 %copy-start.4 = (f32[8,2,4,128]{3,2,1,0:T(4,128)S(1)}, f32[8,2,4,128]{3,2,1,0:T(4,128)}, u32[]{:S(2)}) copy-start(f32[8,2,4,128]{3,2,1,0:T(4,128)} %constant.100.clone.waves) | copy-start | bytes 98308
  24.5 7.2 %collective-permute-start.7 = (f32[8,6,8,128]{3,2,1,0:T(8,128)S(1)}, f32[8,6,8,128]{3,2,1,0:T(8,128)S(1)}, u32[]{:S(2)}, u32[]{:S(2)}) collective-permute-start(f32[8,6,8,128]{3,2,1,0:T(8,128)S(1)} %get-tuple-element.43), channel_id=1, source_target_pairs={{0,1},{1,0},{2,3},{3,2},{4,5},{5,4},{6,7},{7,6},{8,9},{9,8},{10,11... | collective-permute-start | bytes 589832 | tf_op jit(solution)/shard_map/ppermute | solution.py:965
  27.6 15.8 %all-to-all-start = ((f32[32,2,8,128]{3,2,1,0:T(8,128)}), f32[32,2,8,128]{3,2,1,0:T(8,128)S(1)}, u32[]{:S(2)}, u32[]{:S(2)}) async-start(f32[32,2,8,128]{3,2,1,0:T(8,128)} %bitcast.9), calls=%async_computation | async-start | bytes 524288 | tf_op jit(solution)/shard_map/all_to_all | solution.py:974
  32.1 7.7 %collective-permute-start.11 = (f32[12,8,128]{2,1,0:T(8,128)S(1)}, f32[12,8,128]{2,1,0:T(8,128)S(1)}, u32[]{:S(2)}, u32[]{:S(2)}) collective-permute-start(f32[12,8,128]{2,1,0:T(8,128)S(1)} %get-tuple-element.49), channel_id=1, source_target_pairs={{0,2},{2,0},{4,6},{6,4},{8,10},{10,8},{12,14},{14,12},{1,3},{3,1},... | collective-permute-start | bytes 147464 | tf_op jit(solution)/shard_map/ppermute | solution.py:985
  33.9 9.2 %collective-permute-start.12 = (f32[12,8,128]{2,1,0:T(8,128)S(1)}, f32[12,8,128]{2,1,0:T(8,128)S(1)}, u32[]{:S(2)}, u32[]{:S(2)}) collective-permute-start(f32[12,8,128]{2,1,0:T(8,128)S(1)} %get-tuple-element.50), channel_id=1, source_target_pairs={{0,4},{2,6},{4,0},{6,2},{8,12},{10,14},{12,8},{14,10},{1,5},{3,7},... | collective-permute-start | bytes 147464 | tf_op jit(solution)/shard_map/ppermute | solution.py:985
  35.4 9.6 %collective-permute-start.10 = (f32[12,8,128]{2,1,0:T(8,128)S(1)}, f32[12,8,128]{2,1,0:T(8,128)S(1)}, u32[]{:S(2)}, u32[]{:S(2)}) collective-permute-start(f32[12,8,128]{2,1,0:T(8,128)S(1)} %get-tuple-element.46), channel_id=1, source_target_pairs={{0,10},{2,8},{4,14},{6,12},{8,2},{10,0},{12,6},{14,4},{1,11},{3,9}... | collective-permute-start | bytes 147464 | tf_op jit(solution)/shard_map/ppermute | solution.py:985
  37.8 7.2 %collective-permute-start.8 = (f32[12,8,128]{2,1,0:T(8,128)S(1)}, f32[12,8,128]{2,1,0:T(8,128)S(1)}, u32[]{:S(2)}, u32[]{:S(2)}) collective-permute-start(f32[12,8,128]{2,1,0:T(8,128)S(1)} %get-tuple-element.44), channel_id=1, source_target_pairs={{0,6},{2,4},{4,2},{6,0},{8,14},{10,12},{12,10},{14,8},{1,7},{3,5},... | collective-permute-start | bytes 147464 | tf_op jit(solution)/shard_map/ppermute | solution.py:985
  39.2 8.1 %collective-permute-start.9 = (f32[12,8,128]{2,1,0:T(8,128)S(1)}, f32[12,8,128]{2,1,0:T(8,128)S(1)}, u32[]{:S(2)}, u32[]{:S(2)}) collective-permute-start(f32[12,8,128]{2,1,0:T(8,128)S(1)} %get-tuple-element.45), channel_id=1, source_target_pairs={{0,8},{2,10},{4,12},{6,14},{8,0},{10,2},{12,4},{14,6},{1,9},{3,11}... | collective-permute-start | bytes 147464 | tf_op jit(solution)/shard_map/ppermute | solution.py:985
  39.8 11.1 %collective-permute-start.13 = (f32[12,8,128]{2,1,0:T(8,128)S(1)}, f32[12,8,128]{2,1,0:T(8,128)S(1)}, u32[]{:S(2)}, u32[]{:S(2)}) collective-permute-start(f32[12,8,128]{2,1,0:T(8,128)S(1)} %get-tuple-element.54), channel_id=1, source_target_pairs={{0,12},{2,14},{4,8},{6,10},{8,4},{10,6},{12,0},{14,2},{1,13},{3,15... | collective-permute-start | bytes 147464 | tf_op jit(solution)/shard_map/ppermute | solution.py:985
  43.1 7.8 %collective-permute-start.14 = (f32[12,8,128]{2,1,0:T(8,128)S(1)}, f32[12,8,128]{2,1,0:T(8,128)S(1)}, u32[]{:S(2)}, u32[]{:S(2)}) collective-permute-start(f32[12,8,128]{2,1,0:T(8,128)S(1)} %get-tuple-element.55), channel_id=1, source_target_pairs={{0,14},{2,12},{4,10},{6,8},{8,6},{10,4},{12,2},{14,0},{1,15},{3,13... | collective-permute-start | bytes 147464 | tf_op jit(solution)/shard_map/ppermute | solution.py:985
  43.4 16.7 %copy-start.2 = (f32[2,256,256]{2,1,0:T(8,128)S(1)}, f32[2,256,256]{2,1,0:T(8,128)}, u32[]{:S(2)}) copy-start(f32[2,256,256]{2,1,0:T(8,128)} %constant.98.clone.table_y) | copy-start | bytes 1572868
  47.4 11.3 %all-to-all-start.1 = ((f32[8,48,128]{2,1,0:T(8,128)}), f32[8,48,128]{2,1,0:T(8,128)S(1)}, u32[]{:S(2)}, u32[]{:S(2)}) async-start(f32[8,48,128]{2,1,0:T(8,128)} %shard_map.100), calls=%async_computation.1 | async-start | bytes 393216 | tf_op jit(solution)/shard_map/all_to_all | solution.py:1010
  51.0 5.6 %collective-permute-start.15 = (f32[2,12,8,128]{3,2,1,0:T(8,128)S(1)}, f32[2,12,8,128]{3,2,1,0:T(8,128)S(1)}, u32[]{:S(2)}, u32[]{:S(2)}) collective-permute-start(f32[2,12,8,128]{3,2,1,0:T(8,128)S(1)} %pad_maximum_fusion), channel_id=1, source_target_pairs={{0,16},{1,17},{2,18},{3,19},{4,20},{5,21},{6,22},{7,23},{8,24},{9,... | collective-permute-start | bytes 294920 | tf_op jit(solution)/shard_map/ppermute | solution.py:1009
  58.7 1.4 %collective-permute-start.16 = (f32[8,48,128]{2,1,0:T(8,128)S(1)}, f32[8,48,128]{2,1,0:T(8,128)S(1)}, u32[]{:S(2)}, u32[]{:S(2)}) collective-permute-start(f32[8,48,128]{2,1,0:T(8,128)S(1)} %all-to-all-done.1.received), channel_id=1, source_target_pairs={{0,1},{1,0},{2,3},{3,2},{4,5},{5,4},{6,7},{7,6},{8,9},{9,8},{10,11... | collective-permute-start | bytes 589832 | tf_op jit(solution)/shard_map/ppermute | solution.py:1012

commit v8 on v7

--- a/solution.py
+++ b/solution.py
@@ -741,7 +741,7 @@
         packed[g, total_x // 2 : 3 * quarter] = edge
 
 
-def project_kernel(fringe, received, partner, table_y, moved, upstream, velocity_next, pressure):
+def project_kernel(received, partner, table_y, blended, velocity_next, pressure):
     groups = received.shape[0]
     share, total_x, lanes = pressure.shape
     cells_x = total_x // groups
@@ -766,8 +766,6 @@
     values = [f[:, :lanes] for f in fields]
     values[0] = jnp.where(place == 0, values[1], values[0])
     values[-1] = jnp.where(place == groups - 1, -values[-2], values[-1])
-    is_farm = lax.axis_index("sec") == 1
-    outlet = upstream.shape[0]
     for z in range(share):
         now = values[z + 1]
         pressure[z] = now
@@ -776,17 +774,26 @@
             fields[z + 1][:, lanes:],
             0.5 * (values[z + 2] - values[z]),
         ]
-        for s in range(groups):
-            distance = place ^ s
-            columns = s * cells_x + lax.broadcasted_iota(jnp.int32, (cells_x, lanes), 0)
-            inside = jnp.logical_and(columns >= fringe[0], columns < fringe[1])
-            blend = jnp.where(jnp.logical_and(inside, is_farm), FRINGE_BLEND, 0.0)
-            for c in range(3):
+        for c in range(3):
+            velocity_next[c, z] = blended[c, z] - slopes[c]
+
+
+def blend_kernel(fringe, moved, upstream, blended):
+    _, share, total_x, lanes = blended.shape
+    groups, _, cells_x, _ = moved.shape
+    outlet = upstream.shape[0]
+    is_farm = lax.axis_index("sec") == 1
+    for s in range(groups):
+        distance = lax.axis_index("gx") ^ s
+        columns = s * cells_x + lax.broadcasted_iota(jnp.int32, (cells_x, lanes), 0)
+        inside = jnp.logical_and(columns >= fringe[0], columns < fringe[1])
+        blend = jnp.where(jnp.logical_and(inside, is_farm), FRINGE_BLEND, 0.0)
+        for c in range(3):
+            for z in range(share):
                 own = moved[distance, c * share + z]
                 if s >= groups - outlet:
                     own = own + blend * (upstream[s - groups + outlet, c * share + z] - own)
-                spot = slice(s * cells_x, (s + 1) * cells_x)
-                velocity_next[c, z, spot] = own - slopes[c][spot]
+                blended[c, z, s * cells_x : (s + 1) * cells_x] = own
 
 
 def cas(rows, columns, length):
@@ -1010,6 +1017,14 @@
     returned = lax.all_to_all(packed, "gx", 0, 0, tiled=True)
     returned, upstream = lax.optimization_barrier((returned, upstream))
     partner = lax.ppermute(returned, "gy", swap)
+    blended = call(
+        blend_kernel,
+        jax.ShapeDtypeStruct((3, share, total_x, cells_y), f32),
+        [],
+        fringe_bounds,
+        moved,
+        upstream,
+    )
     velocity_next, pressure = call(
         project_kernel,
         [
@@ -1017,12 +1032,10 @@
             jax.ShapeDtypeStruct((share, total_x, cells_y), f32),
         ],
         [],
-        fringe_bounds,
         returned,
         partner,
         backward,
-        moved,
-        upstream,
+        blended,
     )
     return (velocity_next[None], pressure[None])
 

time: 62.4 us -> 62 us (level)
    pallas_call x8 -> x9, Pallas kernels: 12.5 us -> 12.6 us  [call(): pl.pallas_call(kernel, out_shape=out_shapes, in_specs=in_specs, out_specs...]
  transfers between devices with their start and end apart: 19 -> 19, of which waited for: 7 -> 7; matrix products, arithmetic and copies ran while one was open for 4% -> 4% of each run, Pallas kernels for 11% -> 12%
where the time goes in v8:
time: 62 us; the launch traced here: 61.6 us
  starting transfers between devices  33.2 us (54%)
  Pallas kernels  12.6 us (20%)
  waiting for transfers between devices  11.4 us (18%)
  local copies, waits for them, and re-layouts  2.24 us (4%)
  matrix products  1.13 us (2%)
  between operations  0.9 us (1%)
    pallas_call x9, Pallas kernels, call(): pl.pallas_call(kernel, out_shape=out_shapes, in_specs=in_specs, out_specs...  12.6 us
    ppermute x7, starting transfers between devices, paired_plan(): lax.ppermute(block, 'gx', [(i, i ^ d) for i in range(groups)])  11.3 us
    all_to_all x1, starting transfers between devices, paired_plan(): lax.all_to_all(spectra.reshape((4 * groups,) + spectra.shape[3:]), ('sec'...  4.13 us
    all_to_all x1, starting transfers between devices, paired_plan(): returned = lax.all_to_all(packed, 'gx', 0, 0, tiled=True)  3.64 us
    ppermute x1, starting transfers between devices, paired_plan(): around = lax.ppermute(lower, 'gx', pairs_around)  3.6 us
    ppermute x1, starting transfers between devices, paired_plan(): upstream = lax.ppermute(leaving, 'sec', [(0, 1)])  3.39 us
    ppermute x1, starting transfers between devices, paired_plan(): across = lax.ppermute(upper, 'gx', pairs_across)  3.04 us
    ppermute x1, starting transfers between devices, paired_plan(): far_there = lax.ppermute(other, ('gx', 'gy'), crossed)  2.48 us
  transfers between devices with their start and end apart: 19, of which 7 were waited for; matrix products, arithmetic and copies ran while one was open for 4% of the time, Pallas kernels for 12%

profile of v8, /device:TPU:0, one launch (start us, length us, event | category | flops | bytes accessed | tf_op | source)
XLA Modules:
  0.0 61.6 jit_solution(3679009098928790646)
XLA Ops:
  0.6 0.0 copy-start
  0.6 1.0 %copy-done = f32[1,3,32,8,128]{4,3,2,1,0:T(8,128)S(1)} copy-done((f32[1,3,32,8,128]{4,3,2,1,0:T(8,128)S(1)}, f32[1,3,32,8,128]{4,3,2,1,0:T(8,128)}, u32[]{:S(2)}) %copy-start) | copy-done | bytes 393240
  1.6 0.3 shard_map.96
  2.0 3.0 %collective-permute-start.1 = (f32[3,3,4,8,128]{4,3,2,1,0:T(8,128)S(1)}, f32[3,3,4,8,128]{4,3,2,1,0:T(8,128)S(1)}, u32[]{:S(2)}, u32[]{:S(2)}) collective-permute-start(f32[3,3,4,8,128]{4,3,2,1,0:T(8,128)S(1)} %get-tuple-element.33), channel_id=1, source_target_pairs={{0,2},{2,0},{4,6},{6,4},{8,10},{10,8},{12,14},{14,12},{1,3},{3,1},... | collective-permute-start | bytes 442376 | tf_op jit(solution)/shard_map/ppermute | solution.py:899
  5.0 0.4 shard_map.95
  5.4 0.1 collective-permute-start
  5.5 3.6 %collective-permute-start.3 = (f32[3,3,4,8,128]{4,3,2,1,0:T(8,128)S(1)}, f32[3,3,4,8,128]{4,3,2,1,0:T(8,128)S(1)}, u32[]{:S(2)}, u32[]{:S(2)}) collective-permute-start(f32[3,3,4,8,128]{4,3,2,1,0:T(8,128)S(1)} %get-tuple-element.35), channel_id=1, source_target_pairs={{0,14},{2,4},{4,2},{6,8},{8,6},{10,12},{12,10},{14,0},{1,15},{3,5}... | collective-permute-start | bytes 442376 | tf_op jit(solution)/shard_map/ppermute | solution.py:898
  9.1 0.0 collective-permute-start.5
  9.1 0.8 %slice_bitcast_fusion.2 = (s32[64]{0:T(128)S(1)}, s32[64]{0:T(128)S(1)}, s32[64]{0:T(128)S(1)}) fusion(s32[64,3]{0,1:T(4,128)} %param.9), kind=kLoop, calls=%fused_computation.49 | loop fusion | bytes 1536 | tf_op jit(solution)/shard_map/eq | solution.py:861
  9.9 0.1 reshape.174
  10.0 0.1 fusion.12
  10.1 0.1 subtract_multiply_fusion
  10.2 0.6 fusion.2
  10.8 0.2 copy.14
  11.0 2.4 %collective-permute-done.1.across_here = f32[3,3,4,8,128]{4,3,2,1,0:T(8,128)S(1)} collective-permute-done((f32[3,3,4,8,128]{4,3,2,1,0:T(8,128)S(1)}, f32[3,3,4,8,128]{4,3,2,1,0:T(8,128)S(1)}, u32[]{:S(2)}, u32[]{:S(2)}) %collective-permute-start.1) | collective-permute-done | bytes 147488 | tf_op jit(solution)/shard_map/ppermute | solution.py:899
  13.4 0.0 collective-permute-start.2
  13.4 2.5 %collective-permute-start.6 = (f32[4,3,4,8,128]{4,3,2,1,0:T(8,128)S(1)}, f32[4,3,4,8,128]{4,3,2,1,0:T(8,128)S(1)}, u32[]{:S(2)}, u32[]{:S(2)}) collective-permute-start(f32[4,3,4,8,128]{4,3,2,1,0:T(8,128)S(1)} %get-tuple-element.37), channel_id=1, source_target_pairs={{1,2},{3,4},{5,6},{7,8},{9,10},{11,12},{13,14},{15,0},{2,1},{4,3},... | collective-permute-start | bytes 589832 | tf_op jit(solution)/shard_map/ppermute | solution.py:905
  15.9 0.0 collective-permute-done.3.around_here
  15.9 0.1 collective-permute-start.4
  16.0 0.6 fusion.3
  16.6 0.1 copy.15
  16.7 0.0 collective-permute-done.2.across_there
  16.7 0.6 %collective-permute-done.4.around_there = f32[3,3,4,8,128]{4,3,2,1,0:T(8,128)S(1)} collective-permute-done((f32[3,3,4,8,128]{4,3,2,1,0:T(8,128)S(1)}, f32[3,3,4,8,128]{4,3,2,1,0:T(8,128)S(1)}, u32[]{:S(2)}, u32[]{:S(2)}) %collective-permute-start.4) | collective-permute-done | bytes 147488 | tf_op jit(solution)/shard_map/ppermute | solution.py:907
  17.3 0.0 collective-permute-done.own_there
  17.3 3.1 %shard_map.97 = (f32[4,3,4,8,256]{4,3,2,1,0:T(8,128)S(1)}, f32[4,3,4,8,256]{4,3,2,1,0:T(8,128)S(1)}, f32[2,3,4,8,256]{4,3,2,1,0:T(8,128)S(1)}) custom-call(f32[8,3,4,8,128]{4,3,2,1,0:T(8,128)S(1)} %get-tuple-element.31.own_here, f32[8,3,4,8,128]{4,3,2,1,0:T(8,128)S(1)} %collective-permute-done.own_there, ...), custom_call_target="tpu_custom_call" | custom-call | tf_op jit(solution)/shard_map/pallas_call | solution.py:850
  20.4 0.0 collective-permute-done.5.far_here
  20.4 0.9 %collective-permute-done.6.far_there = f32[4,3,4,8,128]{4,3,2,1,0:T(8,128)S(1)} collective-permute-done((f32[4,3,4,8,128]{4,3,2,1,0:T(8,128)S(1)}, f32[4,3,4,8,128]{4,3,2,1,0:T(8,128)S(1)}, u32[]{:S(2)}, u32[]{:S(2)}) %collective-permute-start.6) | collective-permute-done | bytes 196640 | tf_op jit(solution)/shard_map/ppermute | solution.py:905
  21.3 0.0 copy-done.6
  21.3 3.2 %shard_map.98 = (f32[8,6,8,128]{3,2,1,0:T(8,128)S(1)}, f32[8,6,8,128]{3,2,1,0:T(8,128)S(1)}, f32[256,256]{1,0:T(8,128)S(1)}) custom-call(s32[2]{0:T(128)S(1)} %copy-done.6, f32[8,3,4,8,128]{4,3,2,1,0:T(8,128)S(1)} %get-tuple-element.31.own_here, f32[8,3,4,8,128]{4,3,2,1,0:T(8,128)S(1)} %collective-permute-done.own_there, ...), custom_call_target="tpu_custom_call" | custom-call | tf_op jit(solution)/shard_map/pallas_call | solution.py:850
  24.5 0.0 copy-start.1
  24.5 0.0 copy-start.4
  24.5 1.5 %collective-permute-start.7 = (f32[8,6,8,128]{3,2,1,0:T(8,128)S(1)}, f32[8,6,8,128]{3,2,1,0:T(8,128)S(1)}, u32[]{:S(2)}, u32[]{:S(2)}) collective-permute-start(f32[8,6,8,128]{3,2,1,0:T(8,128)S(1)} %get-tuple-element.43), channel_id=1, source_target_pairs={{0,1},{1,0},{2,3},{3,2},{4,5},{5,4},{6,7},{7,6},{8,9},{9,8},{10,11... | collective-permute-start | bytes 589832 | tf_op jit(solution)/shard_map/ppermute | solution.py:972
  26.0 0.0 copy-done.3
  26.0 0.0 copy-done.5
  26.0 1.6 %shard_map.99 = f32[2,8,2,2,8,128]{5,4,3,2,1,0:T(8,128)} custom-call(f32[256,256]{1,0:T(8,128)S(1)} %get-tuple-element.41.source, f32[256,256]{1,0:T(8,128)S(1)} %copy-done.3, f32[32,32]{1,0:T(8,128)S(1)} %copy-done.5), custom_call_target="tpu_custom_call" | custom-call | tf_op jit(solution)/shard_map/pallas_call | solution.py:850
  27.6 4.1 %all-to-all-start = ((f32[32,2,8,128]{3,2,1,0:T(8,128)}), f32[32,2,8,128]{3,2,1,0:T(8,128)S(1)}, u32[]{:S(2)}, u32[]{:S(2)}) async-start(f32[32,2,8,128]{3,2,1,0:T(8,128)} %bitcast.9), calls=%async_computation | async-start | bytes 524288 | tf_op jit(solution)/shard_map/all_to_all | solution.py:981
  31.7 0.0 collective-permute-done.7.piece_there
  31.7 0.3 shard_map.101
  32.1 1.8 %collective-permute-start.11 = (f32[12,8,128]{2,1,0:T(8,128)S(1)}, f32[12,8,128]{2,1,0:T(8,128)S(1)}, u32[]{:S(2)}, u32[]{:S(2)}) collective-permute-start(f32[12,8,128]{2,1,0:T(8,128)S(1)} %get-tuple-element.49), channel_id=1, source_target_pairs={{0,2},{2,0},{4,6},{6,4},{8,10},{10,8},{12,14},{14,12},{1,3},{3,1},... | collective-permute-start | bytes 147464 | tf_op jit(solution)/shard_map/ppermute | solution.py:992
  33.9 1.5 %collective-permute-start.12 = (f32[12,8,128]{2,1,0:T(8,128)S(1)}, f32[12,8,128]{2,1,0:T(8,128)S(1)}, u32[]{:S(2)}, u32[]{:S(2)}) collective-permute-start(f32[12,8,128]{2,1,0:T(8,128)S(1)} %get-tuple-element.50), channel_id=1, source_target_pairs={{0,4},{2,6},{4,0},{6,2},{8,12},{10,14},{12,8},{14,10},{1,5},{3,7},... | collective-permute-start | bytes 147464 | tf_op jit(solution)/shard_map/ppermute | solution.py:992
  35.4 2.4 %collective-permute-start.10 = (f32[12,8,128]{2,1,0:T(8,128)S(1)}, f32[12,8,128]{2,1,0:T(8,128)S(1)}, u32[]{:S(2)}, u32[]{:S(2)}) collective-permute-start(f32[12,8,128]{2,1,0:T(8,128)S(1)} %get-tuple-element.46), channel_id=1, source_target_pairs={{0,10},{2,8},{4,14},{6,12},{8,2},{10,0},{12,6},{14,4},{1,11},{3,9}... | collective-permute-start | bytes 147464 | tf_op jit(solution)/shard_map/ppermute | solution.py:992
  37.8 1.4 %collective-permute-start.8 = (f32[12,8,128]{2,1,0:T(8,128)S(1)}, f32[12,8,128]{2,1,0:T(8,128)S(1)}, u32[]{:S(2)}, u32[]{:S(2)}) collective-permute-start(f32[12,8,128]{2,1,0:T(8,128)S(1)} %get-tuple-element.44), channel_id=1, source_target_pairs={{0,6},{2,4},{4,2},{6,0},{8,14},{10,12},{12,10},{14,8},{1,7},{3,5},... | collective-permute-start | bytes 147464 | tf_op jit(solution)/shard_map/ppermute | solution.py:992
  39.2 0.5 collective-permute-start.9
  39.8 0.0 collective-permute-done.11
  39.8 3.3 %collective-permute-start.13 = (f32[12,8,128]{2,1,0:T(8,128)S(1)}, f32[12,8,128]{2,1,0:T(8,128)S(1)}, u32[]{:S(2)}, u32[]{:S(2)}) collective-permute-start(f32[12,8,128]{2,1,0:T(8,128)S(1)} %get-tuple-element.54), channel_id=1, source_target_pairs={{0,12},{2,14},{4,8},{6,10},{8,4},{10,6},{12,0},{14,2},{1,13},{3,15... | collective-permute-start | bytes 147464 | tf_op jit(solution)/shard_map/ppermute | solution.py:992
  43.1 0.0 collective-permute-done.12
  43.1 0.2 collective-permute-start.14
  43.4 0.0 all-to-all-done
  43.4 0.0 copy-done.1
  43.4 0.0 copy-done.4
  43.4 1.6 %shard_map.100 = f32[8,48,128]{2,1,0:T(8,128)} custom-call(f32[2,8,2,2,8,128]{5,4,3,2,1,0:T(8,128)S(1)} %bitcast.44, f32[8,2,4,128]{3,2,1,0:T(4,128)S(1)} %copy-done.4, f32[640,512]{1,0:T(8,128)S(1)} %copy-done.1), custom_call_target="tpu_custom_call" | custom-call | tf_op jit(solution)/shard_map/pallas_call | solution.py:850
  45.0 0.0 collective-permute-done.10
  45.0 0.0 collective-permute-done.8
  45.0 2.3 %collective-permute-done.9 = f32[12,8,128]{2,1,0:T(8,128)S(1)} collective-permute-done((f32[12,8,128]{2,1,0:T(8,128)S(1)}, f32[12,8,128]{2,1,0:T(8,128)S(1)}, u32[]{:S(2)}, u32[]{:S(2)}) %collective-permute-start.9) | collective-permute-done | bytes 49184 | tf_op jit(solution)/shard_map/ppermute | solution.py:992
  47.4 3.6 %all-to-all-start.1 = ((f32[8,48,128]{2,1,0:T(8,128)}), f32[8,48,128]{2,1,0:T(8,128)S(1)}, u32[]{:S(2)}, u32[]{:S(2)}) async-start(f32[8,48,128]{2,1,0:T(8,128)} %shard_map.100), calls=%async_computation.1 | async-start | bytes 393216 | tf_op jit(solution)/shard_map/all_to_all | solution.py:1017
  51.0 0.0 collective-permute-done.13
  51.1 0.0 collective-permute-done.14
  51.1 3.4 %collective-permute-start.15 = (f32[2,12,8,128]{3,2,1,0:T(8,128)S(1)}, f32[2,12,8,128]{3,2,1,0:T(8,128)S(1)}, u32[]{:S(2)}, u32[]{:S(2)}) collective-permute-start(f32[2,12,8,128]{3,2,1,0:T(8,128)S(1)} %pad_maximum_fusion), channel_id=1, source_target_pairs={{0,16},{1,17},{2,18},{3,19},{4,20},{5,21},{6,22},{7,23},{8,24},{9,... | collective-permute-start | bytes 294920 | tf_op jit(solution)/shard_map/ppermute | solution.py:1016
  54.5 2.2 %collective-permute-done.15.upstream = f32[2,12,8,128]{3,2,1,0:T(8,128)S(1)} collective-permute-done((f32[2,12,8,128]{3,2,1,0:T(8,128)S(1)}, f32[2,12,8,128]{3,2,1,0:T(8,128)S(1)}, u32[]{:S(2)}, u32[]{:S(2)}) %collective-permute-start.15) | collective-permute-done | bytes 98336 | tf_op jit(solution)/shard_map/ppermute | solution.py:1016
  56.7 2.1 %all-to-all-done.1.received = f32[8,48,128]{2,1,0:T(8,128)S(1)} async-done(((f32[8,48,128]{2,1,0:T(8,128)}), f32[8,48,128]{2,1,0:T(8,128)S(1)}, u32[]{:S(2)}, u32[]{:S(2)}) %all-to-all-start.1) | async-done | bytes 196640 | tf_op jit(solution)/shard_map/all_to_all | solution.py:1017
  58.8 0.0 collective-permute-start.16
  58.8 0.6 shard_map.102.blended
  59.4 0.8 %collective-permute-done.16.partner = f32[8,48,128]{2,1,0:T(8,128)S(1)} collective-permute-done((f32[8,48,128]{2,1,0:T(8,128)S(1)}, f32[8,48,128]{2,1,0:T(8,128)S(1)}, u32[]{:S(2)}, u32[]{:S(2)}) %collective-permute-start.16) | collective-permute-done | bytes 196640 | tf_op jit(solution)/shard_map/ppermute | solution.py:1019
  60.2 1.4 %shard_map.103 = (f32[3,4,64,128]{3,2,1,0:T(8,128)}, f32[4,64,128]{2,1,0:T(8,128)}) custom-call(f32[8,48,128]{2,1,0:T(8,128)S(1)} %all-to-all-done.1.received, f32[8,48,128]{2,1,0:T(8,128)S(1)} %collective-permute-done.16.partner, f32[2,256,256]{2,1,0:T(8,128)S(1)} %copy-done.2, f32[3,4,64,128]{3,2,1,0:T(8,128)S(1)} %shard_map.102.blended), custom_call_target="tpu_custom_call" | custom-call | tf_op jit(solution)/shard_map/pallas_call | solution.py:850
  (19 shorter events, 0.1 us)
Async XLA Ops:
  0.6 1.0 %copy-start = (f32[1,3,32,8,128]{4,3,2,1,0:T(8,128)S(1)}, f32[1,3,32,8,128]{4,3,2,1,0:T(8,128)}, u32[]{:S(2)}) copy-start(f32[1,3,32,8,128]{4,3,2,1,0:T(8,128)} %param.8) | copy-start | bytes 1179652
  2.0 11.5 %collective-permute-start.1 = (f32[3,3,4,8,128]{4,3,2,1,0:T(8,128)S(1)}, f32[3,3,4,8,128]{4,3,2,1,0:T(8,128)S(1)}, u32[]{:S(2)}, u32[]{:S(2)}) collective-permute-start(f32[3,3,4,8,128]{4,3,2,1,0:T(8,128)S(1)} %get-tuple-element.33), channel_id=1, source_target_pairs={{0,2},{2,0},{4,6},{6,4},{8,10},{10,8},{12,14},{14,12},{1,3},{3,1},... | collective-permute-start | bytes 442376 | tf_op jit(solution)/shard_map/ppermute | solution.py:899
  5.4 11.9 %collective-permute-start = (f32[8,3,4,8,128]{4,3,2,1,0:T(8,128)S(1)}, f32[8,3,4,8,128]{4,3,2,1,0:T(8,128)S(1)}, u32[]{:S(2)}, u32[]{:S(2)}) collective-permute-start(f32[8,3,4,8,128]{4,3,2,1,0:T(8,128)S(1)} %get-tuple-element.31.own_here), channel_id=1, source_target_pairs={{0,1},{1,0},{2,3},{3,2},{4,5},{5,4},{6,7},{7,6},{8,9},{9,8},{10,11... | collective-permute-start | bytes 1179656 | tf_op jit(solution)/shard_map/ppermute | solution.py:903
  5.5 10.4 %collective-permute-start.3 = (f32[3,3,4,8,128]{4,3,2,1,0:T(8,128)S(1)}, f32[3,3,4,8,128]{4,3,2,1,0:T(8,128)S(1)}, u32[]{:S(2)}, u32[]{:S(2)}) collective-permute-start(f32[3,3,4,8,128]{4,3,2,1,0:T(8,128)S(1)} %get-tuple-element.35), channel_id=1, source_target_pairs={{0,14},{2,4},{4,2},{6,8},{8,6},{10,12},{12,10},{14,0},{1,15},{3,5}... | collective-permute-start | bytes 442376 | tf_op jit(solution)/shard_map/ppermute | solution.py:898
  9.1 11.3 %collective-permute-start.5 = (f32[4,3,4,8,128]{4,3,2,1,0:T(8,128)S(1)}, f32[4,3,4,8,128]{4,3,2,1,0:T(8,128)S(1)}, u32[]{:S(2)}, u32[]{:S(2)}) collective-permute-start(f32[4,3,4,8,128]{4,3,2,1,0:T(8,128)S(1)} %get-tuple-element.36), channel_id=1, source_target_pairs={{0,2},{2,4},{4,6},{6,8},{8,10},{10,12},{12,14},{14,0},{3,1},{5,3},... | collective-permute-start | bytes 589832 | tf_op jit(solution)/shard_map/ppermute | solution.py:922
  13.4 3.2 %collective-permute-start.2 = (f32[3,3,4,8,128]{4,3,2,1,0:T(8,128)S(1)}, f32[3,3,4,8,128]{4,3,2,1,0:T(8,128)S(1)}, u32[]{:S(2)}, u32[]{:S(2)}) collective-permute-start(f32[3,3,4,8,128]{4,3,2,1,0:T(8,128)S(1)} %collective-permute-done.1.across_here), channel_id=1, source_target_pairs={{0,1},{1,0},{2,3},{3,2},{4,5},{5,4},{6,7},{7,6},{8,9},{9,8},{10,11... | collective-permute-start | bytes 442376 | tf_op jit(solution)/shard_map/ppermute | solution.py:906
  13.4 7.9 %collective-permute-start.6 = (f32[4,3,4,8,128]{4,3,2,1,0:T(8,128)S(1)}, f32[4,3,4,8,128]{4,3,2,1,0:T(8,128)S(1)}, u32[]{:S(2)}, u32[]{:S(2)}) collective-permute-start(f32[4,3,4,8,128]{4,3,2,1,0:T(8,128)S(1)} %get-tuple-element.37), channel_id=1, source_target_pairs={{1,2},{3,4},{5,6},{7,8},{9,10},{11,12},{13,14},{15,0},{2,1},{4,3},... | collective-permute-start | bytes 589832 | tf_op jit(solution)/shard_map/ppermute | solution.py:905
  15.9 1.4 %collective-permute-start.4 = (f32[3,3,4,8,128]{4,3,2,1,0:T(8,128)S(1)}, f32[3,3,4,8,128]{4,3,2,1,0:T(8,128)S(1)}, u32[]{:S(2)}, u32[]{:S(2)}) collective-permute-start(f32[3,3,4,8,128]{4,3,2,1,0:T(8,128)S(1)} %collective-permute-done.3.around_here), channel_id=1, source_target_pairs={{0,1},{1,0},{2,3},{3,2},{4,5},{5,4},{6,7},{7,6},{8,9},{9,8},{10,11... | collective-permute-start | bytes 442376 | tf_op jit(solution)/shard_map/ppermute | solution.py:907
  16.6 4.8 %copy-start.6 = (s32[2]{0:T(128)S(1)}, s32[2]{0:T(128)}, u32[]{:S(2)}) copy-start(s32[2]{0:T(128)} %fringe.3) | copy-start | bytes 28
  21.3 4.7 %copy-start.3 = (f32[256,256]{1,0:T(8,128)S(1)}, f32[256,256]{1,0:T(8,128)}, u32[]{:S(2)}) copy-start(f32[256,256]{1,0:T(8,128)} %constant.97.clone.table_y) | copy-start | bytes 786436
  21.3 4.7 %copy-start.5 = (f32[32,32]{1,0:T(8,128)S(1)}, f32[32,32]{1,0:T(8,128)}, u32[]{:S(2)}) copy-start(f32[32,32]{1,0:T(8,128)} %constant.99.clone.table_z) | copy-start | bytes 12292
  24.5 18.9 %copy-start.1 = (f32[640,512]{1,0:T(8,128)S(1)}, f32[640,512]{1,0:T(8,128)}, u32[]{:S(2)}) copy-start(f32[640,512]{1,0:T(8,128)} %constant.96.clone.table) | copy-start | bytes 3932164
  24.5 18.9 %copy-start.4 = (f32[8,2,4,128]{3,2,1,0:T(4,128)S(1)}, f32[8,2,4,128]{3,2,1,0:T(4,128)}, u32[]{:S(2)}) copy-start(f32[8,2,4,128]{3,2,1,0:T(4,128)} %constant.100.clone.waves) | copy-start | bytes 98308
  24.5 7.2 %collective-permute-start.7 = (f32[8,6,8,128]{3,2,1,0:T(8,128)S(1)}, f32[8,6,8,128]{3,2,1,0:T(8,128)S(1)}, u32[]{:S(2)}, u32[]{:S(2)}) collective-permute-start(f32[8,6,8,128]{3,2,1,0:T(8,128)S(1)} %get-tuple-element.43), channel_id=1, source_target_pairs={{0,1},{1,0},{2,3},{3,2},{4,5},{5,4},{6,7},{7,6},{8,9},{9,8},{10,11... | collective-permute-start | bytes 589832 | tf_op jit(solution)/shard_map/ppermute | solution.py:972
  27.6 15.8 %all-to-all-start = ((f32[32,2,8,128]{3,2,1,0:T(8,128)}), f32[32,2,8,128]{3,2,1,0:T(8,128)S(1)}, u32[]{:S(2)}, u32[]{:S(2)}) async-start(f32[32,2,8,128]{3,2,1,0:T(8,128)} %bitcast.9), calls=%async_computation | async-start | bytes 524288 | tf_op jit(solution)/shard_map/all_to_all | solution.py:981
  32.1 7.7 %collective-permute-start.11 = (f32[12,8,128]{2,1,0:T(8,128)S(1)}, f32[12,8,128]{2,1,0:T(8,128)S(1)}, u32[]{:S(2)}, u32[]{:S(2)}) collective-permute-start(f32[12,8,128]{2,1,0:T(8,128)S(1)} %get-tuple-element.49), channel_id=1, source_target_pairs={{0,2},{2,0},{4,6},{6,4},{8,10},{10,8},{12,14},{14,12},{1,3},{3,1},... | collective-permute-start | bytes 147464 | tf_op jit(solution)/shard_map/ppermute | solution.py:992
  33.9 9.2 %collective-permute-start.12 = (f32[12,8,128]{2,1,0:T(8,128)S(1)}, f32[12,8,128]{2,1,0:T(8,128)S(1)}, u32[]{:S(2)}, u32[]{:S(2)}) collective-permute-start(f32[12,8,128]{2,1,0:T(8,128)S(1)} %get-tuple-element.50), channel_id=1, source_target_pairs={{0,4},{2,6},{4,0},{6,2},{8,12},{10,14},{12,8},{14,10},{1,5},{3,7},... | collective-permute-start | bytes 147464 | tf_op jit(solution)/shard_map/ppermute | solution.py:992
  35.4 9.6 %collective-permute-start.10 = (f32[12,8,128]{2,1,0:T(8,128)S(1)}, f32[12,8,128]{2,1,0:T(8,128)S(1)}, u32[]{:S(2)}, u32[]{:S(2)}) collective-permute-start(f32[12,8,128]{2,1,0:T(8,128)S(1)} %get-tuple-element.46), channel_id=1, source_target_pairs={{0,10},{2,8},{4,14},{6,12},{8,2},{10,0},{12,6},{14,4},{1,11},{3,9}... | collective-permute-start | bytes 147464 | tf_op jit(solution)/shard_map/ppermute | solution.py:992
  37.8 7.2 %collective-permute-start.8 = (f32[12,8,128]{2,1,0:T(8,128)S(1)}, f32[12,8,128]{2,1,0:T(8,128)S(1)}, u32[]{:S(2)}, u32[]{:S(2)}) collective-permute-start(f32[12,8,128]{2,1,0:T(8,128)S(1)} %get-tuple-element.44), channel_id=1, source_target_pairs={{0,6},{2,4},{4,2},{6,0},{8,14},{10,12},{12,10},{14,8},{1,7},{3,5},... | collective-permute-start | bytes 147464 | tf_op jit(solution)/shard_map/ppermute | solution.py:992
  39.2 8.1 %collective-permute-start.9 = (f32[12,8,128]{2,1,0:T(8,128)S(1)}, f32[12,8,128]{2,1,0:T(8,128)S(1)}, u32[]{:S(2)}, u32[]{:S(2)}) collective-permute-start(f32[12,8,128]{2,1,0:T(8,128)S(1)} %get-tuple-element.45), channel_id=1, source_target_pairs={{0,8},{2,10},{4,12},{6,14},{8,0},{10,2},{12,4},{14,6},{1,9},{3,11}... | collective-permute-start | bytes 147464 | tf_op jit(solution)/shard_map/ppermute | solution.py:992
  39.8 11.3 %collective-permute-start.13 = (f32[12,8,128]{2,1,0:T(8,128)S(1)}, f32[12,8,128]{2,1,0:T(8,128)S(1)}, u32[]{:S(2)}, u32[]{:S(2)}) collective-permute-start(f32[12,8,128]{2,1,0:T(8,128)S(1)} %get-tuple-element.54), channel_id=1, source_target_pairs={{0,12},{2,14},{4,8},{6,10},{8,4},{10,6},{12,0},{14,2},{1,13},{3,15... | collective-permute-start | bytes 147464 | tf_op jit(solution)/shard_map/ppermute | solution.py:992
  43.1 7.9 %collective-permute-start.14 = (f32[12,8,128]{2,1,0:T(8,128)S(1)}, f32[12,8,128]{2,1,0:T(8,128)S(1)}, u32[]{:S(2)}, u32[]{:S(2)}) collective-permute-start(f32[12,8,128]{2,1,0:T(8,128)S(1)} %get-tuple-element.55), channel_id=1, source_target_pairs={{0,14},{2,12},{4,10},{6,8},{8,6},{10,4},{12,2},{14,0},{1,15},{3,13... | collective-permute-start | bytes 147464 | tf_op jit(solution)/shard_map/ppermute | solution.py:992
  45.0 15.2 %copy-start.2 = (f32[2,256,256]{2,1,0:T(8,128)S(1)}, f32[2,256,256]{2,1,0:T(8,128)}, u32[]{:S(2)}) copy-start(f32[2,256,256]{2,1,0:T(8,128)} %constant.98.clone.table_y) | copy-start | bytes 1572868
  47.4 11.4 %all-to-all-start.1 = ((f32[8,48,128]{2,1,0:T(8,128)}), f32[8,48,128]{2,1,0:T(8,128)S(1)}, u32[]{:S(2)}, u32[]{:S(2)}) async-start(f32[8,48,128]{2,1,0:T(8,128)} %shard_map.100), calls=%async_computation.1 | async-start | bytes 393216 | tf_op jit(solution)/shard_map/all_to_all | solution.py:1017
  51.1 5.6 %collective-permute-start.15 = (f32[2,12,8,128]{3,2,1,0:T(8,128)S(1)}, f32[2,12,8,128]{3,2,1,0:T(8,128)S(1)}, u32[]{:S(2)}, u32[]{:S(2)}) collective-permute-start(f32[2,12,8,128]{3,2,1,0:T(8,128)S(1)} %pad_maximum_fusion), channel_id=1, source_target_pairs={{0,16},{1,17},{2,18},{3,19},{4,20},{5,21},{6,22},{7,23},{8,24},{9,... | collective-permute-start | bytes 294920 | tf_op jit(solution)/shard_map/ppermute | solution.py:1016
  58.8 1.4 %collective-permute-start.16 = (f32[8,48,128]{2,1,0:T(8,128)S(1)}, f32[8,48,128]{2,1,0:T(8,128)S(1)}, u32[]{:S(2)}, u32[]{:S(2)}) collective-permute-start(f32[8,48,128]{2,1,0:T(8,128)S(1)} %all-to-all-done.1.received), channel_id=1, source_target_pairs={{0,1},{1,0},{2,3},{3,2},{4,5},{5,4},{6,7},{7,6},{8,9},{9,8},{10,11... | collective-permute-start | bytes 589832 | tf_op jit(solution)/shard_map/ppermute | solution.py:1019

commit v9 on v8

--- a/solution.py
+++ b/solution.py
@@ -741,27 +741,31 @@
         packed[g, total_x // 2 : 3 * quarter] = edge
 
 
-def project_kernel(received, partner, table_y, blended, velocity_next, pressure):
-    groups = received.shape[0]
+def levels_in(arrays, total_x, share):
+    groups, rows, lanes = arrays.shape
+    width, main_rows = lanes // groups, total_x // 2
+    main = swap_blocks([arrays[s, :main_rows] for s in range(groups)], width)
+    edge = swap_blocks([arrays[s, main_rows:rows] for s in range(groups)], width)
+    inner = [x for n in range(share) for x in (main[n], main[share + n])]
+    outer = [[edge[2 * q + n] for q in range(4)] for n in range(2)]
+    return jnp.concatenate(outer[0] + inner + outer[1], axis=0)
+
+
+def half_kernel(received, table_y, partial):
+    groups, rows, lanes = received.shape
+    total_x = 4 * rows // 3
+    core = lax.axis_index("gy")
+    share = partial.shape[0] // total_x - 2
+    table = table_y[core, pl.ds(pl.multiple_of(core * lanes, lanes), lanes), :]
+    partial[...] = dot(levels_in(received, total_x, share), table)
+
+
+def project_kernel(partial, partner, table_y, blended, velocity_next, pressure):
+    groups = partner.shape[0]
     share, total_x, lanes = pressure.shape
-    cells_x = total_x // groups
-    width = lanes // groups
     place, core = lax.axis_index("gx"), lax.axis_index("gy")
-    main_rows = total_x // 2
-    rows = partner.shape[1]
-
-    def levels_in(arrays):
-        main = swap_blocks([arrays[s, :main_rows] for s in range(groups)], width)
-        edge = swap_blocks([arrays[s, main_rows:rows] for s in range(groups)], width)
-        inner = [jnp.concatenate([main[n], main[share + n]], axis=0) for n in range(share)]
-        outer = [jnp.concatenate([edge[2 * q + n] for q in range(4)], axis=0) for n in range(2)]
-        return [outer[0]] + inner + [outer[1]]
-
-    here, there = levels_in(received), levels_in(partner)
-    here, there = jnp.concatenate(here, axis=0), jnp.concatenate(there, axis=0)
-    low = jnp.where(core == 0, here, there)
-    high = jnp.where(core == 0, there, here)
-    both = dot(jnp.concatenate([low, high], axis=1), table_y[core])
+    table = table_y[core, pl.ds(pl.multiple_of((1 - core) * lanes, lanes), lanes), :]
+    both = partial[...] + dot(levels_in(partner, total_x, share), table)
     fields = [both[n * total_x : (n + 1) * total_x] for n in range(share + 2)]
     values = [f[:, :lanes] for f in fields]
     values[0] = jnp.where(place == 0, values[1], values[0])
@@ -1025,6 +1029,13 @@
         moved,
         upstream,
     )
+    partial = call(
+        half_kernel,
+        jax.ShapeDtypeStruct(((share + 2) * total_x, 2 * cells_y), f32),
+        [],
+        returned,
+        backward,
+    )
     velocity_next, pressure = call(
         project_kernel,
         [
@@ -1032,7 +1043,7 @@
             jax.ShapeDtypeStruct((share, total_x, cells_y), f32),
         ],
         [],
-        returned,
+        partial,
         partner,
         backward,
         blended,

time: 62 us -> 61.9 us (level)
    pallas_call x9 -> x10, Pallas kernels: 12.6 us -> 13.1 us  [call(): pl.pallas_call(kernel, out_shape=out_shapes, in_specs=in_specs, out_specs...]
  transfers between devices with their start and end apart: 19 -> 19, of which waited for: 7 -> 7; matrix products, arithmetic and copies ran while one was open for 4% -> 4% of each run, Pallas kernels for 12% -> 13%
where the time goes in v9:
time: 61.9 us; the launch traced here: 61.6 us
  starting transfers between devices  33.2 us (54%)
  Pallas kernels  13.1 us (21%)
  waiting for transfers between devices  10.8 us (17%)
  local copies, waits for them, and re-layouts  2.24 us (4%)
  matrix products  1.13 us (2%)
  between operations  0.91 us (1%)
    pallas_call x10, Pallas kernels, call(): pl.pallas_call(kernel, out_shape=out_shapes, in_specs=in_specs, out_specs...  13.1 us
    ppermute x7, starting transfers between devices, paired_plan(): lax.ppermute(block, 'gx', [(i, i ^ d) for i in range(groups)])  11.3 us
    all_to_all x1, starting transfers between devices, paired_plan(): lax.all_to_all(spectra.reshape((4 * groups,) + spectra.shape[3:]), ('sec'...  4.13 us
    all_to_all x1, starting transfers between devices, paired_plan(): returned = lax.all_to_all(packed, 'gx', 0, 0, tiled=True)  3.64 us
    ppermute x1, starting transfers between devices, paired_plan(): around = lax.ppermute(lower, 'gx', pairs_around)  3.6 us
    ppermute x1, starting transfers between devices, paired_plan(): upstream = lax.ppermute(leaving, 'sec', [(0, 1)])  3.39 us
    ppermute x1, starting transfers between devices, paired_plan(): across = lax.ppermute(upper, 'gx', pairs_across)  3.04 us
    ppermute x1, starting transfers between devices, paired_plan(): far_there = lax.ppermute(other, ('gx', 'gy'), crossed)  2.48 us
  transfers between devices with their start and end apart: 19, of which 7 were waited for; matrix products, arithmetic and copies ran while one was open for 4% of the time, Pallas kernels for 13%

profile of v9, /device:TPU:0, one launch (start us, length us, event | category | flops | bytes accessed | tf_op | source)
XLA Modules:
  0.0 61.6 jit_solution(11518169939313019067)
XLA Ops:
  0.6 0.0 copy-start.1
  0.6 1.0 %copy-done.1 = f32[1,3,32,8,128]{4,3,2,1,0:T(8,128)S(1)} copy-done((f32[1,3,32,8,128]{4,3,2,1,0:T(8,128)S(1)}, f32[1,3,32,8,128]{4,3,2,1,0:T(8,128)}, u32[]{:S(2)}) %copy-start.1) | copy-done | bytes 393240
  1.6 0.3 shard_map.96
  2.0 3.0 %collective-permute-start.1 = (f32[3,3,4,8,128]{4,3,2,1,0:T(8,128)S(1)}, f32[3,3,4,8,128]{4,3,2,1,0:T(8,128)S(1)}, u32[]{:S(2)}, u32[]{:S(2)}) collective-permute-start(f32[3,3,4,8,128]{4,3,2,1,0:T(8,128)S(1)} %get-tuple-element.33), channel_id=1, source_target_pairs={{0,2},{2,0},{4,6},{6,4},{8,10},{10,8},{12,14},{14,12},{1,3},{3,1},... | collective-permute-start | bytes 442376 | tf_op jit(solution)/shard_map/ppermute | solution.py:903
  5.0 0.4 shard_map.95
  5.4 0.1 collective-permute-start
  5.5 3.6 %collective-permute-start.3 = (f32[3,3,4,8,128]{4,3,2,1,0:T(8,128)S(1)}, f32[3,3,4,8,128]{4,3,2,1,0:T(8,128)S(1)}, u32[]{:S(2)}, u32[]{:S(2)}) collective-permute-start(f32[3,3,4,8,128]{4,3,2,1,0:T(8,128)S(1)} %get-tuple-element.35), channel_id=1, source_target_pairs={{0,14},{2,4},{4,2},{6,8},{8,6},{10,12},{12,10},{14,0},{1,15},{3,5}... | collective-permute-start | bytes 442376 | tf_op jit(solution)/shard_map/ppermute | solution.py:902
  9.1 0.0 collective-permute-start.5
  9.1 0.8 %slice_bitcast_fusion.2 = (s32[64]{0:T(128)S(1)}, s32[64]{0:T(128)S(1)}, s32[64]{0:T(128)S(1)}) fusion(s32[64,3]{0,1:T(4,128)} %param.9), kind=kLoop, calls=%fused_computation.49 | loop fusion | bytes 1536 | tf_op jit(solution)/shard_map/eq | solution.py:865
  9.9 0.1 reshape.174
  10.0 0.1 fusion.12
  10.1 0.1 subtract_multiply_fusion
  10.2 0.6 fusion.2
  10.8 0.2 copy.14
  11.0 2.4 %collective-permute-done.1.across_here = f32[3,3,4,8,128]{4,3,2,1,0:T(8,128)S(1)} collective-permute-done((f32[3,3,4,8,128]{4,3,2,1,0:T(8,128)S(1)}, f32[3,3,4,8,128]{4,3,2,1,0:T(8,128)S(1)}, u32[]{:S(2)}, u32[]{:S(2)}) %collective-permute-start.1) | collective-permute-done | bytes 147488 | tf_op jit(solution)/shard_map/ppermute | solution.py:903
  13.4 0.0 collective-permute-start.2
  13.4 2.5 %collective-permute-start.6 = (f32[4,3,4,8,128]{4,3,2,1,0:T(8,128)S(1)}, f32[4,3,4,8,128]{4,3,2,1,0:T(8,128)S(1)}, u32[]{:S(2)}, u32[]{:S(2)}) collective-permute-start(f32[4,3,4,8,128]{4,3,2,1,0:T(8,128)S(1)} %get-tuple-element.37), channel_id=1, source_target_pairs={{1,2},{3,4},{5,6},{7,8},{9,10},{11,12},{13,14},{15,0},{2,1},{4,3},... | collective-permute-start | bytes 589832 | tf_op jit(solution)/shard_map/ppermute | solution.py:909
  15.9 0.0 collective-permute-done.3.around_here
  15.9 0.1 collective-permute-start.4
  16.0 0.6 fusion.3
  16.6 0.1 copy.15
  16.7 0.0 collective-permute-done.2.across_there
  16.7 0.6 %collective-permute-done.4.around_there = f32[3,3,4,8,128]{4,3,2,1,0:T(8,128)S(1)} collective-permute-done((f32[3,3,4,8,128]{4,3,2,1,0:T(8,128)S(1)}, f32[3,3,4,8,128]{4,3,2,1,0:T(8,128)S(1)}, u32[]{:S(2)}, u32[]{:S(2)}) %collective-permute-start.4) | collective-permute-done | bytes 147488 | tf_op jit(solution)/shard_map/ppermute | solution.py:911
  17.3 0.0 collective-permute-done.own_there
  17.3 3.1 %shard_map.97 = (f32[4,3,4,8,256]{4,3,2,1,0:T(8,128)S(1)}, f32[4,3,4,8,256]{4,3,2,1,0:T(8,128)S(1)}, f32[2,3,4,8,256]{4,3,2,1,0:T(8,128)S(1)}) custom-call(f32[8,3,4,8,128]{4,3,2,1,0:T(8,128)S(1)} %get-tuple-element.31.own_here, f32[8,3,4,8,128]{4,3,2,1,0:T(8,128)S(1)} %collective-permute-done.own_there, ...), custom_call_target="tpu_custom_call" | custom-call | tf_op jit(solution)/shard_map/pallas_call | solution.py:854
  20.4 0.0 collective-permute-done.5.far_here
  20.4 0.9 %collective-permute-done.6.far_there = f32[4,3,4,8,128]{4,3,2,1,0:T(8,128)S(1)} collective-permute-done((f32[4,3,4,8,128]{4,3,2,1,0:T(8,128)S(1)}, f32[4,3,4,8,128]{4,3,2,1,0:T(8,128)S(1)}, u32[]{:S(2)}, u32[]{:S(2)}) %collective-permute-start.6) | collective-permute-done | bytes 196640 | tf_op jit(solution)/shard_map/ppermute | solution.py:909
  21.3 0.0 copy-done.6
  21.3 3.2 %shard_map.98 = (f32[8,6,8,128]{3,2,1,0:T(8,128)S(1)}, f32[8,6,8,128]{3,2,1,0:T(8,128)S(1)}, f32[256,256]{1,0:T(8,128)S(1)}) custom-call(s32[2]{0:T(128)S(1)} %copy-done.6, f32[8,3,4,8,128]{4,3,2,1,0:T(8,128)S(1)} %get-tuple-element.31.own_here, f32[8,3,4,8,128]{4,3,2,1,0:T(8,128)S(1)} %collective-permute-done.own_there, ...), custom_call_target="tpu_custom_call" | custom-call | tf_op jit(solution)/shard_map/pallas_call | solution.py:854
  24.5 0.0 copy-start.2
  24.5 0.0 copy-start.4
  24.5 1.5 %collective-permute-start.7 = (f32[8,6,8,128]{3,2,1,0:T(8,128)S(1)}, f32[8,6,8,128]{3,2,1,0:T(8,128)S(1)}, u32[]{:S(2)}, u32[]{:S(2)}) collective-permute-start(f32[8,6,8,128]{3,2,1,0:T(8,128)S(1)} %get-tuple-element.43), channel_id=1, source_target_pairs={{0,1},{1,0},{2,3},{3,2},{4,5},{5,4},{6,7},{7,6},{8,9},{9,8},{10,11... | collective-permute-start | bytes 589832 | tf_op jit(solution)/shard_map/ppermute | solution.py:976
  26.0 0.0 copy-done.3
  26.0 0.0 copy-done.5
  26.0 1.6 %shard_map.99 = f32[2,8,2,2,8,128]{5,4,3,2,1,0:T(8,128)} custom-call(f32[256,256]{1,0:T(8,128)S(1)} %get-tuple-element.41.source, f32[256,256]{1,0:T(8,128)S(1)} %copy-done.3, f32[32,32]{1,0:T(8,128)S(1)} %copy-done.5), custom_call_target="tpu_custom_call" | custom-call | tf_op jit(solution)/shard_map/pallas_call | solution.py:854
  27.6 4.1 %all-to-all-start = ((f32[32,2,8,128]{3,2,1,0:T(8,128)}), f32[32,2,8,128]{3,2,1,0:T(8,128)S(1)}, u32[]{:S(2)}, u32[]{:S(2)}) async-start(f32[32,2,8,128]{3,2,1,0:T(8,128)} %bitcast.9), calls=%async_computation | async-start | bytes 524288 | tf_op jit(solution)/shard_map/all_to_all | solution.py:985
  31.7 0.0 collective-permute-done.7.piece_there
  31.7 0.3 shard_map.101
  32.1 1.8 %collective-permute-start.11 = (f32[12,8,128]{2,1,0:T(8,128)S(1)}, f32[12,8,128]{2,1,0:T(8,128)S(1)}, u32[]{:S(2)}, u32[]{:S(2)}) collective-permute-start(f32[12,8,128]{2,1,0:T(8,128)S(1)} %get-tuple-element.49), channel_id=1, source_target_pairs={{0,2},{2,0},{4,6},{6,4},{8,10},{10,8},{12,14},{14,12},{1,3},{3,1},... | collective-permute-start | bytes 147464 | tf_op jit(solution)/shard_map/ppermute | solution.py:996
  33.9 1.5 %collective-permute-start.12 = (f32[12,8,128]{2,1,0:T(8,128)S(1)}, f32[12,8,128]{2,1,0:T(8,128)S(1)}, u32[]{:S(2)}, u32[]{:S(2)}) collective-permute-start(f32[12,8,128]{2,1,0:T(8,128)S(1)} %get-tuple-element.50), channel_id=1, source_target_pairs={{0,4},{2,6},{4,0},{6,2},{8,12},{10,14},{12,8},{14,10},{1,5},{3,7},... | collective-permute-start | bytes 147464 | tf_op jit(solution)/shard_map/ppermute | solution.py:996
  35.4 2.4 %collective-permute-start.10 = (f32[12,8,128]{2,1,0:T(8,128)S(1)}, f32[12,8,128]{2,1,0:T(8,128)S(1)}, u32[]{:S(2)}, u32[]{:S(2)}) collective-permute-start(f32[12,8,128]{2,1,0:T(8,128)S(1)} %get-tuple-element.46), channel_id=1, source_target_pairs={{0,10},{2,8},{4,14},{6,12},{8,2},{10,0},{12,6},{14,4},{1,11},{3,9}... | collective-permute-start | bytes 147464 | tf_op jit(solution)/shard_map/ppermute | solution.py:996
  37.8 1.4 %collective-permute-start.8 = (f32[12,8,128]{2,1,0:T(8,128)S(1)}, f32[12,8,128]{2,1,0:T(8,128)S(1)}, u32[]{:S(2)}, u32[]{:S(2)}) collective-permute-start(f32[12,8,128]{2,1,0:T(8,128)S(1)} %get-tuple-element.44), channel_id=1, source_target_pairs={{0,6},{2,4},{4,2},{6,0},{8,14},{10,12},{12,10},{14,8},{1,7},{3,5},... | collective-permute-start | bytes 147464 | tf_op jit(solution)/shard_map/ppermute | solution.py:996
  39.2 0.5 collective-permute-start.9
  39.8 0.0 collective-permute-done.11
  39.8 3.3 %collective-permute-start.13 = (f32[12,8,128]{2,1,0:T(8,128)S(1)}, f32[12,8,128]{2,1,0:T(8,128)S(1)}, u32[]{:S(2)}, u32[]{:S(2)}) collective-permute-start(f32[12,8,128]{2,1,0:T(8,128)S(1)} %get-tuple-element.54), channel_id=1, source_target_pairs={{0,12},{2,14},{4,8},{6,10},{8,4},{10,6},{12,0},{14,2},{1,13},{3,15... | collective-permute-start | bytes 147464 | tf_op jit(solution)/shard_map/ppermute | solution.py:996
  43.1 0.0 collective-permute-done.12
  43.1 0.2 collective-permute-start.14
  43.4 0.0 all-to-all-done
  43.4 0.0 copy-done.2
  43.4 1.6 %shard_map.100 = f32[8,48,128]{2,1,0:T(8,128)} custom-call(f32[2,8,2,2,8,128]{5,4,3,2,1,0:T(8,128)S(1)} %bitcast.44, f32[8,2,4,128]{3,2,1,0:T(4,128)S(1)} %copy-done.4, f32[640,512]{1,0:T(8,128)S(1)} %copy-done.2), custom_call_target="tpu_custom_call" | custom-call | tf_op jit(solution)/shard_map/pallas_call | solution.py:854
  45.0 0.0 collective-permute-done.10
  45.0 0.0 collective-permute-done.8
  45.0 2.3 %collective-permute-done.9 = f32[12,8,128]{2,1,0:T(8,128)S(1)} collective-permute-done((f32[12,8,128]{2,1,0:T(8,128)S(1)}, f32[12,8,128]{2,1,0:T(8,128)S(1)}, u32[]{:S(2)}, u32[]{:S(2)}) %collective-permute-start.9) | collective-permute-done | bytes 49184 | tf_op jit(solution)/shard_map/ppermute | solution.py:996
  47.4 3.6 %all-to-all-start.1 = ((f32[8,48,128]{2,1,0:T(8,128)}), f32[8,48,128]{2,1,0:T(8,128)S(1)}, u32[]{:S(2)}, u32[]{:S(2)}) async-start(f32[8,48,128]{2,1,0:T(8,128)} %shard_map.100), calls=%async_computation.1 | async-start | bytes 393216 | tf_op jit(solution)/shard_map/all_to_all | solution.py:1021
  51.0 0.0 collective-permute-done.13
  51.1 0.0 collective-permute-done.14
  51.1 3.4 %collective-permute-start.15 = (f32[2,12,8,128]{3,2,1,0:T(8,128)S(1)}, f32[2,12,8,128]{3,2,1,0:T(8,128)S(1)}, u32[]{:S(2)}, u32[]{:S(2)}) collective-permute-start(f32[2,12,8,128]{3,2,1,0:T(8,128)S(1)} %pad_maximum_fusion), channel_id=1, source_target_pairs={{0,16},{1,17},{2,18},{3,19},{4,20},{5,21},{6,22},{7,23},{8,24},{9,... | collective-permute-start | bytes 294920 | tf_op jit(solution)/shard_map/ppermute | solution.py:1020
  54.5 2.2 %collective-permute-done.15.upstream = f32[2,12,8,128]{3,2,1,0:T(8,128)S(1)} collective-permute-done((f32[2,12,8,128]{3,2,1,0:T(8,128)S(1)}, f32[2,12,8,128]{3,2,1,0:T(8,128)S(1)}, u32[]{:S(2)}, u32[]{:S(2)}) %collective-permute-start.15) | collective-permute-done | bytes 98336 | tf_op jit(solution)/shard_map/ppermute | solution.py:1020
  56.7 2.1 %all-to-all-done.1.received = f32[8,48,128]{2,1,0:T(8,128)S(1)} async-done(((f32[8,48,128]{2,1,0:T(8,128)}), f32[8,48,128]{2,1,0:T(8,128)S(1)}, u32[]{:S(2)}, u32[]{:S(2)}) %all-to-all-start.1) | async-done | bytes 196640 | tf_op jit(solution)/shard_map/all_to_all | solution.py:1021
  58.8 0.0 collective-permute-start.16
  58.8 0.6 shard_map.103.blended
  59.4 0.6 shard_map.102.partial
  60.0 0.3 collective-permute-done.16.partner
  60.2 1.3 %shard_map.104 = (f32[3,4,64,128]{3,2,1,0:T(8,128)}, f32[4,64,128]{2,1,0:T(8,128)}) custom-call(f32[384,256]{1,0:T(8,128)S(1)} %shard_map.102.partial, f32[8,48,128]{2,1,0:T(8,128)S(1)} %collective-permute-done.16.partner, f32[2,256,256]{2,1,0:T(8,128)S(1)} %copy-done, f32[3,4,64,128]{3,2,1,0:T(8,128)S(1)} %shard_map.103.blended), custom_call_target="tpu_custom_call" | custom-call | tf_op jit(solution)/shard_map/pallas_call | solution.py:854
  (20 shorter events, 0.1 us)
Async XLA Ops:
  0.6 1.0 %copy-start.1 = (f32[1,3,32,8,128]{4,3,2,1,0:T(8,128)S(1)}, f32[1,3,32,8,128]{4,3,2,1,0:T(8,128)}, u32[]{:S(2)}) copy-start(f32[1,3,32,8,128]{4,3,2,1,0:T(8,128)} %param.8) | copy-start | bytes 1179652
  2.0 11.5 %collective-permute-start.1 = (f32[3,3,4,8,128]{4,3,2,1,0:T(8,128)S(1)}, f32[3,3,4,8,128]{4,3,2,1,0:T(8,128)S(1)}, u32[]{:S(2)}, u32[]{:S(2)}) collective-permute-start(f32[3,3,4,8,128]{4,3,2,1,0:T(8,128)S(1)} %get-tuple-element.33), channel_id=1, source_target_pairs={{0,2},{2,0},{4,6},{6,4},{8,10},{10,8},{12,14},{14,12},{1,3},{3,1},... | collective-permute-start | bytes 442376 | tf_op jit(solution)/shard_map/ppermute | solution.py:903
  5.4 11.9 %collective-permute-start = (f32[8,3,4,8,128]{4,3,2,1,0:T(8,128)S(1)}, f32[8,3,4,8,128]{4,3,2,1,0:T(8,128)S(1)}, u32[]{:S(2)}, u32[]{:S(2)}) collective-permute-start(f32[8,3,4,8,128]{4,3,2,1,0:T(8,128)S(1)} %get-tuple-element.31.own_here), channel_id=1, source_target_pairs={{0,1},{1,0},{2,3},{3,2},{4,5},{5,4},{6,7},{7,6},{8,9},{9,8},{10,11... | collective-permute-start | bytes 1179656 | tf_op jit(solution)/shard_map/ppermute | solution.py:907
  5.5 10.4 %collective-permute-start.3 = (f32[3,3,4,8,128]{4,3,2,1,0:T(8,128)S(1)}, f32[3,3,4,8,128]{4,3,2,1,0:T(8,128)S(1)}, u32[]{:S(2)}, u32[]{:S(2)}) collective-permute-start(f32[3,3,4,8,128]{4,3,2,1,0:T(8,128)S(1)} %get-tuple-element.35), channel_id=1, source_target_pairs={{0,14},{2,4},{4,2},{6,8},{8,6},{10,12},{12,10},{14,0},{1,15},{3,5}... | collective-permute-start | bytes 442376 | tf_op jit(solution)/shard_map/ppermute | solution.py:902
  9.1 11.3 %collective-permute-start.5 = (f32[4,3,4,8,128]{4,3,2,1,0:T(8,128)S(1)}, f32[4,3,4,8,128]{4,3,2,1,0:T(8,128)S(1)}, u32[]{:S(2)}, u32[]{:S(2)}) collective-permute-start(f32[4,3,4,8,128]{4,3,2,1,0:T(8,128)S(1)} %get-tuple-element.36), channel_id=1, source_target_pairs={{0,2},{2,4},{4,6},{6,8},{8,10},{10,12},{12,14},{14,0},{3,1},{5,3},... | collective-permute-start | bytes 589832 | tf_op jit(solution)/shard_map/ppermute | solution.py:926
  13.4 3.2 %collective-permute-start.2 = (f32[3,3,4,8,128]{4,3,2,1,0:T(8,128)S(1)}, f32[3,3,4,8,128]{4,3,2,1,0:T(8,128)S(1)}, u32[]{:S(2)}, u32[]{:S(2)}) collective-permute-start(f32[3,3,4,8,128]{4,3,2,1,0:T(8,128)S(1)} %collective-permute-done.1.across_here), channel_id=1, source_target_pairs={{0,1},{1,0},{2,3},{3,2},{4,5},{5,4},{6,7},{7,6},{8,9},{9,8},{10,11... | collective-permute-start | bytes 442376 | tf_op jit(solution)/shard_map/ppermute | solution.py:910
  13.4 7.9 %collective-permute-start.6 = (f32[4,3,4,8,128]{4,3,2,1,0:T(8,128)S(1)}, f32[4,3,4,8,128]{4,3,2,1,0:T(8,128)S(1)}, u32[]{:S(2)}, u32[]{:S(2)}) collective-permute-start(f32[4,3,4,8,128]{4,3,2,1,0:T(8,128)S(1)} %get-tuple-element.37), channel_id=1, source_target_pairs={{1,2},{3,4},{5,6},{7,8},{9,10},{11,12},{13,14},{15,0},{2,1},{4,3},... | collective-permute-start | bytes 589832 | tf_op jit(solution)/shard_map/ppermute | solution.py:909
  15.9 1.4 %collective-permute-start.4 = (f32[3,3,4,8,128]{4,3,2,1,0:T(8,128)S(1)}, f32[3,3,4,8,128]{4,3,2,1,0:T(8,128)S(1)}, u32[]{:S(2)}, u32[]{:S(2)}) collective-permute-start(f32[3,3,4,8,128]{4,3,2,1,0:T(8,128)S(1)} %collective-permute-done.3.around_here), channel_id=1, source_target_pairs={{0,1},{1,0},{2,3},{3,2},{4,5},{5,4},{6,7},{7,6},{8,9},{9,8},{10,11... | collective-permute-start | bytes 442376 | tf_op jit(solution)/shard_map/ppermute | solution.py:911
  16.6 4.8 %copy-start.6 = (s32[2]{0:T(128)S(1)}, s32[2]{0:T(128)}, u32[]{:S(2)}) copy-start(s32[2]{0:T(128)} %fringe.3) | copy-start | bytes 28
  21.3 4.7 %copy-start.3 = (f32[256,256]{1,0:T(8,128)S(1)}, f32[256,256]{1,0:T(8,128)}, u32[]{:S(2)}) copy-start(f32[256,256]{1,0:T(8,128)} %constant.97.clone.table_y) | copy-start | bytes 786436
  21.3 4.7 %copy-start.5 = (f32[32,32]{1,0:T(8,128)S(1)}, f32[32,32]{1,0:T(8,128)}, u32[]{:S(2)}) copy-start(f32[32,32]{1,0:T(8,128)} %constant.99.clone.table_z) | copy-start | bytes 12292
  24.5 18.9 %copy-start.2 = (f32[640,512]{1,0:T(8,128)S(1)}, f32[640,512]{1,0:T(8,128)}, u32[]{:S(2)}) copy-start(f32[640,512]{1,0:T(8,128)} %constant.96.clone.table) | copy-start | bytes 3932164
  24.5 18.9 %copy-start.4 = (f32[8,2,4,128]{3,2,1,0:T(4,128)S(1)}, f32[8,2,4,128]{3,2,1,0:T(4,128)}, u32[]{:S(2)}) copy-start(f32[8,2,4,128]{3,2,1,0:T(4,128)} %constant.100.clone.waves) | copy-start | bytes 98308
  24.5 7.2 %collective-permute-start.7 = (f32[8,6,8,128]{3,2,1,0:T(8,128)S(1)}, f32[8,6,8,128]{3,2,1,0:T(8,128)S(1)}, u32[]{:S(2)}, u32[]{:S(2)}) collective-permute-start(f32[8,6,8,128]{3,2,1,0:T(8,128)S(1)} %get-tuple-element.43), channel_id=1, source_target_pairs={{0,1},{1,0},{2,3},{3,2},{4,5},{5,4},{6,7},{7,6},{8,9},{9,8},{10,11... | collective-permute-start | bytes 589832 | tf_op jit(solution)/shard_map/ppermute | solution.py:976
  27.6 15.8 %all-to-all-start = ((f32[32,2,8,128]{3,2,1,0:T(8,128)}), f32[32,2,8,128]{3,2,1,0:T(8,128)S(1)}, u32[]{:S(2)}, u32[]{:S(2)}) async-start(f32[32,2,8,128]{3,2,1,0:T(8,128)} %bitcast.9), calls=%async_computation | async-start | bytes 524288 | tf_op jit(solution)/shard_map/all_to_all | solution.py:985
  32.1 7.7 %collective-permute-start.11 = (f32[12,8,128]{2,1,0:T(8,128)S(1)}, f32[12,8,128]{2,1,0:T(8,128)S(1)}, u32[]{:S(2)}, u32[]{:S(2)}) collective-permute-start(f32[12,8,128]{2,1,0:T(8,128)S(1)} %get-tuple-element.49), channel_id=1, source_target_pairs={{0,2},{2,0},{4,6},{6,4},{8,10},{10,8},{12,14},{14,12},{1,3},{3,1},... | collective-permute-start | bytes 147464 | tf_op jit(solution)/shard_map/ppermute | solution.py:996
  33.9 9.2 %collective-permute-start.12 = (f32[12,8,128]{2,1,0:T(8,128)S(1)}, f32[12,8,128]{2,1,0:T(8,128)S(1)}, u32[]{:S(2)}, u32[]{:S(2)}) collective-permute-start(f32[12,8,128]{2,1,0:T(8,128)S(1)} %get-tuple-element.50), channel_id=1, source_target_pairs={{0,4},{2,6},{4,0},{6,2},{8,12},{10,14},{12,8},{14,10},{1,5},{3,7},... | collective-permute-start | bytes 147464 | tf_op jit(solution)/shard_map/ppermute | solution.py:996
  35.4 9.6 %collective-permute-start.10 = (f32[12,8,128]{2,1,0:T(8,128)S(1)}, f32[12,8,128]{2,1,0:T(8,128)S(1)}, u32[]{:S(2)}, u32[]{:S(2)}) collective-permute-start(f32[12,8,128]{2,1,0:T(8,128)S(1)} %get-tuple-element.46), channel_id=1, source_target_pairs={{0,10},{2,8},{4,14},{6,12},{8,2},{10,0},{12,6},{14,4},{1,11},{3,9}... | collective-permute-start | bytes 147464 | tf_op jit(solution)/shard_map/ppermute | solution.py:996
  37.8 7.2 %collective-permute-start.8 = (f32[12,8,128]{2,1,0:T(8,128)S(1)}, f32[12,8,128]{2,1,0:T(8,128)S(1)}, u32[]{:S(2)}, u32[]{:S(2)}) collective-permute-start(f32[12,8,128]{2,1,0:T(8,128)S(1)} %get-tuple-element.44), channel_id=1, source_target_pairs={{0,6},{2,4},{4,2},{6,0},{8,14},{10,12},{12,10},{14,8},{1,7},{3,5},... | collective-permute-start | bytes 147464 | tf_op jit(solution)/shard_map/ppermute | solution.py:996
  39.2 8.1 %collective-permute-start.9 = (f32[12,8,128]{2,1,0:T(8,128)S(1)}, f32[12,8,128]{2,1,0:T(8,128)S(1)}, u32[]{:S(2)}, u32[]{:S(2)}) collective-permute-start(f32[12,8,128]{2,1,0:T(8,128)S(1)} %get-tuple-element.45), channel_id=1, source_target_pairs={{0,8},{2,10},{4,12},{6,14},{8,0},{10,2},{12,4},{14,6},{1,9},{3,11}... | collective-permute-start | bytes 147464 | tf_op jit(solution)/shard_map/ppermute | solution.py:996
  39.8 11.3 %collective-permute-start.13 = (f32[12,8,128]{2,1,0:T(8,128)S(1)}, f32[12,8,128]{2,1,0:T(8,128)S(1)}, u32[]{:S(2)}, u32[]{:S(2)}) collective-permute-start(f32[12,8,128]{2,1,0:T(8,128)S(1)} %get-tuple-element.54), channel_id=1, source_target_pairs={{0,12},{2,14},{4,8},{6,10},{8,4},{10,6},{12,0},{14,2},{1,13},{3,15... | collective-permute-start | bytes 147464 | tf_op jit(solution)/shard_map/ppermute | solution.py:996
  43.1 7.9 %collective-permute-start.14 = (f32[12,8,128]{2,1,0:T(8,128)S(1)}, f32[12,8,128]{2,1,0:T(8,128)S(1)}, u32[]{:S(2)}, u32[]{:S(2)}) collective-permute-start(f32[12,8,128]{2,1,0:T(8,128)S(1)} %get-tuple-element.55), channel_id=1, source_target_pairs={{0,14},{2,12},{4,10},{6,8},{8,6},{10,4},{12,2},{14,0},{1,15},{3,13... | collective-permute-start | bytes 147464 | tf_op jit(solution)/shard_map/ppermute | solution.py:996
  45.0 14.4 %copy-start = (f32[2,256,256]{2,1,0:T(8,128)S(1)}, f32[2,256,256]{2,1,0:T(8,128)}, u32[]{:S(2)}) copy-start(f32[2,256,256]{2,1,0:T(8,128)} %constant.98.clone.table_y) | copy-start | bytes 1572868
  47.4 11.4 %all-to-all-start.1 = ((f32[8,48,128]{2,1,0:T(8,128)}), f32[8,48,128]{2,1,0:T(8,128)S(1)}, u32[]{:S(2)}, u32[]{:S(2)}) async-start(f32[8,48,128]{2,1,0:T(8,128)} %shard_map.100), calls=%async_computation.1 | async-start | bytes 393216 | tf_op jit(solution)/shard_map/all_to_all | solution.py:1021
  51.1 5.6 %collective-permute-start.15 = (f32[2,12,8,128]{3,2,1,0:T(8,128)S(1)}, f32[2,12,8,128]{3,2,1,0:T(8,128)S(1)}, u32[]{:S(2)}, u32[]{:S(2)}) collective-permute-start(f32[2,12,8,128]{3,2,1,0:T(8,128)S(1)} %pad_maximum_fusion), channel_id=1, source_target_pairs={{0,16},{1,17},{2,18},{3,19},{4,20},{5,21},{6,22},{7,23},{8,24},{9,... | collective-permute-start | bytes 294920 | tf_op jit(solution)/shard_map/ppermute | solution.py:1020
  58.8 1.4 %collective-permute-start.16 = (f32[8,48,128]{2,1,0:T(8,128)S(1)}, f32[8,48,128]{2,1,0:T(8,128)S(1)}, u32[]{:S(2)}, u32[]{:S(2)}) collective-permute-start(f32[8,48,128]{2,1,0:T(8,128)S(1)} %all-to-all-done.1.received), channel_id=1, source_target_pairs={{0,1},{1,0},{2,3},{3,2},{4,5},{5,4},{6,7},{7,6},{8,9},{9,8},{10,11... | collective-permute-start | bytes 589832 | tf_op jit(solution)/shard_map/ppermute | solution.py:1023
